TPU v7x, 128 devices: a whole 4x4x4 slice. The times are simulated.
128 devices in a mesh: slot: 4 (over x_hi, core), horiz: 32 (over x_lo, z, y).
Axes of the slice: x: 4 (x_hi: 2, x_lo: 2; x = x_hi * 2 + x_lo), y: 4, z: 4, core: 2. Of those that a mesh axis runs over, the one named last changes fastest.
Arguments:
- control: bfloat16 [32, 80, 64, 512], P(None, None, 'horiz'), may hold values from -6 to 6
- land_mask: int32 [80, 64, 512], P(None, 'horiz'), may hold values 0 or 1
- tile_id: int32 [16, 128], replicated, may hold values from 0 to 15
- tile_scale: float32 [16, 80], replicated, may hold values from 0.3 to 3
- inverse_x: bfloat16 [512, 512], replicated
- inverse_y: bfloat16 [64, 64], replicated
- inverse_z: bfloat16 [80, 80], replicated
- perturbations: bfloat16 [4, 32, 80, 64, 512], P('slot', None, None, 'horiz'), may hold values from -6 to 6
- obs_cell: int32 [4, 262144], P('slot', 'horiz'), may hold values from 0 to 81919
- obs_value: float32 [4, 262144], P('slot', 'horiz'), may hold values from -6 to 6
- obs_weight: float32 [4, 262144], P('slot', 'horiz'), may hold values from 1 to 8
Outputs:
- gradient: bfloat16 [32, 80, 64, 512], P(None, None, 'horiz')
Inputs may be any that keep to these rules, and one draw needn't show every extreme that they name: obs_cell[s, j] indexes the cells of tile j // 8192 (rows j // 8192 * 2 onward), level-major, then row, then column.
All inputs are finite; a program needn't handle non-finite values. No bound on the sum of `land_mask` on one device may be relied on, other than what follows from the above.
Results may differ from a plain program's by a relative error of at most 0.006.
Values may be sent and summed in bfloat16 or wider, within the bound.
No kernel may reach another device: no remote copies, remote signals or barrier semaphores. Data moves between devices by JAX's collectives and lax.ppermute only.
A program may use at most 192 MiB of HBM per device.

v0:
```python
import math

import jax
import jax.numpy as jnp
from jax import lax
from jax.sharding import PartitionSpec as P


def local_sigma(tile_id, tile_scale, dev_index, row_count):
    regions = tile_scale.shape[0]
    tile_rows = max(row_count // 4, 1)
    picked = lax.dynamic_slice_in_dim(tile_id, dev_index * row_count // 4, tile_rows, 0)
    onehot = (picked[None] == jnp.arange(regions, dtype=jnp.int32)[:, None, None]).astype(
        jnp.float32
    )
    scale_table = jnp.einsum("rz,rab->zab", tile_scale, onehot, precision=lax.Precision.HIGHEST)
    expanded = jnp.repeat(scale_table, 4, axis=1)
    expanded = lax.dynamic_slice_in_dim(expanded, dev_index * row_count % 4, row_count, 1)
    return jnp.repeat(expanded, 4, axis=2)


def columns_filter(received, inverse_y, inverse_z):
    across = jnp.einsum(
        "mzyx,yk->mzkx", received, inverse_y, preferred_element_type=jnp.float32
    ).astype(jnp.bfloat16)
    return jnp.einsum(
        "mzyx,zk->mkyx", across, inverse_z, preferred_element_type=jnp.float32
    ).astype(jnp.bfloat16)


def forward_filter(control, sea_mask, mask_half, weight_mask, inverse_x, inverse_y, inverse_z):
    masked = (weight_mask * control.astype(jnp.float32)).astype(jnp.bfloat16)
    along_x = (sea_mask * jnp.dot(masked, inverse_x, preferred_element_type=jnp.float32)).astype(
        jnp.bfloat16
    )
    deeper = columns_filter(
        lax.all_to_all(along_x, "horiz", split_axis=3, concat_axis=2, tiled=True),
        inverse_y,
        inverse_z,
    )
    returned = lax.all_to_all(deeper, "horiz", split_axis=2, concat_axis=3, tiled=True)
    return returned * mask_half


def adjoint_filter(slot_sum, sea_mask, weight_mask, inverse_x, inverse_y, inverse_z):
    back_first = (sea_mask * slot_sum).astype(jnp.bfloat16)
    back_deep = jnp.einsum(
        "mkyx,zk->mzyx",
        lax.all_to_all(back_first, "horiz", split_axis=3, concat_axis=2, tiled=True),
        inverse_z,
        preferred_element_type=jnp.float32,
    ).astype(jnp.bfloat16)
    back_across = jnp.einsum(
        "mzkx,yk->mzyx", back_deep, inverse_y, preferred_element_type=jnp.float32
    ).astype(jnp.bfloat16)
    returned = lax.all_to_all(back_across, "horiz", split_axis=2, concat_axis=3, tiled=True)
    along_x = lax.dot_general(
        returned * sea_mask.astype(jnp.bfloat16),
        inverse_x,
        (((3,), (1,)), ((), ())),
        preferred_element_type=jnp.float32,
    )
    return weight_mask * along_x


def observe(increment, cells, values, weights):
    flat_inc = increment.reshape(-1)
    misfit = weights * (flat_inc[cells] - values)
    return jnp.zeros(flat_inc.shape, jnp.float32).at[cells].add(misfit).reshape(increment.shape)


def per_device(
    control,
    land_mask,
    tile_id,
    tile_scale,
    inverse_x,
    inverse_y,
    inverse_z,
    perturbations,
    obs_cell,
    obs_value,
    obs_weight,
):
    members, levels, row_count, col_count = control.shape
    dev_index = lax.axis_index("horiz")
    sea_mask = land_mask.astype(jnp.float32)
    mask_half = land_mask.astype(jnp.bfloat16)
    weight_mask = sea_mask * local_sigma(tile_id, tile_scale, dev_index, row_count)
    spread_w = forward_filter(
        control, sea_mask, mask_half, weight_mask, inverse_x, inverse_y, inverse_z
    )
    norm_scale = 1.0 / math.sqrt(members)
    perturbed = perturbations[0]
    increment = (
        jnp.einsum("mzyx,mzyx->zyx", perturbed, spread_w, preferred_element_type=jnp.float32)
        * norm_scale
    )
    adjoint_obs = observe(increment, obs_cell[0], obs_value[0], obs_weight[0])
    summed = perturbed * (adjoint_obs * norm_scale)[None]
    slot_sum = lax.psum(summed.astype(jnp.bfloat16), "slot").astype(jnp.float32)
    filtered = adjoint_filter(slot_sum, sea_mask, weight_mask, inverse_x, inverse_y, inverse_z)
    gradient = (control.astype(jnp.float32) + filtered).astype(jnp.bfloat16)
    return gradient


def solution(mesh):
    return jax.shard_map(
        per_device,
        mesh=mesh,
        in_specs=(
            P(None, None, "horiz", None),
            P(None, "horiz", None),
            P(),
            P(),
            P(),
            P(),
            P(),
            P("slot", None, None, "horiz", None),
            P("slot", "horiz"),
            P("slot", "horiz"),
            P("slot", "horiz"),
        ),
        out_specs=P(None, None, "horiz", None),
        check_vma=False,
    )
```

profile of v0, /device:TPU:37, one launch (start us, length us, event | category | flops | bytes accessed | tf_op | source)
XLA Modules:
  0.0 916.8 jit_solution(15047967145024313417)
XLA Ops:
  18.4 19.1 %copy.42 = bf16[32,80,2,512]{1,2,0,3:T(2,128)(2,1)} copy(bf16[32,80,2,512]{3,1,2,0:T(8,128)(2,1)} %multiply_convert_fusion.2) | data formatting | bytes 10485760 | tf_op jit(solution)/shard_map/convert_element_type | solution.py:33
  37.5 100.6 %all_to_all.72 = bf16[32,80,2,512]{1,2,0,3:T(2,128)(2,1)} all-to-all(bf16[32,80,2,512]{1,2,0,3:T(2,128)(2,1)} %copy.42), channel_id=1, replica_groups=mesh['slot'=4,'horiz'=32] {'horiz'}, dimensions={3} | all-to-all | bytes 10485760 | tf_op jit(solution)/shard_map/all_to_all | solution.py:37
  138.1 16.3 %copy.43 = bf16[32,80,2,512]{1,3,2,0:T(8,128)(2,1)} copy(bf16[32,80,2,512]{1,2,0,3:T(2,128)(2,1)} %all_to_all.72) | data formatting | bytes 10485760 | tf_op jit(solution)/shard_map/all_to_all | solution.py:37
  154.4 8.3 copy.44
  162.8 10.2 %convert_bitcast_fusion.1 = bf16[32,80,64,16]{1,2,3,0:T(8,128)(2,1)} fusion(bf16[32,80,64,16]{1,3,2,0:T(8,128)(2,1)} %bitcast.83, bf16[80,80]{1,0:T(8,128)(2,1)S(1)} %copy-done.1, bf16[64,64]{1,0:T(8,128)(2,1)S(1)} %copy-done.2), kind=kOutput, calls=%fused_computation.23 | convolution fusion | flops 760217600 | bytes 10506752 | tf_op jit(solution)/shard_map/mzyx,zk->mkyx/dot_general | solution.py:26
  173.0 12.0 %copy.47 = bf16[32,80,64,16]{1,3,0,2:T(8,128)(2,1)} copy(bf16[32,80,64,16]{1,2,3,0:T(8,128)(2,1)} %convert_bitcast_fusion.1) | data formatting | bytes 10485760 | tf_op jit(solution)/shard_map/convert_element_type | solution.py:28
  185.0 8.5 all-to-all-start.1
  194.2 120.7 %all-to-all-done.1 = bf16[32,80,64,16]{1,3,0,2:T(8,128)(2,1)} async-done(((bf16[32,80,64,16]{1,3,0,2:T(8,128)(2,1)}), bf16[32,80,64,16]{1,3,0,2:T(8,128)(2,1)}, u32[]{:S(2)}, u32[]{:S(2)}) %all-to-all-start.1) | async-done | bytes 5242912 | tf_op jit(solution)/shard_map/all_to_all | solution.py:41
  314.9 9.0 copy.48
  323.9 10.2 %bitcast_convert_fusion = f32[80,2,512,32]{0,2,1,3:T(8,128)} fusion(bf16[80,2,512]{0,2,1:T(8,128)(2,1)S(1)} %copy.49, bf16[32,80,32,2,16]{1,4,2,3,0:T(8,128)(2,1)} %copy.48), kind=kLoop, calls=%fused_computation.16 | loop fusion | flops 5242880 | bytes 15892480
  334.1 14.6 %copy.68 = f32[80,2,512,32]{2,0,1,3:T(8,128)} copy(f32[80,2,512,32]{0,2,1,3:T(8,128)} %bitcast_convert_fusion) | data formatting | bytes 20971520
  356.7 45.5 %gather_fusion = f32[8192]{0:T(1024)S(1)} fusion(f32[81920]{0:T(1024)S(1)} %bitcast.82, s32[8192]{0:T(1024)S(1)} %broadcast_clamp_fusion), kind=kCustom, calls=%fused_computation | custom fusion | bytes 98304 | tf_op jit(solution)/shard_map/gather | solution.py:68
  402.2 43.3 %scatter_custom_fusion = f32[81920]{0:T(1024)S(1)} fusion(s32[8192]{0:T(1024)S(1)} %bitcast.90, f32[8192]{0:T(1024)S(1)} %subtract_multiply_fusion, f32[]{:T(128)} %constant.33.clone.1), kind=kCustom, calls=%fused_computation.35 | custom fusion | flops 8192 | bytes 327684 | tf_op jit(solution)/shard_map/scatter-add | solution.py:69
  452.1 117.7 %all-reduce.2.cloned.1.call-done = bf16[32,80,2,512]{3,1,2,0:T(8,128)(2,1)} async-done(((bf16[32,80,2,512]{3,1,2,0:T(8,128)(2,1)}), bf16[32,80,2,512]{3,1,2,0:T(8,128)(2,1)}) %all-reduce.2.cloned.1.call-update) | async-done | bytes 5242896 | tf_op jit(solution)/shard_map/psum | solution.py:101
  576.1 19.1 %copy.51 = bf16[32,80,2,512]{1,2,0,3:T(2,128)(2,1)} copy(bf16[32,80,2,512]{3,1,2,0:T(8,128)(2,1)} %multiply_convert_fusion) | data formatting | bytes 10485760 | tf_op jit(solution)/shard_map/convert_element_type | solution.py:46
  595.2 101.3 %all_to_all.73 = bf16[32,80,2,512]{1,2,0,3:T(2,128)(2,1)} all-to-all(bf16[32,80,2,512]{1,2,0,3:T(2,128)(2,1)} %copy.51), channel_id=1, replica_groups=mesh['slot'=4,'horiz'=32] {'horiz'}, dimensions={3} | all-to-all | bytes 10485760 | tf_op jit(solution)/shard_map/all_to_all | solution.py:49
  696.6 16.3 %copy.52 = bf16[32,80,2,512]{1,3,2,0:T(8,128)(2,1)} copy(bf16[32,80,2,512]{1,2,0,3:T(2,128)(2,1)} %all_to_all.73) | data formatting | bytes 10485760 | tf_op jit(solution)/shard_map/all_to_all | solution.py:49
  712.9 8.3 copy.53
  721.2 9.3 %convert_bitcast_fusion = bf16[32,80,64,16]{1,2,3,0:T(8,128)(2,1)} fusion(bf16[32,80,64,16]{1,3,2,0:T(8,128)(2,1)} %bitcast.84, bf16[80,80]{1,0:T(8,128)(2,1)S(1)} %copy-done.1, bf16[64,64]{1,0:T(8,128)(2,1)S(1)} %copy-done.2), kind=kOutput, calls=%fused_computation.21 | convolution fusion | flops 760217600 | bytes 10506752 | tf_op jit(solution)/shard_map/mzkx,yk->mzyx/dot_general | solution.py:53
  730.5 12.0 %copy.55 = bf16[32,80,64,16]{1,3,0,2:T(8,128)(2,1)} copy(bf16[32,80,64,16]{1,2,3,0:T(8,128)(2,1)} %convert_bitcast_fusion) | data formatting | bytes 10485760 | tf_op jit(solution)/shard_map/convert_element_type | solution.py:55
  750.4 122.1 %all-to-all-done.3 = bf16[32,80,64,16]{1,3,0,2:T(8,128)(2,1)} async-done(((bf16[32,80,64,16]{1,3,0,2:T(8,128)(2,1)}), bf16[32,80,64,16]{1,3,0,2:T(8,128)(2,1)}, u32[]{:S(2)}, u32[]{:S(2)}) %all-to-all-start.3) | async-done | bytes 5242912 | tf_op jit(solution)/shard_map/all_to_all | solution.py:56
  872.5 9.0 copy.56
  888.9 10.6 %fusion.1 = bf16[32,80,2,512]{3,1,2,0:T(8,128)(2,1)} fusion(f32[80,2,512]{2,0,1:T(8,128)S(1)} %copy.39, bf16[32,80,2,512]{3,2,1,0:T(2,128)(2,1)} %param.11, bf16[32,80,2,512]{1,3,2,0:T(8,128)(2,1)} %bitcast_multiply_fusion, bf16[512,512]{1,0:T(8,128)(2,1)S(1)} %copy-done), kind=kOutput, calls=%fused_computation.5 | convolution fusion | flops 2694840320 | bytes 16580608 | tf_op jit(solution)/shard_map/dot_general | solution.py:57
  899.5 10.2 %copy.59 = bf16[32,80,2,512]{3,2,1,0:T(2,128)(2,1)} copy(bf16[32,80,2,512]{3,1,2,0:T(8,128)(2,1)} %fusion.1) | data formatting | bytes 10485760 | tf_op jit(solution)/shard_map/convert_element_type | solution.py:103
  (40 shorter events, 48.6 us)
Async XLA Ops:
  6.5 4.6 copy-start
  154.4 8.4 copy-start.1
  154.4 8.4 copy-start.2
  185.0 9.2 copy-start.3
  185.0 129.9 %all-to-all-start.1 = ((bf16[32,80,64,16]{1,3,0,2:T(8,128)(2,1)}), bf16[32,80,64,16]{1,3,0,2:T(8,128)(2,1)}, u32[]{:S(2)}, u32[]{:S(2)}) async-start(bf16[32,80,64,16]{1,3,0,2:T(8,128)(2,1)} %copy.47), calls=%async_computation.1 | async-start | bytes 16777216 | tf_op jit(solution)/shard_map/all_to_all | solution.py:41
  193.4 376.4 %all-reduce.2.cloned.1.call-start = ((), (), s32[]{:S(2)}) async-start(), calls=%async_computation.4 | async-start | bytes 10485760 | tf_op jit(solution)/shard_map/psum | solution.py:101
  356.6 45.6 %copy-start.4 = (f32[1,8192]{1,0:T(1,128)S(1)}, f32[1,8192]{1,0:T(1,128)}, u32[]{:S(2)}) copy-start(f32[1,8192]{1,0:T(1,128)} %param.21) | copy-start | bytes 98308
  356.7 45.6 %copy-start.5 = (f32[1,8192]{1,0:T(1,128)S(1)}, f32[1,8192]{1,0:T(1,128)}, u32[]{:S(2)}) copy-start(f32[1,8192]{1,0:T(1,128)} %param.20) | copy-start | bytes 98308
  742.5 130.0 %all-to-all-start.3 = ((bf16[32,80,64,16]{1,3,0,2:T(8,128)(2,1)}), bf16[32,80,64,16]{1,3,0,2:T(8,128)(2,1)}, u32[]{:S(2)}, u32[]{:S(2)}) async-start(bf16[32,80,64,16]{1,3,0,2:T(8,128)(2,1)} %copy.55), calls=%async_computation.3 | async-start | bytes 16777216 | tf_op jit(solution)/shard_map/all_to_all | solution.py:56
Sparse Core Ops, SparseCore 0:
  452.2 117.5 all-reduce.1
where the time goes:
time: 929 us; the launch traced here: 917 us
  waiting for transfers between devices  360 us (39%)
  local copies, waits for them, and re-layouts  202 us (22%)
  blocking collectives  202 us (22%)
  other arithmetic  83.5 us (9%)
  matrix products  38.2 us (4%)
  starting transfers between devices  16.7 us (2%)
  between operations  13.9 us (1%)
    all_to_all x1, waiting for transfers between devices, adjoint_filter(): lax.all_to_all(back_across, 'horiz', split_axis=2, concat_axis=3, tiled=T...  122 us
    all_to_all x1, waiting for transfers between devices, forward_filter(): lax.all_to_all(deeper, 'horiz', split_axis=2, concat_axis=3, tiled=True)  121 us
    psum x1, waiting for transfers between devices, per_device(): slot_sum = lax.psum(summed.astype(jnp.bfloat16), 'slot').astype(jnp.float32)  118 us
    all_to_all x1, blocking collectives, adjoint_filter(): lax.all_to_all(back_first, 'horiz', split_axis=3, concat_axis=2, tiled=True)  101 us
    all_to_all x1, blocking collectives, forward_filter(): lax.all_to_all(along_x, 'horiz', split_axis=3, concat_axis=2, tiled=True)  101 us
    gather x1, local copies, waits for them, and re-layouts, observe(): misfit = weights * (flat_inc[cells] - values)  45.5 us
    scatter-add x1, other arithmetic, observe(): jnp.zeros(flat_inc.shape, jnp.float32).at[cells].add(misfit)  43.3 us
    all_to_all x2, local copies, waits for them, and re-layouts, forward_filter(): lax.all_to_all(along_x, 'horiz', split_axis=3, concat_axis=2, tiled=True)  24.6 us
  transfers between devices with their start and end apart: 3, of which 3 were waited for; matrix products, arithmetic and copies ran while one was open for 0% of the time, Pallas kernels for 0%

commit v1 on v0

v1 whole, which is shorter than its diff:
```python
import math

import jax
import jax.numpy as jnp
from jax import lax
from jax.experimental import pallas as pl
from jax.experimental.pallas import tpu as pltpu
from jax.sharding import PartitionSpec as P

OBS_BLOCK = 1024


def local_sigma(tile_id, tile_scale, dev_index, row_count):
    regions = tile_scale.shape[0]
    tile_rows = max(row_count // 4, 1)
    picked = lax.dynamic_slice_in_dim(tile_id, dev_index * row_count // 4, tile_rows, 0)
    onehot = (picked[None] == jnp.arange(regions, dtype=jnp.int32)[:, None, None]).astype(
        jnp.float32
    )
    scale_table = jnp.einsum("rz,rab->zab", tile_scale, onehot, precision=lax.Precision.HIGHEST)
    expanded = jnp.repeat(scale_table, 4, axis=1)
    expanded = lax.dynamic_slice_in_dim(expanded, dev_index * row_count % 4, row_count, 1)
    return jnp.repeat(expanded, 4, axis=2)


def obs_kernel(cell_ref, value_ref, weight_ref, out_ref):
    @pl.when(pl.program_id(0) == 0)
    def _():
        out_ref[...] = jnp.zeros_like(out_ref)

    cell = cell_ref[...]
    weight = weight_ref[...]
    weighted = weight * value_ref[...]
    count = cell.shape[1]
    rows = out_ref.shape[0]
    levels = rows // 8
    row = (((cell >> 7) & 3) * 2 + ((cell >> 9) & 1)) * levels + (cell >> 10)
    row_hot = lax.broadcasted_iota(jnp.int32, (rows, count), 0) == row
    lane_hot = lax.broadcasted_iota(jnp.int32, (128, count), 0) == (cell & 127)
    parts = []
    for value in (weight, weighted):
        high = value.astype(jnp.bfloat16).astype(jnp.float32)
        for part in (high, value - high):
            parts.append(jnp.where(lane_hot, part, 0.0).astype(jnp.bfloat16))
    spread = jnp.concatenate(parts, axis=0)
    out_ref[...] += lax.dot_general(
        jnp.where(row_hot, 1.0, 0.0).astype(jnp.bfloat16),
        spread,
        (((1,), (1,)), ((), ())),
        preferred_element_type=jnp.float32,
    )


def obs_fields(cells, values, weights, levels):
    count = cells.shape[1]
    rows = levels * 8
    block = pl.BlockSpec((1, OBS_BLOCK), lambda i: (0, i))
    table = pl.pallas_call(
        obs_kernel,
        grid=(count // OBS_BLOCK,),
        in_specs=[block, block, block],
        out_specs=pl.BlockSpec((rows, 512), lambda i: (0, 0)),
        out_shape=jax.ShapeDtypeStruct((rows, 512), jnp.float32),
        compiler_params=pltpu.CompilerParams(vmem_limit_bytes=32 << 20),
        cost_estimate=pl.CostEstimate(
            flops=2 * rows * 512 * count, bytes_accessed=rows * 512 * 4, transcendentals=0
        ),
    )(cells, values, weights)
    weight_sum = table[:, :128] + table[:, 128:256]
    value_sum = table[:, 256:384] + table[:, 384:]
    return weight_sum.reshape(4, 2, levels, 128), value_sum.reshape(4, 2, levels, 128)


def to_tiles(field):
    lead = field.shape[:-3]
    levels, rows, cols = field.shape[-3:]
    split = field.reshape(*lead, levels, rows, cols // 128, 128)
    n = len(lead)
    return split.transpose(*range(n), n + 2, n + 1, n, n + 3)


def from_tiles(field):
    lead = field.shape[:-4]
    tiles, rows, levels, lanes = field.shape[-4:]
    n = len(lead)
    return field.transpose(*range(n), n + 2, n + 1, n, n + 3).reshape(
        *lead, levels, rows, tiles * lanes
    )


def swap_columns(tiles):
    shape = tiles.shape
    flat = tiles.reshape(shape[0] * shape[1], *shape[2:])
    return lax.all_to_all(flat, "horiz", split_axis=0, concat_axis=0, tiled=True).reshape(shape)


def swap_slot(arr, k):
    return lax.ppermute(arr, "slot", [(i, i ^ k) for i in range(4)])


def per_device(
    control,
    land_mask,
    tile_id,
    tile_scale,
    inverse_x,
    inverse_y,
    inverse_z,
    perturbations,
    obs_cell,
    obs_value,
    obs_weight,
):
    members, levels, row_count, col_count = control.shape
    own = members // 4
    slot = lax.axis_index("slot")
    dev_index = lax.axis_index("horiz")
    norm_scale = 1.0 / math.sqrt(members)
    perturbed = perturbations[0]

    def group(k):
        return lax.dynamic_slice_in_dim(perturbed, (slot ^ k) * own, own, 0)

    pert = [group(0)] + [swap_slot(group(k), k) for k in (1, 2, 3)]

    weight_sum, value_sum = obs_fields(obs_cell, obs_value, obs_weight, levels)

    sea_mask = land_mask.astype(jnp.float32)
    weight_mask = sea_mask * local_sigma(tile_id, tile_scale, dev_index, row_count)
    sea_tiles = to_tiles(land_mask.astype(jnp.bfloat16))

    mine = lax.dynamic_slice_in_dim(control, slot * own, own, 0)
    masked = (weight_mask * mine.astype(jnp.float32)).astype(jnp.bfloat16)
    along_x = (sea_mask * jnp.dot(masked, inverse_x, preferred_element_type=jnp.float32)).astype(
        jnp.bfloat16
    )
    received = swap_columns(to_tiles(along_x)).reshape(-1, levels, 128)
    across = jnp.einsum(
        "yzx,yk->kzx", received, inverse_y, preferred_element_type=jnp.float32
    ).astype(jnp.bfloat16)
    deeper = jnp.einsum(
        "kzx,zw->kwx", across, inverse_z, preferred_element_type=jnp.float32
    ).astype(jnp.bfloat16)
    tile_shape = (own, col_count // 128, row_count, levels, 128)
    spread_w = (swap_columns(deeper.reshape(tile_shape)) * sea_tiles).astype(jnp.float32)

    pert = [to_tiles(p) for p in pert]
    partial = [jnp.sum(p.astype(jnp.float32) * spread_w, axis=0) for p in pert]
    got = swap_slot(jnp.stack([partial[1], partial[3]]).astype(jnp.bfloat16), 1).astype(jnp.float32)
    far = swap_slot((partial[2] + got[1]).astype(jnp.bfloat16), 2).astype(jnp.float32)
    increment = (partial[0] + got[0] + far) * norm_scale
    adjoint = ((weight_sum * increment - value_sum) * norm_scale).astype(jnp.bfloat16)
    pair = jnp.stack([adjoint, swap_slot(adjoint, 2)])
    other = swap_slot(pair, 1)
    fields = [pair[0], other[0], pair[1], other[1]]
    slot_sum = sum(
        p.astype(jnp.float32) * f.astype(jnp.float32)[None] for p, f in zip(pert, fields)
    )
    back_first = slot_sum.astype(jnp.bfloat16) * sea_tiles

    received = swap_columns(back_first).reshape(-1, levels, 128)
    back_deep = jnp.einsum(
        "kwx,zw->kzx", received, inverse_z, preferred_element_type=jnp.float32
    ).astype(jnp.bfloat16)
    back_across = jnp.einsum(
        "kzx,yk->yzx", back_deep, inverse_y, preferred_element_type=jnp.float32
    ).astype(jnp.bfloat16)
    returned = from_tiles(swap_columns(back_across.reshape(tile_shape)) * sea_tiles)
    filtered = weight_mask * lax.dot_general(
        returned, inverse_x, (((3,), (1,)), ((), ())), preferred_element_type=jnp.float32
    )
    gradient = (mine.astype(jnp.float32) + filtered).astype(jnp.bfloat16)

    half = swap_slot(gradient, 2)
    both = jnp.stack([gradient, half])
    other = swap_slot(both, 1)
    result = jnp.zeros(control.shape, jnp.bfloat16)
    for k, part in enumerate((gradient, other[0], half, other[1])):
        result = lax.dynamic_update_slice_in_dim(result, part, (slot ^ k) * own, 0)
    return result


def solution(mesh):
    return jax.shard_map(
        per_device,
        mesh=mesh,
        in_specs=(
            P(None, None, "horiz", None),
            P(None, "horiz", None),
            P(),
            P(),
            P(),
            P(),
            P(),
            P("slot", None, None, "horiz", None),
            P("slot", "horiz"),
            P("slot", "horiz"),
            P("slot", "horiz"),
        ),
        out_specs=P(None, None, "horiz", None),
        check_vma=False,
    )
```

time: 929 us -> 263 us (0.28)
  the two profiles are of different devices: /device:TPU:37 before, /device:TPU:1 now
where the time goes in v1:
time: 263 us; the launch traced here: 259 us
  waiting for transfers between devices  83 us (32%)
  blocking collectives  56.8 us (22%)
  local copies, waits for them, and re-layouts  47.4 us (18%)
  starting transfers between devices  35 us (13%)
  other arithmetic  20.6 us (8%)
  matrix products  8.12 us (3%)
  Pallas kernels  7.24 us (3%)
    ppermute x9, waiting for transfers between devices, swap_slot(): return lax.ppermute(arr, 'slot', [(i, i ^ k) for i in range(4)])  69.2 us
    all_to_all x2, blocking collectives, swap_columns(): lax.all_to_all(flat, 'horiz', split_axis=0, concat_axis=0, tiled=True)  56.8 us
    ppermute x9, starting transfers between devices, swap_slot(): return lax.ppermute(arr, 'slot', [(i, i ^ k) for i in range(4)])  17.9 us
    all_to_all x2, starting transfers between devices, swap_columns(): lax.all_to_all(flat, 'horiz', split_axis=0, concat_axis=0, tiled=True)  17.1 us
    all_to_all x2, waiting for transfers between devices, swap_columns(): lax.all_to_all(flat, 'horiz', split_axis=0, concat_axis=0, tiled=True)  13.7 us
    convert_element_type x3, local copies, waits for them, and re-layouts, per_device(): partial = [jnp.sum(p.astype(jnp.float32) * spread_w, axis=0) for p in pert]  11 us
    dynamic_update_slice x4, local copies, waits for them, and re-layouts, per_device(): result = lax.dynamic_update_slice_in_dim(result, part, (slot ^ k) * own, 0)  9.62 us
    dynamic_slice x1, other arithmetic, group(): return lax.dynamic_slice_in_dim(perturbed, (slot ^ k) * own, own, 0)  8.11 us
  transfers between devices with their start and end apart: 11, of which 8 were waited for; matrix products, arithmetic and copies ran while one was open for 16% of the time, Pallas kernels for 3%

profile of v1, /device:TPU:1, one launch (start us, length us, event | category | flops | bytes accessed | tf_op | source)
XLA Modules:
  0.0 258.6 jit_solution(17198709955304473732)
XLA Ops:
  8.4 9.8 %all-to-all-start = ((bf16[32,2,80,128]{3,2,1,0:T(8,128)(2,1)}), bf16[32,2,80,128]{3,2,1,0:T(8,128)(2,1)S(1)}, u32[]{:S(2)}, u32[]{:S(2)}) async-start(bf16[32,2,80,128]{3,2,1,0:T(8,128)(2,1)} %bitcast.8), calls=%async_computation | async-start | bytes 2621440 | tf_op jit(solution)/shard_map/all_to_all | solution.py:94
  18.2 8.1 %constant_dynamic-slice_fusion.2 = (bf16[1,8,80,2,512]{4,3,2,1,0:T(2,128)(2,1)S(1)}, bf16[1,8,80,2,512]{4,3,2,1,0:T(2,128)(2,1)S(1)}, f32[1,8,80,2,512]{4,3,2,1,0:T(2,128)}, bf16[1,8,80,2,512]{4,3,2,1,0:T(2,128)(2,1)S(1)}) fusion(bf16[1,32,80,2,512]{4,3,2,1,0:T(2,128)(2,1)} %param.18, s32[]{:T(128)S(6)} %select_n.33, s32[]{:T(128)S(6)} %select_n.34, ...), kind=kLoop, calls=%fused_computation.82 | loop fusion | flops 655360 | bytes 11796496 | tf_op jit(solution)/shard_map/dynamic_slice | solution.py:122
  40.1 7.2 %all-to-all-start.1 = ((bf16[32,2,80,128]{3,2,1,0:T(8,128)(2,1)}), bf16[32,2,80,128]{3,2,1,0:T(8,128)(2,1)}, u32[]{:S(2)}, u32[]{:S(2)}) async-start(bf16[32,2,80,128]{3,2,1,0:T(8,128)(2,1)} %bitcast.14), calls=%async_computation.1 | async-start | bytes 2621440 | tf_op jit(solution)/shard_map/all_to_all | solution.py:94
  47.3 3.9 %reshape.89 = f32[8,80,2,4,128]{4,3,2,1,0:T(4,128)S(1)} reshape(f32[1,8,80,2,512]{4,3,2,1,0:T(2,128)} %get-tuple-element.13) | data formatting | bytes 5242880 | tf_op jit(solution)/shard_map/convert_element_type | solution.py:157
  51.4 3.7 %reshape.81 = f32[8,80,2,4,128]{4,3,1,2,0:T(4,128)} reshape(bf16[8,80,2,512]{3,1,2,0:T(8,128)(2,1)} %collective-permute-done) | data formatting | bytes 3932160 | tf_op jit(solution)/shard_map/convert_element_type | solution.py:148
  55.1 9.9 %collective-permute-done.1 = bf16[8,80,2,512]{3,1,2,0:T(8,128)(2,1)} collective-permute-done((bf16[8,80,2,512]{3,1,2,0:T(8,128)(2,1)}, bf16[8,80,2,512]{3,1,2,0:T(8,128)(2,1)}, u32[]{:S(2)}, u32[]{:S(2)}) %collective-permute-start.1) | collective-permute-done | bytes 1310752 | tf_op jit(solution)/shard_map/ppermute | solution.py:98
  65.0 3.6 %reshape.82 = f32[8,80,2,4,128]{4,3,1,2,0:T(4,128)} reshape(bf16[8,80,2,512]{3,1,2,0:T(8,128)(2,1)} %collective-permute-done.1) | data formatting | bytes 3932160 | tf_op jit(solution)/shard_map/convert_element_type | solution.py:148
  68.7 22.4 %collective-permute-done.3 = bf16[8,80,2,512]{3,1,2,0:T(8,128)(2,1)} collective-permute-done((bf16[8,80,2,512]{3,1,2,0:T(8,128)(2,1)}, bf16[8,80,2,512]{3,1,2,0:T(8,128)(2,1)}, u32[]{:S(2)}, u32[]{:S(2)}) %collective-permute-start.3) | collective-permute-done | bytes 1310752 | tf_op jit(solution)/shard_map/ppermute | solution.py:98
  91.1 3.7 %reshape.83 = f32[8,80,2,4,128]{4,3,1,2,0:T(4,128)} reshape(bf16[8,80,2,512]{3,1,2,0:T(8,128)(2,1)} %collective-permute-done.3) | data formatting | bytes 3932160 | tf_op jit(solution)/shard_map/convert_element_type | solution.py:148
  94.8 12.2 %all-to-all-done.1 = bf16[32,2,80,128]{3,2,1,0:T(8,128)(2,1)} async-done(((bf16[32,2,80,128]{3,2,1,0:T(8,128)(2,1)}), bf16[32,2,80,128]{3,2,1,0:T(8,128)(2,1)}, u32[]{:S(2)}, u32[]{:S(2)}) %all-to-all-start.1) | async-done | bytes 1310752 | tf_op jit(solution)/shard_map/all_to_all | solution.py:94
  107.0 5.4 %fusion.2 = (f32[4,2,80,128]{3,0,2,1:T(4,128)S(1)}, f32[4,2,80,128]{3,0,2,1:T(4,128)S(1)}, bf16[4,2,80,128]{3,0,2,1:T(4,128)(2,1)S(1)}, bf16[4,2,80,128]{3,0,2,1:T(4,128)(2,1)S(1)}) fusion(f32[8,80,2,4,128]{4,3,2,1,0:T(4,128)S(1)} %reshape.89, bf16[4,2,80,128]{3,0,2,1:T(4,128)(2,1)S(1)} %bitcast.169, bf16[8,4,2,80,128]{4,3,2,1,0:T(8,128)(2,1)} %bitcast.15, ...), kind=kLoop, calls=%fused_computation.8 | loop fusion | flops 7536640 | bytes 12943360 | tf_op jit(solution)/shard_map/reduce_sum | solution.py:148
  114.0 7.2 %shard_map.109 = f32[640,512]{1,0:T(8,128)S(1)} custom-call(s32[1,8192]{1,0:T(1,128)S(1)} %copy-done.1, f32[1,8192]{1,0:T(1,128)S(1)} %copy-done.2, f32[1,8192]{1,0:T(1,128)S(1)} %copy-done.3), custom_call_target="tpu_custom_call" | custom-call | flops 5368709120 | bytes 1310720 | tf_op jit(solution)/shard_map/pallas_call | solution.py:58
  121.4 2.6 collective-permute-start.4
  124.1 4.7 %collective-permute-done.4 = bf16[4,2,80,128]{3,0,2,1:T(4,128)(2,1)S(1)} collective-permute-done((bf16[4,2,80,128]{3,0,2,1:T(4,128)(2,1)S(1)}, bf16[4,2,80,128]{3,0,2,1:T(4,128)(2,1)S(1)}, u32[]{:S(2)}, u32[]{:S(2)}) %collective-permute-start.4) | collective-permute-done | bytes 163872 | tf_op jit(solution)/shard_map/ppermute | solution.py:98
  129.4 2.6 collective-permute-start.5
  132.0 3.9 %collective-permute-done.5 = bf16[4,2,80,128]{3,0,2,1:T(4,128)(2,1)S(1)} collective-permute-done((bf16[4,2,80,128]{3,0,2,1:T(4,128)(2,1)S(1)}, bf16[4,2,80,128]{3,0,2,1:T(4,128)(2,1)S(1)}, u32[]{:S(2)}, u32[]{:S(2)}) %collective-permute-start.5) | collective-permute-done | bytes 163872 | tf_op jit(solution)/shard_map/ppermute | solution.py:98
  141.2 33.5 %all_to_all.20 = bf16[32,2,80,128]{3,2,1,0:T(8,128)(2,1)S(1)} all-to-all(bf16[32,2,80,128]{3,2,1,0:T(8,128)(2,1)S(1)} %bitcast.166), channel_id=1, replica_groups=mesh['slot'=4,'horiz'=32] {'horiz'}, dimensions={0} | all-to-all | bytes 2621440 | tf_op jit(solution)/shard_map/all_to_all | solution.py:94
  177.3 23.2 %all_to_all.21 = bf16[32,2,80,128]{3,2,1,0:T(8,128)(2,1)S(1)} all-to-all(bf16[32,2,80,128]{3,2,1,0:T(8,128)(2,1)S(1)} %copy.110), channel_id=1, replica_groups=mesh['slot'=4,'horiz'=32] {'horiz'}, dimensions={0} | all-to-all | bytes 2621440 | tf_op jit(solution)/shard_map/all_to_all | solution.py:94
  202.7 2.6 %fusion.1 = bf16[8,80,2,512]{3,1,2,0:T(8,128)(2,1)S(1)} fusion(bf16[8,80,2,512]{3,1,2,0:T(8,128)(2,1)} %reshape.77, f32[80,2,512]{2,0,1:T(8,128)S(1)} %copy-done.10, bf16[8,80,2,512]{3,2,1,0:T(2,128)(2,1)} %copy-done.8, bf16[512,512]{1,0:T(8,128)(2,1)S(1)} %copy-done), kind=kOutput, calls=%fused_computation.7 | convolution fusion | flops 673710080 | bytes 4784128 | tf_op jit(solution)/shard_map/dot_general | solution.py:169
  207.6 27.0 %collective-permute-done.7 = bf16[8,80,2,512]{3,1,2,0:T(8,128)(2,1)S(1)} collective-permute-done((bf16[8,80,2,512]{3,1,2,0:T(8,128)(2,1)S(1)}, bf16[8,80,2,512]{3,1,2,0:T(8,128)(2,1)S(1)}, u32[]{:S(2)}, u32[]{:S(2)}) %collective-permute-start.7) | collective-permute-done | bytes 1310752 | tf_op jit(solution)/shard_map/ppermute | solution.py:98
  236.3 3.5 %collective-permute-start.8 = (bf16[2,8,80,2,512]{4,2,3,1,0:T(8,128)(2,1)}, bf16[2,8,80,2,512]{4,2,3,1,0:T(8,128)(2,1)}, u32[]{:S(2)}, u32[]{:S(2)}) collective-permute-start(bf16[2,8,80,2,512]{4,2,3,1,0:T(8,128)(2,1)} %pad_maximum_fusion), channel_id=1, source_target_pairs={{0,32},{32,0},{64,96},{96,64},{1,33},{33,1},{65,97},{97,65},{2,34}... | collective-permute-start | bytes 7864328 | tf_op jit(solution)/shard_map/ppermute | solution.py:98
  239.8 7.1 %broadcast_in_dim.8 = bf16[32,80,2,512]{3,2,1,0:T(2,128)(2,1)} broadcast(bf16[]{:T(256)} %constant.36.clone.1), dimensions={} | broadcast | bytes 5242882 | tf_op jit(solution)/shard_map/broadcast_in_dim | solution.py:177
  246.9 2.4 copy_dynamic-update-slice_fusion.3
  251.2 2.4 copy_dynamic-update-slice_fusion.2
  (76 shorter events, 45.2 us)
Async XLA Ops:
  0.0 6.0 %copy-start = (bf16[512,512]{1,0:T(8,128)(2,1)S(1)}, bf16[512,512]{1,0:T(8,128)(2,1)}, u32[]{:S(2)}) copy-start(bf16[512,512]{1,0:T(8,128)(2,1)} %param.15) | copy-start | bytes 1572868
  0.0 3.3 %copy-start.7 = (s32[80,2,512]{2,1,0:T(2,128)S(1)}, s32[80,2,512]{2,1,0:T(2,128)}, u32[]{:S(2)}) copy-start(s32[80,2,512]{2,1,0:T(2,128)} %param.12) | copy-start | bytes 983044
  3.5 2.5 copy-start.9
  6.0 1.1 copy-start.8
  8.4 27.3 %all-to-all-start = ((bf16[32,2,80,128]{3,2,1,0:T(8,128)(2,1)}), bf16[32,2,80,128]{3,2,1,0:T(8,128)(2,1)S(1)}, u32[]{:S(2)}, u32[]{:S(2)}) async-start(bf16[32,2,80,128]{3,2,1,0:T(8,128)(2,1)} %bitcast.8), calls=%async_computation | async-start | bytes 2621440 | tf_op jit(solution)/shard_map/all_to_all | solution.py:94
  27.7 23.7 %collective-permute-start = (bf16[8,80,2,512]{3,1,2,0:T(8,128)(2,1)}, bf16[8,80,2,512]{3,1,2,0:T(8,128)(2,1)}, u32[]{:S(2)}, u32[]{:S(2)}) collective-permute-start(bf16[8,80,2,512]{3,1,2,0:T(8,128)(2,1)} %bitcast.160), channel_id=1, source_target_pairs={{0,32},{32,0},{64,96},{96,64},{1,33},{33,1},{65,97},{97,65},{2,34}... | collective-permute-start | bytes 3932168 | tf_op jit(solution)/shard_map/ppermute | solution.py:98
  30.0 35.0 %collective-permute-start.1 = (bf16[8,80,2,512]{3,1,2,0:T(8,128)(2,1)}, bf16[8,80,2,512]{3,1,2,0:T(8,128)(2,1)}, u32[]{:S(2)}, u32[]{:S(2)}) collective-permute-start(bf16[8,80,2,512]{3,1,2,0:T(8,128)(2,1)} %bitcast.159), channel_id=1, source_target_pairs={{0,96},{32,64},{64,32},{96,0},{1,97},{33,65},{65,33},{97,1},{2,98}... | collective-permute-start | bytes 3932168 | tf_op jit(solution)/shard_map/ppermute | solution.py:98
  33.6 3.5 %copy-start.12 = (bf16[64,64]{1,0:T(8,128)(2,1)S(1)}, bf16[64,64]{1,0:T(8,128)(2,1)}, u32[]{:S(2)}) copy-start(bf16[64,64]{1,0:T(8,128)(2,1)} %param.16) | copy-start | bytes 24580
  33.6 57.5 %collective-permute-start.3 = (bf16[8,80,2,512]{3,1,2,0:T(8,128)(2,1)}, bf16[8,80,2,512]{3,1,2,0:T(8,128)(2,1)}, u32[]{:S(2)}, u32[]{:S(2)}) collective-permute-start(bf16[8,80,2,512]{3,1,2,0:T(8,128)(2,1)} %bitcast.158), channel_id=1, source_target_pairs={{0,64},{32,96},{64,0},{96,32},{1,65},{33,97},{65,1},{97,33},{2,66}... | collective-permute-start | bytes 3932168 | tf_op jit(solution)/shard_map/ppermute | solution.py:98
  37.1 0.7 copy-start.11
  40.1 66.9 %all-to-all-start.1 = ((bf16[32,2,80,128]{3,2,1,0:T(8,128)(2,1)}), bf16[32,2,80,128]{3,2,1,0:T(8,128)(2,1)}, u32[]{:S(2)}, u32[]{:S(2)}) async-start(bf16[32,2,80,128]{3,2,1,0:T(8,128)(2,1)} %bitcast.14), calls=%async_computation.1 | async-start | bytes 2621440 | tf_op jit(solution)/shard_map/all_to_all | solution.py:94
  107.0 7.0 %copy-start.1 = (s32[1,8192]{1,0:T(1,128)S(1)}, s32[1,8192]{1,0:T(1,128)}, u32[]{:S(2)}) copy-start(s32[1,8192]{1,0:T(1,128)} %cell_ref.1) | copy-start | bytes 98308
  107.0 7.0 %copy-start.2 = (f32[1,8192]{1,0:T(1,128)S(1)}, f32[1,8192]{1,0:T(1,128)}, u32[]{:S(2)}) copy-start(f32[1,8192]{1,0:T(1,128)} %value_ref.1) | copy-start | bytes 98308
  107.0 7.0 %copy-start.3 = (f32[1,8192]{1,0:T(1,128)S(1)}, f32[1,8192]{1,0:T(1,128)}, u32[]{:S(2)}) copy-start(f32[1,8192]{1,0:T(1,128)} %weight_ref.1) | copy-start | bytes 98308
  112.7 8.6 %collective-permute-start.2 = (bf16[2,4,2,80,128]{4,1,3,2,0:T(4,128)(2,1)S(1)}, bf16[2,4,2,80,128]{4,1,3,2,0:T(4,128)(2,1)S(1)}, u32[]{:S(2)}, u32[]{:S(2)}) collective-permute-start(bf16[2,4,2,80,128]{4,1,3,2,0:T(4,128)(2,1)S(1)} %pad_maximum_fusion.1), channel_id=1, source_target_pairs={{0,32},{32,0},{64,96},{96,64},{1,33},{33,1},{65,97},{97,65},{2,34}... | collective-permute-start | bytes 983048 | tf_op jit(solution)/shard_map/ppermute | solution.py:98
  121.3 18.0 %copy-start.6 = (f32[8,80,2,4,128]{4,3,1,2,0:T(4,128)S(1)}, f32[8,80,2,4,128]{4,3,1,2,0:T(4,128)}, u32[]{:S(2)}) copy-start(f32[8,80,2,4,128]{4,3,1,2,0:T(4,128)} %reshape.83) | copy-start | bytes 7864324
  121.4 7.4 %collective-permute-start.4 = (bf16[4,2,80,128]{3,0,2,1:T(4,128)(2,1)S(1)}, bf16[4,2,80,128]{3,0,2,1:T(4,128)(2,1)S(1)}, u32[]{:S(2)}, u32[]{:S(2)}) collective-permute-start(bf16[4,2,80,128]{3,0,2,1:T(4,128)(2,1)S(1)} %fusion.23), channel_id=1, source_target_pairs={{0,64},{32,96},{64,0},{96,32},{1,65},{33,97},{65,1},{97,33},{2,66}... | collective-permute-start | bytes 491528 | tf_op jit(solution)/shard_map/ppermute | solution.py:98
  124.0 15.2 %copy-start.5 = (f32[8,80,2,4,128]{4,3,1,2,0:T(4,128)S(1)}, f32[8,80,2,4,128]{4,3,1,2,0:T(4,128)}, u32[]{:S(2)}) copy-start(f32[8,80,2,4,128]{4,3,1,2,0:T(4,128)} %reshape.82) | copy-start | bytes 7864324
  128.8 10.4 %copy-start.4 = (f32[8,80,2,4,128]{4,3,1,2,0:T(4,128)S(1)}, f32[8,80,2,4,128]{4,3,1,2,0:T(4,128)}, u32[]{:S(2)}) copy-start(f32[8,80,2,4,128]{4,3,1,2,0:T(4,128)} %reshape.81) | copy-start | bytes 7864324
  129.4 6.5 %collective-permute-start.5 = (bf16[4,2,80,128]{3,0,2,1:T(4,128)(2,1)S(1)}, bf16[4,2,80,128]{3,0,2,1:T(4,128)(2,1)S(1)}, u32[]{:S(2)}, u32[]{:S(2)}) collective-permute-start(bf16[4,2,80,128]{3,0,2,1:T(4,128)(2,1)S(1)} %get-tuple-element.10), channel_id=1, source_target_pairs={{0,64},{32,96},{64,0},{96,32},{1,65},{33,97},{65,1},{97,33},{2,66}... | collective-permute-start | bytes 491528 | tf_op jit(solution)/shard_map/ppermute | solution.py:98
  136.1 3.0 %collective-permute-start.6 = (bf16[2,4,2,80,128]{4,1,3,2,0:T(4,128)(2,1)S(1)}, bf16[2,4,2,80,128]{4,1,3,2,0:T(4,128)(2,1)S(1)}, u32[]{:S(2)}, u32[]{:S(2)}) collective-permute-start(bf16[2,4,2,80,128]{4,1,3,2,0:T(4,128)(2,1)S(1)} %pad_maximum_fusion.2), channel_id=1, source_target_pairs={{0,32},{32,0},{64,96},{96,64},{1,33},{33,1},{65,97},{97,65},{2,34}... | collective-permute-start | bytes 983048 | tf_op jit(solution)/shard_map/ppermute | solution.py:98
  201.3 1.4 copy-start.10
  205.3 29.3 %collective-permute-start.7 = (bf16[8,80,2,512]{3,1,2,0:T(8,128)(2,1)S(1)}, bf16[8,80,2,512]{3,1,2,0:T(8,128)(2,1)S(1)}, u32[]{:S(2)}, u32[]{:S(2)}) collective-permute-start(bf16[8,80,2,512]{3,1,2,0:T(8,128)(2,1)S(1)} %fusion.1), channel_id=1, source_target_pairs={{0,64},{32,96},{64,0},{96,32},{1,65},{33,97},{65,1},{97,33},{2,66}... | collective-permute-start | bytes 3932168 | tf_op jit(solution)/shard_map/ppermute | solution.py:98
  236.3 13.0 %collective-permute-start.8 = (bf16[2,8,80,2,512]{4,2,3,1,0:T(8,128)(2,1)}, bf16[2,8,80,2,512]{4,2,3,1,0:T(8,128)(2,1)}, u32[]{:S(2)}, u32[]{:S(2)}) collective-permute-start(bf16[2,8,80,2,512]{4,2,3,1,0:T(8,128)(2,1)} %pad_maximum_fusion), channel_id=1, source_target_pairs={{0,32},{32,0},{64,96},{96,64},{1,33},{33,1},{65,97},{97,65},{2,34}... | collective-permute-start | bytes 7864328 | tf_op jit(solution)/shard_map/ppermute | solution.py:98

commit v2 on v1

v2 whole, which is shorter than its diff:
```python
import functools
import math

import jax
import jax.numpy as jnp
from jax import lax
from jax.experimental import pallas as pl
from jax.experimental.layout import Layout, with_layout_constraint
from jax.experimental.pallas import tpu as pltpu
from jax.sharding import PartitionSpec as P

OBS_BLOCK = 1024


def local_sigma(tile_id, tile_scale, dev_index, row_count):
    regions = tile_scale.shape[0]
    tile_rows = max(row_count // 4, 1)
    picked = lax.dynamic_slice_in_dim(tile_id, dev_index * row_count // 4, tile_rows, 0)
    onehot = (picked[None] == jnp.arange(regions, dtype=jnp.int32)[:, None, None]).astype(
        jnp.float32
    )
    scale_table = jnp.einsum("rz,rab->zab", tile_scale, onehot, precision=lax.Precision.HIGHEST)
    expanded = jnp.repeat(scale_table, 4, axis=1)
    expanded = lax.dynamic_slice_in_dim(expanded, dev_index * row_count % 4, row_count, 1)
    return jnp.repeat(expanded, 4, axis=2)


def obs_kernel(cell_ref, value_ref, weight_ref, weight_out, value_out, total):
    step = pl.program_id(1)

    @pl.when(step == 0)
    def _():
        total[...] = jnp.zeros_like(total)

    cell = cell_ref[0].astype(jnp.int32)
    weight = weight_ref[0]
    weighted = weight * value_ref[0]
    count = cell.shape[1]
    rows = total.shape[0]
    levels = rows // 8
    row = (((cell >> 7) & 3) * 2 + ((cell >> 9) & 1)) * levels + (cell >> 10)
    row_hot = lax.broadcasted_iota(jnp.int32, (rows, count), 0) == row
    lane_hot = lax.broadcasted_iota(jnp.int32, (128, count), 0) == (cell & 127)
    parts = []
    for value in (weight, weighted):
        high = value.astype(jnp.bfloat16).astype(jnp.float32)
        for part in (high, value - high):
            parts.append(jnp.where(lane_hot, part, 0.0).astype(jnp.bfloat16))
    spread = jnp.concatenate(parts, axis=0)
    total[...] += lax.dot_general(
        jnp.where(row_hot, 1.0, 0.0).astype(jnp.bfloat16),
        spread,
        (((1,), (1,)), ((), ())),
        preferred_element_type=jnp.float32,
    )

    @pl.when(step == pl.num_programs(1) - 1)
    def _():
        for tile in range(4):
            for row in range(2):
                at = pl.ds((tile * 2 + row) * levels, levels)
                lanes = pl.ds(tile * 128, 128)
                weight_out[0, row, :, lanes] = total[at, 0:128] + total[at, 128:256]
                value_out[0, row, :, lanes] = total[at, 256:384] + total[at, 384:512]


def obs_fields(obs, levels):
    slots, _, _, count = obs.shape

    def part(k):
        return pl.BlockSpec((1, None, 1, OBS_BLOCK), lambda s, i: (s, k, 0, i))

    out = pl.BlockSpec((1, 2, levels, 512), lambda s, i: (s, 0, 0, 0))
    shape = jax.ShapeDtypeStruct((slots, 2, levels, 512), jnp.float32)
    return pl.pallas_call(
        obs_kernel,
        grid=(slots, count // OBS_BLOCK),
        in_specs=[part(0), part(1), part(2)],
        out_specs=[out, out],
        out_shape=[shape, shape],
        scratch_shapes=[pltpu.VMEM((levels * 8, 512), jnp.float32)],
        compiler_params=pltpu.CompilerParams(vmem_limit_bytes=32 << 20),
        cost_estimate=pl.CostEstimate(
            flops=2 * levels * 8 * 512 * count * slots * 2,
            bytes_accessed=levels * 8 * 512 * 4,
            transcendentals=0,
        ),
    )(obs, obs, obs)


def increment_kernel(spread_ref, p0, p1, p2, p3, keep_ref, send_ref):
    members = spread_ref.shape[0]
    for row in range(2):
        for low in range(0, spread_ref.shape[3], 16):
            at = pl.ds(low, 16)
            sums = [jnp.zeros((16, 128), jnp.float32) for _ in range(4)]
            for m in range(members):
                field = spread_ref[m, 0, row, at, :].astype(jnp.float32)
                for k, p in enumerate((p0, p1, p2, p3)):
                    sums[k] += p[m, row, at, :].astype(jnp.float32) * field
            keep_ref[0, row, at, :] = sums[0]
            keep_ref[1, row, at, :] = sums[2]
            send_ref[0, row, at, :] = sums[1].astype(jnp.bfloat16)
            send_ref[1, row, at, :] = sums[3].astype(jnp.bfloat16)


def increments(spread, pert):
    members, tiles, rows, levels, lanes = spread.shape
    field = pl.BlockSpec((members, rows, levels, lanes), lambda t: (0, 0, 0, t))
    out = pl.BlockSpec((2, rows, levels, lanes), lambda t: (0, 0, 0, t))
    shape = (2, rows, levels, tiles * lanes)
    return pl.pallas_call(
        increment_kernel,
        grid=(tiles,),
        in_specs=[
            pl.BlockSpec((members, 1, rows, levels, lanes), lambda t: (0, t, 0, 0, 0)),
            field,
            field,
            field,
            field,
        ],
        out_specs=[out, out],
        out_shape=[
            jax.ShapeDtypeStruct(shape, jnp.float32),
            jax.ShapeDtypeStruct(shape, jnp.bfloat16),
        ],
        compiler_params=pltpu.CompilerParams(vmem_limit_bytes=32 << 20),
        cost_estimate=pl.CostEstimate(
            flops=8 * spread.size, bytes_accessed=10 * spread.size, transcendentals=0
        ),
    )(spread, *pert)


def slot_sum_kernel(sea_ref, own_ref, other_ref, p0, p1, p2, p3, out_ref):
    members = out_ref.shape[0]
    for row in range(2):
        for low in range(0, out_ref.shape[3], 16):
            at = pl.ds(low, 16)
            sea = sea_ref[row, at, :].astype(jnp.float32)
            fields = [
                ref[k, row, at, :].astype(jnp.float32) * sea
                for k, ref in ((0, own_ref), (0, other_ref), (1, own_ref), (1, other_ref))
            ]
            for m in range(members):
                total = p0[m, row, at, :].astype(jnp.float32) * fields[0]
                for k, p in ((1, p1), (2, p2), (3, p3)):
                    total += p[m, row, at, :].astype(jnp.float32) * fields[k]
                out_ref[m, 0, row, at, :] = total.astype(jnp.bfloat16)


def slot_sums(sea, own, other, pert):
    members, rows, levels, cols = pert[0].shape
    tiles = cols // 128
    field = pl.BlockSpec((members, rows, levels, 128), lambda t: (0, 0, 0, t))
    pair = pl.BlockSpec((2, rows, levels, 128), lambda t: (0, 0, 0, t))
    return pl.pallas_call(
        slot_sum_kernel,
        grid=(tiles,),
        in_specs=[
            pl.BlockSpec((rows, levels, 128), lambda t: (0, 0, t)),
            pair,
            pair,
            field,
            field,
            field,
            field,
        ],
        out_specs=pl.BlockSpec((members, 1, rows, levels, 128), lambda t: (0, t, 0, 0, 0)),
        out_shape=jax.ShapeDtypeStruct((members, tiles, rows, levels, 128), jnp.bfloat16),
        compiler_params=pltpu.CompilerParams(vmem_limit_bytes=32 << 20),
        cost_estimate=pl.CostEstimate(
            flops=8 * pert[0].size, bytes_accessed=10 * pert[0].size, transcendentals=0
        ),
    )(sea, own, other, *pert)


def pick_kernel(slot_ref, whole, *refs):
    outs, sems = refs[:-1], refs[-1]
    count = outs[0].shape[0]
    copies = []
    for i, out in enumerate(outs):
        at = pl.ds((slot_ref[0] ^ (i + 1)) * count, count)
        copies.append(pltpu.make_async_copy(whole.at[at], out, sems.at[i]))
        copies[-1].start()
    for copy in copies:
        copy.wait()


def pick(slot, whole):
    anywhere = pl.BlockSpec(memory_space=pl.ANY)
    shape = (whole.shape[0] // 4, *whole.shape[1:])
    return pl.pallas_call(
        pick_kernel,
        in_specs=[pl.BlockSpec(memory_space=pltpu.SMEM), anywhere],
        out_specs=[anywhere] * 3,
        out_shape=[jax.ShapeDtypeStruct(shape, whole.dtype)] * 3,
        scratch_shapes=[pltpu.SemaphoreType.DMA((3,))],
        cost_estimate=pl.CostEstimate(
            flops=0, bytes_accessed=3 * whole.size, transcendentals=0
        ),
    )(slot.reshape(1), whole)


def place_kernel(groups, slot_ref, *refs):
    parts = refs[: len(groups)]
    out, sems = refs[-2:]
    count = parts[0].shape[0]
    copies = []
    for i, (k, part) in enumerate(zip(groups, parts)):
        at = pl.ds((slot_ref[0] ^ k) * count, count)
        copies.append(pltpu.make_async_copy(part, out.at[at], sems.at[i]))
        copies[-1].start()
    for copy in copies:
        copy.wait()


def place(slot, groups, parts, members, base=None):
    anywhere = pl.BlockSpec(memory_space=pl.ANY)
    operands = list(parts) + ([] if base is None else [base])
    return pl.pallas_call(
        functools.partial(place_kernel, groups),
        in_specs=[pl.BlockSpec(memory_space=pltpu.SMEM)] + [anywhere] * len(operands),
        out_specs=anywhere,
        out_shape=jax.ShapeDtypeStruct((members, *parts[0].shape[1:]), jnp.bfloat16),
        scratch_shapes=[pltpu.SemaphoreType.DMA((len(groups),))],
        input_output_aliases={} if base is None else {len(operands): 0},
        cost_estimate=pl.CostEstimate(
            flops=0, bytes_accessed=4 * len(parts) * parts[0].size, transcendentals=0
        ),
    )(slot.reshape(1), *operands)


def swap_columns(tiles):
    shape = tiles.shape
    flat = tiles.reshape(shape[0] * shape[1], *shape[2:])
    return lax.all_to_all(flat, "horiz", split_axis=0, concat_axis=0, tiled=True).reshape(shape)


def swap_slot(arr, k):
    return lax.ppermute(arr, "slot", [(i, i ^ k) for i in range(4)])


def row_major(arr):
    return with_layout_constraint(arr, Layout(tuple(range(arr.ndim))))


def per_device(
    control,
    land_mask,
    tile_id,
    tile_scale,
    inverse_x,
    inverse_y,
    inverse_z,
    perturbations,
    obs_cell,
    obs_value,
    obs_weight,
):
    members, levels, row_count, col_count = control.shape
    own = members // 4
    tiles = col_count // 128
    slot = lax.axis_index("slot")
    dev_index = lax.axis_index("horiz")
    norm_scale = 1.0 / math.sqrt(members)
    perturbed = perturbations[0]

    sent = dict(zip((1, 2, 3), pick(slot, perturbed)))
    control, land_mask, obs_cell, sent = lax.optimization_barrier(
        (control, land_mask, obs_cell, sent)
    )
    got = {k: row_major(swap_slot(sent[k], k)) for k in (2, 3, 1)}
    pert = [lax.dynamic_slice_in_dim(perturbed, slot * own, own, 0), got[1], got[2], got[3]]

    obs = jnp.stack([obs_cell.astype(jnp.float32), obs_value, obs_weight])
    obs = jnp.stack([obs, swap_slot(obs, 2)])
    weight_sum, value_sum = obs_fields(obs, levels)

    sea = land_mask.astype(jnp.float32).transpose(1, 0, 2)
    weight_mask = sea * local_sigma(tile_id, tile_scale, dev_index, row_count).transpose(1, 0, 2)

    mine = lax.dynamic_slice_in_dim(control, slot * own, own, 0).transpose(0, 2, 1, 3)
    masked = (weight_mask * mine.astype(jnp.float32)).astype(jnp.bfloat16)
    along_x = (sea * jnp.dot(masked, inverse_x, preferred_element_type=jnp.float32)).astype(
        jnp.bfloat16
    )
    along_x = along_x.reshape(own, row_count, levels, tiles, 128).transpose(0, 3, 1, 2, 4)
    received = swap_columns(along_x)
    received, weight_sum, value_sum = lax.optimization_barrier((received, weight_sum, value_sum))
    received = received.reshape(-1, levels, 128)
    across = jnp.einsum(
        "yzx,yk->kzx", received, inverse_y, preferred_element_type=jnp.float32
    ).astype(jnp.bfloat16)
    deeper = jnp.einsum(
        "kzx,zw->kwx", across, inverse_z, preferred_element_type=jnp.float32
    ).astype(jnp.bfloat16)
    tile_shape = (own, tiles, row_count, levels, 128)
    spread = swap_columns(deeper.reshape(tile_shape))

    pert = [p.transpose(0, 2, 1, 3) for p in pert]
    keep, send = increments(spread, pert)
    keep = keep + swap_slot(send, 1).astype(jnp.float32)
    far = swap_slot(keep.astype(jnp.bfloat16), 2).astype(jnp.float32)
    increment = (keep + far[::-1]) * sea * norm_scale
    adjoint = ((weight_sum * increment - value_sum) * norm_scale).astype(jnp.bfloat16)
    back_first = slot_sums(sea, adjoint, swap_slot(adjoint, 1), pert)

    received = swap_columns(back_first).reshape(-1, levels, 128)
    back_deep = jnp.einsum(
        "kwx,zw->kzx", received, inverse_z, preferred_element_type=jnp.float32
    ).astype(jnp.bfloat16)
    back_across = jnp.einsum(
        "kzx,yk->yzx", back_deep, inverse_y, preferred_element_type=jnp.float32
    ).astype(jnp.bfloat16)
    returned = swap_columns(back_across.reshape(tile_shape))
    returned = returned.transpose(0, 2, 3, 1, 4).reshape(own, row_count, levels, col_count)
    filtered = weight_mask * lax.dot_general(
        returned * sea.astype(jnp.bfloat16),
        inverse_x,
        (((3,), (1,)), ((), ())),
        preferred_element_type=jnp.float32,
    )
    gradient = (mine.astype(jnp.float32) + filtered).astype(jnp.bfloat16)
    gradient = row_major(gradient.transpose(0, 2, 1, 3))

    half = row_major(swap_slot(gradient, 2))
    beside = row_major(swap_slot(gradient, 1))
    result = place(slot, (0, 1), (gradient, beside), members)
    half, result = lax.optimization_barrier((half, result))
    across_both = row_major(swap_slot(half, 1))
    return place(slot, (2, 3), (half, across_both), members, result)


def solution(mesh):
    return jax.shard_map(
        per_device,
        mesh=mesh,
        in_specs=(
            P(None, None, "horiz", None),
            P(None, "horiz", None),
            P(),
            P(),
            P(),
            P(),
            P(),
            P("slot", None, None, "horiz", None),
            P("slot", "horiz"),
            P("slot", "horiz"),
            P("slot", "horiz"),
        ),
        out_specs=P(None, None, "horiz", None),
        check_vma=False,
    )
```

time: 263 us -> 480 us (1.83)
  the two profiles are of different devices: /device:TPU:1 before, /device:TPU:37 now
where the time goes in v2:
time: 480 us; the launch traced here: 476 us
  Pallas kernels  301 us (63%)
  waiting for transfers between devices  74.3 us (15%)
  starting transfers between devices  40.4 us (8%)
  blocking collectives  23.2 us (5%)
  local copies, waits for them, and re-layouts  20.6 us (4%)
  other arithmetic  9.63 us (2%)
  matrix products  6.52 us (1%)
    pallas_call x2, Pallas kernels, place(): pl.pallas_call(functools.partial(place_kernel, groups), in_specs=[pl.Bloc...  161 us
    pallas_call x1, Pallas kernels, pick(): pl.pallas_call(pick_kernel, in_specs=[pl.BlockSpec(memory_space=pltpu.SME...  120 us
    ppermute x10, waiting for transfers between devices, swap_slot(): return lax.ppermute(arr, 'slot', [(i, i ^ k) for i in range(4)])  50.6 us
    all_to_all x3, waiting for transfers between devices, swap_columns(): lax.all_to_all(flat, 'horiz', split_axis=0, concat_axis=0, tiled=True)  23.7 us
    all_to_all x1, blocking collectives, swap_columns(): lax.all_to_all(flat, 'horiz', split_axis=0, concat_axis=0, tiled=True)  23.2 us
    all_to_all x3, starting transfers between devices, swap_columns(): lax.all_to_all(flat, 'horiz', split_axis=0, concat_axis=0, tiled=True)  22.8 us
    ppermute x10, starting transfers between devices, swap_slot(): return lax.ppermute(arr, 'slot', [(i, i ^ k) for i in range(4)])  17.6 us
    pallas_call x1, Pallas kernels, obs_fields(): pl.pallas_call(obs_kernel, grid=(slots, count // OBS_BLOCK), in_specs=[pa...  14.7 us
  transfers between devices with their start and end apart: 13, of which 9 were waited for; matrix products, arithmetic and copies ran while one was open for 4% of the time, Pallas kernels for 20%

profile of v2, /device:TPU:37, one launch (start us, length us, event | category | flops | bytes accessed | tf_op | source)
XLA Modules:
  0.0 476.2 jit_solution(13286458273487487708)
XLA Ops:
  0.0 120.2 %shard_map.109 = (bf16[8,80,2,512]{3,2,1,0:T(2,128)(2,1)}, bf16[8,80,2,512]{3,2,1,0:T(2,128)(2,1)}, bf16[8,80,2,512]{3,2,1,0:T(2,128)(2,1)}) custom-call(s32[1]{0:T(128)} %bitcast.slot_ref, bf16[32,80,2,512]{3,2,1,0:T(2,128)(2,1)} %bitcast.94), custom_call_target="tpu_custom_call" | custom-call | bytes 7864320 | tf_op jit(solution)/shard_map/pallas_call | solution.py:192
  123.1 2.5 fusion.2
  127.9 9.2 %all-to-all-start = ((bf16[32,2,80,128]{3,2,1,0:T(8,128)(2,1)}), bf16[32,2,80,128]{3,2,1,0:T(8,128)(2,1)S(1)}, u32[]{:S(2)}, u32[]{:S(2)}) async-start(bf16[32,2,80,128]{3,2,1,0:T(8,128)(2,1)} %bitcast.9), calls=%async_computation | async-start | bytes 2621440 | tf_op jit(solution)/shard_map/all_to_all | solution.py:236
  142.2 14.7 %shard_map.110 = (f32[2,2,80,512]{3,2,1,0:T(8,128)S(1)}, f32[2,2,80,512]{3,2,1,0:T(8,128)S(1)}) custom-call(f32[2,3,1,8192]{3,2,1,0:T(1,128)S(1)} %pad_maximum_fusion.1.cell_ref.value_ref.weight_ref, f32[2,3,1,8192]{3,2,1,0:T(1,128)S(1)} %pad_maximum_fusion.1.cell_ref.value_ref.weight_ref, f32[2,3,1,8192]{3,2,1,0:T(1,128)S(1)} %pad_maximum_fusion.1.cell_ref.value_ref.weight_ref), custom_call_target="tpu_custom_call" | custom-call | flops 21474836480 | bytes 1310720 | tf_op jit(solution)/shard_map/pallas_call | solution.py:75
  160.0 2.1 convolution_convert_fusion.2
  162.1 7.8 %all-to-all-start.1 = ((bf16[32,2,80,128]{3,2,1,0:T(8,128)(2,1)}), bf16[32,2,80,128]{3,2,1,0:T(8,128)(2,1)}, u32[]{:S(2)}, u32[]{:S(2)}) async-start(bf16[32,2,80,128]{3,2,1,0:T(8,128)(2,1)} %bitcast.21), calls=%async_computation.1 | async-start | bytes 2621440 | tf_op jit(solution)/shard_map/all_to_all | solution.py:236
  170.0 2.3 constant_dynamic-slice_fusion
  174.1 6.0 %collective-permute-done.2 = bf16[8,80,2,512]{3,2,1,0:T(2,128)(2,1)} collective-permute-done((bf16[8,80,2,512]{3,2,1,0:T(2,128)(2,1)}, bf16[8,80,2,512]{3,2,1,0:T(2,128)(2,1)}, u32[]{:S(2)}, u32[]{:S(2)}) %collective-permute-start.2) | collective-permute-done | bytes 1310752 | tf_op jit(solution)/shard_map/ppermute | solution.py:240
  180.2 2.6 copy.102
  182.8 28.7 %collective-permute-done.3 = bf16[8,80,2,512]{3,2,1,0:T(2,128)(2,1)} collective-permute-done((bf16[8,80,2,512]{3,2,1,0:T(2,128)(2,1)}, bf16[8,80,2,512]{3,2,1,0:T(2,128)(2,1)}, u32[]{:S(2)}, u32[]{:S(2)}) %collective-permute-start.3) | collective-permute-done | bytes 1310752 | tf_op jit(solution)/shard_map/ppermute | solution.py:240
  211.5 2.7 copy.101
  214.1 8.5 %all-to-all-done.1 = bf16[32,2,80,128]{3,2,1,0:T(8,128)(2,1)} async-done(((bf16[32,2,80,128]{3,2,1,0:T(8,128)(2,1)}), bf16[32,2,80,128]{3,2,1,0:T(8,128)(2,1)}, u32[]{:S(2)}, u32[]{:S(2)}) %all-to-all-start.1) | async-done | bytes 1310752 | tf_op jit(solution)/shard_map/all_to_all | solution.py:236
  225.3 2.6 shard_map.111
  227.9 3.8 collective-permute-start.4
  234.5 9.2 %collective-permute-done.5 = bf16[2,2,80,512]{3,2,1,0:T(8,128)(2,1)S(1)} collective-permute-done((bf16[2,2,80,512]{3,2,1,0:T(8,128)(2,1)S(1)}, bf16[2,2,80,512]{3,2,1,0:T(8,128)(2,1)S(1)}, u32[]{:S(2)}, u32[]{:S(2)}) %collective-permute-start.5) | collective-permute-done | bytes 327712 | tf_op jit(solution)/shard_map/ppermute | solution.py:240
  246.7 2.3 shard_map.112
  249.1 23.2 %all_to_all.20 = bf16[32,2,80,128]{3,2,1,0:T(8,128)(2,1)S(1)} all-to-all(bf16[32,2,80,128]{3,2,1,0:T(8,128)(2,1)S(1)} %bitcast.93), channel_id=1, replica_groups=mesh['slot'=4,'horiz'=32] {'horiz'}, dimensions={0} | all-to-all | bytes 2621440 | tf_op jit(solution)/shard_map/all_to_all | solution.py:236
  275.2 5.8 %all-to-all-start.3 = ((bf16[32,2,80,128]{3,1,2,0:T(2,128)(2,1)}), bf16[32,2,80,128]{3,1,2,0:T(2,128)(2,1)S(1)}, u32[]{:S(2)}, u32[]{:S(2)}) async-start(bf16[32,2,80,128]{3,1,2,0:T(2,128)(2,1)} %copy.73), calls=%async_computation.3 | async-start | bytes 2621440 | tf_op jit(solution)/shard_map/all_to_all | solution.py:236
  281.4 15.2 %all-to-all-done.3 = bf16[32,2,80,128]{3,1,2,0:T(2,128)(2,1)S(1)} async-done(((bf16[32,2,80,128]{3,1,2,0:T(2,128)(2,1)}), bf16[32,2,80,128]{3,1,2,0:T(2,128)(2,1)S(1)}, u32[]{:S(2)}, u32[]{:S(2)}) %all-to-all-start.3) | async-done | bytes 1310752 | tf_op jit(solution)/shard_map/all_to_all | solution.py:236
  299.6 4.1 fusion.refs_0_
  303.7 4.2 collective-permute-start.8
  310.7 80.5 %shard_map.113.refs_2_ = bf16[32,80,2,512]{3,2,1,0:T(2,128)(2,1)} custom-call(s32[1]{0:T(128)} %bitcast.slot_ref, bf16[8,80,2,512]{3,2,1,0:T(2,128)(2,1)} %copy-done.7, bf16[8,80,2,512]{3,2,1,0:T(2,128)(2,1)} %collective-permute-done.8.refs_1_), custom_call_target="tpu_custom_call" | custom-call | bytes 5242880 | tf_op jit(solution)/shard_map/pallas_call | solution.py:220
  391.7 2.7 collective-permute-done.9.refs_1_
  395.5 80.5 %shard_map.114 = bf16[32,80,2,512]{3,2,1,0:T(2,128)(2,1)} custom-call(s32[1]{0:T(128)} %bitcast.slot_ref, bf16[8,80,2,512]{3,2,1,0:T(2,128)(2,1)} %copy-done.12, bf16[8,80,2,512]{3,2,1,0:T(2,128)(2,1)} %copy-done.13, bf16[32,80,2,512]{3,2,1,0:T(2,128)(2,1)} %shard_map.113.refs_2_), custom_call_target="tpu_custom_call", output_to_operand_aliasing={{}: (3, {})} | custom-call | bytes 5242880 | tf_op jit(solution)/shard_map/pallas_call | solution.py:220
  (85 shorter events, 34.1 us)
Async XLA Ops:
  0.0 125.6 %copy-start = (bf16[512,512]{1,0:T(8,128)(2,1)S(1)}, bf16[512,512]{1,0:T(8,128)(2,1)}, u32[]{:S(2)}) copy-start(bf16[512,512]{1,0:T(8,128)(2,1)} %param.15) | copy-start | bytes 1572868
  0.0 120.3 %copy-start.18 = (s32[1,8192]{1,0:T(1,128)S(1)}, s32[1,8192]{1,0:T(1,128)}, u32[]{:S(2)}) copy-start(s32[1,8192]{1,0:T(1,128)} %param.19) | copy-start | bytes 98308
  0.0 120.3 %copy-start.14 = (f32[1,8192]{1,0:T(1,128)S(1)}, f32[1,8192]{1,0:T(1,128)}, u32[]{:S(2)}) copy-start(f32[1,8192]{1,0:T(1,128)} %param.21) | copy-start | bytes 98308
  0.0 120.3 %copy-start.15 = (f32[1,8192]{1,0:T(1,128)S(1)}, f32[1,8192]{1,0:T(1,128)}, u32[]{:S(2)}) copy-start(f32[1,8192]{1,0:T(1,128)} %param.20) | copy-start | bytes 98308
  0.0 121.4 %copy-start.19 = (f32[16,80]{1,0:T(8,128)S(1)}, f32[16,80]{1,0:T(8,128)}, u32[]{:S(2)}) copy-start(f32[16,80]{1,0:T(8,128)} %param.14) | copy-start | bytes 15364
  120.5 21.6 %collective-permute-start = (f32[3,1,8192]{2,1,0:T(1,128)S(1)}, f32[3,1,8192]{2,1,0:T(1,128)S(1)}, u32[]{:S(2)}, u32[]{:S(2)}) collective-permute-start(f32[3,1,8192]{2,1,0:T(1,128)S(1)} %pad_maximum_fusion.2), channel_id=1, source_target_pairs={{0,64},{32,96},{64,0},{96,32},{1,65},{33,97},{65,1},{97,33},{2,66}... | collective-permute-start | bytes 294920 | tf_op jit(solution)/shard_map/ppermute | solution.py:240
  122.0 3.6 copy-start.10
  127.9 29.9 %all-to-all-start = ((bf16[32,2,80,128]{3,2,1,0:T(8,128)(2,1)}), bf16[32,2,80,128]{3,2,1,0:T(8,128)(2,1)S(1)}, u32[]{:S(2)}, u32[]{:S(2)}) async-start(bf16[32,2,80,128]{3,2,1,0:T(8,128)(2,1)} %bitcast.9), calls=%async_computation | async-start | bytes 2621440 | tf_op jit(solution)/shard_map/all_to_all | solution.py:236
  137.1 35.5 %collective-permute-start.1 = (bf16[8,80,2,512]{3,2,1,0:T(2,128)(2,1)}, bf16[8,80,2,512]{3,2,1,0:T(2,128)(2,1)}, u32[]{:S(2)}, u32[]{:S(2)}) collective-permute-start(bf16[8,80,2,512]{3,2,1,0:T(2,128)(2,1)} %get-tuple-element.33), channel_id=1, source_target_pairs={{0,32},{32,0},{64,96},{96,64},{1,33},{33,1},{65,97},{97,65},{2,34}... | collective-permute-start | bytes 3932168 | tf_op jit(solution)/shard_map/ppermute | solution.py:240
  138.7 41.5 %collective-permute-start.2 = (bf16[8,80,2,512]{3,2,1,0:T(2,128)(2,1)}, bf16[8,80,2,512]{3,2,1,0:T(2,128)(2,1)}, u32[]{:S(2)}, u32[]{:S(2)}) collective-permute-start(bf16[8,80,2,512]{3,2,1,0:T(2,128)(2,1)} %get-tuple-element.34), channel_id=1, source_target_pairs={{0,64},{32,96},{64,0},{96,32},{1,65},{33,97},{65,1},{97,33},{2,66}... | collective-permute-start | bytes 3932168 | tf_op jit(solution)/shard_map/ppermute | solution.py:240
  140.0 71.5 %collective-permute-start.3 = (bf16[8,80,2,512]{3,2,1,0:T(2,128)(2,1)}, bf16[8,80,2,512]{3,2,1,0:T(2,128)(2,1)}, u32[]{:S(2)}, u32[]{:S(2)}) collective-permute-start(bf16[8,80,2,512]{3,2,1,0:T(2,128)(2,1)} %get-tuple-element.35), channel_id=1, source_target_pairs={{0,96},{32,64},{64,32},{96,0},{1,97},{33,65},{65,33},{97,1},{2,98}... | collective-permute-start | bytes 3932168 | tf_op jit(solution)/shard_map/ppermute | solution.py:240
  162.1 60.5 %all-to-all-start.1 = ((bf16[32,2,80,128]{3,2,1,0:T(8,128)(2,1)}), bf16[32,2,80,128]{3,2,1,0:T(8,128)(2,1)}, u32[]{:S(2)}, u32[]{:S(2)}) async-start(bf16[32,2,80,128]{3,2,1,0:T(8,128)(2,1)} %bitcast.21), calls=%async_computation.1 | async-start | bytes 2621440 | tf_op jit(solution)/shard_map/all_to_all | solution.py:236
  227.9 15.9 %copy-start.4 = (f32[2,2,80,512]{3,2,1,0:T(8,128)S(1)}, f32[2,2,80,512]{3,2,1,0:T(8,128)}, u32[]{:S(2)}) copy-start(f32[2,2,80,512]{3,2,1,0:T(8,128)} %copy-done.3) | copy-start | bytes 1966084
  227.9 15.9 %copy-start.6 = (f32[2,2,80,512]{3,2,1,0:T(8,128)S(1)}, f32[2,2,80,512]{3,2,1,0:T(8,128)}, u32[]{:S(2)}) copy-start(f32[2,2,80,512]{3,2,1,0:T(8,128)} %copy-done.5) | copy-start | bytes 1966084
  227.9 5.0 %collective-permute-start.4 = (bf16[2,2,80,512]{3,2,1,0:T(8,128)(2,1)S(1)}, bf16[2,2,80,512]{3,2,1,0:T(8,128)(2,1)S(1)}, u32[]{:S(2)}, u32[]{:S(2)}) collective-permute-start(bf16[2,2,80,512]{3,2,1,0:T(8,128)(2,1)S(1)} %get-tuple-element.37), channel_id=1, source_target_pairs={{0,32},{32,0},{64,96},{96,64},{1,33},{33,1},{65,97},{97,65},{2,34}... | collective-permute-start | bytes 983048 | tf_op jit(solution)/shard_map/ppermute | solution.py:240
  233.0 10.7 %collective-permute-start.5 = (bf16[2,2,80,512]{3,2,1,0:T(8,128)(2,1)S(1)}, bf16[2,2,80,512]{3,2,1,0:T(8,128)(2,1)S(1)}, u32[]{:S(2)}, u32[]{:S(2)}) collective-permute-start(bf16[2,2,80,512]{3,2,1,0:T(8,128)(2,1)S(1)} %fusion.13), channel_id=1, source_target_pairs={{0,64},{32,96},{64,0},{96,32},{1,65},{33,97},{65,1},{97,33},{2,66}... | collective-permute-start | bytes 983048 | tf_op jit(solution)/shard_map/ppermute | solution.py:240
  244.2 2.5 collective-permute-start.6
  275.2 5.8 %copy-start.9 = (s32[80,2,512]{2,1,0:T(2,128)S(1)}, s32[80,2,512]{2,1,0:T(2,128)}, u32[]{:S(2)}) copy-start(s32[80,2,512]{2,1,0:T(2,128)} %param.12) | copy-start | bytes 983044
  275.2 5.8 %copy-start.11 = (f32[80,512]{1,0:T(8,128)S(1)}, f32[80,512]{1,0:T(8,128)}, u32[]{:S(2)}) copy-start(f32[80,512]{1,0:T(8,128)} %copy-done.10) | copy-start | bytes 491524
  275.2 21.4 %all-to-all-start.3 = ((bf16[32,2,80,128]{3,1,2,0:T(2,128)(2,1)}), bf16[32,2,80,128]{3,1,2,0:T(2,128)(2,1)S(1)}, u32[]{:S(2)}, u32[]{:S(2)}) async-start(bf16[32,2,80,128]{3,1,2,0:T(2,128)(2,1)} %copy.73), calls=%async_computation.3 | async-start | bytes 2621440 | tf_op jit(solution)/shard_map/all_to_all | solution.py:236
  303.7 7.0 %copy-start.7 = (bf16[8,80,2,512]{3,2,1,0:T(2,128)(2,1)}, bf16[8,80,2,512]{3,2,1,0:T(2,128)(2,1)S(1)}, u32[]{:S(2)}) copy-start(bf16[8,80,2,512]{3,2,1,0:T(2,128)(2,1)S(1)} %fusion.refs_0_) | copy-start | bytes 3932164
  303.7 7.0 %collective-permute-start.8 = (bf16[8,80,2,512]{3,2,1,0:T(2,128)(2,1)S(1)}, bf16[8,80,2,512]{3,2,1,0:T(2,128)(2,1)}, u32[]{:S(2)}, u32[]{:S(2)}) collective-permute-start(bf16[8,80,2,512]{3,2,1,0:T(2,128)(2,1)S(1)} %fusion.refs_0_), channel_id=1, source_target_pairs={{0,32},{32,0},{64,96},{96,64},{1,33},{33,1},{65,97},{97,65},{2,34}... | collective-permute-start | bytes 3932168 | tf_op jit(solution)/shard_map/ppermute | solution.py:240
  307.9 83.3 %collective-permute-start.7 = (bf16[8,80,2,512]{3,2,1,0:T(2,128)(2,1)S(1)}, bf16[8,80,2,512]{3,2,1,0:T(2,128)(2,1)S(1)}, u32[]{:S(2)}, u32[]{:S(2)}) collective-permute-start(bf16[8,80,2,512]{3,2,1,0:T(2,128)(2,1)S(1)} %fusion.refs_0_), channel_id=1, source_target_pairs={{0,64},{32,96},{64,0},{96,32},{1,65},{33,97},{65,1},{97,33},{2,66}... | collective-permute-start | bytes 3932168 | tf_op jit(solution)/shard_map/ppermute | solution.py:240
  391.3 3.1 collective-permute-start.9
  (9 other events, 13.1 us)

commit v3 on v2

--- a/solution.py
+++ b/solution.py
@@ -124,7 +124,7 @@
             jax.ShapeDtypeStruct(shape, jnp.float32),
             jax.ShapeDtypeStruct(shape, jnp.bfloat16),
         ],
-        compiler_params=pltpu.CompilerParams(vmem_limit_bytes=32 << 20),
+        compiler_params=pltpu.CompilerParams(vmem_limit_bytes=56 << 20),
         cost_estimate=pl.CostEstimate(
             flops=8 * spread.size, bytes_accessed=10 * spread.size, transcendentals=0
         ),
@@ -167,34 +167,46 @@
         ],
         out_specs=pl.BlockSpec((members, 1, rows, levels, 128), lambda t: (0, t, 0, 0, 0)),
         out_shape=jax.ShapeDtypeStruct((members, tiles, rows, levels, 128), jnp.bfloat16),
-        compiler_params=pltpu.CompilerParams(vmem_limit_bytes=32 << 20),
+        compiler_params=pltpu.CompilerParams(vmem_limit_bytes=56 << 20),
         cost_estimate=pl.CostEstimate(
             flops=8 * pert[0].size, bytes_accessed=10 * pert[0].size, transcendentals=0
         ),
     )(sea, own, other, *pert)
 
 
-def pick_kernel(slot_ref, whole, *refs):
-    outs, sems = refs[:-1], refs[-1]
+def pick_kernel(order, slot_ref, whole, *refs):
+    outs = refs[: len(order)]
+    held, arrive, leave = refs[len(order) :]
     count = outs[0].shape[0]
-    copies = []
-    for i, out in enumerate(outs):
-        at = pl.ds((slot_ref[0] ^ (i + 1)) * count, count)
-        copies.append(pltpu.make_async_copy(whole.at[at], out, sems.at[i]))
-        copies[-1].start()
-    for copy in copies:
+    arriving = []
+    for i, k in enumerate(order):
+        at = pl.ds((slot_ref[0] ^ k) * count, count)
+        arriving.append(pltpu.make_async_copy(whole.at[at], held.at[i], arrive.at[i]))
+        arriving[-1].start()
+    leaving = []
+    for i, copy in enumerate(arriving):
         copy.wait()
-
-
-def pick(slot, whole):
+        leaving.append(pltpu.make_async_copy(held.at[i], outs[i], leave.at[i]))
+        leaving[-1].start()
+    for copy in leaving:
+        copy.wait()
+
+
+def pick(slot, order, whole):
     anywhere = pl.BlockSpec(memory_space=pl.ANY)
     shape = (whole.shape[0] // 4, *whole.shape[1:])
-    return pl.pallas_call(
-        pick_kernel,
+    count = len(order)
+    return pl.pallas_call(
+        functools.partial(pick_kernel, order),
         in_specs=[pl.BlockSpec(memory_space=pltpu.SMEM), anywhere],
-        out_specs=[anywhere] * 3,
-        out_shape=[jax.ShapeDtypeStruct(shape, whole.dtype)] * 3,
-        scratch_shapes=[pltpu.SemaphoreType.DMA((3,))],
+        out_specs=[anywhere] * count,
+        out_shape=[jax.ShapeDtypeStruct(shape, whole.dtype)] * count,
+        scratch_shapes=[
+            pltpu.VMEM((count, *shape), whole.dtype),
+            pltpu.SemaphoreType.DMA((count,)),
+            pltpu.SemaphoreType.DMA((count,)),
+        ],
+        compiler_params=pltpu.CompilerParams(vmem_limit_bytes=32 << 20),
         cost_estimate=pl.CostEstimate(
             flops=0, bytes_accessed=3 * whole.size, transcendentals=0
         ),
@@ -206,8 +218,8 @@
     out, sems = refs[-2:]
     count = parts[0].shape[0]
     copies = []
-    for i, (k, part) in enumerate(zip(groups, parts)):
-        at = pl.ds((slot_ref[0] ^ k) * count, count)
+    for i, ((k, half), part) in enumerate(zip(groups, parts)):
+        at = pl.ds(((slot_ref[0] ^ k) * 2 + half) * count, count)
         copies.append(pltpu.make_async_copy(part, out.at[at], sems.at[i]))
         copies[-1].start()
     for copy in copies:
@@ -216,18 +228,22 @@
 
 def place(slot, groups, parts, members, base=None):
     anywhere = pl.BlockSpec(memory_space=pl.ANY)
-    operands = list(parts) + ([] if base is None else [base])
+    vmem = pl.BlockSpec(memory_space=pltpu.VMEM)
+    extra = [] if base is None else [base]
     return pl.pallas_call(
         functools.partial(place_kernel, groups),
-        in_specs=[pl.BlockSpec(memory_space=pltpu.SMEM)] + [anywhere] * len(operands),
+        in_specs=[pl.BlockSpec(memory_space=pltpu.SMEM)]
+        + [vmem] * len(parts)
+        + [anywhere] * len(extra),
         out_specs=anywhere,
         out_shape=jax.ShapeDtypeStruct((members, *parts[0].shape[1:]), jnp.bfloat16),
         scratch_shapes=[pltpu.SemaphoreType.DMA((len(groups),))],
-        input_output_aliases={} if base is None else {len(operands): 0},
+        input_output_aliases={} if base is None else {len(parts) + 1: 0},
+        compiler_params=pltpu.CompilerParams(vmem_limit_bytes=32 << 20),
         cost_estimate=pl.CostEstimate(
             flops=0, bytes_accessed=4 * len(parts) * parts[0].size, transcendentals=0
         ),
-    )(slot.reshape(1), *operands)
+    )(slot.reshape(1), *parts, *extra)
 
 
 def swap_columns(tiles):
@@ -265,11 +281,12 @@
     norm_scale = 1.0 / math.sqrt(members)
     perturbed = perturbations[0]
 
-    sent = dict(zip((1, 2, 3), pick(slot, perturbed)))
+    order = (2, 3, 1)
+    sent = dict(zip(order, pick(slot, order, perturbed)))
     control, land_mask, obs_cell, sent = lax.optimization_barrier(
         (control, land_mask, obs_cell, sent)
     )
-    got = {k: row_major(swap_slot(sent[k], k)) for k in (2, 3, 1)}
+    got = {k: row_major(swap_slot(sent[k], k)) for k in order}
     pert = [lax.dynamic_slice_in_dim(perturbed, slot * own, own, 0), got[1], got[2], got[3]]
 
     obs = jnp.stack([obs_cell.astype(jnp.float32), obs_value, obs_weight])
@@ -314,21 +331,26 @@
     ).astype(jnp.bfloat16)
     returned = swap_columns(back_across.reshape(tile_shape))
     returned = returned.transpose(0, 2, 3, 1, 4).reshape(own, row_count, levels, col_count)
-    filtered = weight_mask * lax.dot_general(
-        returned * sea.astype(jnp.bfloat16),
-        inverse_x,
-        (((3,), (1,)), ((), ())),
-        preferred_element_type=jnp.float32,
-    )
-    gradient = (mine.astype(jnp.float32) + filtered).astype(jnp.bfloat16)
-    gradient = row_major(gradient.transpose(0, 2, 1, 3))
-
-    half = row_major(swap_slot(gradient, 2))
-    beside = row_major(swap_slot(gradient, 1))
-    result = place(slot, (0, 1), (gradient, beside), members)
-    half, result = lax.optimization_barrier((half, result))
-    across_both = row_major(swap_slot(half, 1))
-    return place(slot, (2, 3), (half, across_both), members, result)
+    returned = returned * sea.astype(jnp.bfloat16)
+    halves = []
+    for half in range(2):
+        at = slice(half * (own // 2), (half + 1) * (own // 2))
+        filtered = weight_mask * lax.dot_general(
+            returned[at],
+            inverse_x,
+            (((3,), (1,)), ((), ())),
+            preferred_element_type=jnp.float32,
+        )
+        gradient = (mine[at].astype(jnp.float32) + filtered).astype(jnp.bfloat16)
+        halves.append(row_major(gradient.transpose(0, 2, 1, 3)))
+
+    far = [row_major(swap_slot(g, 2)) for g in halves]
+    near = [row_major(swap_slot(g, 1)) for g in halves]
+    result = place(slot, ((0, 0), (0, 1), (1, 0), (1, 1)), (*halves, *near), members)
+    far[1], result = lax.optimization_barrier((far[1], result))
+    both = [row_major(swap_slot(g, 1)) for g in far]
+    result = place(slot, ((2, 0), (3, 0), (2, 1)), (far[0], both[0], far[1]), members, result)
+    return place(slot, ((3, 1),), (both[1],), members, result)
 
 
 def solution(mesh):

time: 480 us -> 239 us (0.50)
  Pallas kernels: 301 us -> 29.6 us
  starting transfers between devices: 40.4 us -> 54.9 us
  local copies, waits for them, and re-layouts: 20.6 us -> 30.9 us
    pallas_call x2 -> x3, Pallas kernels: 161 us -> 3.65 us  [place(): pl.pallas_call(functools.partial(place_kernel, groups), in_specs=[pl.Bloc...]
    pallas_call x1, Pallas kernels: 120 us -> 1.84 us  [pick(): pl.pallas_call(functools.partial(pick_kernel, order), in_specs=[pl.BlockS...]
    ppermute x10 -> x13, starting transfers between devices: 17.6 us -> 32.6 us  [swap_slot(): return lax.ppermute(arr, 'slot', [(i, i ^ k) for i in range(4)])]
    transpose x0 -> x1, other arithmetic: none -> 5.42 us  [per_device(): halves.append(row_major(gradient.transpose(0, 2, 1, 3)))]
    ppermute x10 -> x13, waiting for transfers between devices: 50.6 us -> 54.7 us  [swap_slot(): return lax.ppermute(arr, 'slot', [(i, i ^ k) for i in range(4)])]
  transfers between devices with their start and end apart: 13 -> 16, of which waited for: 9 -> 10; matrix products, arithmetic and copies ran while one was open for 4% -> 9% of each run, Pallas kernels for 20% -> 7%
where the time goes in v3:
time: 239 us; the launch traced here: 234 us
  waiting for transfers between devices  77.1 us (32%)
  starting transfers between devices  54.9 us (23%)
  local copies, waits for them, and re-layouts  30.9 us (13%)
  Pallas kernels  29.6 us (12%)
  blocking collectives  23.6 us (10%)
  other arithmetic  11.3 us (5%)
  matrix products  6.52 us (3%)
    ppermute x13, waiting for transfers between devices, swap_slot(): return lax.ppermute(arr, 'slot', [(i, i ^ k) for i in range(4)])  54.7 us
    ppermute x13, starting transfers between devices, swap_slot(): return lax.ppermute(arr, 'slot', [(i, i ^ k) for i in range(4)])  32.6 us
    all_to_all x1, blocking collectives, swap_columns(): lax.all_to_all(flat, 'horiz', split_axis=0, concat_axis=0, tiled=True)  23.6 us
    all_to_all x3, waiting for transfers between devices, swap_columns(): lax.all_to_all(flat, 'horiz', split_axis=0, concat_axis=0, tiled=True)  22.5 us
    all_to_all x3, starting transfers between devices, swap_columns(): lax.all_to_all(flat, 'horiz', split_axis=0, concat_axis=0, tiled=True)  22.3 us
    pallas_call x1, Pallas kernels, obs_fields(): pl.pallas_call(obs_kernel, grid=(slots, count // OBS_BLOCK), in_specs=[pa...  14.7 us
    another operation x3, local copies, waits for them, and re-layouts, row_major(): return with_layout_constraint(arr, Layout(tuple(range(arr.ndim))))  8.03 us
    unnamed x42, local copies, waits for them, and re-layouts  5.99 us
  transfers between devices with their start and end apart: 16, of which 10 were waited for; matrix products, arithmetic and copies ran while one was open for 9% of the time, Pallas kernels for 7%

profile of v3, /device:TPU:37, one launch (start us, length us, event | category | flops | bytes accessed | tf_op | source)
XLA Modules:
  0.0 234.5 jit_solution(1780008835121314631)
XLA Ops:
  8.0 3.6 %copy.59 = bf16[32,80,2,512]{3,1,2,0:T(8,128)(2,1)} copy(bf16[32,80,2,512]{3,2,1,0:T(2,128)(2,1)S(1)} %copy-done.2) | data formatting | bytes 10485760 | tf_op jit(solution)/shard_map/optimization_barrier | solution.py:286
  15.6 8.5 %all-to-all-start = ((bf16[32,2,80,128]{3,2,1,0:T(8,128)(2,1)}), bf16[32,2,80,128]{3,2,1,0:T(8,128)(2,1)}, u32[]{:S(2)}, u32[]{:S(2)}) async-start(bf16[32,2,80,128]{3,2,1,0:T(8,128)(2,1)} %bitcast.9), calls=%async_computation | async-start | bytes 2621440 | tf_op jit(solution)/shard_map/all_to_all | solution.py:252
  24.8 3.9 %collective-permute-start.3 = (bf16[8,80,2,512]{3,2,1,0:T(2,128)(2,1)}, bf16[8,80,2,512]{3,2,1,0:T(2,128)(2,1)}, u32[]{:S(2)}, u32[]{:S(2)}) collective-permute-start(bf16[8,80,2,512]{3,2,1,0:T(2,128)(2,1)} %get-tuple-element.35), channel_id=1, source_target_pairs={{0,96},{32,64},{64,32},{96,0},{1,97},{33,65},{65,33},{97,1},{2,98}... | collective-permute-start | bytes 3932168 | tf_op jit(solution)/shard_map/ppermute | solution.py:256
  29.3 11.4 %collective-permute-done = f32[3,1,8192]{2,1,0:T(1,128)S(1)} collective-permute-done((f32[3,1,8192]{2,1,0:T(1,128)S(1)}, f32[3,1,8192]{2,1,0:T(1,128)S(1)}, u32[]{:S(2)}, u32[]{:S(2)}) %collective-permute-start) | collective-permute-done | bytes 98336 | tf_op jit(solution)/shard_map/ppermute | solution.py:256
  40.9 14.7 %shard_map.110 = (f32[2,2,80,512]{3,2,1,0:T(8,128)S(1)}, f32[2,2,80,512]{3,2,1,0:T(8,128)S(1)}) custom-call(f32[2,3,1,8192]{3,2,1,0:T(1,128)S(1)} %pad_maximum_fusion.1.cell_ref.value_ref.weight_ref, f32[2,3,1,8192]{3,2,1,0:T(1,128)S(1)} %pad_maximum_fusion.1.cell_ref.value_ref.weight_ref, f32[2,3,1,8192]{3,2,1,0:T(1,128)S(1)} %pad_maximum_fusion.1.cell_ref.value_ref.weight_ref), custom_call_target="tpu_custom_call" | custom-call | flops 21474836480 | bytes 1310720 | tf_op jit(solution)/shard_map/pallas_call | solution.py:75
  55.6 2.8 %copy.64 = bf16[8,4,2,80,128]{4,2,1,0,3:T(2,128)(2,1)S(1)} copy(bf16[8,4,2,80,128]{4,3,2,1,0:T(8,128)(2,1)} %bitcast.10) | data formatting | bytes 2621440 | tf_op jit(solution)/shard_map/optimization_barrier | solution.py:306
  61.2 8.0 %all-to-all-start.1 = ((bf16[32,2,80,128]{3,2,1,0:T(8,128)(2,1)}), bf16[32,2,80,128]{3,2,1,0:T(8,128)(2,1)}, u32[]{:S(2)}, u32[]{:S(2)}) async-start(bf16[32,2,80,128]{3,2,1,0:T(8,128)(2,1)} %bitcast.94), calls=%async_computation.1 | async-start | bytes 2621440 | tf_op jit(solution)/shard_map/all_to_all | solution.py:252
  72.9 2.7 %copy.121 = bf16[8,80,2,512]{3,1,2,0:T(8,128)(2,1)} copy(bf16[8,80,2,512]{3,2,1,0:T(2,128)(2,1)} %collective-permute-done.3) | data formatting | bytes 2621440 | tf_op jit(solution)/shard_map/layout_constraint | solution.py:260
  75.6 21.2 %collective-permute-done.2 = bf16[8,80,2,512]{3,2,1,0:T(2,128)(2,1)} collective-permute-done((bf16[8,80,2,512]{3,2,1,0:T(2,128)(2,1)}, bf16[8,80,2,512]{3,2,1,0:T(2,128)(2,1)}, u32[]{:S(2)}, u32[]{:S(2)}) %collective-permute-start.2) | collective-permute-done | bytes 1310752 | tf_op jit(solution)/shard_map/ppermute | solution.py:256
  99.5 2.7 %copy.123 = bf16[8,80,2,512]{3,1,2,0:T(8,128)(2,1)} copy(bf16[8,80,2,512]{3,2,1,0:T(2,128)(2,1)} %collective-permute-done.1) | data formatting | bytes 2621440 | tf_op jit(solution)/shard_map/layout_constraint | solution.py:260
  102.2 9.8 %all-to-all-done.1 = bf16[32,2,80,128]{3,2,1,0:T(8,128)(2,1)} async-done(((bf16[32,2,80,128]{3,2,1,0:T(8,128)(2,1)}), bf16[32,2,80,128]{3,2,1,0:T(8,128)(2,1)}, u32[]{:S(2)}, u32[]{:S(2)}) %all-to-all-start.1) | async-done | bytes 1310752 | tf_op jit(solution)/shard_map/all_to_all | solution.py:252
  111.9 4.5 %shard_map.111 = (f32[2,2,80,512]{3,2,1,0:T(8,128)}, bf16[2,2,80,512]{3,2,1,0:T(8,128)(2,1)}) custom-call(bf16[8,4,2,80,128]{4,3,2,1,0:T(8,128)(2,1)} %bitcast.22.spread_ref, bf16[8,2,80,512]{3,2,1,0:T(8,128)(2,1)} %bitcast.85, bf16[8,2,80,512]{3,2,1,0:T(8,128)(2,1)} %bitcast.91, bf16[8,2,80,512]{3,2,1,0:T(8,128)(2,1)} %bitcast.89, ...), custom_call_target="tpu_custom_call" | custom-call | flops 5242880 | bytes 6553600 | tf_op jit(solution)/shard_map/pallas_call | solution.py:112
  116.5 3.3 %collective-permute-start.4 = (bf16[2,2,80,512]{3,2,1,0:T(8,128)(2,1)}, bf16[2,2,80,512]{3,2,1,0:T(8,128)(2,1)S(1)}, u32[]{:S(2)}, u32[]{:S(2)}) collective-permute-start(bf16[2,2,80,512]{3,2,1,0:T(8,128)(2,1)} %get-tuple-element.37), channel_id=1, source_target_pairs={{0,32},{32,0},{64,96},{96,64},{1,33},{33,1},{65,97},{97,65},{2,34}... | collective-permute-start | bytes 983048 | tf_op jit(solution)/shard_map/ppermute | solution.py:256
  123.2 9.9 %collective-permute-done.5 = bf16[2,2,80,512]{3,2,1,0:T(8,128)(2,1)S(1)} collective-permute-done((bf16[2,2,80,512]{3,2,1,0:T(8,128)(2,1)S(1)}, bf16[2,2,80,512]{3,2,1,0:T(8,128)(2,1)S(1)}, u32[]{:S(2)}, u32[]{:S(2)}) %collective-permute-start.5) | collective-permute-done | bytes 327712 | tf_op jit(solution)/shard_map/ppermute | solution.py:256
  136.9 4.9 %shard_map.112 = bf16[8,4,2,80,128]{4,3,2,1,0:T(8,128)(2,1)} custom-call(f32[2,80,512]{2,1,0:T(8,128)} %copy-done.7, bf16[2,2,80,512]{3,2,1,0:T(8,128)(2,1)} %copy-done.10, bf16[2,2,80,512]{3,2,1,0:T(8,128)(2,1)} %copy-done.15, bf16[8,2,80,512]{3,2,1,0:T(8,128)(2,1)} %bitcast.86, bf16[8,2,80,512]{3,2,1,0:T(8,128)(2,1)} %bitcast.92, ...), custom_call_target="tpu_custom_call" | custom-call | flops 5242880 | bytes 6553600 | tf_op jit(solution)/shard_map/pallas_call | solution.py:156
  141.8 23.6 %all_to_all.20 = bf16[32,2,80,128]{3,2,1,0:T(8,128)(2,1)S(1)} all-to-all(bf16[32,2,80,128]{3,2,1,0:T(8,128)(2,1)} %bitcast.93), channel_id=1, replica_groups=mesh['slot'=4,'horiz'=32] {'horiz'}, dimensions={0} | all-to-all | bytes 2621440 | tf_op jit(solution)/shard_map/all_to_all | solution.py:252
  168.3 5.8 %all-to-all-start.3 = ((bf16[32,2,80,128]{3,1,2,0:T(2,128)(2,1)}), bf16[32,2,80,128]{3,1,2,0:T(2,128)(2,1)S(1)}, u32[]{:S(2)}, u32[]{:S(2)}) async-start(bf16[32,2,80,128]{3,1,2,0:T(2,128)(2,1)} %copy.73), calls=%async_computation.3 | async-start | bytes 2621440 | tf_op jit(solution)/shard_map/all_to_all | solution.py:252
  177.0 12.7 %all-to-all-done.3 = bf16[32,2,80,128]{3,1,2,0:T(2,128)(2,1)S(1)} async-done(((bf16[32,2,80,128]{3,1,2,0:T(2,128)(2,1)}), bf16[32,2,80,128]{3,1,2,0:T(2,128)(2,1)S(1)}, u32[]{:S(2)}, u32[]{:S(2)}) %all-to-all-start.3) | async-done | bytes 1310752 | tf_op jit(solution)/shard_map/all_to_all | solution.py:252
  193.5 5.4 %fusion.14 = (bf16[4,80,2,512]{3,2,1,0:T(2,128)(2,1)S(1)}, bf16[4,80,2,512]{3,2,1,0:T(2,128)(2,1)S(1)}) fusion(f32[4,2,80,512]{3,2,1,0:T(8,128)S(1)} %fusion.7, f32[2,80,512]{2,0,1:T(2,128)S(1)} %copy-done.14, f32[4,2,80,512]{3,2,1,0:T(8,128)S(1)} %copy-done.5, f32[4,2,80,512]{3,2,1,0:T(8,128)S(1)} %fusion.9, f32[4,2,80,512]{3,2,1,0:T(8,128)S(1)} %copy-done.6), kind=kLoop, calls=%fused_computation.36 | loop fusion | flops 1966080 | bytes 6881280 | tf_op jit(solution)/shard_map/transpose | solution.py:345
  199.6 4.4 %collective-permute-start.8 = (bf16[4,80,2,512]{3,2,1,0:T(2,128)(2,1)S(1)}, bf16[4,80,2,512]{3,2,1,0:T(2,128)(2,1)S(1)}, u32[]{:S(2)}, u32[]{:S(2)}) collective-permute-start(bf16[4,80,2,512]{3,2,1,0:T(2,128)(2,1)S(1)} %get-tuple-element.47.refs_0_), channel_id=1, source_target_pairs={{0,32},{32,0},{64,96},{96,64},{1,33},{33,1},{65,97},{97,65},{2,34}... | collective-permute-start | bytes 1966088 | tf_op jit(solution)/shard_map/ppermute | solution.py:256
  206.4 6.2 %collective-permute-done.11.refs_0_ = bf16[4,80,2,512]{3,2,1,0:T(2,128)(2,1)S(1)} collective-permute-done((bf16[4,80,2,512]{3,2,1,0:T(2,128)(2,1)S(1)}, bf16[4,80,2,512]{3,2,1,0:T(2,128)(2,1)S(1)}, u32[]{:S(2)}, u32[]{:S(2)}) %collective-permute-start.11) | collective-permute-done | bytes 655392 | tf_op jit(solution)/shard_map/ppermute | solution.py:256
  212.6 9.7 %collective-permute-start.12 = (bf16[4,80,2,512]{3,2,1,0:T(2,128)(2,1)S(1)}, bf16[4,80,2,512]{3,2,1,0:T(2,128)(2,1)S(1)}, u32[]{:S(2)}, u32[]{:S(2)}) collective-permute-start(bf16[4,80,2,512]{3,2,1,0:T(2,128)(2,1)S(1)} %collective-permute-done.11.refs_0_), channel_id=1, source_target_pairs={{0,32},{32,0},{64,96},{96,64},{1,33},{33,1},{65,97},{97,65},{2,34}... | collective-permute-start | bytes 1966088 | tf_op jit(solution)/shard_map/ppermute | solution.py:256
  223.9 2.8 %collective-permute-done.7.refs_2_ = bf16[4,80,2,512]{3,2,1,0:T(2,128)(2,1)S(1)} collective-permute-done((bf16[4,80,2,512]{3,2,1,0:T(2,128)(2,1)S(1)}, bf16[4,80,2,512]{3,2,1,0:T(2,128)(2,1)S(1)}, u32[]{:S(2)}, u32[]{:S(2)}) %collective-permute-start.7) | collective-permute-done | bytes 655392 | tf_op jit(solution)/shard_map/ppermute | solution.py:256
  226.7 5.1 %collective-permute-start.10 = (bf16[4,80,2,512]{3,2,1,0:T(2,128)(2,1)S(1)}, bf16[4,80,2,512]{3,2,1,0:T(2,128)(2,1)S(1)}, u32[]{:S(2)}, u32[]{:S(2)}) collective-permute-start(bf16[4,80,2,512]{3,2,1,0:T(2,128)(2,1)S(1)} %collective-permute-done.7.refs_2_), channel_id=1, source_target_pairs={{0,32},{32,0},{64,96},{96,64},{1,33},{33,1},{65,97},{97,65},{2,34}... | collective-permute-start | bytes 1966088 | tf_op jit(solution)/shard_map/ppermute | solution.py:256
  (95 shorter events, 46.4 us)
Async XLA Ops:
  0.0 13.0 %copy-start = (bf16[512,512]{1,0:T(8,128)(2,1)S(1)}, bf16[512,512]{1,0:T(8,128)(2,1)}, u32[]{:S(2)}) copy-start(bf16[512,512]{1,0:T(8,128)(2,1)} %param.15) | copy-start | bytes 1572868
  7.1 126.1 %copy-start.7 = (f32[2,80,512]{2,1,0:T(8,128)}, f32[2,80,512]{2,1,0:T(8,128)S(1)}, u32[]{:S(2)}) copy-start(f32[2,80,512]{2,1,0:T(8,128)S(1)} %get-tuple-element.50.sea_ref) | copy-start | bytes 983044
  15.6 8.5 %copy-start.20 = (s32[1,8192]{1,0:T(1,128)S(1)}, s32[1,8192]{1,0:T(1,128)}, u32[]{:S(2)}) copy-start(s32[1,8192]{1,0:T(1,128)} %param.19) | copy-start | bytes 98308
  15.6 8.5 %copy-start.16 = (f32[1,8192]{1,0:T(1,128)S(1)}, f32[1,8192]{1,0:T(1,128)}, u32[]{:S(2)}) copy-start(f32[1,8192]{1,0:T(1,128)} %param.21) | copy-start | bytes 98308
  15.6 8.5 %copy-start.17 = (f32[1,8192]{1,0:T(1,128)S(1)}, f32[1,8192]{1,0:T(1,128)}, u32[]{:S(2)}) copy-start(f32[1,8192]{1,0:T(1,128)} %param.20) | copy-start | bytes 98308
  15.6 39.9 %all-to-all-start = ((bf16[32,2,80,128]{3,2,1,0:T(8,128)(2,1)}), bf16[32,2,80,128]{3,2,1,0:T(8,128)(2,1)}, u32[]{:S(2)}, u32[]{:S(2)}) async-start(bf16[32,2,80,128]{3,2,1,0:T(8,128)(2,1)} %bitcast.9), calls=%async_computation | async-start | bytes 2621440 | tf_op jit(solution)/shard_map/all_to_all | solution.py:252
  24.2 16.4 %collective-permute-start = (f32[3,1,8192]{2,1,0:T(1,128)S(1)}, f32[3,1,8192]{2,1,0:T(1,128)S(1)}, u32[]{:S(2)}, u32[]{:S(2)}) collective-permute-start(f32[3,1,8192]{2,1,0:T(1,128)S(1)} %pad_maximum_fusion.2), channel_id=1, source_target_pairs={{0,64},{32,96},{64,0},{96,32},{1,65},{33,97},{65,1},{97,33},{2,66}... | collective-permute-start | bytes 294920 | tf_op jit(solution)/shard_map/ppermute | solution.py:256
  24.8 48.1 %collective-permute-start.3 = (bf16[8,80,2,512]{3,2,1,0:T(2,128)(2,1)}, bf16[8,80,2,512]{3,2,1,0:T(2,128)(2,1)}, u32[]{:S(2)}, u32[]{:S(2)}) collective-permute-start(bf16[8,80,2,512]{3,2,1,0:T(2,128)(2,1)} %get-tuple-element.35), channel_id=1, source_target_pairs={{0,96},{32,64},{64,32},{96,0},{1,97},{33,65},{65,33},{97,1},{2,98}... | collective-permute-start | bytes 3932168 | tf_op jit(solution)/shard_map/ppermute | solution.py:256
  28.7 68.2 %collective-permute-start.2 = (bf16[8,80,2,512]{3,2,1,0:T(2,128)(2,1)}, bf16[8,80,2,512]{3,2,1,0:T(2,128)(2,1)}, u32[]{:S(2)}, u32[]{:S(2)}) collective-permute-start(bf16[8,80,2,512]{3,2,1,0:T(2,128)(2,1)} %get-tuple-element.34), channel_id=1, source_target_pairs={{0,64},{32,96},{64,0},{96,32},{1,65},{33,97},{65,1},{97,33},{2,66}... | collective-permute-start | bytes 3932168 | tf_op jit(solution)/shard_map/ppermute | solution.py:256
  29.2 70.3 %collective-permute-start.1 = (bf16[8,80,2,512]{3,2,1,0:T(2,128)(2,1)S(1)}, bf16[8,80,2,512]{3,2,1,0:T(2,128)(2,1)}, u32[]{:S(2)}, u32[]{:S(2)}) collective-permute-start(bf16[8,80,2,512]{3,2,1,0:T(2,128)(2,1)S(1)} %get-tuple-element.33), channel_id=1, source_target_pairs={{0,32},{32,0},{64,96},{96,64},{1,33},{33,1},{65,97},{97,65},{2,34}... | collective-permute-start | bytes 3932168 | tf_op jit(solution)/shard_map/ppermute | solution.py:256
  61.2 50.7 %all-to-all-start.1 = ((bf16[32,2,80,128]{3,2,1,0:T(8,128)(2,1)}), bf16[32,2,80,128]{3,2,1,0:T(8,128)(2,1)}, u32[]{:S(2)}, u32[]{:S(2)}) async-start(bf16[32,2,80,128]{3,2,1,0:T(8,128)(2,1)} %bitcast.94), calls=%async_computation.1 | async-start | bytes 2621440 | tf_op jit(solution)/shard_map/all_to_all | solution.py:252
  116.5 16.7 %copy-start.8 = (f32[2,2,80,512]{3,2,1,0:T(8,128)S(1)}, f32[2,2,80,512]{3,2,1,0:T(8,128)}, u32[]{:S(2)}) copy-start(f32[2,2,80,512]{3,2,1,0:T(8,128)} %get-tuple-element.36) | copy-start | bytes 1966084
  116.5 4.8 %collective-permute-start.4 = (bf16[2,2,80,512]{3,2,1,0:T(8,128)(2,1)}, bf16[2,2,80,512]{3,2,1,0:T(8,128)(2,1)S(1)}, u32[]{:S(2)}, u32[]{:S(2)}) collective-permute-start(bf16[2,2,80,512]{3,2,1,0:T(8,128)(2,1)} %get-tuple-element.37), channel_id=1, source_target_pairs={{0,32},{32,0},{64,96},{96,64},{1,33},{33,1},{65,97},{97,65},{2,34}... | collective-permute-start | bytes 983048 | tf_op jit(solution)/shard_map/ppermute | solution.py:256
  122.4 10.7 %collective-permute-start.5 = (bf16[2,2,80,512]{3,2,1,0:T(8,128)(2,1)S(1)}, bf16[2,2,80,512]{3,2,1,0:T(8,128)(2,1)S(1)}, u32[]{:S(2)}, u32[]{:S(2)}) collective-permute-start(bf16[2,2,80,512]{3,2,1,0:T(8,128)(2,1)S(1)} %fusion.18), channel_id=1, source_target_pairs={{0,64},{32,96},{64,0},{96,32},{1,65},{33,97},{65,1},{97,33},{2,66}... | collective-permute-start | bytes 983048 | tf_op jit(solution)/shard_map/ppermute | solution.py:256
  133.6 2.5 %collective-permute-start.6 = (bf16[2,2,80,512]{3,2,1,0:T(8,128)(2,1)S(1)}, bf16[2,2,80,512]{3,2,1,0:T(8,128)(2,1)S(1)}, u32[]{:S(2)}, u32[]{:S(2)}) collective-permute-start(bf16[2,2,80,512]{3,2,1,0:T(8,128)(2,1)S(1)} %multiply_convert_fusion.3.own_ref), channel_id=1, source_target_pairs={{0,32},{32,0},{64,96},{96,64},{1,33},{33,1},{65,97},{97,65},{2,34}... | collective-permute-start | bytes 983048 | tf_op jit(solution)/shard_map/ppermute | solution.py:256
  168.3 5.8 %copy-start.13 = (f32[2,80,512]{2,1,0:T(8,128)S(1)}, f32[2,80,512]{2,1,0:T(8,128)}, u32[]{:S(2)}) copy-start(f32[2,80,512]{2,1,0:T(8,128)} %copy-done.12) | copy-start | bytes 983044
  168.3 6.8 %copy-start.4 = (bf16[8,2,80,512]{3,2,1,0:T(8,128)(2,1)S(1)}, bf16[8,2,80,512]{3,2,1,0:T(8,128)(2,1)}, u32[]{:S(2)}) copy-start(bf16[8,2,80,512]{3,2,1,0:T(8,128)(2,1)} %copy-done.3) | copy-start | bytes 3932164
  168.3 21.4 %all-to-all-start.3 = ((bf16[32,2,80,128]{3,1,2,0:T(2,128)(2,1)}), bf16[32,2,80,128]{3,1,2,0:T(2,128)(2,1)S(1)}, u32[]{:S(2)}, u32[]{:S(2)}) async-start(bf16[32,2,80,128]{3,1,2,0:T(2,128)(2,1)} %copy.73), calls=%async_computation.3 | async-start | bytes 2621440 | tf_op jit(solution)/shard_map/all_to_all | solution.py:252
  199.0 13.7 %collective-permute-start.11 = (bf16[4,80,2,512]{3,2,1,0:T(2,128)(2,1)S(1)}, bf16[4,80,2,512]{3,2,1,0:T(2,128)(2,1)S(1)}, u32[]{:S(2)}, u32[]{:S(2)}) collective-permute-start(bf16[4,80,2,512]{3,2,1,0:T(2,128)(2,1)S(1)} %get-tuple-element.47.refs_0_), channel_id=1, source_target_pairs={{0,64},{32,96},{64,0},{96,32},{1,65},{33,97},{65,1},{97,33},{2,66}... | collective-permute-start | bytes 1966088 | tf_op jit(solution)/shard_map/ppermute | solution.py:256
  199.6 22.8 %collective-permute-start.8 = (bf16[4,80,2,512]{3,2,1,0:T(2,128)(2,1)S(1)}, bf16[4,80,2,512]{3,2,1,0:T(2,128)(2,1)S(1)}, u32[]{:S(2)}, u32[]{:S(2)}) collective-permute-start(bf16[4,80,2,512]{3,2,1,0:T(2,128)(2,1)S(1)} %get-tuple-element.47.refs_0_), channel_id=1, source_target_pairs={{0,32},{32,0},{64,96},{96,64},{1,33},{33,1},{65,97},{97,65},{2,34}... | collective-permute-start | bytes 1966088 | tf_op jit(solution)/shard_map/ppermute | solution.py:256
  204.0 18.4 %collective-permute-start.9 = (bf16[4,80,2,512]{3,2,1,0:T(2,128)(2,1)S(1)}, bf16[4,80,2,512]{3,2,1,0:T(2,128)(2,1)S(1)}, u32[]{:S(2)}, u32[]{:S(2)}) collective-permute-start(bf16[4,80,2,512]{3,2,1,0:T(2,128)(2,1)S(1)} %get-tuple-element.48.refs_1_), channel_id=1, source_target_pairs={{0,32},{32,0},{64,96},{96,64},{1,33},{33,1},{65,97},{97,65},{2,34}... | collective-permute-start | bytes 1966088 | tf_op jit(solution)/shard_map/ppermute | solution.py:256
  204.0 22.7 %collective-permute-start.7 = (bf16[4,80,2,512]{3,2,1,0:T(2,128)(2,1)S(1)}, bf16[4,80,2,512]{3,2,1,0:T(2,128)(2,1)S(1)}, u32[]{:S(2)}, u32[]{:S(2)}) collective-permute-start(bf16[4,80,2,512]{3,2,1,0:T(2,128)(2,1)S(1)} %get-tuple-element.48.refs_1_), channel_id=1, source_target_pairs={{0,64},{32,96},{64,0},{96,32},{1,65},{33,97},{65,1},{97,33},{2,66}... | collective-permute-start | bytes 1966088 | tf_op jit(solution)/shard_map/ppermute | solution.py:256
  212.6 19.1 %collective-permute-start.12 = (bf16[4,80,2,512]{3,2,1,0:T(2,128)(2,1)S(1)}, bf16[4,80,2,512]{3,2,1,0:T(2,128)(2,1)S(1)}, u32[]{:S(2)}, u32[]{:S(2)}) collective-permute-start(bf16[4,80,2,512]{3,2,1,0:T(2,128)(2,1)S(1)} %collective-permute-done.11.refs_0_), channel_id=1, source_target_pairs={{0,32},{32,0},{64,96},{96,64},{1,33},{33,1},{65,97},{97,65},{2,34}... | collective-permute-start | bytes 1966088 | tf_op jit(solution)/shard_map/ppermute | solution.py:256
  226.7 6.8 %collective-permute-start.10 = (bf16[4,80,2,512]{3,2,1,0:T(2,128)(2,1)S(1)}, bf16[4,80,2,512]{3,2,1,0:T(2,128)(2,1)S(1)}, u32[]{:S(2)}, u32[]{:S(2)}) collective-permute-start(bf16[4,80,2,512]{3,2,1,0:T(2,128)(2,1)S(1)} %collective-permute-done.7.refs_2_), channel_id=1, source_target_pairs={{0,32},{32,0},{64,96},{96,64},{1,33},{33,1},{65,97},{97,65},{2,34}... | collective-permute-start | bytes 1966088 | tf_op jit(solution)/shard_map/ppermute | solution.py:256
  (13 other events, 28.5 us)

commit v4 on v3

--- a/solution.py
+++ b/solution.py
@@ -79,7 +79,7 @@
         out_specs=[out, out],
         out_shape=[shape, shape],
         scratch_shapes=[pltpu.VMEM((levels * 8, 512), jnp.float32)],
-        compiler_params=pltpu.CompilerParams(vmem_limit_bytes=32 << 20),
+        compiler_params=pltpu.CompilerParams(vmem_limit_bytes=16 << 20),
         cost_estimate=pl.CostEstimate(
             flops=2 * levels * 8 * 512 * count * slots * 2,
             bytes_accessed=levels * 8 * 512 * 4,
@@ -124,7 +124,7 @@
             jax.ShapeDtypeStruct(shape, jnp.float32),
             jax.ShapeDtypeStruct(shape, jnp.bfloat16),
         ],
-        compiler_params=pltpu.CompilerParams(vmem_limit_bytes=56 << 20),
+        compiler_params=pltpu.CompilerParams(vmem_limit_bytes=12 << 20),
         cost_estimate=pl.CostEstimate(
             flops=8 * spread.size, bytes_accessed=10 * spread.size, transcendentals=0
         ),
@@ -167,7 +167,7 @@
         ],
         out_specs=pl.BlockSpec((members, 1, rows, levels, 128), lambda t: (0, t, 0, 0, 0)),
         out_shape=jax.ShapeDtypeStruct((members, tiles, rows, levels, 128), jnp.bfloat16),
-        compiler_params=pltpu.CompilerParams(vmem_limit_bytes=56 << 20),
+        compiler_params=pltpu.CompilerParams(vmem_limit_bytes=12 << 20),
         cost_estimate=pl.CostEstimate(
             flops=8 * pert[0].size, bytes_accessed=10 * pert[0].size, transcendentals=0
         ),
@@ -206,7 +206,7 @@
             pltpu.SemaphoreType.DMA((count,)),
             pltpu.SemaphoreType.DMA((count,)),
         ],
-        compiler_params=pltpu.CompilerParams(vmem_limit_bytes=32 << 20),
+        compiler_params=pltpu.CompilerParams(vmem_limit_bytes=56 << 20),
         cost_estimate=pl.CostEstimate(
             flops=0, bytes_accessed=3 * whole.size, transcendentals=0
         ),
@@ -239,7 +239,7 @@
         out_shape=jax.ShapeDtypeStruct((members, *parts[0].shape[1:]), jnp.bfloat16),
         scratch_shapes=[pltpu.SemaphoreType.DMA((len(groups),))],
         input_output_aliases={} if base is None else {len(parts) + 1: 0},
-        compiler_params=pltpu.CompilerParams(vmem_limit_bytes=32 << 20),
+        compiler_params=pltpu.CompilerParams(vmem_limit_bytes=12 << 20),
         cost_estimate=pl.CostEstimate(
             flops=0, bytes_accessed=4 * len(parts) * parts[0].size, transcendentals=0
         ),
@@ -283,9 +283,7 @@
 
     order = (2, 3, 1)
     sent = dict(zip(order, pick(slot, order, perturbed)))
-    control, land_mask, obs_cell, sent = lax.optimization_barrier(
-        (control, land_mask, obs_cell, sent)
-    )
+    land_mask, tile_id, sent = lax.optimization_barrier((land_mask, tile_id, sent))
     got = {k: row_major(swap_slot(sent[k], k)) for k in order}
     pert = [lax.dynamic_slice_in_dim(perturbed, slot * own, own, 0), got[1], got[2], got[3]]
 
@@ -303,7 +301,6 @@
     )
     along_x = along_x.reshape(own, row_count, levels, tiles, 128).transpose(0, 3, 1, 2, 4)
     received = swap_columns(along_x)
-    received, weight_sum, value_sum = lax.optimization_barrier((received, weight_sum, value_sum))
     received = received.reshape(-1, levels, 128)
     across = jnp.einsum(
         "yzx,yk->kzx", received, inverse_y, preferred_element_type=jnp.float32
@@ -315,6 +312,7 @@
     spread = swap_columns(deeper.reshape(tile_shape))
 
     pert = [p.transpose(0, 2, 1, 3) for p in pert]
+    spread, weight_sum, value_sum = lax.optimization_barrier((spread, weight_sum, value_sum))
     keep, send = increments(spread, pert)
     keep = keep + swap_slot(send, 1).astype(jnp.float32)
     far = swap_slot(keep.astype(jnp.bfloat16), 2).astype(jnp.float32)

time: 239 us -> 230 us (0.962)
  local copies, waits for them, and re-layouts: 30.9 us -> 26.5 us
  Pallas kernels: 29.6 us -> 26.6 us
    optimization_barrier x2 -> x0, local copies, waits for them, and re-layouts: 6.42 us -> none  [the longest x1 3.63 us: per_device(): lax.optimization_barrier((control, land_mask, obs_cell, sent))]
    all_to_all x0 -> x1, local copies, waits for them, and re-layouts: none -> 2.78 us  [swap_columns(): lax.all_to_all(flat, 'horiz', split_axis=0, concat_axis=0, tiled=True)]
    pallas_call x1, Pallas kernels: 4.91 us -> 2.32 us  [slot_sums(): pl.pallas_call(slot_sum_kernel, grid=(tiles,), in_specs=[pl.BlockSpec((ro...]
    dynamic_slice x0 -> x1, local copies, waits for them, and re-layouts: none -> 2.44 us  [per_device(): lax.dynamic_slice_in_dim(control, slot * own, own, 0).transpose(0, 2, 1, 3)]
    unnamed x42 -> x49, local copies, waits for them, and re-layouts: 5.99 us -> 6.54 us
  transfers between devices with their start and end apart: 16 -> 16, of which waited for: 10 -> 11; matrix products, arithmetic and copies ran while one was open for 9% -> 8% of each run, Pallas kernels for 7% -> 8%
where the time goes in v4:
time: 230 us; the launch traced here: 225 us
  waiting for transfers between devices  77.3 us (34%)
  starting transfers between devices  54.8 us (24%)
  Pallas kernels  26.6 us (12%)
  local copies, waits for them, and re-layouts  26.5 us (12%)
  blocking collectives  23.4 us (10%)
  other arithmetic  10.3 us (4%)
  matrix products  5.82 us (3%)
    ppermute x13, waiting for transfers between devices, swap_slot(): return lax.ppermute(arr, 'slot', [(i, i ^ k) for i in range(4)])  55 us
    ppermute x13, starting transfers between devices, swap_slot(): return lax.ppermute(arr, 'slot', [(i, i ^ k) for i in range(4)])  32.5 us
    all_to_all x1, blocking collectives, swap_columns(): lax.all_to_all(flat, 'horiz', split_axis=0, concat_axis=0, tiled=True)  23.4 us
    all_to_all x3, starting transfers between devices, swap_columns(): lax.all_to_all(flat, 'horiz', split_axis=0, concat_axis=0, tiled=True)  22.3 us
    all_to_all x3, waiting for transfers between devices, swap_columns(): lax.all_to_all(flat, 'horiz', split_axis=0, concat_axis=0, tiled=True)  22.3 us
    pallas_call x1, Pallas kernels, obs_fields(): pl.pallas_call(obs_kernel, grid=(slots, count // OBS_BLOCK), in_specs=[pa...  14.7 us
    another operation x3, local copies, waits for them, and re-layouts, row_major(): return with_layout_constraint(arr, Layout(tuple(range(arr.ndim))))  6.84 us
    unnamed x49, local copies, waits for them, and re-layouts  6.54 us
  transfers between devices with their start and end apart: 16, of which 11 were waited for; matrix products, arithmetic and copies ran while one was open for 8% of the time, Pallas kernels for 8%

profile of v4, /device:TPU:37, one launch (start us, length us, event | category | flops | bytes accessed | tf_op | source)
XLA Modules:
  0.0 225.4 jit_solution(7909214884952615235)
XLA Ops:
  0.0 3.4 %shard_map.109 = (bf16[8,80,2,512]{3,2,1,0:T(2,128)(2,1)}, bf16[8,80,2,512]{3,2,1,0:T(2,128)(2,1)}, bf16[8,80,2,512]{3,2,1,0:T(2,128)(2,1)}) custom-call(s32[1]{0:T(128)} %bitcast.slot_ref, bf16[32,80,2,512]{3,2,1,0:T(2,128)(2,1)} %bitcast.96), custom_call_target="tpu_custom_call" | custom-call | bytes 7864320 | tf_op jit(solution)/shard_map/pallas_call | solution.py:199
  10.5 8.5 %all-to-all-start = ((bf16[32,2,80,128]{3,2,1,0:T(8,128)(2,1)}), bf16[32,2,80,128]{3,2,1,0:T(8,128)(2,1)}, u32[]{:S(2)}, u32[]{:S(2)}) async-start(bf16[32,2,80,128]{3,2,1,0:T(8,128)(2,1)} %bitcast.9), calls=%async_computation | async-start | bytes 2621440 | tf_op jit(solution)/shard_map/all_to_all | solution.py:252
  19.7 3.9 %collective-permute-start.3 = (bf16[8,80,2,512]{3,2,1,0:T(2,128)(2,1)}, bf16[8,80,2,512]{3,2,1,0:T(2,128)(2,1)}, u32[]{:S(2)}, u32[]{:S(2)}) collective-permute-start(bf16[8,80,2,512]{3,2,1,0:T(2,128)(2,1)} %get-tuple-element.33), channel_id=1, source_target_pairs={{0,96},{32,64},{64,32},{96,0},{1,97},{33,65},{65,33},{97,1},{2,98}... | collective-permute-start | bytes 3932168 | tf_op jit(solution)/shard_map/ppermute | solution.py:256
  26.8 8.8 %collective-permute-done = f32[3,1,8192]{2,1,0:T(1,128)S(1)} collective-permute-done((f32[3,1,8192]{2,1,0:T(1,128)S(1)}, f32[3,1,8192]{2,1,0:T(1,128)S(1)}, u32[]{:S(2)}, u32[]{:S(2)}) %collective-permute-start) | collective-permute-done | bytes 98336 | tf_op jit(solution)/shard_map/ppermute | solution.py:256
  35.8 2.8 %copy.64 = bf16[32,2,80,128]{3,1,0,2:T(2,128)(2,1)S(1)} copy(bf16[32,2,80,128]{3,2,1,0:T(8,128)(2,1)} %all-to-all-done) | data formatting | bytes 2621440 | tf_op jit(solution)/shard_map/all_to_all | solution.py:252
  41.4 8.0 %all-to-all-start.1 = ((bf16[32,2,80,128]{3,2,1,0:T(8,128)(2,1)}), bf16[32,2,80,128]{3,2,1,0:T(8,128)(2,1)}, u32[]{:S(2)}, u32[]{:S(2)}) async-start(bf16[32,2,80,128]{3,2,1,0:T(8,128)(2,1)} %bitcast.97), calls=%async_computation.1 | async-start | bytes 2621440 | tf_op jit(solution)/shard_map/all_to_all | solution.py:252
  49.4 14.7 %shard_map.110 = (f32[2,2,80,512]{3,2,1,0:T(8,128)S(1)}, f32[2,2,80,512]{3,2,1,0:T(8,128)S(1)}) custom-call(f32[2,3,1,8192]{3,2,1,0:T(1,128)S(1)} %pad_maximum_fusion.1.cell_ref.value_ref.weight_ref, f32[2,3,1,8192]{3,2,1,0:T(1,128)S(1)} %pad_maximum_fusion.1.cell_ref.value_ref.weight_ref, f32[2,3,1,8192]{3,2,1,0:T(1,128)S(1)} %pad_maximum_fusion.1.cell_ref.value_ref.weight_ref), custom_call_target="tpu_custom_call" | custom-call | flops 21474836480 | bytes 1310720 | tf_op jit(solution)/shard_map/pallas_call | solution.py:75
  67.9 23.9 %collective-permute-done.2 = bf16[8,80,2,512]{3,2,1,0:T(2,128)(2,1)} collective-permute-done((bf16[8,80,2,512]{3,2,1,0:T(2,128)(2,1)}, bf16[8,80,2,512]{3,2,1,0:T(2,128)(2,1)}, u32[]{:S(2)}, u32[]{:S(2)}) %collective-permute-start.2) | collective-permute-done | bytes 1310752 | tf_op jit(solution)/shard_map/ppermute | solution.py:256
  91.7 2.6 %copy.128 = bf16[8,80,2,512]{3,1,2,0:T(8,128)(2,1)} copy(bf16[8,80,2,512]{3,2,1,0:T(2,128)(2,1)} %collective-permute-done.2) | data formatting | bytes 2621440 | tf_op jit(solution)/shard_map/layout_constraint | solution.py:260
  94.4 2.6 %copy.129 = bf16[8,80,2,512]{3,1,2,0:T(8,128)(2,1)} copy(bf16[8,80,2,512]{3,2,1,0:T(2,128)(2,1)} %collective-permute-done.1) | data formatting | bytes 2621440 | tf_op jit(solution)/shard_map/layout_constraint | solution.py:260
  97.0 9.8 %all-to-all-done.1 = bf16[32,2,80,128]{3,2,1,0:T(8,128)(2,1)} async-done(((bf16[32,2,80,128]{3,2,1,0:T(8,128)(2,1)}), bf16[32,2,80,128]{3,2,1,0:T(8,128)(2,1)}, u32[]{:S(2)}, u32[]{:S(2)}) %all-to-all-start.1) | async-done | bytes 1310752 | tf_op jit(solution)/shard_map/all_to_all | solution.py:252
  109.5 2.6 %shard_map.111 = (f32[2,2,80,512]{3,2,1,0:T(8,128)S(1)}, bf16[2,2,80,512]{3,2,1,0:T(8,128)(2,1)S(1)}) custom-call(bf16[8,4,2,80,128]{4,3,2,1,0:T(8,128)(2,1)} %bitcast.16.spread_ref, bf16[8,2,80,512]{3,2,1,0:T(8,128)(2,1)S(1)} %bitcast.87, bf16[8,2,80,512]{3,2,1,0:T(8,128)(2,1)S(1)} %bitcast.93, bf16[8,2,80,512]{3,2,1,0:T(8,128)(2,1)S(1)} %bitcast.91, ...), custom_call_target="tpu_custom_call" | custom-call | flops 5242880 | bytes 6553600 | tf_op jit(solution)/shard_map/pallas_call | solution.py:112
  112.1 3.3 %collective-permute-start.4 = (bf16[2,2,80,512]{3,2,1,0:T(8,128)(2,1)S(1)}, bf16[2,2,80,512]{3,2,1,0:T(8,128)(2,1)S(1)}, u32[]{:S(2)}, u32[]{:S(2)}) collective-permute-start(bf16[2,2,80,512]{3,2,1,0:T(8,128)(2,1)S(1)} %get-tuple-element.35), channel_id=1, source_target_pairs={{0,32},{32,0},{64,96},{96,64},{1,33},{33,1},{65,97},{97,65},{2,34}... | collective-permute-start | bytes 983048 | tf_op jit(solution)/shard_map/ppermute | solution.py:256
  117.5 9.9 %collective-permute-done.5 = bf16[2,2,80,512]{3,2,1,0:T(8,128)(2,1)S(1)} collective-permute-done((bf16[2,2,80,512]{3,2,1,0:T(8,128)(2,1)S(1)}, bf16[2,2,80,512]{3,2,1,0:T(8,128)(2,1)S(1)}, u32[]{:S(2)}, u32[]{:S(2)}) %collective-permute-start.5) | collective-permute-done | bytes 327712 | tf_op jit(solution)/shard_map/ppermute | solution.py:256
  132.8 23.4 %all_to_all.20 = bf16[32,2,80,128]{3,2,1,0:T(8,128)(2,1)S(1)} all-to-all(bf16[32,2,80,128]{3,2,1,0:T(8,128)(2,1)S(1)} %bitcast.95), channel_id=1, replica_groups=mesh['slot'=4,'horiz'=32] {'horiz'}, dimensions={0} | all-to-all | bytes 2621440 | tf_op jit(solution)/shard_map/all_to_all | solution.py:252
  159.2 5.8 %all-to-all-start.3 = ((bf16[32,2,80,128]{3,1,2,0:T(2,128)(2,1)}), bf16[32,2,80,128]{3,1,2,0:T(2,128)(2,1)S(1)}, u32[]{:S(2)}, u32[]{:S(2)}) async-start(bf16[32,2,80,128]{3,1,2,0:T(2,128)(2,1)} %copy.73), calls=%async_computation.3 | async-start | bytes 2621440 | tf_op jit(solution)/shard_map/all_to_all | solution.py:252
  168.1 12.4 %all-to-all-done.3 = bf16[32,2,80,128]{3,1,2,0:T(2,128)(2,1)S(1)} async-done(((bf16[32,2,80,128]{3,1,2,0:T(2,128)(2,1)}), bf16[32,2,80,128]{3,1,2,0:T(2,128)(2,1)S(1)}, u32[]{:S(2)}, u32[]{:S(2)}) %all-to-all-start.3) | async-done | bytes 1310752 | tf_op jit(solution)/shard_map/all_to_all | solution.py:252
  184.4 5.4 %fusion.14 = (bf16[4,80,2,512]{3,2,1,0:T(2,128)(2,1)S(1)}, bf16[4,80,2,512]{3,2,1,0:T(2,128)(2,1)S(1)}) fusion(f32[4,2,80,512]{3,2,1,0:T(8,128)S(1)} %fusion.7, f32[2,80,512]{2,0,1:T(2,128)S(1)} %copy-done.17, f32[4,2,80,512]{3,2,1,0:T(8,128)S(1)} %copy-done.11, f32[4,2,80,512]{3,2,1,0:T(8,128)S(1)} %fusion.9, f32[4,2,80,512]{3,2,1,0:T(8,128)S(1)} %copy-done.12), kind=kLoop, calls=%fused_computation.36 | loop fusion | flops 1966080 | bytes 6881280 | tf_op jit(solution)/shard_map/transpose | solution.py:343
  190.4 4.4 %collective-permute-start.8 = (bf16[4,80,2,512]{3,2,1,0:T(2,128)(2,1)S(1)}, bf16[4,80,2,512]{3,2,1,0:T(2,128)(2,1)S(1)}, u32[]{:S(2)}, u32[]{:S(2)}) collective-permute-start(bf16[4,80,2,512]{3,2,1,0:T(2,128)(2,1)S(1)} %get-tuple-element.45.refs_0_), channel_id=1, source_target_pairs={{0,32},{32,0},{64,96},{96,64},{1,33},{33,1},{65,97},{97,65},{2,34}... | collective-permute-start | bytes 1966088 | tf_op jit(solution)/shard_map/ppermute | solution.py:256
  194.9 2.5 %collective-permute-start.7 = (bf16[4,80,2,512]{3,2,1,0:T(2,128)(2,1)S(1)}, bf16[4,80,2,512]{3,2,1,0:T(2,128)(2,1)S(1)}, u32[]{:S(2)}, u32[]{:S(2)}) collective-permute-start(bf16[4,80,2,512]{3,2,1,0:T(2,128)(2,1)S(1)} %get-tuple-element.46.refs_1_), channel_id=1, source_target_pairs={{0,64},{32,96},{64,0},{96,32},{1,65},{33,97},{65,1},{97,33},{2,66}... | collective-permute-start | bytes 1966088 | tf_op jit(solution)/shard_map/ppermute | solution.py:256
  197.3 6.2 %collective-permute-done.11.refs_0_ = bf16[4,80,2,512]{3,2,1,0:T(2,128)(2,1)S(1)} collective-permute-done((bf16[4,80,2,512]{3,2,1,0:T(2,128)(2,1)S(1)}, bf16[4,80,2,512]{3,2,1,0:T(2,128)(2,1)S(1)}, u32[]{:S(2)}, u32[]{:S(2)}) %collective-permute-start.11) | collective-permute-done | bytes 655392 | tf_op jit(solution)/shard_map/ppermute | solution.py:256
  203.5 9.7 %collective-permute-start.12 = (bf16[4,80,2,512]{3,2,1,0:T(2,128)(2,1)S(1)}, bf16[4,80,2,512]{3,2,1,0:T(2,128)(2,1)S(1)}, u32[]{:S(2)}, u32[]{:S(2)}) collective-permute-start(bf16[4,80,2,512]{3,2,1,0:T(2,128)(2,1)S(1)} %collective-permute-done.11.refs_0_), channel_id=1, source_target_pairs={{0,32},{32,0},{64,96},{96,64},{1,33},{33,1},{65,97},{97,65},{2,34}... | collective-permute-start | bytes 1966088 | tf_op jit(solution)/shard_map/ppermute | solution.py:256
  214.8 2.8 %collective-permute-done.7.refs_2_ = bf16[4,80,2,512]{3,2,1,0:T(2,128)(2,1)S(1)} collective-permute-done((bf16[4,80,2,512]{3,2,1,0:T(2,128)(2,1)S(1)}, bf16[4,80,2,512]{3,2,1,0:T(2,128)(2,1)S(1)}, u32[]{:S(2)}, u32[]{:S(2)}) %collective-permute-start.7) | collective-permute-done | bytes 655392 | tf_op jit(solution)/shard_map/ppermute | solution.py:256
  217.6 5.0 %collective-permute-start.10 = (bf16[4,80,2,512]{3,2,1,0:T(2,128)(2,1)S(1)}, bf16[4,80,2,512]{3,2,1,0:T(2,128)(2,1)S(1)}, u32[]{:S(2)}, u32[]{:S(2)}) collective-permute-start(bf16[4,80,2,512]{3,2,1,0:T(2,128)(2,1)S(1)} %collective-permute-done.7.refs_2_), channel_id=1, source_target_pairs={{0,32},{32,0},{64,96},{96,64},{1,33},{33,1},{65,97},{97,65},{2,34}... | collective-permute-start | bytes 1966088 | tf_op jit(solution)/shard_map/ppermute | solution.py:256
  (101 shorter events, 42.3 us)
Async XLA Ops:
  0.0 7.9 %copy-start = (bf16[512,512]{1,0:T(8,128)(2,1)S(1)}, bf16[512,512]{1,0:T(8,128)(2,1)}, u32[]{:S(2)}) copy-start(bf16[512,512]{1,0:T(8,128)(2,1)} %param.15) | copy-start | bytes 1572868
  10.5 8.5 %copy-start.22 = (s32[1,8192]{1,0:T(1,128)S(1)}, s32[1,8192]{1,0:T(1,128)}, u32[]{:S(2)}) copy-start(s32[1,8192]{1,0:T(1,128)} %param.19) | copy-start | bytes 98308
  10.5 8.5 %copy-start.18 = (f32[1,8192]{1,0:T(1,128)S(1)}, f32[1,8192]{1,0:T(1,128)}, u32[]{:S(2)}) copy-start(f32[1,8192]{1,0:T(1,128)} %param.21) | copy-start | bytes 98308
  10.5 8.5 %copy-start.19 = (f32[1,8192]{1,0:T(1,128)S(1)}, f32[1,8192]{1,0:T(1,128)}, u32[]{:S(2)}) copy-start(f32[1,8192]{1,0:T(1,128)} %param.20) | copy-start | bytes 98308
  10.5 25.3 %all-to-all-start = ((bf16[32,2,80,128]{3,2,1,0:T(8,128)(2,1)}), bf16[32,2,80,128]{3,2,1,0:T(8,128)(2,1)}, u32[]{:S(2)}, u32[]{:S(2)}) async-start(bf16[32,2,80,128]{3,2,1,0:T(8,128)(2,1)} %bitcast.9), calls=%async_computation | async-start | bytes 2621440 | tf_op jit(solution)/shard_map/all_to_all | solution.py:252
  19.1 16.4 %collective-permute-start = (f32[3,1,8192]{2,1,0:T(1,128)S(1)}, f32[3,1,8192]{2,1,0:T(1,128)S(1)}, u32[]{:S(2)}, u32[]{:S(2)}) collective-permute-start(f32[3,1,8192]{2,1,0:T(1,128)S(1)} %pad_maximum_fusion.2), channel_id=1, source_target_pairs={{0,64},{32,96},{64,0},{96,32},{1,65},{33,97},{65,1},{97,33},{2,66}... | collective-permute-start | bytes 294920 | tf_op jit(solution)/shard_map/ppermute | solution.py:256
  19.7 46.6 %collective-permute-start.3 = (bf16[8,80,2,512]{3,2,1,0:T(2,128)(2,1)}, bf16[8,80,2,512]{3,2,1,0:T(2,128)(2,1)}, u32[]{:S(2)}, u32[]{:S(2)}) collective-permute-start(bf16[8,80,2,512]{3,2,1,0:T(2,128)(2,1)} %get-tuple-element.33), channel_id=1, source_target_pairs={{0,96},{32,64},{64,32},{96,0},{1,97},{33,65},{65,33},{97,1},{2,98}... | collective-permute-start | bytes 3932168 | tf_op jit(solution)/shard_map/ppermute | solution.py:256
  23.6 68.2 %collective-permute-start.2 = (bf16[8,80,2,512]{3,2,1,0:T(2,128)(2,1)}, bf16[8,80,2,512]{3,2,1,0:T(2,128)(2,1)}, u32[]{:S(2)}, u32[]{:S(2)}) collective-permute-start(bf16[8,80,2,512]{3,2,1,0:T(2,128)(2,1)} %get-tuple-element.32), channel_id=1, source_target_pairs={{0,64},{32,96},{64,0},{96,32},{1,65},{33,97},{65,1},{97,33},{2,66}... | collective-permute-start | bytes 3932168 | tf_op jit(solution)/shard_map/ppermute | solution.py:256
  24.1 70.3 %collective-permute-start.1 = (bf16[8,80,2,512]{3,2,1,0:T(2,128)(2,1)}, bf16[8,80,2,512]{3,2,1,0:T(2,128)(2,1)}, u32[]{:S(2)}, u32[]{:S(2)}) collective-permute-start(bf16[8,80,2,512]{3,2,1,0:T(2,128)(2,1)} %get-tuple-element.31), channel_id=1, source_target_pairs={{0,32},{32,0},{64,96},{96,64},{1,33},{33,1},{65,97},{97,65},{2,34}... | collective-permute-start | bytes 3932168 | tf_op jit(solution)/shard_map/ppermute | solution.py:256
  41.4 65.4 %all-to-all-start.1 = ((bf16[32,2,80,128]{3,2,1,0:T(8,128)(2,1)}), bf16[32,2,80,128]{3,2,1,0:T(8,128)(2,1)}, u32[]{:S(2)}, u32[]{:S(2)}) async-start(bf16[32,2,80,128]{3,2,1,0:T(8,128)(2,1)} %bitcast.97), calls=%async_computation.1 | async-start | bytes 2621440 | tf_op jit(solution)/shard_map/all_to_all | solution.py:252
  112.1 15.5 %copy-start.6 = (f32[2,2,80,512]{3,2,1,0:T(8,128)S(1)}, f32[2,2,80,512]{3,2,1,0:T(8,128)}, u32[]{:S(2)}) copy-start(f32[2,2,80,512]{3,2,1,0:T(8,128)} %copy-done.5) | copy-start | bytes 1966084
  112.1 15.5 %copy-start.8 = (f32[2,2,80,512]{3,2,1,0:T(8,128)S(1)}, f32[2,2,80,512]{3,2,1,0:T(8,128)}, u32[]{:S(2)}) copy-start(f32[2,2,80,512]{3,2,1,0:T(8,128)} %copy-done.7) | copy-start | bytes 1966084
  112.1 4.6 %collective-permute-start.4 = (bf16[2,2,80,512]{3,2,1,0:T(8,128)(2,1)S(1)}, bf16[2,2,80,512]{3,2,1,0:T(8,128)(2,1)S(1)}, u32[]{:S(2)}, u32[]{:S(2)}) collective-permute-start(bf16[2,2,80,512]{3,2,1,0:T(8,128)(2,1)S(1)} %get-tuple-element.35), channel_id=1, source_target_pairs={{0,32},{32,0},{64,96},{96,64},{1,33},{33,1},{65,97},{97,65},{2,34}... | collective-permute-start | bytes 983048 | tf_op jit(solution)/shard_map/ppermute | solution.py:256
  116.8 10.7 %collective-permute-start.5 = (bf16[2,2,80,512]{3,2,1,0:T(8,128)(2,1)S(1)}, bf16[2,2,80,512]{3,2,1,0:T(8,128)(2,1)S(1)}, u32[]{:S(2)}, u32[]{:S(2)}) collective-permute-start(bf16[2,2,80,512]{3,2,1,0:T(8,128)(2,1)S(1)} %fusion.18), channel_id=1, source_target_pairs={{0,64},{32,96},{64,0},{96,32},{1,65},{33,97},{65,1},{97,33},{2,66}... | collective-permute-start | bytes 983048 | tf_op jit(solution)/shard_map/ppermute | solution.py:256
  128.0 2.5 %collective-permute-start.6 = (bf16[2,2,80,512]{3,2,1,0:T(8,128)(2,1)S(1)}, bf16[2,2,80,512]{3,2,1,0:T(8,128)(2,1)S(1)}, u32[]{:S(2)}, u32[]{:S(2)}) collective-permute-start(bf16[2,2,80,512]{3,2,1,0:T(8,128)(2,1)S(1)} %multiply_convert_fusion.3.own_ref), channel_id=1, source_target_pairs={{0,32},{32,0},{64,96},{96,64},{1,33},{33,1},{65,97},{97,65},{2,34}... | collective-permute-start | bytes 983048 | tf_op jit(solution)/shard_map/ppermute | solution.py:256
  159.2 5.8 %copy-start.16 = (f32[2,80,512]{2,1,0:T(8,128)S(1)}, f32[2,80,512]{2,1,0:T(8,128)}, u32[]{:S(2)}) copy-start(f32[2,80,512]{2,1,0:T(8,128)} %copy-done.15) | copy-start | bytes 983044
  159.2 6.8 %copy-start.10 = (bf16[8,80,2,512]{3,2,1,0:T(2,128)(2,1)S(1)}, bf16[8,80,2,512]{3,2,1,0:T(2,128)(2,1)}, u32[]{:S(2)}) copy-start(bf16[8,80,2,512]{3,2,1,0:T(2,128)(2,1)} %copy-done.9) | copy-start | bytes 3932164
  159.2 21.4 %all-to-all-start.3 = ((bf16[32,2,80,128]{3,1,2,0:T(2,128)(2,1)}), bf16[32,2,80,128]{3,1,2,0:T(2,128)(2,1)S(1)}, u32[]{:S(2)}, u32[]{:S(2)}) async-start(bf16[32,2,80,128]{3,1,2,0:T(2,128)(2,1)} %copy.73), calls=%async_computation.3 | async-start | bytes 2621440 | tf_op jit(solution)/shard_map/all_to_all | solution.py:252
  189.9 13.7 %collective-permute-start.11 = (bf16[4,80,2,512]{3,2,1,0:T(2,128)(2,1)S(1)}, bf16[4,80,2,512]{3,2,1,0:T(2,128)(2,1)S(1)}, u32[]{:S(2)}, u32[]{:S(2)}) collective-permute-start(bf16[4,80,2,512]{3,2,1,0:T(2,128)(2,1)S(1)} %get-tuple-element.45.refs_0_), channel_id=1, source_target_pairs={{0,64},{32,96},{64,0},{96,32},{1,65},{33,97},{65,1},{97,33},{2,66}... | collective-permute-start | bytes 1966088 | tf_op jit(solution)/shard_map/ppermute | solution.py:256
  190.4 22.8 %collective-permute-start.8 = (bf16[4,80,2,512]{3,2,1,0:T(2,128)(2,1)S(1)}, bf16[4,80,2,512]{3,2,1,0:T(2,128)(2,1)S(1)}, u32[]{:S(2)}, u32[]{:S(2)}) collective-permute-start(bf16[4,80,2,512]{3,2,1,0:T(2,128)(2,1)S(1)} %get-tuple-element.45.refs_0_), channel_id=1, source_target_pairs={{0,32},{32,0},{64,96},{96,64},{1,33},{33,1},{65,97},{97,65},{2,34}... | collective-permute-start | bytes 1966088 | tf_op jit(solution)/shard_map/ppermute | solution.py:256
  194.8 18.4 %collective-permute-start.9 = (bf16[4,80,2,512]{3,2,1,0:T(2,128)(2,1)S(1)}, bf16[4,80,2,512]{3,2,1,0:T(2,128)(2,1)S(1)}, u32[]{:S(2)}, u32[]{:S(2)}) collective-permute-start(bf16[4,80,2,512]{3,2,1,0:T(2,128)(2,1)S(1)} %get-tuple-element.46.refs_1_), channel_id=1, source_target_pairs={{0,32},{32,0},{64,96},{96,64},{1,33},{33,1},{65,97},{97,65},{2,34}... | collective-permute-start | bytes 1966088 | tf_op jit(solution)/shard_map/ppermute | solution.py:256
  194.9 22.7 %collective-permute-start.7 = (bf16[4,80,2,512]{3,2,1,0:T(2,128)(2,1)S(1)}, bf16[4,80,2,512]{3,2,1,0:T(2,128)(2,1)S(1)}, u32[]{:S(2)}, u32[]{:S(2)}) collective-permute-start(bf16[4,80,2,512]{3,2,1,0:T(2,128)(2,1)S(1)} %get-tuple-element.46.refs_1_), channel_id=1, source_target_pairs={{0,64},{32,96},{64,0},{96,32},{1,65},{33,97},{65,1},{97,33},{2,66}... | collective-permute-start | bytes 1966088 | tf_op jit(solution)/shard_map/ppermute | solution.py:256
  203.5 19.1 %collective-permute-start.12 = (bf16[4,80,2,512]{3,2,1,0:T(2,128)(2,1)S(1)}, bf16[4,80,2,512]{3,2,1,0:T(2,128)(2,1)S(1)}, u32[]{:S(2)}, u32[]{:S(2)}) collective-permute-start(bf16[4,80,2,512]{3,2,1,0:T(2,128)(2,1)S(1)} %collective-permute-done.11.refs_0_), channel_id=1, source_target_pairs={{0,32},{32,0},{64,96},{96,64},{1,33},{33,1},{65,97},{97,65},{2,34}... | collective-permute-start | bytes 1966088 | tf_op jit(solution)/shard_map/ppermute | solution.py:256
  217.6 6.8 %collective-permute-start.10 = (bf16[4,80,2,512]{3,2,1,0:T(2,128)(2,1)S(1)}, bf16[4,80,2,512]{3,2,1,0:T(2,128)(2,1)S(1)}, u32[]{:S(2)}, u32[]{:S(2)}) collective-permute-start(bf16[4,80,2,512]{3,2,1,0:T(2,128)(2,1)S(1)} %collective-permute-done.7.refs_2_), channel_id=1, source_target_pairs={{0,32},{32,0},{64,96},{96,64},{1,33},{33,1},{65,97},{97,65},{2,34}... | collective-permute-start | bytes 1966088 | tf_op jit(solution)/shard_map/ppermute | solution.py:256
  (16 other events, 31.1 us)

commit v5 on v4

--- a/solution.py
+++ b/solution.py
@@ -10,6 +10,7 @@
 from jax.sharding import PartitionSpec as P
 
 OBS_BLOCK = 1024
+LEVEL_CUT = 48
 
 
 def local_sigma(tile_id, tile_scale, dev_index, row_count):
@@ -216,17 +217,17 @@
 def place_kernel(groups, slot_ref, *refs):
     parts = refs[: len(groups)]
     out, sems = refs[-2:]
-    count = parts[0].shape[0]
     copies = []
-    for i, ((k, half), part) in enumerate(zip(groups, parts)):
-        at = pl.ds(((slot_ref[0] ^ k) * 2 + half) * count, count)
-        copies.append(pltpu.make_async_copy(part, out.at[at], sems.at[i]))
+    for i, ((k, low), part) in enumerate(zip(groups, parts)):
+        count, levels = part.shape[:2]
+        at = out.at[pl.ds((slot_ref[0] ^ k) * count, count), pl.ds(low, levels)]
+        copies.append(pltpu.make_async_copy(part, at, sems.at[i]))
         copies[-1].start()
     for copy in copies:
         copy.wait()
 
 
-def place(slot, groups, parts, members, base=None):
+def place(slot, groups, parts, shape, base=None):
     anywhere = pl.BlockSpec(memory_space=pl.ANY)
     vmem = pl.BlockSpec(memory_space=pltpu.VMEM)
     extra = [] if base is None else [base]
@@ -236,7 +237,7 @@
         + [vmem] * len(parts)
         + [anywhere] * len(extra),
         out_specs=anywhere,
-        out_shape=jax.ShapeDtypeStruct((members, *parts[0].shape[1:]), jnp.bfloat16),
+        out_shape=jax.ShapeDtypeStruct(shape, jnp.bfloat16),
         scratch_shapes=[pltpu.SemaphoreType.DMA((len(groups),))],
         input_output_aliases={} if base is None else {len(parts) + 1: 0},
         compiler_params=pltpu.CompilerParams(vmem_limit_bytes=12 << 20),
@@ -327,28 +328,41 @@
     back_across = jnp.einsum(
         "kzx,yk->yzx", back_deep, inverse_y, preferred_element_type=jnp.float32
     ).astype(jnp.bfloat16)
-    returned = swap_columns(back_across.reshape(tile_shape))
-    returned = returned.transpose(0, 2, 3, 1, 4).reshape(own, row_count, levels, col_count)
-    returned = returned * sea.astype(jnp.bfloat16)
-    halves = []
-    for half in range(2):
-        at = slice(half * (own // 2), (half + 1) * (own // 2))
-        filtered = weight_mask * lax.dot_general(
-            returned[at],
+    back_across = back_across.reshape(tile_shape)
+    sea_half = sea.astype(jnp.bfloat16)
+    bounds = ((0, LEVEL_CUT), (LEVEL_CUT, levels))
+    gradients = []
+    for low, high in bounds:
+        returned = swap_columns(back_across[:, :, :, low:high])
+        returned = returned.transpose(0, 2, 3, 1, 4).reshape(own, row_count, -1, col_count)
+        filtered = weight_mask[:, low:high] * lax.dot_general(
+            returned * sea_half[:, low:high],
             inverse_x,
             (((3,), (1,)), ((), ())),
             preferred_element_type=jnp.float32,
         )
-        gradient = (mine[at].astype(jnp.float32) + filtered).astype(jnp.bfloat16)
-        halves.append(row_major(gradient.transpose(0, 2, 1, 3)))
-
-    far = [row_major(swap_slot(g, 2)) for g in halves]
-    near = [row_major(swap_slot(g, 1)) for g in halves]
-    result = place(slot, ((0, 0), (0, 1), (1, 0), (1, 1)), (*halves, *near), members)
+        gradient = (mine[:, :, low:high].astype(jnp.float32) + filtered).astype(jnp.bfloat16)
+        gradients.append(row_major(gradient.transpose(0, 2, 1, 3)))
+
+    lows = [low for low, _ in bounds]
+    far = [row_major(swap_slot(g, 2)) for g in gradients]
+    near = [row_major(swap_slot(g, 1)) for g in gradients]
+    result = place(
+        slot,
+        ((0, lows[0]), (0, lows[1]), (1, lows[0]), (1, lows[1])),
+        (*gradients, *near),
+        control.shape,
+    )
     far[1], result = lax.optimization_barrier((far[1], result))
     both = [row_major(swap_slot(g, 1)) for g in far]
-    result = place(slot, ((2, 0), (3, 0), (2, 1)), (far[0], both[0], far[1]), members, result)
-    return place(slot, ((3, 1),), (both[1],), members, result)
+    result = place(
+        slot,
+        ((2, lows[0]), (3, lows[0]), (2, lows[1])),
+        (far[0], both[0], far[1]),
+        control.shape,
+        result,
+    )
+    return place(slot, ((3, lows[1]),), (both[1],), control.shape, result)
 
 
 def solution(mesh):

time: 230 us -> 226 us (0.983)
  waiting for transfers between devices: 77.3 us -> 71.4 us
    all_to_all x3 -> x4, starting transfers between devices: 22.3 us -> 28.7 us  [swap_columns(): lax.all_to_all(flat, 'horiz', split_axis=0, concat_axis=0, tiled=True)]
    ppermute x13, starting transfers between devices: 32.5 us -> 27.7 us  [swap_slot(): return lax.ppermute(arr, 'slot', [(i, i ^ k) for i in range(4)])]
    slice x1 -> x13, local copies, waits for them, and re-layouts: 0.24 us -> 4.89 us  [the longest x4 4.3 us: per_device(): returned = swap_columns(back_across[:, :, :, low:high])]
    all_to_all x3 -> x4, waiting for transfers between devices: 22.3 us -> 18.4 us  [swap_columns(): lax.all_to_all(flat, 'horiz', split_axis=0, concat_axis=0, tiled=True)]
    transpose x1 -> x2, other arithmetic: 5.42 us -> 3.48 us  [per_device(): gradients.append(row_major(gradient.transpose(0, 2, 1, 3)))]
    unnamed x49 -> x45, local copies, waits for them, and re-layouts: 6.54 us -> 5.63 us
  transfers between devices with their start and end apart: 16 -> 17, of which waited for: 11 -> 12; matrix products, arithmetic and copies ran while one was open for 8% -> 12% of each run, Pallas kernels for 8% -> 8%
where the time goes in v5:
time: 226 us; the launch traced here: 222 us
  waiting for transfers between devices  71.4 us (32%)
  starting transfers between devices  56.4 us (25%)
  Pallas kernels  26.6 us (12%)
  local copies, waits for them, and re-layouts  26.1 us (12%)
  blocking collectives  23.4 us (10%)
  other arithmetic  8.93 us (4%)
  matrix products  8.09 us (4%)
    ppermute x13, waiting for transfers between devices, swap_slot(): return lax.ppermute(arr, 'slot', [(i, i ^ k) for i in range(4)])  53 us
    all_to_all x4, starting transfers between devices, swap_columns(): lax.all_to_all(flat, 'horiz', split_axis=0, concat_axis=0, tiled=True)  28.7 us
    ppermute x13, starting transfers between devices, swap_slot(): return lax.ppermute(arr, 'slot', [(i, i ^ k) for i in range(4)])  27.7 us
    all_to_all x1, blocking collectives, swap_columns(): lax.all_to_all(flat, 'horiz', split_axis=0, concat_axis=0, tiled=True)  23.4 us
    all_to_all x4, waiting for transfers between devices, swap_columns(): lax.all_to_all(flat, 'horiz', split_axis=0, concat_axis=0, tiled=True)  18.4 us
    pallas_call x1, Pallas kernels, obs_fields(): pl.pallas_call(obs_kernel, grid=(slots, count // OBS_BLOCK), in_specs=[pa...  14.7 us
    another operation x3, local copies, waits for them, and re-layouts, row_major(): return with_layout_constraint(arr, Layout(tuple(range(arr.ndim))))  6.84 us
    unnamed x45, local copies, waits for them, and re-layouts  5.63 us
  transfers between devices with their start and end apart: 17, of which 12 were waited for; matrix products, arithmetic and copies ran while one was open for 12% of the time, Pallas kernels for 8%

profile of v5, /device:TPU:37, one launch (start us, length us, event | category | flops | bytes accessed | tf_op | source)
XLA Modules:
  0.0 221.6 jit_solution(4388250650052786267)
XLA Ops:
  0.0 3.4 %shard_map.109 = (bf16[8,80,2,512]{3,2,1,0:T(2,128)(2,1)}, bf16[8,80,2,512]{3,2,1,0:T(2,128)(2,1)}, bf16[8,80,2,512]{3,2,1,0:T(2,128)(2,1)}) custom-call(s32[1]{0:T(128)} %bitcast.slot_ref, bf16[32,80,2,512]{3,2,1,0:T(2,128)(2,1)} %bitcast.108), custom_call_target="tpu_custom_call" | custom-call | bytes 7864320 | tf_op jit(solution)/shard_map/pallas_call | solution.py:200
  5.4 2.4 %constant_dynamic-slice_fusion.2 = bf16[8,80,2,512]{3,2,1,0:T(2,128)(2,1)S(1)} fusion(bf16[32,80,2,512]{3,2,1,0:T(2,128)(2,1)} %param.11, s32[]{:T(128)S(6)} %select_n.17), kind=kLoop, calls=%fused_computation.56 | loop fusion | bytes 2621444 | tf_op jit(solution)/shard_map/dynamic_slice | solution.py:298
  10.5 8.5 %all-to-all-start = ((bf16[32,2,80,128]{3,2,1,0:T(8,128)(2,1)}), bf16[32,2,80,128]{3,2,1,0:T(8,128)(2,1)}, u32[]{:S(2)}, u32[]{:S(2)}) async-start(bf16[32,2,80,128]{3,2,1,0:T(8,128)(2,1)} %bitcast.9), calls=%async_computation | async-start | bytes 2621440 | tf_op jit(solution)/shard_map/all_to_all | solution.py:253
  19.7 3.9 %collective-permute-start.3 = (bf16[8,80,2,512]{3,2,1,0:T(2,128)(2,1)}, bf16[8,80,2,512]{3,2,1,0:T(2,128)(2,1)}, u32[]{:S(2)}, u32[]{:S(2)}) collective-permute-start(bf16[8,80,2,512]{3,2,1,0:T(2,128)(2,1)} %get-tuple-element.33), channel_id=1, source_target_pairs={{0,96},{32,64},{64,32},{96,0},{1,97},{33,65},{65,33},{97,1},{2,98}... | collective-permute-start | bytes 3932168 | tf_op jit(solution)/shard_map/ppermute | solution.py:257
  26.8 8.8 %collective-permute-done = f32[3,1,8192]{2,1,0:T(1,128)S(1)} collective-permute-done((f32[3,1,8192]{2,1,0:T(1,128)S(1)}, f32[3,1,8192]{2,1,0:T(1,128)S(1)}, u32[]{:S(2)}, u32[]{:S(2)}) %collective-permute-start) | collective-permute-done | bytes 98336 | tf_op jit(solution)/shard_map/ppermute | solution.py:257
  35.7 2.8 %copy.69 = bf16[32,2,80,128]{3,1,0,2:T(2,128)(2,1)S(1)} copy(bf16[32,2,80,128]{3,2,1,0:T(8,128)(2,1)} %all-to-all-done) | data formatting | bytes 2621440 | tf_op jit(solution)/shard_map/all_to_all | solution.py:253
  41.4 8.0 %all-to-all-start.1 = ((bf16[32,2,80,128]{3,2,1,0:T(8,128)(2,1)}), bf16[32,2,80,128]{3,2,1,0:T(8,128)(2,1)}, u32[]{:S(2)}, u32[]{:S(2)}) async-start(bf16[32,2,80,128]{3,2,1,0:T(8,128)(2,1)} %bitcast.109), calls=%async_computation.1 | async-start | bytes 2621440 | tf_op jit(solution)/shard_map/all_to_all | solution.py:253
  49.4 14.7 %shard_map.110 = (f32[2,2,80,512]{3,2,1,0:T(8,128)S(1)}, f32[2,2,80,512]{3,2,1,0:T(8,128)S(1)}) custom-call(f32[2,3,1,8192]{3,2,1,0:T(1,128)S(1)} %pad_maximum_fusion.1.cell_ref.value_ref.weight_ref, f32[2,3,1,8192]{3,2,1,0:T(1,128)S(1)} %pad_maximum_fusion.1.cell_ref.value_ref.weight_ref, f32[2,3,1,8192]{3,2,1,0:T(1,128)S(1)} %pad_maximum_fusion.1.cell_ref.value_ref.weight_ref), custom_call_target="tpu_custom_call" | custom-call | flops 21474836480 | bytes 1310720 | tf_op jit(solution)/shard_map/pallas_call | solution.py:76
  67.8 23.9 %collective-permute-done.2 = bf16[8,80,2,512]{3,2,1,0:T(2,128)(2,1)} collective-permute-done((bf16[8,80,2,512]{3,2,1,0:T(2,128)(2,1)}, bf16[8,80,2,512]{3,2,1,0:T(2,128)(2,1)}, u32[]{:S(2)}, u32[]{:S(2)}) %collective-permute-start.2) | collective-permute-done | bytes 1310752 | tf_op jit(solution)/shard_map/ppermute | solution.py:257
  91.7 2.6 %copy.144 = bf16[8,80,2,512]{3,1,2,0:T(8,128)(2,1)} copy(bf16[8,80,2,512]{3,2,1,0:T(2,128)(2,1)} %collective-permute-done.2) | data formatting | bytes 2621440 | tf_op jit(solution)/shard_map/layout_constraint | solution.py:261
  94.4 2.6 %copy.145 = bf16[8,80,2,512]{3,1,2,0:T(8,128)(2,1)} copy(bf16[8,80,2,512]{3,2,1,0:T(2,128)(2,1)} %collective-permute-done.1) | data formatting | bytes 2621440 | tf_op jit(solution)/shard_map/layout_constraint | solution.py:261
  97.0 9.8 %all-to-all-done.1 = bf16[32,2,80,128]{3,2,1,0:T(8,128)(2,1)} async-done(((bf16[32,2,80,128]{3,2,1,0:T(8,128)(2,1)}), bf16[32,2,80,128]{3,2,1,0:T(8,128)(2,1)}, u32[]{:S(2)}, u32[]{:S(2)}) %all-to-all-start.1) | async-done | bytes 1310752 | tf_op jit(solution)/shard_map/all_to_all | solution.py:253
  109.4 2.6 %shard_map.111 = (f32[2,2,80,512]{3,2,1,0:T(8,128)S(1)}, bf16[2,2,80,512]{3,2,1,0:T(8,128)(2,1)S(1)}) custom-call(bf16[8,4,2,80,128]{4,3,2,1,0:T(8,128)(2,1)} %bitcast.16.spread_ref, bf16[8,2,80,512]{3,2,1,0:T(8,128)(2,1)S(1)} %bitcast.99, bf16[8,2,80,512]{3,2,1,0:T(8,128)(2,1)S(1)} %bitcast.105, bf16[8,2,80,512]{3,2,1,0:T(8,128)(2,1)S(1)} %bitcast.103, ...), custom_call_target="tpu_custom_call" | custom-call | flops 5242880 | bytes 6553600 | tf_op jit(solution)/shard_map/pallas_call | solution.py:113
  112.1 3.3 %collective-permute-start.4 = (bf16[2,2,80,512]{3,2,1,0:T(8,128)(2,1)S(1)}, bf16[2,2,80,512]{3,2,1,0:T(8,128)(2,1)S(1)}, u32[]{:S(2)}, u32[]{:S(2)}) collective-permute-start(bf16[2,2,80,512]{3,2,1,0:T(8,128)(2,1)S(1)} %get-tuple-element.35), channel_id=1, source_target_pairs={{0,32},{32,0},{64,96},{96,64},{1,33},{33,1},{65,97},{97,65},{2,34}... | collective-permute-start | bytes 983048 | tf_op jit(solution)/shard_map/ppermute | solution.py:257
  117.5 9.9 %collective-permute-done.5 = bf16[2,2,80,512]{3,2,1,0:T(8,128)(2,1)S(1)} collective-permute-done((bf16[2,2,80,512]{3,2,1,0:T(8,128)(2,1)S(1)}, bf16[2,2,80,512]{3,2,1,0:T(8,128)(2,1)S(1)}, u32[]{:S(2)}, u32[]{:S(2)}) %collective-permute-start.5) | collective-permute-done | bytes 327712 | tf_op jit(solution)/shard_map/ppermute | solution.py:257
  132.8 23.4 %all_to_all.25 = bf16[32,2,80,128]{3,2,1,0:T(8,128)(2,1)S(1)} all-to-all(bf16[32,2,80,128]{3,2,1,0:T(8,128)(2,1)S(1)} %bitcast.107), channel_id=1, replica_groups=mesh['slot'=4,'horiz'=32] {'horiz'}, dimensions={0} | all-to-all | bytes 2621440 | tf_op jit(solution)/shard_map/all_to_all | solution.py:253
  159.7 5.9 %all-to-all-start.4 = ((bf16[32,2,48,128]{3,2,1,0:T(8,128)(2,1)}), bf16[32,2,48,128]{3,2,1,0:T(8,128)(2,1)}, u32[]{:S(2)}, u32[]{:S(2)}) async-start(bf16[32,2,48,128]{3,2,1,0:T(8,128)(2,1)} %bitcast.116), calls=%async_computation.4 | async-start | bytes 1572864 | tf_op jit(solution)/shard_map/all_to_all | solution.py:253
  171.1 4.9 %all-to-all-done.4 = bf16[32,2,48,128]{3,2,1,0:T(8,128)(2,1)} async-done(((bf16[32,2,48,128]{3,2,1,0:T(8,128)(2,1)}), bf16[32,2,48,128]{3,2,1,0:T(8,128)(2,1)}, u32[]{:S(2)}, u32[]{:S(2)}) %all-to-all-start.4) | async-done | bytes 786464 | tf_op jit(solution)/shard_map/all_to_all | solution.py:253
  176.0 6.3 %all-to-all-start.3 = ((bf16[32,2,32,128]{3,2,1,0:T(8,128)(2,1)}), bf16[32,2,32,128]{3,2,1,0:T(8,128)(2,1)}, u32[]{:S(2)}, u32[]{:S(2)}) async-start(bf16[32,2,32,128]{3,2,1,0:T(8,128)(2,1)} %bitcast.34), calls=%async_computation.3 | async-start | bytes 1048576 | tf_op jit(solution)/shard_map/all_to_all | solution.py:253
  186.9 3.7 %all-to-all-done.3 = bf16[32,2,32,128]{3,2,1,0:T(8,128)(2,1)} async-done(((bf16[32,2,32,128]{3,2,1,0:T(8,128)(2,1)}), bf16[32,2,32,128]{3,2,1,0:T(8,128)(2,1)}, u32[]{:S(2)}, u32[]{:S(2)}) %all-to-all-start.3) | async-done | bytes 524320 | tf_op jit(solution)/shard_map/all_to_all | solution.py:253
  192.1 4.7 %collective-permute-start.8 = (bf16[8,48,2,512]{3,2,1,0:T(2,128)(2,1)S(1)}, bf16[8,48,2,512]{3,2,1,0:T(2,128)(2,1)S(1)}, u32[]{:S(2)}, u32[]{:S(2)}) collective-permute-start(bf16[8,48,2,512]{3,2,1,0:T(2,128)(2,1)S(1)} %fusion.9.refs_0_), channel_id=1, source_target_pairs={{0,32},{32,0},{64,96},{96,64},{1,33},{33,1},{65,97},{97,65},{2,34}... | collective-permute-start | bytes 2359304 | tf_op jit(solution)/shard_map/ppermute | solution.py:257
  198.6 5.3 %collective-permute-done.11.refs_0_ = bf16[8,48,2,512]{3,2,1,0:T(2,128)(2,1)S(1)} collective-permute-done((bf16[8,48,2,512]{3,2,1,0:T(2,128)(2,1)S(1)}, bf16[8,48,2,512]{3,2,1,0:T(2,128)(2,1)S(1)}, u32[]{:S(2)}, u32[]{:S(2)}) %collective-permute-start.11) | collective-permute-done | bytes 786464 | tf_op jit(solution)/shard_map/ppermute | solution.py:257
  203.9 7.7 %collective-permute-start.12 = (bf16[8,48,2,512]{3,2,1,0:T(2,128)(2,1)S(1)}, bf16[8,48,2,512]{3,2,1,0:T(2,128)(2,1)S(1)}, u32[]{:S(2)}, u32[]{:S(2)}) collective-permute-start(bf16[8,48,2,512]{3,2,1,0:T(2,128)(2,1)S(1)} %collective-permute-done.11.refs_0_), channel_id=1, source_target_pairs={{0,32},{32,0},{64,96},{96,64},{1,33},{33,1},{65,97},{97,65},{2,34}... | collective-permute-start | bytes 2359304 | tf_op jit(solution)/shard_map/ppermute | solution.py:257
  215.1 4.0 %collective-permute-start.10 = (bf16[8,32,2,512]{3,2,1,0:T(2,128)(2,1)S(1)}, bf16[8,32,2,512]{3,2,1,0:T(2,128)(2,1)S(1)}, u32[]{:S(2)}, u32[]{:S(2)}) collective-permute-start(bf16[8,32,2,512]{3,2,1,0:T(2,128)(2,1)S(1)} %collective-permute-done.7.refs_2_), channel_id=1, source_target_pairs={{0,32},{32,0},{64,96},{96,64},{1,33},{33,1},{65,97},{97,65},{2,34}... | collective-permute-start | bytes 1572872 | tf_op jit(solution)/shard_map/ppermute | solution.py:257
  (109 shorter events, 47.9 us)
Async XLA Ops:
  0.0 7.9 %copy-start = (bf16[512,512]{1,0:T(8,128)(2,1)S(1)}, bf16[512,512]{1,0:T(8,128)(2,1)}, u32[]{:S(2)}) copy-start(bf16[512,512]{1,0:T(8,128)(2,1)} %param.15) | copy-start | bytes 1572868
  10.5 8.5 %copy-start.20 = (s32[1,8192]{1,0:T(1,128)S(1)}, s32[1,8192]{1,0:T(1,128)}, u32[]{:S(2)}) copy-start(s32[1,8192]{1,0:T(1,128)} %param.19) | copy-start | bytes 98308
  10.5 8.5 %copy-start.16 = (f32[1,8192]{1,0:T(1,128)S(1)}, f32[1,8192]{1,0:T(1,128)}, u32[]{:S(2)}) copy-start(f32[1,8192]{1,0:T(1,128)} %param.21) | copy-start | bytes 98308
  10.5 8.5 %copy-start.17 = (f32[1,8192]{1,0:T(1,128)S(1)}, f32[1,8192]{1,0:T(1,128)}, u32[]{:S(2)}) copy-start(f32[1,8192]{1,0:T(1,128)} %param.20) | copy-start | bytes 98308
  10.5 25.3 %all-to-all-start = ((bf16[32,2,80,128]{3,2,1,0:T(8,128)(2,1)}), bf16[32,2,80,128]{3,2,1,0:T(8,128)(2,1)}, u32[]{:S(2)}, u32[]{:S(2)}) async-start(bf16[32,2,80,128]{3,2,1,0:T(8,128)(2,1)} %bitcast.9), calls=%async_computation | async-start | bytes 2621440 | tf_op jit(solution)/shard_map/all_to_all | solution.py:253
  19.1 16.4 %collective-permute-start = (f32[3,1,8192]{2,1,0:T(1,128)S(1)}, f32[3,1,8192]{2,1,0:T(1,128)S(1)}, u32[]{:S(2)}, u32[]{:S(2)}) collective-permute-start(f32[3,1,8192]{2,1,0:T(1,128)S(1)} %pad_maximum_fusion.2), channel_id=1, source_target_pairs={{0,64},{32,96},{64,0},{96,32},{1,65},{33,97},{65,1},{97,33},{2,66}... | collective-permute-start | bytes 294920 | tf_op jit(solution)/shard_map/ppermute | solution.py:257
  19.7 46.6 %collective-permute-start.3 = (bf16[8,80,2,512]{3,2,1,0:T(2,128)(2,1)}, bf16[8,80,2,512]{3,2,1,0:T(2,128)(2,1)}, u32[]{:S(2)}, u32[]{:S(2)}) collective-permute-start(bf16[8,80,2,512]{3,2,1,0:T(2,128)(2,1)} %get-tuple-element.33), channel_id=1, source_target_pairs={{0,96},{32,64},{64,32},{96,0},{1,97},{33,65},{65,33},{97,1},{2,98}... | collective-permute-start | bytes 3932168 | tf_op jit(solution)/shard_map/ppermute | solution.py:257
  23.6 68.2 %collective-permute-start.2 = (bf16[8,80,2,512]{3,2,1,0:T(2,128)(2,1)}, bf16[8,80,2,512]{3,2,1,0:T(2,128)(2,1)}, u32[]{:S(2)}, u32[]{:S(2)}) collective-permute-start(bf16[8,80,2,512]{3,2,1,0:T(2,128)(2,1)} %get-tuple-element.32), channel_id=1, source_target_pairs={{0,64},{32,96},{64,0},{96,32},{1,65},{33,97},{65,1},{97,33},{2,66}... | collective-permute-start | bytes 3932168 | tf_op jit(solution)/shard_map/ppermute | solution.py:257
  24.1 70.3 %collective-permute-start.1 = (bf16[8,80,2,512]{3,2,1,0:T(2,128)(2,1)}, bf16[8,80,2,512]{3,2,1,0:T(2,128)(2,1)}, u32[]{:S(2)}, u32[]{:S(2)}) collective-permute-start(bf16[8,80,2,512]{3,2,1,0:T(2,128)(2,1)} %get-tuple-element.31), channel_id=1, source_target_pairs={{0,32},{32,0},{64,96},{96,64},{1,33},{33,1},{65,97},{97,65},{2,34}... | collective-permute-start | bytes 3932168 | tf_op jit(solution)/shard_map/ppermute | solution.py:257
  41.4 65.4 %all-to-all-start.1 = ((bf16[32,2,80,128]{3,2,1,0:T(8,128)(2,1)}), bf16[32,2,80,128]{3,2,1,0:T(8,128)(2,1)}, u32[]{:S(2)}, u32[]{:S(2)}) async-start(bf16[32,2,80,128]{3,2,1,0:T(8,128)(2,1)} %bitcast.109), calls=%async_computation.1 | async-start | bytes 2621440 | tf_op jit(solution)/shard_map/all_to_all | solution.py:253
  112.0 15.5 %copy-start.6 = (f32[2,2,80,512]{3,2,1,0:T(8,128)S(1)}, f32[2,2,80,512]{3,2,1,0:T(8,128)}, u32[]{:S(2)}) copy-start(f32[2,2,80,512]{3,2,1,0:T(8,128)} %copy-done.5) | copy-start | bytes 1966084
  112.1 15.5 %copy-start.8 = (f32[2,2,80,512]{3,2,1,0:T(8,128)S(1)}, f32[2,2,80,512]{3,2,1,0:T(8,128)}, u32[]{:S(2)}) copy-start(f32[2,2,80,512]{3,2,1,0:T(8,128)} %copy-done.7) | copy-start | bytes 1966084
  112.1 4.6 %collective-permute-start.4 = (bf16[2,2,80,512]{3,2,1,0:T(8,128)(2,1)S(1)}, bf16[2,2,80,512]{3,2,1,0:T(8,128)(2,1)S(1)}, u32[]{:S(2)}, u32[]{:S(2)}) collective-permute-start(bf16[2,2,80,512]{3,2,1,0:T(8,128)(2,1)S(1)} %get-tuple-element.35), channel_id=1, source_target_pairs={{0,32},{32,0},{64,96},{96,64},{1,33},{33,1},{65,97},{97,65},{2,34}... | collective-permute-start | bytes 983048 | tf_op jit(solution)/shard_map/ppermute | solution.py:257
  116.8 10.7 %collective-permute-start.5 = (bf16[2,2,80,512]{3,2,1,0:T(8,128)(2,1)S(1)}, bf16[2,2,80,512]{3,2,1,0:T(8,128)(2,1)S(1)}, u32[]{:S(2)}, u32[]{:S(2)}) collective-permute-start(bf16[2,2,80,512]{3,2,1,0:T(8,128)(2,1)S(1)} %fusion.16), channel_id=1, source_target_pairs={{0,64},{32,96},{64,0},{96,32},{1,65},{33,97},{65,1},{97,33},{2,66}... | collective-permute-start | bytes 983048 | tf_op jit(solution)/shard_map/ppermute | solution.py:257
  127.9 2.5 %collective-permute-start.6 = (bf16[2,2,80,512]{3,2,1,0:T(8,128)(2,1)S(1)}, bf16[2,2,80,512]{3,2,1,0:T(8,128)(2,1)S(1)}, u32[]{:S(2)}, u32[]{:S(2)}) collective-permute-start(bf16[2,2,80,512]{3,2,1,0:T(8,128)(2,1)S(1)} %multiply_convert_fusion.3.own_ref), channel_id=1, source_target_pairs={{0,32},{32,0},{64,96},{96,64},{1,33},{33,1},{65,97},{97,65},{2,34}... | collective-permute-start | bytes 983048 | tf_op jit(solution)/shard_map/ppermute | solution.py:257
  159.7 16.3 %all-to-all-start.4 = ((bf16[32,2,48,128]{3,2,1,0:T(8,128)(2,1)}), bf16[32,2,48,128]{3,2,1,0:T(8,128)(2,1)}, u32[]{:S(2)}, u32[]{:S(2)}) async-start(bf16[32,2,48,128]{3,2,1,0:T(8,128)(2,1)} %bitcast.116), calls=%async_computation.4 | async-start | bytes 1572864 | tf_op jit(solution)/shard_map/all_to_all | solution.py:253
  176.0 14.6 %all-to-all-start.3 = ((bf16[32,2,32,128]{3,2,1,0:T(8,128)(2,1)}), bf16[32,2,32,128]{3,2,1,0:T(8,128)(2,1)}, u32[]{:S(2)}, u32[]{:S(2)}) async-start(bf16[32,2,32,128]{3,2,1,0:T(8,128)(2,1)} %bitcast.34), calls=%async_computation.3 | async-start | bytes 1048576 | tf_op jit(solution)/shard_map/all_to_all | solution.py:253
  186.3 10.5 %copy-start.12 = (f32[8,2,32,512]{3,2,1,0:T(8,128)S(1)}, f32[8,2,32,512]{3,2,1,0:T(8,128)}, u32[]{:S(2)}) copy-start(f32[8,2,32,512]{3,2,1,0:T(8,128)} %slice_convert_fusion.1) | copy-start | bytes 3145732
  186.3 17.6 %collective-permute-start.11 = (bf16[8,48,2,512]{3,2,1,0:T(2,128)(2,1)S(1)}, bf16[8,48,2,512]{3,2,1,0:T(2,128)(2,1)S(1)}, u32[]{:S(2)}, u32[]{:S(2)}) collective-permute-start(bf16[8,48,2,512]{3,2,1,0:T(2,128)(2,1)S(1)} %fusion.9.refs_0_), channel_id=1, source_target_pairs={{0,64},{32,96},{64,0},{96,32},{1,65},{33,97},{65,1},{97,33},{2,66}... | collective-permute-start | bytes 2359304 | tf_op jit(solution)/shard_map/ppermute | solution.py:257
  192.1 19.5 %collective-permute-start.8 = (bf16[8,48,2,512]{3,2,1,0:T(2,128)(2,1)S(1)}, bf16[8,48,2,512]{3,2,1,0:T(2,128)(2,1)S(1)}, u32[]{:S(2)}, u32[]{:S(2)}) collective-permute-start(bf16[8,48,2,512]{3,2,1,0:T(2,128)(2,1)S(1)} %fusion.9.refs_0_), channel_id=1, source_target_pairs={{0,32},{32,0},{64,96},{96,64},{1,33},{33,1},{65,97},{97,65},{2,34}... | collective-permute-start | bytes 2359304 | tf_op jit(solution)/shard_map/ppermute | solution.py:257
  198.2 13.4 %collective-permute-start.9 = (bf16[8,32,2,512]{3,2,1,0:T(2,128)(2,1)S(1)}, bf16[8,32,2,512]{3,2,1,0:T(2,128)(2,1)S(1)}, u32[]{:S(2)}, u32[]{:S(2)}) collective-permute-start(bf16[8,32,2,512]{3,2,1,0:T(2,128)(2,1)S(1)} %fusion.15.refs_1_), channel_id=1, source_target_pairs={{0,32},{32,0},{64,96},{96,64},{1,33},{33,1},{65,97},{97,65},{2,34}... | collective-permute-start | bytes 1572872 | tf_op jit(solution)/shard_map/ppermute | solution.py:257
  198.3 16.8 %collective-permute-start.7 = (bf16[8,32,2,512]{3,2,1,0:T(2,128)(2,1)S(1)}, bf16[8,32,2,512]{3,2,1,0:T(2,128)(2,1)S(1)}, u32[]{:S(2)}, u32[]{:S(2)}) collective-permute-start(bf16[8,32,2,512]{3,2,1,0:T(2,128)(2,1)S(1)} %fusion.15.refs_1_), channel_id=1, source_target_pairs={{0,64},{32,96},{64,0},{96,32},{1,65},{33,97},{65,1},{97,33},{2,66}... | collective-permute-start | bytes 1572872 | tf_op jit(solution)/shard_map/ppermute | solution.py:257
  203.9 15.2 %collective-permute-start.12 = (bf16[8,48,2,512]{3,2,1,0:T(2,128)(2,1)S(1)}, bf16[8,48,2,512]{3,2,1,0:T(2,128)(2,1)S(1)}, u32[]{:S(2)}, u32[]{:S(2)}) collective-permute-start(bf16[8,48,2,512]{3,2,1,0:T(2,128)(2,1)S(1)} %collective-permute-done.11.refs_0_), channel_id=1, source_target_pairs={{0,32},{32,0},{64,96},{96,64},{1,33},{33,1},{65,97},{97,65},{2,34}... | collective-permute-start | bytes 2359304 | tf_op jit(solution)/shard_map/ppermute | solution.py:257
  215.1 5.5 %collective-permute-start.10 = (bf16[8,32,2,512]{3,2,1,0:T(2,128)(2,1)S(1)}, bf16[8,32,2,512]{3,2,1,0:T(2,128)(2,1)S(1)}, u32[]{:S(2)}, u32[]{:S(2)}) collective-permute-start(bf16[8,32,2,512]{3,2,1,0:T(2,128)(2,1)S(1)} %collective-permute-done.7.refs_2_), channel_id=1, source_target_pairs={{0,32},{32,0},{64,96},{96,64},{1,33},{33,1},{65,97},{97,65},{2,34}... | collective-permute-start | bytes 1572872 | tf_op jit(solution)/shard_map/ppermute | solution.py:257
  (17 other events, 36.8 us)

commit v6 on v5

--- a/solution.py
+++ b/solution.py
@@ -253,6 +253,24 @@
     return lax.all_to_all(flat, "horiz", split_axis=0, concat_axis=0, tiled=True).reshape(shape)
 
 
+def swap_across(tiles):
+    shape = tiles.shape
+    flat = tiles.reshape(shape[0] * shape[1], *shape[2:])
+    groups = [
+        [((half ^ (h // 16)) * 2 + core) * 32 + h for h in range(32)]
+        for half in range(2)
+        for core in range(2)
+    ]
+    return lax.all_to_all(
+        flat,
+        ("slot", "horiz"),
+        split_axis=0,
+        concat_axis=0,
+        axis_index_groups=groups,
+        tiled=True,
+    ).reshape(shape)
+
+
 def swap_slot(arr, k):
     return lax.ppermute(arr, "slot", [(i, i ^ k) for i in range(4)])
 
@@ -289,19 +307,25 @@
     pert = [lax.dynamic_slice_in_dim(perturbed, slot * own, own, 0), got[1], got[2], got[3]]
 
     obs = jnp.stack([obs_cell.astype(jnp.float32), obs_value, obs_weight])
-    obs = jnp.stack([obs, swap_slot(obs, 2)])
-    weight_sum, value_sum = obs_fields(obs, levels)
+    far_obs = swap_slot(obs, 2)
 
     sea = land_mask.astype(jnp.float32).transpose(1, 0, 2)
     weight_mask = sea * local_sigma(tile_id, tile_scale, dev_index, row_count).transpose(1, 0, 2)
 
-    mine = lax.dynamic_slice_in_dim(control, slot * own, own, 0).transpose(0, 2, 1, 3)
-    masked = (weight_mask * mine.astype(jnp.float32)).astype(jnp.bfloat16)
+    half_x, core, side = slot >> 1, slot & 1, dev_index // 16
+    part = own // 2
+    starts = [(((half_x ^ side ^ d) * 2 + core) * 2 + d) * part for d in range(2)]
+    asked = jnp.concatenate(
+        [lax.dynamic_slice_in_dim(control, start, part, 0) for start in starts]
+    ).transpose(0, 2, 1, 3)
+    masked = (weight_mask * asked.astype(jnp.float32)).astype(jnp.bfloat16)
     along_x = (sea * jnp.dot(masked, inverse_x, preferred_element_type=jnp.float32)).astype(
         jnp.bfloat16
     )
     along_x = along_x.reshape(own, row_count, levels, tiles, 128).transpose(0, 3, 1, 2, 4)
-    received = swap_columns(along_x)
+    along_x, far_obs = lax.optimization_barrier((along_x, far_obs))
+    weight_sum, value_sum = obs_fields(jnp.stack([obs, far_obs]), levels)
+    received = swap_across(along_x)
     received = received.reshape(-1, levels, 128)
     across = jnp.einsum(
         "yzx,yk->kzx", received, inverse_y, preferred_element_type=jnp.float32
@@ -311,6 +335,7 @@
     ).astype(jnp.bfloat16)
     tile_shape = (own, tiles, row_count, levels, 128)
     spread = swap_columns(deeper.reshape(tile_shape))
+    mine = lax.dynamic_slice_in_dim(control, slot * own, own, 0).transpose(0, 2, 1, 3)
 
     pert = [p.transpose(0, 2, 1, 3) for p in pert]
     spread, weight_sum, value_sum = lax.optimization_barrier((spread, weight_sum, value_sum))

time: 226 us -> 238 us (1.053)
  waiting for transfers between devices: 71.4 us -> 80.2 us
  local copies, waits for them, and re-layouts: 26.1 us -> 29.9 us
  blocking collectives: 23.4 us -> 25.8 us
    all_to_all x0 -> x1, waiting for transfers between devices: none -> 54.7 us  [swap_across(): lax.all_to_all(flat, ('slot', 'horiz'), split_axis=0, concat_axis=0, axis...]
    ppermute x13, waiting for transfers between devices: 53 us -> 19.7 us  [swap_slot(): return lax.ppermute(arr, 'slot', [(i, i ^ k) for i in range(4)])]
    all_to_all x4 -> x3, waiting for transfers between devices: 18.4 us -> 5.78 us  [swap_columns(): lax.all_to_all(flat, 'horiz', split_axis=0, concat_axis=0, tiled=True)]
    all_to_all x4 -> x3, starting transfers between devices: 28.7 us -> 19.1 us  [swap_columns(): lax.all_to_all(flat, 'horiz', split_axis=0, concat_axis=0, tiled=True)]
    all_to_all x0 -> x1, starting transfers between devices: none -> 9.16 us  [swap_across(): lax.all_to_all(flat, ('slot', 'horiz'), split_axis=0, concat_axis=0, axis...]
    unnamed x45 -> x41, local copies, waits for them, and re-layouts: 5.63 us -> 4.93 us
  transfers between devices with their start and end apart: 17 -> 17, of which waited for: 12 -> 9; matrix products, arithmetic and copies ran while one was open for 12% -> 15% of each run, Pallas kernels for 8% -> 9%
where the time goes in v6:
time: 238 us; the launch traced here: 234 us
  waiting for transfers between devices  80.2 us (34%)
  starting transfers between devices  54.8 us (23%)
  local copies, waits for them, and re-layouts  29.9 us (13%)
  Pallas kernels  26.5 us (11%)
  blocking collectives  25.8 us (11%)
  other arithmetic  8.31 us (3%)
  matrix products  8.12 us (3%)
    all_to_all x1, waiting for transfers between devices, swap_across(): lax.all_to_all(flat, ('slot', 'horiz'), split_axis=0, concat_axis=0, axis...  54.7 us
    ppermute x13, starting transfers between devices, swap_slot(): return lax.ppermute(arr, 'slot', [(i, i ^ k) for i in range(4)])  26.5 us
    all_to_all x1, blocking collectives, swap_columns(): lax.all_to_all(flat, 'horiz', split_axis=0, concat_axis=0, tiled=True)  25.8 us
    ppermute x13, waiting for transfers between devices, swap_slot(): return lax.ppermute(arr, 'slot', [(i, i ^ k) for i in range(4)])  19.7 us
    all_to_all x3, starting transfers between devices, swap_columns(): lax.all_to_all(flat, 'horiz', split_axis=0, concat_axis=0, tiled=True)  19.1 us
    pallas_call x1, Pallas kernels, obs_fields(): pl.pallas_call(obs_kernel, grid=(slots, count // OBS_BLOCK), in_specs=[pa...  14.7 us
    all_to_all x1, starting transfers between devices, swap_across(): lax.all_to_all(flat, ('slot', 'horiz'), split_axis=0, concat_axis=0, axis...  9.16 us
    another operation x3, local copies, waits for them, and re-layouts, row_major(): return with_layout_constraint(arr, Layout(tuple(range(arr.ndim))))  6.9 us
  transfers between devices with their start and end apart: 17, of which 9 were waited for; matrix products, arithmetic and copies ran while one was open for 15% of the time, Pallas kernels for 9%

profile of v6, /device:TPU:37, one launch (start us, length us, event | category | flops | bytes accessed | tf_op | source)
XLA Modules:
  0.0 234.4 jit_solution(2386737652581575603)
XLA Ops:
  2.0 3.3 %shard_map.109 = (bf16[8,80,2,512]{3,2,1,0:T(2,128)(2,1)}, bf16[8,80,2,512]{3,2,1,0:T(2,128)(2,1)}, bf16[8,80,2,512]{3,2,1,0:T(2,128)(2,1)}) custom-call(s32[1]{0:T(128)} %bitcast.slot_ref, bf16[32,80,2,512]{3,2,1,0:T(2,128)(2,1)} %bitcast.118), custom_call_target="tpu_custom_call" | custom-call | bytes 7864320 | tf_op jit(solution)/shard_map/pallas_call | solution.py:200
  5.3 3.7 %collective-permute-start.3 = (bf16[8,80,2,512]{3,2,1,0:T(2,128)(2,1)}, bf16[8,80,2,512]{3,2,1,0:T(2,128)(2,1)}, u32[]{:S(2)}, u32[]{:S(2)}) collective-permute-start(bf16[8,80,2,512]{3,2,1,0:T(2,128)(2,1)} %get-tuple-element.37), channel_id=1, source_target_pairs={{0,96},{32,64},{64,32},{96,0},{1,97},{33,65},{65,33},{97,1},{2,98}... | collective-permute-start | bytes 3932168 | tf_op jit(solution)/shard_map/ppermute | solution.py:275
  16.2 9.2 %all-to-all-start = ((bf16[32,2,80,128]{3,2,1,0:T(8,128)(2,1)}), bf16[32,2,80,128]{3,2,1,0:T(8,128)(2,1)}, u32[]{:S(2)}, u32[]{:S(2)}) async-start(bf16[32,2,80,128]{3,2,1,0:T(8,128)(2,1)} %bitcast.14), calls=%async_computation | async-start | bytes 2621440 | tf_op jit(solution)/shard_map/all_to_all | solution.py:264
  25.5 2.3 constant_dynamic-slice_fusion
  28.3 54.7 %all-to-all-done = bf16[32,2,80,128]{3,2,1,0:T(8,128)(2,1)} async-done(((bf16[32,2,80,128]{3,2,1,0:T(8,128)(2,1)}), bf16[32,2,80,128]{3,2,1,0:T(8,128)(2,1)}, u32[]{:S(2)}, u32[]{:S(2)}) %all-to-all-start) | async-done | bytes 1310752 | tf_op jit(solution)/shard_map/all_to_all | solution.py:264
  83.0 2.8 %copy.74 = bf16[32,2,80,128]{3,1,0,2:T(2,128)(2,1)S(1)} copy(bf16[32,2,80,128]{3,2,1,0:T(8,128)(2,1)} %all-to-all-done) | data formatting | bytes 2621440 | tf_op jit(solution)/shard_map/all_to_all | solution.py:264
  88.6 6.9 %all-to-all-start.1 = ((bf16[32,2,80,128]{3,2,1,0:T(8,128)(2,1)}), bf16[32,2,80,128]{3,2,1,0:T(8,128)(2,1)}, u32[]{:S(2)}, u32[]{:S(2)}) async-start(bf16[32,2,80,128]{3,2,1,0:T(8,128)(2,1)} %bitcast.119), calls=%async_computation.1 | async-start | bytes 2621440 | tf_op jit(solution)/shard_map/all_to_all | solution.py:253
  95.6 14.7 %shard_map.110 = (f32[2,2,80,512]{3,2,1,0:T(8,128)S(1)}, f32[2,2,80,512]{3,2,1,0:T(8,128)S(1)}) custom-call(f32[2,3,1,8192]{3,2,1,0:T(1,128)S(1)} %pad_maximum_fusion.cell_ref.value_ref.weight_ref, f32[2,3,1,8192]{3,2,1,0:T(1,128)S(1)} %pad_maximum_fusion.cell_ref.value_ref.weight_ref, f32[2,3,1,8192]{3,2,1,0:T(1,128)S(1)} %pad_maximum_fusion.cell_ref.value_ref.weight_ref), custom_call_target="tpu_custom_call" | custom-call | flops 21474836480 | bytes 1310720 | tf_op jit(solution)/shard_map/pallas_call | solution.py:76
  113.5 2.6 %copy.151 = bf16[8,80,2,512]{3,1,2,0:T(8,128)(2,1)} copy(bf16[8,80,2,512]{3,2,1,0:T(2,128)(2,1)} %collective-permute-done.2) | data formatting | bytes 2621440 | tf_op jit(solution)/shard_map/layout_constraint | solution.py:279
  116.1 2.7 %copy.152 = bf16[8,80,2,512]{3,1,2,0:T(8,128)(2,1)} copy(bf16[8,80,2,512]{3,2,1,0:T(2,128)(2,1)} %collective-permute-done.1) | data formatting | bytes 2621440 | tf_op jit(solution)/shard_map/layout_constraint | solution.py:279
  121.5 2.6 %shard_map.111 = (f32[2,2,80,512]{3,2,1,0:T(8,128)S(1)}, bf16[2,2,80,512]{3,2,1,0:T(8,128)(2,1)S(1)}) custom-call(bf16[8,4,2,80,128]{4,3,2,1,0:T(8,128)(2,1)} %bitcast.21.spread_ref, bf16[8,2,80,512]{3,2,1,0:T(8,128)(2,1)S(1)} %bitcast.109, bf16[8,2,80,512]{3,2,1,0:T(8,128)(2,1)S(1)} %bitcast.115, bf16[8,2,80,512]{3,2,1,0:T(8,128)(2,1)S(1)} %bitcast.113, ...), custom_call_target="tpu_custom_call" | custom-call | flops 5242880 | bytes 6553600 | tf_op jit(solution)/shard_map/pallas_call | solution.py:113
  128.1 9.1 %collective-permute-done.5 = bf16[2,2,80,512]{3,2,1,0:T(8,128)(2,1)S(1)} collective-permute-done((bf16[2,2,80,512]{3,2,1,0:T(8,128)(2,1)S(1)}, bf16[2,2,80,512]{3,2,1,0:T(8,128)(2,1)S(1)}, u32[]{:S(2)}, u32[]{:S(2)}) %collective-permute-start.5) | collective-permute-done | bytes 327712 | tf_op jit(solution)/shard_map/ppermute | solution.py:275
  140.3 2.3 shard_map.112
  142.7 25.8 %all_to_all.25 = bf16[32,2,80,128]{3,2,1,0:T(8,128)(2,1)S(1)} all-to-all(bf16[32,2,80,128]{3,2,1,0:T(8,128)(2,1)S(1)} %bitcast.117), channel_id=1, replica_groups=mesh['slot'=4,'horiz'=32] {'horiz'}, dimensions={0} | all-to-all | bytes 2621440 | tf_op jit(solution)/shard_map/all_to_all | solution.py:253
  171.9 5.9 %all-to-all-start.4 = ((bf16[32,2,48,128]{3,2,1,0:T(8,128)(2,1)}), bf16[32,2,48,128]{3,2,1,0:T(8,128)(2,1)}, u32[]{:S(2)}, u32[]{:S(2)}) async-start(bf16[32,2,48,128]{3,2,1,0:T(8,128)(2,1)} %bitcast.41), calls=%async_computation.4 | async-start | bytes 1572864 | tf_op jit(solution)/shard_map/all_to_all | solution.py:253
  178.6 2.3 constant_dynamic-slice_fusion.4
  185.3 2.9 %all-to-all-done.4 = bf16[32,2,48,128]{3,2,1,0:T(8,128)(2,1)} async-done(((bf16[32,2,48,128]{3,2,1,0:T(8,128)(2,1)}), bf16[32,2,48,128]{3,2,1,0:T(8,128)(2,1)}, u32[]{:S(2)}, u32[]{:S(2)}) %all-to-all-start.4) | async-done | bytes 786464 | tf_op jit(solution)/shard_map/all_to_all | solution.py:253
  188.2 6.3 %all-to-all-start.3 = ((bf16[32,2,32,128]{3,2,1,0:T(8,128)(2,1)}), bf16[32,2,32,128]{3,2,1,0:T(8,128)(2,1)}, u32[]{:S(2)}, u32[]{:S(2)}) async-start(bf16[32,2,32,128]{3,2,1,0:T(8,128)(2,1)} %bitcast.36), calls=%async_computation.3 | async-start | bytes 1048576 | tf_op jit(solution)/shard_map/all_to_all | solution.py:253
  199.9 2.9 %all-to-all-done.3 = bf16[32,2,32,128]{3,2,1,0:T(8,128)(2,1)} async-done(((bf16[32,2,32,128]{3,2,1,0:T(8,128)(2,1)}), bf16[32,2,32,128]{3,2,1,0:T(8,128)(2,1)}, u32[]{:S(2)}, u32[]{:S(2)}) %all-to-all-start.3) | async-done | bytes 524320 | tf_op jit(solution)/shard_map/all_to_all | solution.py:253
  204.3 4.4 %collective-permute-start.8 = (bf16[8,48,2,512]{3,2,1,0:T(2,128)(2,1)S(1)}, bf16[8,48,2,512]{3,2,1,0:T(2,128)(2,1)S(1)}, u32[]{:S(2)}, u32[]{:S(2)}) collective-permute-start(bf16[8,48,2,512]{3,2,1,0:T(2,128)(2,1)S(1)} %fusion.15.refs_0_), channel_id=1, source_target_pairs={{0,32},{32,0},{64,96},{96,64},{1,33},{33,1},{65,97},{97,65},{2,34}... | collective-permute-start | bytes 2359304 | tf_op jit(solution)/shard_map/ppermute | solution.py:275
  212.0 5.0 %collective-permute-done.11.refs_0_ = bf16[8,48,2,512]{3,2,1,0:T(2,128)(2,1)S(1)} collective-permute-done((bf16[8,48,2,512]{3,2,1,0:T(2,128)(2,1)S(1)}, bf16[8,48,2,512]{3,2,1,0:T(2,128)(2,1)S(1)}, u32[]{:S(2)}, u32[]{:S(2)}) %collective-permute-start.11) | collective-permute-done | bytes 786464 | tf_op jit(solution)/shard_map/ppermute | solution.py:275
  217.0 6.8 %collective-permute-start.12 = (bf16[8,48,2,512]{3,2,1,0:T(2,128)(2,1)S(1)}, bf16[8,48,2,512]{3,2,1,0:T(2,128)(2,1)S(1)}, u32[]{:S(2)}, u32[]{:S(2)}) collective-permute-start(bf16[8,48,2,512]{3,2,1,0:T(2,128)(2,1)S(1)} %collective-permute-done.11.refs_0_), channel_id=1, source_target_pairs={{0,32},{32,0},{64,96},{96,64},{1,33},{33,1},{65,97},{97,65},{2,34}... | collective-permute-start | bytes 2359304 | tf_op jit(solution)/shard_map/ppermute | solution.py:275
  225.4 2.9 %collective-permute-done.7.refs_2_ = bf16[8,32,2,512]{3,2,1,0:T(2,128)(2,1)S(1)} collective-permute-done((bf16[8,32,2,512]{3,2,1,0:T(2,128)(2,1)S(1)}, bf16[8,32,2,512]{3,2,1,0:T(2,128)(2,1)S(1)}, u32[]{:S(2)}, u32[]{:S(2)}) %collective-permute-start.7) | collective-permute-done | bytes 524320 | tf_op jit(solution)/shard_map/ppermute | solution.py:275
  228.2 3.6 %collective-permute-start.10 = (bf16[8,32,2,512]{3,2,1,0:T(2,128)(2,1)S(1)}, bf16[8,32,2,512]{3,2,1,0:T(2,128)(2,1)S(1)}, u32[]{:S(2)}, u32[]{:S(2)}) collective-permute-start(bf16[8,32,2,512]{3,2,1,0:T(2,128)(2,1)S(1)} %collective-permute-done.7.refs_2_), channel_id=1, source_target_pairs={{0,32},{32,0},{64,96},{96,64},{1,33},{33,1},{65,97},{97,65},{2,34}... | collective-permute-start | bytes 1572872 | tf_op jit(solution)/shard_map/ppermute | solution.py:275
  (105 shorter events, 48.0 us)
Async XLA Ops:
  0.0 14.0 %copy-start = (bf16[512,512]{1,0:T(8,128)(2,1)S(1)}, bf16[512,512]{1,0:T(8,128)(2,1)}, u32[]{:S(2)}) copy-start(bf16[512,512]{1,0:T(8,128)(2,1)} %param.15) | copy-start | bytes 1572868
  1.7 14.5 %collective-permute-start = (f32[3,1,8192]{2,1,0:T(1,128)S(1)}, f32[3,1,8192]{2,1,0:T(1,128)S(1)}, u32[]{:S(2)}, u32[]{:S(2)}) collective-permute-start(f32[3,1,8192]{2,1,0:T(1,128)S(1)} %pad_maximum_fusion.1), channel_id=1, source_target_pairs={{0,64},{32,96},{64,0},{96,32},{1,65},{33,97},{65,1},{97,33},{2,66}... | collective-permute-start | bytes 294920 | tf_op jit(solution)/shard_map/ppermute | solution.py:275
  5.3 106.6 %collective-permute-start.3 = (bf16[8,80,2,512]{3,2,1,0:T(2,128)(2,1)}, bf16[8,80,2,512]{3,2,1,0:T(2,128)(2,1)}, u32[]{:S(2)}, u32[]{:S(2)}) collective-permute-start(bf16[8,80,2,512]{3,2,1,0:T(2,128)(2,1)} %get-tuple-element.37), channel_id=1, source_target_pairs={{0,96},{32,64},{64,32},{96,0},{1,97},{33,65},{65,33},{97,1},{2,98}... | collective-permute-start | bytes 3932168 | tf_op jit(solution)/shard_map/ppermute | solution.py:275
  9.0 104.5 %collective-permute-start.2 = (bf16[8,80,2,512]{3,2,1,0:T(2,128)(2,1)}, bf16[8,80,2,512]{3,2,1,0:T(2,128)(2,1)}, u32[]{:S(2)}, u32[]{:S(2)}) collective-permute-start(bf16[8,80,2,512]{3,2,1,0:T(2,128)(2,1)} %get-tuple-element.36), channel_id=1, source_target_pairs={{0,64},{32,96},{64,0},{96,32},{1,65},{33,97},{65,1},{97,33},{2,66}... | collective-permute-start | bytes 3932168 | tf_op jit(solution)/shard_map/ppermute | solution.py:275
  9.2 106.9 %collective-permute-start.1 = (bf16[8,80,2,512]{3,2,1,0:T(2,128)(2,1)}, bf16[8,80,2,512]{3,2,1,0:T(2,128)(2,1)}, u32[]{:S(2)}, u32[]{:S(2)}) collective-permute-start(bf16[8,80,2,512]{3,2,1,0:T(2,128)(2,1)} %get-tuple-element.35), channel_id=1, source_target_pairs={{0,32},{32,0},{64,96},{96,64},{1,33},{33,1},{65,97},{97,65},{2,34}... | collective-permute-start | bytes 3932168 | tf_op jit(solution)/shard_map/ppermute | solution.py:275
  16.2 9.2 %copy-start.14 = (f32[1,8192]{1,0:T(1,128)S(1)}, f32[1,8192]{1,0:T(1,128)}, u32[]{:S(2)}) copy-start(f32[1,8192]{1,0:T(1,128)} %param.21) | copy-start | bytes 98308
  16.2 9.2 %copy-start.15 = (f32[1,8192]{1,0:T(1,128)S(1)}, f32[1,8192]{1,0:T(1,128)}, u32[]{:S(2)}) copy-start(f32[1,8192]{1,0:T(1,128)} %param.20) | copy-start | bytes 98308
  16.2 66.8 %all-to-all-start = ((bf16[32,2,80,128]{3,2,1,0:T(8,128)(2,1)}), bf16[32,2,80,128]{3,2,1,0:T(8,128)(2,1)}, u32[]{:S(2)}, u32[]{:S(2)}) async-start(bf16[32,2,80,128]{3,2,1,0:T(8,128)(2,1)} %bitcast.14), calls=%async_computation | async-start | bytes 2621440 | tf_op jit(solution)/shard_map/all_to_all | solution.py:264
  28.3 57.5 %copy-start.17 = (bf16[64,64]{1,0:T(8,128)(2,1)S(1)}, bf16[64,64]{1,0:T(8,128)(2,1)}, u32[]{:S(2)}) copy-start(bf16[64,64]{1,0:T(8,128)(2,1)} %param.16) | copy-start | bytes 24580
  88.6 30.2 %all-to-all-start.1 = ((bf16[32,2,80,128]{3,2,1,0:T(8,128)(2,1)}), bf16[32,2,80,128]{3,2,1,0:T(8,128)(2,1)}, u32[]{:S(2)}, u32[]{:S(2)}) async-start(bf16[32,2,80,128]{3,2,1,0:T(8,128)(2,1)} %bitcast.119), calls=%async_computation.1 | async-start | bytes 2621440 | tf_op jit(solution)/shard_map/all_to_all | solution.py:253
  124.1 13.3 %copy-start.6 = (f32[2,2,80,512]{3,2,1,0:T(8,128)S(1)}, f32[2,2,80,512]{3,2,1,0:T(8,128)}, u32[]{:S(2)}) copy-start(f32[2,2,80,512]{3,2,1,0:T(8,128)} %copy-done.5) | copy-start | bytes 1966084
  124.1 13.3 %copy-start.8 = (f32[2,2,80,512]{3,2,1,0:T(8,128)S(1)}, f32[2,2,80,512]{3,2,1,0:T(8,128)}, u32[]{:S(2)}) copy-start(f32[2,2,80,512]{3,2,1,0:T(8,128)} %copy-done.7) | copy-start | bytes 1966084
  124.1 2.4 %collective-permute-start.4 = (bf16[2,2,80,512]{3,2,1,0:T(8,128)(2,1)S(1)}, bf16[2,2,80,512]{3,2,1,0:T(8,128)(2,1)S(1)}, u32[]{:S(2)}, u32[]{:S(2)}) collective-permute-start(bf16[2,2,80,512]{3,2,1,0:T(8,128)(2,1)S(1)} %get-tuple-element.39), channel_id=1, source_target_pairs={{0,32},{32,0},{64,96},{96,64},{1,33},{33,1},{65,97},{97,65},{2,34}... | collective-permute-start | bytes 983048 | tf_op jit(solution)/shard_map/ppermute | solution.py:275
  126.6 10.7 %collective-permute-start.5 = (bf16[2,2,80,512]{3,2,1,0:T(8,128)(2,1)S(1)}, bf16[2,2,80,512]{3,2,1,0:T(8,128)(2,1)S(1)}, u32[]{:S(2)}, u32[]{:S(2)}) collective-permute-start(bf16[2,2,80,512]{3,2,1,0:T(8,128)(2,1)S(1)} %fusion.22), channel_id=1, source_target_pairs={{0,64},{32,96},{64,0},{96,32},{1,65},{33,97},{65,1},{97,33},{2,66}... | collective-permute-start | bytes 983048 | tf_op jit(solution)/shard_map/ppermute | solution.py:275
  137.8 2.5 %collective-permute-start.6 = (bf16[2,2,80,512]{3,2,1,0:T(8,128)(2,1)S(1)}, bf16[2,2,80,512]{3,2,1,0:T(8,128)(2,1)S(1)}, u32[]{:S(2)}, u32[]{:S(2)}) collective-permute-start(bf16[2,2,80,512]{3,2,1,0:T(8,128)(2,1)S(1)} %multiply_convert_fusion.1.own_ref), channel_id=1, source_target_pairs={{0,32},{32,0},{64,96},{96,64},{1,33},{33,1},{65,97},{97,65},{2,34}... | collective-permute-start | bytes 983048 | tf_op jit(solution)/shard_map/ppermute | solution.py:275
  171.9 16.3 %all-to-all-start.4 = ((bf16[32,2,48,128]{3,2,1,0:T(8,128)(2,1)}), bf16[32,2,48,128]{3,2,1,0:T(8,128)(2,1)}, u32[]{:S(2)}, u32[]{:S(2)}) async-start(bf16[32,2,48,128]{3,2,1,0:T(8,128)(2,1)} %bitcast.41), calls=%async_computation.4 | async-start | bytes 1572864 | tf_op jit(solution)/shard_map/all_to_all | solution.py:253
  183.9 10.7 %copy-start.13 = (bf16[2,48,512]{2,1,0:T(8,128)(2,1)S(1)}, bf16[2,48,512]{2,1,0:T(8,128)(2,1)}, u32[]{:S(2)}) copy-start(bf16[2,48,512]{2,1,0:T(8,128)(2,1)} %slice.39) | copy-start | bytes 294916
  188.2 14.6 %all-to-all-start.3 = ((bf16[32,2,32,128]{3,2,1,0:T(8,128)(2,1)}), bf16[32,2,32,128]{3,2,1,0:T(8,128)(2,1)}, u32[]{:S(2)}, u32[]{:S(2)}) async-start(bf16[32,2,32,128]{3,2,1,0:T(8,128)(2,1)} %bitcast.36), calls=%async_computation.3 | async-start | bytes 1048576 | tf_op jit(solution)/shard_map/all_to_all | solution.py:253
  198.5 18.5 %collective-permute-start.11 = (bf16[8,48,2,512]{3,2,1,0:T(2,128)(2,1)S(1)}, bf16[8,48,2,512]{3,2,1,0:T(2,128)(2,1)S(1)}, u32[]{:S(2)}, u32[]{:S(2)}) collective-permute-start(bf16[8,48,2,512]{3,2,1,0:T(2,128)(2,1)S(1)} %fusion.15.refs_0_), channel_id=1, source_target_pairs={{0,64},{32,96},{64,0},{96,32},{1,65},{33,97},{65,1},{97,33},{2,66}... | collective-permute-start | bytes 2359304 | tf_op jit(solution)/shard_map/ppermute | solution.py:275
  204.3 19.5 %collective-permute-start.8 = (bf16[8,48,2,512]{3,2,1,0:T(2,128)(2,1)S(1)}, bf16[8,48,2,512]{3,2,1,0:T(2,128)(2,1)S(1)}, u32[]{:S(2)}, u32[]{:S(2)}) collective-permute-start(bf16[8,48,2,512]{3,2,1,0:T(2,128)(2,1)S(1)} %fusion.15.refs_0_), channel_id=1, source_target_pairs={{0,32},{32,0},{64,96},{96,64},{1,33},{33,1},{65,97},{97,65},{2,34}... | collective-permute-start | bytes 2359304 | tf_op jit(solution)/shard_map/ppermute | solution.py:275
  210.1 13.7 %collective-permute-start.9 = (bf16[8,32,2,512]{3,2,1,0:T(2,128)(2,1)S(1)}, bf16[8,32,2,512]{3,2,1,0:T(2,128)(2,1)S(1)}, u32[]{:S(2)}, u32[]{:S(2)}) collective-permute-start(bf16[8,32,2,512]{3,2,1,0:T(2,128)(2,1)S(1)} %fusion.21.refs_1_), channel_id=1, source_target_pairs={{0,32},{32,0},{64,96},{96,64},{1,33},{33,1},{65,97},{97,65},{2,34}... | collective-permute-start | bytes 1572872 | tf_op jit(solution)/shard_map/ppermute | solution.py:275
  210.2 18.0 %collective-permute-start.7 = (bf16[8,32,2,512]{3,2,1,0:T(2,128)(2,1)S(1)}, bf16[8,32,2,512]{3,2,1,0:T(2,128)(2,1)S(1)}, u32[]{:S(2)}, u32[]{:S(2)}) collective-permute-start(bf16[8,32,2,512]{3,2,1,0:T(2,128)(2,1)S(1)} %fusion.21.refs_1_), channel_id=1, source_target_pairs={{0,64},{32,96},{64,0},{96,32},{1,65},{33,97},{65,1},{97,33},{2,66}... | collective-permute-start | bytes 1572872 | tf_op jit(solution)/shard_map/ppermute | solution.py:275
  217.0 14.9 %collective-permute-start.12 = (bf16[8,48,2,512]{3,2,1,0:T(2,128)(2,1)S(1)}, bf16[8,48,2,512]{3,2,1,0:T(2,128)(2,1)S(1)}, u32[]{:S(2)}, u32[]{:S(2)}) collective-permute-start(bf16[8,48,2,512]{3,2,1,0:T(2,128)(2,1)S(1)} %collective-permute-done.11.refs_0_), channel_id=1, source_target_pairs={{0,32},{32,0},{64,96},{96,64},{1,33},{33,1},{65,97},{97,65},{2,34}... | collective-permute-start | bytes 2359304 | tf_op jit(solution)/shard_map/ppermute | solution.py:275
  228.2 5.2 %collective-permute-start.10 = (bf16[8,32,2,512]{3,2,1,0:T(2,128)(2,1)S(1)}, bf16[8,32,2,512]{3,2,1,0:T(2,128)(2,1)S(1)}, u32[]{:S(2)}, u32[]{:S(2)}) collective-permute-start(bf16[8,32,2,512]{3,2,1,0:T(2,128)(2,1)S(1)} %collective-permute-done.7.refs_2_), channel_id=1, source_target_pairs={{0,32},{32,0},{64,96},{96,64},{1,33},{33,1},{65,97},{97,65},{2,34}... | collective-permute-start | bytes 1572872 | tf_op jit(solution)/shard_map/ppermute | solution.py:275
  (14 other events, 46.4 us)

commit v7 on v5

--- a/solution.py
+++ b/solution.py
@@ -11,6 +11,7 @@
 
 OBS_BLOCK = 1024
 LEVEL_CUT = 48
+EARLY_MEMBERS = 2
 
 
 def local_sigma(tile_id, tile_scale, dev_index, row_count):
@@ -177,17 +178,18 @@
 
 def pick_kernel(order, slot_ref, whole, *refs):
     outs = refs[: len(order)]
-    held, arrive, leave = refs[len(order) :]
-    count = outs[0].shape[0]
+    held = refs[len(order) : -2]
+    arrive, leave = refs[-2:]
+    group = whole.shape[0] // 4
     arriving = []
-    for i, k in enumerate(order):
-        at = pl.ds((slot_ref[0] ^ k) * count, count)
-        arriving.append(pltpu.make_async_copy(whole.at[at], held.at[i], arrive.at[i]))
+    for i, (k, low, high) in enumerate(order):
+        at = pl.ds((slot_ref[0] ^ k) * group + low, high - low)
+        arriving.append(pltpu.make_async_copy(whole.at[at], held[i], arrive.at[i]))
         arriving[-1].start()
     leaving = []
     for i, copy in enumerate(arriving):
         copy.wait()
-        leaving.append(pltpu.make_async_copy(held.at[i], outs[i], leave.at[i]))
+        leaving.append(pltpu.make_async_copy(held[i], outs[i], leave.at[i]))
         leaving[-1].start()
     for copy in leaving:
         copy.wait()
@@ -195,18 +197,15 @@
 
 def pick(slot, order, whole):
     anywhere = pl.BlockSpec(memory_space=pl.ANY)
-    shape = (whole.shape[0] // 4, *whole.shape[1:])
+    shapes = [(high - low, *whole.shape[1:]) for _, low, high in order]
     count = len(order)
     return pl.pallas_call(
         functools.partial(pick_kernel, order),
         in_specs=[pl.BlockSpec(memory_space=pltpu.SMEM), anywhere],
         out_specs=[anywhere] * count,
-        out_shape=[jax.ShapeDtypeStruct(shape, whole.dtype)] * count,
-        scratch_shapes=[
-            pltpu.VMEM((count, *shape), whole.dtype),
-            pltpu.SemaphoreType.DMA((count,)),
-            pltpu.SemaphoreType.DMA((count,)),
-        ],
+        out_shape=[jax.ShapeDtypeStruct(shape, whole.dtype) for shape in shapes],
+        scratch_shapes=[pltpu.VMEM(shape, whole.dtype) for shape in shapes]
+        + [pltpu.SemaphoreType.DMA((count,)), pltpu.SemaphoreType.DMA((count,))],
         compiler_params=pltpu.CompilerParams(vmem_limit_bytes=56 << 20),
         cost_estimate=pl.CostEstimate(
             flops=0, bytes_accessed=3 * whole.size, transcendentals=0
@@ -282,11 +281,11 @@
     norm_scale = 1.0 / math.sqrt(members)
     perturbed = perturbations[0]
 
-    order = (2, 3, 1)
-    sent = dict(zip(order, pick(slot, order, perturbed)))
+    early = EARLY_MEMBERS
+    order = ((2, 0, early), (2, early, own), (3, 0, own), (1, 0, own))
+    sent = pick(slot, order, perturbed)
     land_mask, tile_id, sent = lax.optimization_barrier((land_mask, tile_id, sent))
-    got = {k: row_major(swap_slot(sent[k], k)) for k in order}
-    pert = [lax.dynamic_slice_in_dim(perturbed, slot * own, own, 0), got[1], got[2], got[3]]
+    first = row_major(swap_slot(sent[0], 2))
 
     obs = jnp.stack([obs_cell.astype(jnp.float32), obs_value, obs_weight])
     obs = jnp.stack([obs, swap_slot(obs, 2)])
@@ -301,6 +300,10 @@
         jnp.bfloat16
     )
     along_x = along_x.reshape(own, row_count, levels, tiles, 128).transpose(0, 3, 1, 2, 4)
+    along_x, first, sent = lax.optimization_barrier((along_x, first, sent))
+    rest, mates, near = [
+        row_major(swap_slot(part, k)) for part, (k, _, _) in zip(sent[1:], order[1:])
+    ]
     received = swap_columns(along_x)
     received = received.reshape(-1, levels, 128)
     across = jnp.einsum(
@@ -312,6 +315,12 @@
     tile_shape = (own, tiles, row_count, levels, 128)
     spread = swap_columns(deeper.reshape(tile_shape))
 
+    pert = [
+        lax.dynamic_slice_in_dim(perturbed, slot * own, own, 0),
+        near,
+        jnp.concatenate([first, rest]),
+        mates,
+    ]
     pert = [p.transpose(0, 2, 1, 3) for p in pert]
     spread, weight_sum, value_sum = lax.optimization_barrier((spread, weight_sum, value_sum))
     keep, send = increments(spread, pert)

time: 226 us -> 220 us (0.973)
  waiting for transfers between devices: 71.4 us -> 61.9 us
  starting transfers between devices: 56.4 us -> 61.8 us
    ppermute x13 -> x14, waiting for transfers between devices: 53 us -> 43.7 us  [swap_slot(): return lax.ppermute(arr, 'slot', [(i, i ^ k) for i in range(4)])]
    ppermute x13 -> x14, starting transfers between devices: 27.7 us -> 34.3 us  [swap_slot(): return lax.ppermute(arr, 'slot', [(i, i ^ k) for i in range(4)])]
    unnamed x45 -> x49, local copies, waits for them, and re-layouts: 5.63 us -> 6.35 us
  transfers between devices with their start and end apart: 17 -> 18, of which waited for: 12 -> 12; matrix products, arithmetic and copies ran while one was open for 12% -> 15% of each run, Pallas kernels for 8% -> 8%
where the time goes in v7:
time: 220 us; the launch traced here: 216 us
  waiting for transfers between devices  61.9 us (28%)
  starting transfers between devices  61.8 us (28%)
  Pallas kernels  26.6 us (12%)
  local copies, waits for them, and re-layouts  26.5 us (12%)
  blocking collectives  22.9 us (10%)
  matrix products  8.11 us (4%)
  other arithmetic  7.82 us (4%)
    ppermute x14, waiting for transfers between devices, swap_slot(): return lax.ppermute(arr, 'slot', [(i, i ^ k) for i in range(4)])  43.7 us
    ppermute x14, starting transfers between devices, swap_slot(): return lax.ppermute(arr, 'slot', [(i, i ^ k) for i in range(4)])  34.3 us
    all_to_all x4, starting transfers between devices, swap_columns(): lax.all_to_all(flat, 'horiz', split_axis=0, concat_axis=0, tiled=True)  27.5 us
    all_to_all x1, blocking collectives, swap_columns(): lax.all_to_all(flat, 'horiz', split_axis=0, concat_axis=0, tiled=True)  22.9 us
    all_to_all x4, waiting for transfers between devices, swap_columns(): lax.all_to_all(flat, 'horiz', split_axis=0, concat_axis=0, tiled=True)  18.3 us
    pallas_call x1, Pallas kernels, obs_fields(): pl.pallas_call(obs_kernel, grid=(slots, count // OBS_BLOCK), in_specs=[pa...  14.7 us
    unnamed x49, local copies, waits for them, and re-layouts  6.35 us
    another operation x3, local copies, waits for them, and re-layouts, row_major(): return with_layout_constraint(arr, Layout(tuple(range(arr.ndim))))  5.44 us
  transfers between devices with their start and end apart: 18, of which 12 were waited for; matrix products, arithmetic and copies ran while one was open for 15% of the time, Pallas kernels for 8%

profile of v7, /device:TPU:37, one launch (start us, length us, event | category | flops | bytes accessed | tf_op | source)
XLA Modules:
  0.0 216.5 jit_solution(17978175029147526312)
XLA Ops:
  0.0 3.4 %shard_map.109 = (bf16[2,80,2,512]{3,2,1,0:T(2,128)(2,1)}, bf16[6,80,2,512]{3,2,1,0:T(2,128)(2,1)}, bf16[8,80,2,512]{3,2,1,0:T(2,128)(2,1)}, bf16[8,80,2,512]{3,2,1,0:T(2,128)(2,1)}) custom-call(s32[1]{0:T(128)} %bitcast.slot_ref, bf16[32,80,2,512]{3,2,1,0:T(2,128)(2,1)} %bitcast.113), custom_call_target="tpu_custom_call" | custom-call | bytes 7864320 | tf_op jit(solution)/shard_map/pallas_call | solution.py:202
  3.9 2.8 %collective-permute-start.1 = (f32[3,1,8192]{2,1,0:T(1,128)S(1)}, f32[3,1,8192]{2,1,0:T(1,128)S(1)}, u32[]{:S(2)}, u32[]{:S(2)}) collective-permute-start(f32[3,1,8192]{2,1,0:T(1,128)S(1)} %pad_maximum_fusion.1), channel_id=1, source_target_pairs={{0,64},{32,96},{64,0},{96,32},{1,65},{33,97},{65,1},{97,33},{2,66}... | collective-permute-start | bytes 294920 | tf_op jit(solution)/shard_map/ppermute | solution.py:256
  14.6 8.3 %all-to-all-start = ((bf16[32,2,80,128]{3,2,1,0:T(8,128)(2,1)}), bf16[32,2,80,128]{3,2,1,0:T(8,128)(2,1)}, u32[]{:S(2)}, u32[]{:S(2)}) async-start(bf16[32,2,80,128]{3,2,1,0:T(8,128)(2,1)} %bitcast.10), calls=%async_computation | async-start | bytes 2621440 | tf_op jit(solution)/shard_map/all_to_all | solution.py:252
  26.4 5.8 %collective-permute-start.4 = (bf16[8,80,2,512]{3,2,1,0:T(2,128)(2,1)}, bf16[8,80,2,512]{3,2,1,0:T(2,128)(2,1)}, u32[]{:S(2)}, u32[]{:S(2)}) collective-permute-start(bf16[8,80,2,512]{3,2,1,0:T(2,128)(2,1)} %get-tuple-element.47), channel_id=1, source_target_pairs={{0,96},{32,64},{64,32},{96,0},{1,97},{33,65},{65,33},{97,1},{2,98}... | collective-permute-start | bytes 3932168 | tf_op jit(solution)/shard_map/ppermute | solution.py:256
  32.2 6.1 %all-to-all-done = bf16[32,2,80,128]{3,2,1,0:T(8,128)(2,1)} async-done(((bf16[32,2,80,128]{3,2,1,0:T(8,128)(2,1)}), bf16[32,2,80,128]{3,2,1,0:T(8,128)(2,1)}, u32[]{:S(2)}, u32[]{:S(2)}) %all-to-all-start) | async-done | bytes 1310752 | tf_op jit(solution)/shard_map/all_to_all | solution.py:252
  38.3 2.8 %copy.75 = bf16[32,2,80,128]{3,1,0,2:T(2,128)(2,1)S(1)} copy(bf16[32,2,80,128]{3,2,1,0:T(8,128)(2,1)} %all-to-all-done) | data formatting | bytes 2621440 | tf_op jit(solution)/shard_map/all_to_all | solution.py:252
  44.0 7.0 %all-to-all-start.1 = ((bf16[32,2,80,128]{3,2,1,0:T(8,128)(2,1)}), bf16[32,2,80,128]{3,2,1,0:T(8,128)(2,1)}, u32[]{:S(2)}, u32[]{:S(2)}) async-start(bf16[32,2,80,128]{3,2,1,0:T(8,128)(2,1)} %bitcast.114), calls=%async_computation.1 | async-start | bytes 2621440 | tf_op jit(solution)/shard_map/all_to_all | solution.py:252
  51.0 14.7 %shard_map.110 = (f32[2,2,80,512]{3,2,1,0:T(8,128)S(1)}, f32[2,2,80,512]{3,2,1,0:T(8,128)S(1)}) custom-call(f32[2,3,1,8192]{3,2,1,0:T(1,128)S(1)} %pad_maximum_fusion.cell_ref.value_ref.weight_ref, f32[2,3,1,8192]{3,2,1,0:T(1,128)S(1)} %pad_maximum_fusion.cell_ref.value_ref.weight_ref, f32[2,3,1,8192]{3,2,1,0:T(1,128)S(1)} %pad_maximum_fusion.cell_ref.value_ref.weight_ref), custom_call_target="tpu_custom_call" | custom-call | flops 21474836480 | bytes 1310720 | tf_op jit(solution)/shard_map/pallas_call | solution.py:77
  67.6 23.5 %collective-permute-done.4 = bf16[8,80,2,512]{3,2,1,0:T(2,128)(2,1)} collective-permute-done((bf16[8,80,2,512]{3,2,1,0:T(2,128)(2,1)}, bf16[8,80,2,512]{3,2,1,0:T(2,128)(2,1)}, u32[]{:S(2)}, u32[]{:S(2)}) %collective-permute-start.4) | collective-permute-done | bytes 1310752 | tf_op jit(solution)/shard_map/ppermute | solution.py:256
  91.2 2.6 %copy.152 = bf16[8,80,2,512]{3,1,2,0:T(8,128)(2,1)} copy(bf16[8,80,2,512]{3,2,1,0:T(2,128)(2,1)} %collective-permute-done.4) | data formatting | bytes 2621440 | tf_op jit(solution)/shard_map/layout_constraint | solution.py:260
  93.8 2.6 %copy.153 = bf16[8,80,2,512]{3,1,2,0:T(8,128)(2,1)} copy(bf16[8,80,2,512]{3,2,1,0:T(2,128)(2,1)} %collective-permute-done.2) | data formatting | bytes 2621440 | tf_op jit(solution)/shard_map/layout_constraint | solution.py:260
  96.5 3.7 %all-to-all-done.1 = bf16[32,2,80,128]{3,2,1,0:T(8,128)(2,1)} async-done(((bf16[32,2,80,128]{3,2,1,0:T(8,128)(2,1)}), bf16[32,2,80,128]{3,2,1,0:T(8,128)(2,1)}, u32[]{:S(2)}, u32[]{:S(2)}) %all-to-all-start.1) | async-done | bytes 1310752 | tf_op jit(solution)/shard_map/all_to_all | solution.py:252
  102.7 2.6 %shard_map.111 = (f32[2,2,80,512]{3,2,1,0:T(8,128)S(1)}, bf16[2,2,80,512]{3,2,1,0:T(8,128)(2,1)S(1)}) custom-call(bf16[8,4,2,80,128]{4,3,2,1,0:T(8,128)(2,1)} %bitcast.17.spread_ref, bf16[8,2,80,512]{3,2,1,0:T(8,128)(2,1)S(1)} %bitcast.106, bf16[8,2,80,512]{3,2,1,0:T(8,128)(2,1)S(1)} %bitcast.110, bf16[8,2,80,512]{3,2,1,0:T(8,128)(2,1)S(1)} %maximum_bitcast_fusion.p2, ...), custom_call_target="tpu_custom_call" | custom-call | flops 5242880 | bytes 6553600 | tf_op jit(solution)/shard_map/pallas_call | solution.py:114
  105.4 5.4 %collective-permute-start.5 = (bf16[2,2,80,512]{3,2,1,0:T(8,128)(2,1)S(1)}, bf16[2,2,80,512]{3,2,1,0:T(8,128)(2,1)S(1)}, u32[]{:S(2)}, u32[]{:S(2)}) collective-permute-start(bf16[2,2,80,512]{3,2,1,0:T(8,128)(2,1)S(1)} %get-tuple-element.49), channel_id=1, source_target_pairs={{0,32},{32,0},{64,96},{96,64},{1,33},{33,1},{65,97},{97,65},{2,34}... | collective-permute-start | bytes 983048 | tf_op jit(solution)/shard_map/ppermute | solution.py:256
  112.9 9.9 %collective-permute-done.6 = bf16[2,2,80,512]{3,2,1,0:T(8,128)(2,1)S(1)} collective-permute-done((bf16[2,2,80,512]{3,2,1,0:T(8,128)(2,1)S(1)}, bf16[2,2,80,512]{3,2,1,0:T(8,128)(2,1)S(1)}, u32[]{:S(2)}, u32[]{:S(2)}) %collective-permute-start.6) | collective-permute-done | bytes 327712 | tf_op jit(solution)/shard_map/ppermute | solution.py:256
  128.2 22.9 %all_to_all.25 = bf16[32,2,80,128]{3,2,1,0:T(8,128)(2,1)S(1)} all-to-all(bf16[32,2,80,128]{3,2,1,0:T(8,128)(2,1)S(1)} %bitcast.112), channel_id=1, replica_groups=mesh['slot'=4,'horiz'=32] {'horiz'}, dimensions={0} | all-to-all | bytes 2621440 | tf_op jit(solution)/shard_map/all_to_all | solution.py:252
  154.5 5.9 %all-to-all-start.4 = ((bf16[32,2,48,128]{3,2,1,0:T(8,128)(2,1)}), bf16[32,2,48,128]{3,2,1,0:T(8,128)(2,1)}, u32[]{:S(2)}, u32[]{:S(2)}) async-start(bf16[32,2,48,128]{3,2,1,0:T(8,128)(2,1)} %bitcast.121), calls=%async_computation.4 | async-start | bytes 1572864 | tf_op jit(solution)/shard_map/all_to_all | solution.py:252
  166.0 4.8 %all-to-all-done.4 = bf16[32,2,48,128]{3,2,1,0:T(8,128)(2,1)} async-done(((bf16[32,2,48,128]{3,2,1,0:T(8,128)(2,1)}), bf16[32,2,48,128]{3,2,1,0:T(8,128)(2,1)}, u32[]{:S(2)}, u32[]{:S(2)}) %all-to-all-start.4) | async-done | bytes 786464 | tf_op jit(solution)/shard_map/all_to_all | solution.py:252
  170.9 6.3 %all-to-all-start.3 = ((bf16[32,2,32,128]{3,2,1,0:T(8,128)(2,1)}), bf16[32,2,32,128]{3,2,1,0:T(8,128)(2,1)}, u32[]{:S(2)}, u32[]{:S(2)}) async-start(bf16[32,2,32,128]{3,2,1,0:T(8,128)(2,1)} %bitcast.35), calls=%async_computation.3 | async-start | bytes 1048576 | tf_op jit(solution)/shard_map/all_to_all | solution.py:252
  181.8 3.7 %all-to-all-done.3 = bf16[32,2,32,128]{3,2,1,0:T(8,128)(2,1)} async-done(((bf16[32,2,32,128]{3,2,1,0:T(8,128)(2,1)}), bf16[32,2,32,128]{3,2,1,0:T(8,128)(2,1)}, u32[]{:S(2)}, u32[]{:S(2)}) %all-to-all-start.3) | async-done | bytes 524320 | tf_op jit(solution)/shard_map/all_to_all | solution.py:252
  187.0 4.7 %collective-permute-start.9 = (bf16[8,48,2,512]{3,2,1,0:T(2,128)(2,1)S(1)}, bf16[8,48,2,512]{3,2,1,0:T(2,128)(2,1)S(1)}, u32[]{:S(2)}, u32[]{:S(2)}) collective-permute-start(bf16[8,48,2,512]{3,2,1,0:T(2,128)(2,1)S(1)} %fusion.10.refs_0_), channel_id=1, source_target_pairs={{0,32},{32,0},{64,96},{96,64},{1,33},{33,1},{65,97},{97,65},{2,34}... | collective-permute-start | bytes 2359304 | tf_op jit(solution)/shard_map/ppermute | solution.py:256
  193.4 5.3 %collective-permute-done.12.refs_0_ = bf16[8,48,2,512]{3,2,1,0:T(2,128)(2,1)S(1)} collective-permute-done((bf16[8,48,2,512]{3,2,1,0:T(2,128)(2,1)S(1)}, bf16[8,48,2,512]{3,2,1,0:T(2,128)(2,1)S(1)}, u32[]{:S(2)}, u32[]{:S(2)}) %collective-permute-start.12) | collective-permute-done | bytes 786464 | tf_op jit(solution)/shard_map/ppermute | solution.py:256
  198.8 7.7 %collective-permute-start.13 = (bf16[8,48,2,512]{3,2,1,0:T(2,128)(2,1)S(1)}, bf16[8,48,2,512]{3,2,1,0:T(2,128)(2,1)S(1)}, u32[]{:S(2)}, u32[]{:S(2)}) collective-permute-start(bf16[8,48,2,512]{3,2,1,0:T(2,128)(2,1)S(1)} %collective-permute-done.12.refs_0_), channel_id=1, source_target_pairs={{0,32},{32,0},{64,96},{96,64},{1,33},{33,1},{65,97},{97,65},{2,34}... | collective-permute-start | bytes 2359304 | tf_op jit(solution)/shard_map/ppermute | solution.py:256
  210.0 4.0 %collective-permute-start.11 = (bf16[8,32,2,512]{3,2,1,0:T(2,128)(2,1)S(1)}, bf16[8,32,2,512]{3,2,1,0:T(2,128)(2,1)S(1)}, u32[]{:S(2)}, u32[]{:S(2)}) collective-permute-start(bf16[8,32,2,512]{3,2,1,0:T(2,128)(2,1)S(1)} %collective-permute-done.8.refs_2_), channel_id=1, source_target_pairs={{0,32},{32,0},{64,96},{96,64},{1,33},{33,1},{65,97},{97,65},{2,34}... | collective-permute-start | bytes 1572872 | tf_op jit(solution)/shard_map/ppermute | solution.py:256
  (116 shorter events, 49.2 us)
Async XLA Ops:
  0.0 11.2 %copy-start = (bf16[512,512]{1,0:T(8,128)(2,1)S(1)}, bf16[512,512]{1,0:T(8,128)(2,1)}, u32[]{:S(2)}) copy-start(bf16[512,512]{1,0:T(8,128)(2,1)} %param.15) | copy-start | bytes 1572868
  3.5 10.4 %collective-permute-start = (bf16[2,80,2,512]{3,2,1,0:T(2,128)(2,1)}, bf16[2,80,2,512]{3,2,1,0:T(2,128)(2,1)S(1)}, u32[]{:S(2)}, u32[]{:S(2)}) collective-permute-start(bf16[2,80,2,512]{3,2,1,0:T(2,128)(2,1)} %get-tuple-element.35), channel_id=1, source_target_pairs={{0,64},{32,96},{64,0},{96,32},{1,65},{33,97},{65,1},{97,33},{2,66}... | collective-permute-start | bytes 983048 | tf_op jit(solution)/shard_map/ppermute | solution.py:256
  3.9 21.7 %collective-permute-start.1 = (f32[3,1,8192]{2,1,0:T(1,128)S(1)}, f32[3,1,8192]{2,1,0:T(1,128)S(1)}, u32[]{:S(2)}, u32[]{:S(2)}) collective-permute-start(f32[3,1,8192]{2,1,0:T(1,128)S(1)} %pad_maximum_fusion.1), channel_id=1, source_target_pairs={{0,64},{32,96},{64,0},{96,32},{1,65},{33,97},{65,1},{97,33},{2,66}... | collective-permute-start | bytes 294920 | tf_op jit(solution)/shard_map/ppermute | solution.py:256
  14.6 23.7 %all-to-all-start = ((bf16[32,2,80,128]{3,2,1,0:T(8,128)(2,1)}), bf16[32,2,80,128]{3,2,1,0:T(8,128)(2,1)}, u32[]{:S(2)}, u32[]{:S(2)}) async-start(bf16[32,2,80,128]{3,2,1,0:T(8,128)(2,1)} %bitcast.10), calls=%async_computation | async-start | bytes 2621440 | tf_op jit(solution)/shard_map/all_to_all | solution.py:252
  25.8 15.3 %copy-start.21 = (bf16[64,64]{1,0:T(8,128)(2,1)S(1)}, bf16[64,64]{1,0:T(8,128)(2,1)}, u32[]{:S(2)}) copy-start(bf16[64,64]{1,0:T(8,128)(2,1)} %param.16) | copy-start | bytes 24580
  25.8 40.7 %collective-permute-start.3 = (bf16[6,80,2,512]{3,2,1,0:T(2,128)(2,1)}, bf16[6,80,2,512]{3,2,1,0:T(2,128)(2,1)S(1)}, u32[]{:S(2)}, u32[]{:S(2)}) collective-permute-start(bf16[6,80,2,512]{3,2,1,0:T(2,128)(2,1)} %get-tuple-element.46), channel_id=1, source_target_pairs={{0,64},{32,96},{64,0},{96,32},{1,65},{33,97},{65,1},{97,33},{2,66}... | collective-permute-start | bytes 2949128 | tf_op jit(solution)/shard_map/ppermute | solution.py:256
  26.4 64.8 %collective-permute-start.4 = (bf16[8,80,2,512]{3,2,1,0:T(2,128)(2,1)}, bf16[8,80,2,512]{3,2,1,0:T(2,128)(2,1)}, u32[]{:S(2)}, u32[]{:S(2)}) collective-permute-start(bf16[8,80,2,512]{3,2,1,0:T(2,128)(2,1)} %get-tuple-element.47), channel_id=1, source_target_pairs={{0,96},{32,64},{64,32},{96,0},{1,97},{33,65},{65,33},{97,1},{2,98}... | collective-permute-start | bytes 3932168 | tf_op jit(solution)/shard_map/ppermute | solution.py:256
  32.2 61.6 %collective-permute-start.2 = (bf16[8,80,2,512]{3,2,1,0:T(2,128)(2,1)}, bf16[8,80,2,512]{3,2,1,0:T(2,128)(2,1)}, u32[]{:S(2)}, u32[]{:S(2)}) collective-permute-start(bf16[8,80,2,512]{3,2,1,0:T(2,128)(2,1)} %get-tuple-element.44), channel_id=1, source_target_pairs={{0,32},{32,0},{64,96},{96,64},{1,33},{33,1},{65,97},{97,65},{2,34}... | collective-permute-start | bytes 3932168 | tf_op jit(solution)/shard_map/ppermute | solution.py:256
  44.0 56.2 %all-to-all-start.1 = ((bf16[32,2,80,128]{3,2,1,0:T(8,128)(2,1)}), bf16[32,2,80,128]{3,2,1,0:T(8,128)(2,1)}, u32[]{:S(2)}, u32[]{:S(2)}) async-start(bf16[32,2,80,128]{3,2,1,0:T(8,128)(2,1)} %bitcast.114), calls=%async_computation.1 | async-start | bytes 2621440 | tf_op jit(solution)/shard_map/all_to_all | solution.py:252
  50.9 15.5 %copy-start.17 = (bf16[2,80,2,512]{3,2,1,0:T(2,128)(2,1)S(1)}, bf16[2,80,2,512]{3,2,1,0:T(2,128)(2,1)}, u32[]{:S(2)}) copy-start(bf16[2,80,2,512]{3,2,1,0:T(2,128)(2,1)} %copy-done.16) | copy-start | bytes 983044
  105.3 17.6 %copy-start.6 = (f32[2,2,80,512]{3,2,1,0:T(8,128)S(1)}, f32[2,2,80,512]{3,2,1,0:T(8,128)}, u32[]{:S(2)}) copy-start(f32[2,2,80,512]{3,2,1,0:T(8,128)} %copy-done.5) | copy-start | bytes 1966084
  105.3 17.6 %copy-start.8 = (f32[2,2,80,512]{3,2,1,0:T(8,128)S(1)}, f32[2,2,80,512]{3,2,1,0:T(8,128)}, u32[]{:S(2)}) copy-start(f32[2,2,80,512]{3,2,1,0:T(8,128)} %copy-done.7) | copy-start | bytes 1966084
  105.4 6.7 %collective-permute-start.5 = (bf16[2,2,80,512]{3,2,1,0:T(8,128)(2,1)S(1)}, bf16[2,2,80,512]{3,2,1,0:T(8,128)(2,1)S(1)}, u32[]{:S(2)}, u32[]{:S(2)}) collective-permute-start(bf16[2,2,80,512]{3,2,1,0:T(8,128)(2,1)S(1)} %get-tuple-element.49), channel_id=1, source_target_pairs={{0,32},{32,0},{64,96},{96,64},{1,33},{33,1},{65,97},{97,65},{2,34}... | collective-permute-start | bytes 983048 | tf_op jit(solution)/shard_map/ppermute | solution.py:256
  112.1 10.7 %collective-permute-start.6 = (bf16[2,2,80,512]{3,2,1,0:T(8,128)(2,1)S(1)}, bf16[2,2,80,512]{3,2,1,0:T(8,128)(2,1)S(1)}, u32[]{:S(2)}, u32[]{:S(2)}) collective-permute-start(bf16[2,2,80,512]{3,2,1,0:T(8,128)(2,1)S(1)} %fusion.17), channel_id=1, source_target_pairs={{0,64},{32,96},{64,0},{96,32},{1,65},{33,97},{65,1},{97,33},{2,66}... | collective-permute-start | bytes 983048 | tf_op jit(solution)/shard_map/ppermute | solution.py:256
  123.3 2.5 %collective-permute-start.7 = (bf16[2,2,80,512]{3,2,1,0:T(8,128)(2,1)S(1)}, bf16[2,2,80,512]{3,2,1,0:T(8,128)(2,1)S(1)}, u32[]{:S(2)}, u32[]{:S(2)}) collective-permute-start(bf16[2,2,80,512]{3,2,1,0:T(8,128)(2,1)S(1)} %multiply_convert_fusion.3.own_ref), channel_id=1, source_target_pairs={{0,32},{32,0},{64,96},{96,64},{1,33},{33,1},{65,97},{97,65},{2,34}... | collective-permute-start | bytes 983048 | tf_op jit(solution)/shard_map/ppermute | solution.py:256
  154.5 16.3 %all-to-all-start.4 = ((bf16[32,2,48,128]{3,2,1,0:T(8,128)(2,1)}), bf16[32,2,48,128]{3,2,1,0:T(8,128)(2,1)}, u32[]{:S(2)}, u32[]{:S(2)}) async-start(bf16[32,2,48,128]{3,2,1,0:T(8,128)(2,1)} %bitcast.121), calls=%async_computation.4 | async-start | bytes 1572864 | tf_op jit(solution)/shard_map/all_to_all | solution.py:252
  170.9 14.6 %all-to-all-start.3 = ((bf16[32,2,32,128]{3,2,1,0:T(8,128)(2,1)}), bf16[32,2,32,128]{3,2,1,0:T(8,128)(2,1)}, u32[]{:S(2)}, u32[]{:S(2)}) async-start(bf16[32,2,32,128]{3,2,1,0:T(8,128)(2,1)} %bitcast.35), calls=%async_computation.3 | async-start | bytes 1048576 | tf_op jit(solution)/shard_map/all_to_all | solution.py:252
  181.2 10.6 %copy-start.12 = (f32[8,2,32,512]{3,2,1,0:T(8,128)S(1)}, f32[8,2,32,512]{3,2,1,0:T(8,128)}, u32[]{:S(2)}) copy-start(f32[8,2,32,512]{3,2,1,0:T(8,128)} %slice_convert_fusion.1) | copy-start | bytes 3145732
  181.2 17.6 %collective-permute-start.12 = (bf16[8,48,2,512]{3,2,1,0:T(2,128)(2,1)S(1)}, bf16[8,48,2,512]{3,2,1,0:T(2,128)(2,1)S(1)}, u32[]{:S(2)}, u32[]{:S(2)}) collective-permute-start(bf16[8,48,2,512]{3,2,1,0:T(2,128)(2,1)S(1)} %fusion.10.refs_0_), channel_id=1, source_target_pairs={{0,64},{32,96},{64,0},{96,32},{1,65},{33,97},{65,1},{97,33},{2,66}... | collective-permute-start | bytes 2359304 | tf_op jit(solution)/shard_map/ppermute | solution.py:256
  187.0 19.5 %collective-permute-start.9 = (bf16[8,48,2,512]{3,2,1,0:T(2,128)(2,1)S(1)}, bf16[8,48,2,512]{3,2,1,0:T(2,128)(2,1)S(1)}, u32[]{:S(2)}, u32[]{:S(2)}) collective-permute-start(bf16[8,48,2,512]{3,2,1,0:T(2,128)(2,1)S(1)} %fusion.10.refs_0_), channel_id=1, source_target_pairs={{0,32},{32,0},{64,96},{96,64},{1,33},{33,1},{65,97},{97,65},{2,34}... | collective-permute-start | bytes 2359304 | tf_op jit(solution)/shard_map/ppermute | solution.py:256
  193.1 13.4 %collective-permute-start.10 = (bf16[8,32,2,512]{3,2,1,0:T(2,128)(2,1)S(1)}, bf16[8,32,2,512]{3,2,1,0:T(2,128)(2,1)S(1)}, u32[]{:S(2)}, u32[]{:S(2)}) collective-permute-start(bf16[8,32,2,512]{3,2,1,0:T(2,128)(2,1)S(1)} %fusion.16.refs_1_), channel_id=1, source_target_pairs={{0,32},{32,0},{64,96},{96,64},{1,33},{33,1},{65,97},{97,65},{2,34}... | collective-permute-start | bytes 1572872 | tf_op jit(solution)/shard_map/ppermute | solution.py:256
  193.2 16.8 %collective-permute-start.8 = (bf16[8,32,2,512]{3,2,1,0:T(2,128)(2,1)S(1)}, bf16[8,32,2,512]{3,2,1,0:T(2,128)(2,1)S(1)}, u32[]{:S(2)}, u32[]{:S(2)}) collective-permute-start(bf16[8,32,2,512]{3,2,1,0:T(2,128)(2,1)S(1)} %fusion.16.refs_1_), channel_id=1, source_target_pairs={{0,64},{32,96},{64,0},{96,32},{1,65},{33,97},{65,1},{97,33},{2,66}... | collective-permute-start | bytes 1572872 | tf_op jit(solution)/shard_map/ppermute | solution.py:256
  198.8 15.2 %collective-permute-start.13 = (bf16[8,48,2,512]{3,2,1,0:T(2,128)(2,1)S(1)}, bf16[8,48,2,512]{3,2,1,0:T(2,128)(2,1)S(1)}, u32[]{:S(2)}, u32[]{:S(2)}) collective-permute-start(bf16[8,48,2,512]{3,2,1,0:T(2,128)(2,1)S(1)} %collective-permute-done.12.refs_0_), channel_id=1, source_target_pairs={{0,32},{32,0},{64,96},{96,64},{1,33},{33,1},{65,97},{97,65},{2,34}... | collective-permute-start | bytes 2359304 | tf_op jit(solution)/shard_map/ppermute | solution.py:256
  210.0 5.5 %collective-permute-start.11 = (bf16[8,32,2,512]{3,2,1,0:T(2,128)(2,1)S(1)}, bf16[8,32,2,512]{3,2,1,0:T(2,128)(2,1)S(1)}, u32[]{:S(2)}, u32[]{:S(2)}) collective-permute-start(bf16[8,32,2,512]{3,2,1,0:T(2,128)(2,1)S(1)} %collective-permute-done.8.refs_2_), channel_id=1, source_target_pairs={{0,32},{32,0},{64,96},{96,64},{1,33},{33,1},{65,97},{97,65},{2,34}... | collective-permute-start | bytes 1572872 | tf_op jit(solution)/shard_map/ppermute | solution.py:256
  (20 other events, 49.3 us)

commit v8 on v7

--- a/solution.py
+++ b/solution.py
@@ -10,7 +10,7 @@
 from jax.sharding import PartitionSpec as P
 
 OBS_BLOCK = 1024
-LEVEL_CUT = 48
+LEVEL_CUT = 32
 EARLY_MEMBERS = 2
 
 
@@ -216,12 +216,19 @@
 def place_kernel(groups, slot_ref, *refs):
     parts = refs[: len(groups)]
     out, sems = refs[-2:]
+    slot = slot_ref[0]
+    count = out.shape[0] // 4
     copies = []
-    for i, ((k, low), part) in enumerate(zip(groups, parts)):
-        count, levels = part.shape[:2]
-        at = out.at[pl.ds((slot_ref[0] ^ k) * count, count), pl.ds(low, levels)]
-        copies.append(pltpu.make_async_copy(part, at, sems.at[i]))
-        copies[-1].start()
+    for (k, low), part in zip(groups, parts):
+        levels = part.shape[1]
+        if part.shape[0] == count:
+            rows = [(part, slot ^ k)]
+        else:
+            rows = [(part.at[pl.ds(i * count, count)], 2 * i + ((slot ^ k) & 1)) for i in range(2)]
+        for piece, group in rows:
+            at = out.at[pl.ds(group * count, count), pl.ds(low, levels)]
+            copies.append(pltpu.make_async_copy(piece, at, sems.at[len(copies)]))
+            copies[-1].start()
     for copy in copies:
         copy.wait()
 
@@ -237,7 +244,7 @@
         + [anywhere] * len(extra),
         out_specs=anywhere,
         out_shape=jax.ShapeDtypeStruct(shape, jnp.bfloat16),
-        scratch_shapes=[pltpu.SemaphoreType.DMA((len(groups),))],
+        scratch_shapes=[pltpu.SemaphoreType.DMA((2 * len(groups),))],
         input_output_aliases={} if base is None else {len(parts) + 1: 0},
         compiler_params=pltpu.CompilerParams(vmem_limit_bytes=12 << 20),
         cost_estimate=pl.CostEstimate(
@@ -250,6 +257,20 @@
     shape = tiles.shape
     flat = tiles.reshape(shape[0] * shape[1], *shape[2:])
     return lax.all_to_all(flat, "horiz", split_axis=0, concat_axis=0, tiled=True).reshape(shape)
+
+
+def swap_to_both(tiles):
+    shape = tiles.shape
+    flat = tiles.reshape(2 * shape[1] * shape[2], *shape[3:])
+    groups = [[(2 * half + core) * 32 + h for half in range(2) for h in range(32)] for core in range(2)]
+    return lax.all_to_all(
+        flat,
+        ("slot", "horiz"),
+        split_axis=0,
+        concat_axis=0,
+        axis_index_groups=groups,
+        tiled=True,
+    ).reshape(shape)
 
 
 def swap_slot(arr, k):
@@ -339,39 +360,41 @@
     ).astype(jnp.bfloat16)
     back_across = back_across.reshape(tile_shape)
     sea_half = sea.astype(jnp.bfloat16)
-    bounds = ((0, LEVEL_CUT), (LEVEL_CUT, levels))
-    gradients = []
-    for low, high in bounds:
-        returned = swap_columns(back_across[:, :, :, low:high])
-        returned = returned.transpose(0, 2, 3, 1, 4).reshape(own, row_count, -1, col_count)
+
+    def finish(blocks, start, low, high):
+        rows = blocks.transpose(0, 2, 3, 1, 4).reshape(blocks.shape[0], row_count, -1, col_count)
         filtered = weight_mask[:, low:high] * lax.dot_general(
-            returned * sea_half[:, low:high],
+            rows * sea_half[:, low:high],
             inverse_x,
             (((3,), (1,)), ((), ())),
             preferred_element_type=jnp.float32,
         )
-        gradient = (mine[:, :, low:high].astype(jnp.float32) + filtered).astype(jnp.bfloat16)
-        gradients.append(row_major(gradient.transpose(0, 2, 1, 3)))
-
-    lows = [low for low, _ in bounds]
-    far = [row_major(swap_slot(g, 2)) for g in gradients]
-    near = [row_major(swap_slot(g, 1)) for g in gradients]
+        return row_major((start.astype(jnp.float32) + filtered).astype(jnp.bfloat16).transpose(0, 2, 1, 3))
+
+    cut = LEVEL_CUT
+    twice = jnp.stack([back_across[:, :, :, cut:]] * 2)
+    blocks, twice = lax.optimization_barrier((swap_columns(back_across[:, :, :, :cut]), twice))
+    own_part = finish(blocks, mine[:, :, :cut], 0, cut)
+    core = slot & 1
+    both_start = jnp.concatenate(
+        [lax.dynamic_slice_in_dim(control, (2 * i + core) * own, own, 0)[:, cut:] for i in range(2)]
+    ).transpose(0, 2, 1, 3)
+    far = row_major(swap_slot(own_part, 2))
+    near = row_major(swap_slot(own_part, 1))
+    blocks, own_part = lax.optimization_barrier((swap_to_both(twice), own_part))
+    both_part = finish(blocks.reshape(2 * own, *blocks.shape[2:]), both_start, cut, levels)
+
+    far, both_part = lax.optimization_barrier((far, both_part))
+    near_both = row_major(swap_slot(both_part, 1))
+    mate = row_major(swap_slot(far, 1))
     result = place(
         slot,
-        ((0, lows[0]), (0, lows[1]), (1, lows[0]), (1, lows[1])),
-        (*gradients, *near),
+        ((0, 0), (1, 0), (2, 0), (0, cut)),
+        (own_part, near, far, both_part),
         control.shape,
     )
-    far[1], result = lax.optimization_barrier((far[1], result))
-    both = [row_major(swap_slot(g, 1)) for g in far]
-    result = place(
-        slot,
-        ((2, lows[0]), (3, lows[0]), (2, lows[1])),
-        (far[0], both[0], far[1]),
-        control.shape,
-        result,
-    )
-    return place(slot, ((3, lows[1]),), (both[1],), control.shape, result)
+    near_both, result = lax.optimization_barrier((near_both, result))
+    return place(slot, ((3, 0), (1, cut)), (mate, near_both), control.shape, result)
 
 
 def solution(mesh):

time: 220 us -> 224 us (1.018)
  local copies, waits for them, and re-layouts: 26.5 us -> 32.5 us
  waiting for transfers between devices: 61.9 us -> 65.6 us
  starting transfers between devices: 61.8 us -> 59.4 us
    all_to_all x0 -> x1, waiting for transfers between devices: none -> 8.47 us  [swap_to_both(): lax.all_to_all(flat, ('slot', 'horiz'), split_axis=0, concat_axis=0, axis...]
    all_to_all x0 -> x1, starting transfers between devices: none -> 7.8 us  [swap_to_both(): lax.all_to_all(flat, ('slot', 'horiz'), split_axis=0, concat_axis=0, axis...]
    all_to_all x4 -> x3, starting transfers between devices: 27.5 us -> 21 us  [swap_columns(): lax.all_to_all(flat, 'horiz', split_axis=0, concat_axis=0, tiled=True)]
    ppermute x14 -> x12, starting transfers between devices: 34.3 us -> 30.6 us  [swap_slot(): return lax.ppermute(arr, 'slot', [(i, i ^ k) for i in range(4)])]
    all_to_all x4 -> x3, waiting for transfers between devices: 18.3 us -> 15.6 us  [swap_columns(): lax.all_to_all(flat, 'horiz', split_axis=0, concat_axis=0, tiled=True)]
    unnamed x49 -> x56, local copies, waits for them, and re-layouts: 6.35 us -> 8.9 us
    slice x12 -> x9, local copies, waits for them, and re-layouts: 4.66 us -> 6.95 us  [the longest x1 3.7 us: per_device(): lax.dynamic_slice_in_dim(control, (2 * i + core) * own, own, 0)[:, cut:]]
    ppermute x14 -> x12, waiting for transfers between devices: 43.7 us -> 41.6 us  [swap_slot(): return lax.ppermute(arr, 'slot', [(i, i ^ k) for i in range(4)])]
  transfers between devices with their start and end apart: 18 -> 16, of which waited for: 12 -> 11; matrix products, arithmetic and copies ran while one was open for 15% -> 17% of each run, Pallas kernels for 8% -> 7%
where the time goes in v8:
time: 224 us; the launch traced here: 223 us
  waiting for transfers between devices  65.6 us (29%)
  starting transfers between devices  59.4 us (27%)
  local copies, waits for them, and re-layouts  32.5 us (15%)
  Pallas kernels  26.1 us (12%)
  blocking collectives  22.9 us (10%)
  other arithmetic  9.13 us (4%)
  matrix products  6.24 us (3%)
    ppermute x12, waiting for transfers between devices, swap_slot(): return lax.ppermute(arr, 'slot', [(i, i ^ k) for i in range(4)])  41.6 us
    ppermute x12, starting transfers between devices, swap_slot(): return lax.ppermute(arr, 'slot', [(i, i ^ k) for i in range(4)])  30.6 us
    all_to_all x1, blocking collectives, swap_columns(): lax.all_to_all(flat, 'horiz', split_axis=0, concat_axis=0, tiled=True)  22.9 us
    all_to_all x3, starting transfers between devices, swap_columns(): lax.all_to_all(flat, 'horiz', split_axis=0, concat_axis=0, tiled=True)  21 us
    all_to_all x3, waiting for transfers between devices, swap_columns(): lax.all_to_all(flat, 'horiz', split_axis=0, concat_axis=0, tiled=True)  15.6 us
    pallas_call x1, Pallas kernels, obs_fields(): pl.pallas_call(obs_kernel, grid=(slots, count // OBS_BLOCK), in_specs=[pa...  14.7 us
    unnamed x56, local copies, waits for them, and re-layouts  8.9 us
    all_to_all x1, waiting for transfers between devices, swap_to_both(): lax.all_to_all(flat, ('slot', 'horiz'), split_axis=0, concat_axis=0, axis...  8.47 us
  transfers between devices with their start and end apart: 16, of which 11 were waited for; matrix products, arithmetic and copies ran while one was open for 17% of the time, Pallas kernels for 7%

profile of v8, /device:TPU:37, one launch (start us, length us, event | category | flops | bytes accessed | tf_op | source)
XLA Modules:
  0.0 222.6 jit_solution(8437801771519305753)
XLA Ops:
  0.0 3.4 %shard_map.109 = (bf16[2,80,2,512]{3,2,1,0:T(2,128)(2,1)}, bf16[6,80,2,512]{3,2,1,0:T(2,128)(2,1)}, bf16[8,80,2,512]{3,2,1,0:T(2,128)(2,1)}, bf16[8,80,2,512]{3,2,1,0:T(2,128)(2,1)}) custom-call(s32[1]{0:T(128)} %bitcast.slot_ref, bf16[32,80,2,512]{3,2,1,0:T(2,128)(2,1)} %bitcast.125), custom_call_target="tpu_custom_call" | custom-call | bytes 7864320 | tf_op jit(solution)/shard_map/pallas_call | solution.py:202
  3.9 2.8 %collective-permute-start.1 = (f32[3,1,8192]{2,1,0:T(1,128)S(1)}, f32[3,1,8192]{2,1,0:T(1,128)S(1)}, u32[]{:S(2)}, u32[]{:S(2)}) collective-permute-start(f32[3,1,8192]{2,1,0:T(1,128)S(1)} %pad_maximum_fusion.2), channel_id=1, source_target_pairs={{0,64},{32,96},{64,0},{96,32},{1,65},{33,97},{65,1},{97,33},{2,66}... | collective-permute-start | bytes 294920 | tf_op jit(solution)/shard_map/ppermute | solution.py:277
  14.6 8.3 %all-to-all-start = ((bf16[32,2,80,128]{3,2,1,0:T(8,128)(2,1)}), bf16[32,2,80,128]{3,2,1,0:T(8,128)(2,1)}, u32[]{:S(2)}, u32[]{:S(2)}) async-start(bf16[32,2,80,128]{3,2,1,0:T(8,128)(2,1)} %bitcast.10), calls=%async_computation | async-start | bytes 2621440 | tf_op jit(solution)/shard_map/all_to_all | solution.py:259
  26.4 5.8 %collective-permute-start.4 = (bf16[8,80,2,512]{3,2,1,0:T(2,128)(2,1)}, bf16[8,80,2,512]{3,2,1,0:T(2,128)(2,1)}, u32[]{:S(2)}, u32[]{:S(2)}) collective-permute-start(bf16[8,80,2,512]{3,2,1,0:T(2,128)(2,1)} %get-tuple-element.53), channel_id=1, source_target_pairs={{0,96},{32,64},{64,32},{96,0},{1,97},{33,65},{65,33},{97,1},{2,98}... | collective-permute-start | bytes 3932168 | tf_op jit(solution)/shard_map/ppermute | solution.py:277
  32.2 6.1 %all-to-all-done = bf16[32,2,80,128]{3,2,1,0:T(8,128)(2,1)} async-done(((bf16[32,2,80,128]{3,2,1,0:T(8,128)(2,1)}), bf16[32,2,80,128]{3,2,1,0:T(8,128)(2,1)}, u32[]{:S(2)}, u32[]{:S(2)}) %all-to-all-start) | async-done | bytes 1310752 | tf_op jit(solution)/shard_map/all_to_all | solution.py:259
  38.3 2.8 %copy.75 = bf16[32,2,80,128]{3,1,0,2:T(2,128)(2,1)S(1)} copy(bf16[32,2,80,128]{3,2,1,0:T(8,128)(2,1)} %all-to-all-done) | data formatting | bytes 2621440 | tf_op jit(solution)/shard_map/all_to_all | solution.py:259
  44.0 7.0 %all-to-all-start.1 = ((bf16[32,2,80,128]{3,2,1,0:T(8,128)(2,1)}), bf16[32,2,80,128]{3,2,1,0:T(8,128)(2,1)}, u32[]{:S(2)}, u32[]{:S(2)}) async-start(bf16[32,2,80,128]{3,2,1,0:T(8,128)(2,1)} %bitcast.127), calls=%async_computation.1 | async-start | bytes 2621440 | tf_op jit(solution)/shard_map/all_to_all | solution.py:259
  51.0 14.7 %shard_map.110 = (f32[2,2,80,512]{3,2,1,0:T(8,128)S(1)}, f32[2,2,80,512]{3,2,1,0:T(8,128)S(1)}) custom-call(f32[2,3,1,8192]{3,2,1,0:T(1,128)S(1)} %pad_maximum_fusion.1.cell_ref.value_ref.weight_ref, f32[2,3,1,8192]{3,2,1,0:T(1,128)S(1)} %pad_maximum_fusion.1.cell_ref.value_ref.weight_ref, f32[2,3,1,8192]{3,2,1,0:T(1,128)S(1)} %pad_maximum_fusion.1.cell_ref.value_ref.weight_ref), custom_call_target="tpu_custom_call" | custom-call | flops 21474836480 | bytes 1310720 | tf_op jit(solution)/shard_map/pallas_call | solution.py:77
  67.6 23.5 %collective-permute-done.4 = bf16[8,80,2,512]{3,2,1,0:T(2,128)(2,1)} collective-permute-done((bf16[8,80,2,512]{3,2,1,0:T(2,128)(2,1)}, bf16[8,80,2,512]{3,2,1,0:T(2,128)(2,1)}, u32[]{:S(2)}, u32[]{:S(2)}) %collective-permute-start.4) | collective-permute-done | bytes 1310752 | tf_op jit(solution)/shard_map/ppermute | solution.py:277
  91.2 2.6 %copy.144 = bf16[8,80,2,512]{3,1,2,0:T(8,128)(2,1)} copy(bf16[8,80,2,512]{3,2,1,0:T(2,128)(2,1)} %collective-permute-done.4) | data formatting | bytes 2621440 | tf_op jit(solution)/shard_map/layout_constraint | solution.py:281
  93.8 2.6 %copy.145 = bf16[8,80,2,512]{3,1,2,0:T(8,128)(2,1)} copy(bf16[8,80,2,512]{3,2,1,0:T(2,128)(2,1)} %collective-permute-done.2) | data formatting | bytes 2621440 | tf_op jit(solution)/shard_map/layout_constraint | solution.py:281
  96.5 3.7 %all-to-all-done.1 = bf16[32,2,80,128]{3,2,1,0:T(8,128)(2,1)} async-done(((bf16[32,2,80,128]{3,2,1,0:T(8,128)(2,1)}), bf16[32,2,80,128]{3,2,1,0:T(8,128)(2,1)}, u32[]{:S(2)}, u32[]{:S(2)}) %all-to-all-start.1) | async-done | bytes 1310752 | tf_op jit(solution)/shard_map/all_to_all | solution.py:259
  102.7 2.6 %shard_map.111 = (f32[2,2,80,512]{3,2,1,0:T(8,128)S(1)}, bf16[2,2,80,512]{3,2,1,0:T(8,128)(2,1)S(1)}) custom-call(bf16[8,4,2,80,128]{4,3,2,1,0:T(8,128)(2,1)} %bitcast.17.spread_ref, bf16[8,2,80,512]{3,2,1,0:T(8,128)(2,1)S(1)} %bitcast.118, bf16[8,2,80,512]{3,2,1,0:T(8,128)(2,1)S(1)} %bitcast.122, bf16[8,2,80,512]{3,2,1,0:T(8,128)(2,1)S(1)} %maximum_bitcast_fusion.p2, ...), custom_call_target="tpu_custom_call" | custom-call | flops 5242880 | bytes 6553600 | tf_op jit(solution)/shard_map/pallas_call | solution.py:114
  105.4 5.4 %collective-permute-start.5 = (bf16[2,2,80,512]{3,2,1,0:T(8,128)(2,1)S(1)}, bf16[2,2,80,512]{3,2,1,0:T(8,128)(2,1)S(1)}, u32[]{:S(2)}, u32[]{:S(2)}) collective-permute-start(bf16[2,2,80,512]{3,2,1,0:T(8,128)(2,1)S(1)} %get-tuple-element.55), channel_id=1, source_target_pairs={{0,32},{32,0},{64,96},{96,64},{1,33},{33,1},{65,97},{97,65},{2,34}... | collective-permute-start | bytes 983048 | tf_op jit(solution)/shard_map/ppermute | solution.py:277
  112.9 9.9 %collective-permute-done.6 = bf16[2,2,80,512]{3,2,1,0:T(8,128)(2,1)S(1)} collective-permute-done((bf16[2,2,80,512]{3,2,1,0:T(8,128)(2,1)S(1)}, bf16[2,2,80,512]{3,2,1,0:T(8,128)(2,1)S(1)}, u32[]{:S(2)}, u32[]{:S(2)}) %collective-permute-start.6) | collective-permute-done | bytes 327712 | tf_op jit(solution)/shard_map/ppermute | solution.py:277
  128.2 22.9 %all_to_all.25 = bf16[32,2,80,128]{3,2,1,0:T(8,128)(2,1)S(1)} all-to-all(bf16[32,2,80,128]{3,2,1,0:T(8,128)(2,1)S(1)} %bitcast.124), channel_id=1, replica_groups=mesh['slot'=4,'horiz'=32] {'horiz'}, dimensions={0} | all-to-all | bytes 2621440 | tf_op jit(solution)/shard_map/all_to_all | solution.py:259
  153.9 5.7 %all-to-all-start.3 = ((bf16[32,2,32,128]{3,2,1,0:T(8,128)(2,1)}), bf16[32,2,32,128]{3,2,1,0:T(8,128)(2,1)S(1)}, u32[]{:S(2)}, u32[]{:S(2)}) async-start(bf16[32,2,32,128]{3,2,1,0:T(8,128)(2,1)} %bitcast.35), calls=%async_computation.3 | async-start | bytes 1048576 | tf_op jit(solution)/shard_map/all_to_all | solution.py:259
  162.5 5.8 %all-to-all-done.3 = bf16[32,2,32,128]{3,2,1,0:T(8,128)(2,1)S(1)} async-done(((bf16[32,2,32,128]{3,2,1,0:T(8,128)(2,1)}), bf16[32,2,32,128]{3,2,1,0:T(8,128)(2,1)S(1)}, u32[]{:S(2)}, u32[]{:S(2)}) %all-to-all-start.3) | async-done | bytes 524320 | tf_op jit(solution)/shard_map/all_to_all | solution.py:259
  169.1 7.8 %all-to-all-start.4 = ((bf16[64,2,48,128]{3,2,1,0:T(8,128)(2,1)}), bf16[64,2,48,128]{3,2,1,0:T(8,128)(2,1)S(1)}, u32[]{:S(2)}, u32[]{:S(2)}) async-start(bf16[64,2,48,128]{3,2,1,0:T(8,128)(2,1)} %bitcast.42), calls=%async_computation.4 | async-start | bytes 3145728 | tf_op jit(solution)/shard_map/all_to_all | solution.py:266
  180.2 3.7 %constant_dynamic-slice_fusion.1 = (bf16[8,48,2,512]{3,2,1,0:T(2,128)(2,1)}, bf16[8,48,2,512]{3,2,1,0:T(2,128)(2,1)}) fusion(bf16[32,80,2,512]{3,2,1,0:T(2,128)(2,1)} %param.11, s32[]{:T(128)S(6)} %select_n.26, s32[]{:T(128)S(6)} %add.42, s32[]{:T(128)S(6)} %select_n.27), kind=kLoop, calls=%fused_computation.57 | loop fusion | bytes 3145740 | tf_op jit(solution)/shard_map/slice | solution.py:380
  187.5 8.5 %all-to-all-done.4 = bf16[64,2,48,128]{3,2,1,0:T(8,128)(2,1)S(1)} async-done(((bf16[64,2,48,128]{3,2,1,0:T(8,128)(2,1)}), bf16[64,2,48,128]{3,2,1,0:T(8,128)(2,1)S(1)}, u32[]{:S(2)}, u32[]{:S(2)}) %all-to-all-start.4) | async-done | bytes 1572896 | tf_op jit(solution)/shard_map/all_to_all | solution.py:266
  197.3 3.4 %fusion.1.refs_3_ = bf16[16,48,2,512]{3,2,1,0:T(2,128)(2,1)S(1)} fusion(f32[16,2,48,512]{3,2,1,0:T(8,128)S(1)} %fusion.2, bf16[8,48,2,512]{3,2,1,0:T(2,128)(2,1)S(1)} %copy-done.12, bf16[8,48,2,512]{3,2,1,0:T(2,128)(2,1)S(1)} %copy-done.11, f32[48,2,512]{2,1,0:T(2,128)S(1)} %copy.90), kind=kLoop, calls=%fused_computation.2 | loop fusion | flops 3932160 | bytes 6488064 | tf_op jit(solution)/shard_map/convert_element_type | solution.py:372
  202.8 12.7 %collective-permute-start.10 = (bf16[16,48,2,512]{3,2,1,0:T(2,128)(2,1)S(1)}, bf16[16,48,2,512]{3,2,1,0:T(2,128)(2,1)S(1)}, u32[]{:S(2)}, u32[]{:S(2)}) collective-permute-start(bf16[16,48,2,512]{3,2,1,0:T(2,128)(2,1)S(1)} %fusion.1.refs_3_), channel_id=1, source_target_pairs={{0,32},{32,0},{64,96},{96,64},{1,33},{33,1},{65,97},{97,65},{2,34}... | collective-permute-start | bytes 4718600 | tf_op jit(solution)/shard_map/ppermute | solution.py:277
  216.0 3.3 %collective-permute-done.11.refs_1_ = bf16[8,32,2,512]{3,2,1,0:T(2,128)(2,1)S(1)} collective-permute-done((bf16[8,32,2,512]{3,2,1,0:T(2,128)(2,1)S(1)}, bf16[8,32,2,512]{3,2,1,0:T(2,128)(2,1)S(1)}, u32[]{:S(2)}, u32[]{:S(2)}) %collective-permute-start.11) | collective-permute-done | bytes 524320 | tf_op jit(solution)/shard_map/ppermute | solution.py:277
  (117 shorter events, 46.9 us)
Async XLA Ops:
  0.0 11.2 %copy-start = (bf16[512,512]{1,0:T(8,128)(2,1)S(1)}, bf16[512,512]{1,0:T(8,128)(2,1)}, u32[]{:S(2)}) copy-start(bf16[512,512]{1,0:T(8,128)(2,1)} %param.15) | copy-start | bytes 1572868
  0.0 7.4 %copy-start.26 = (f32[16,80]{1,0:T(8,128)S(1)}, f32[16,80]{1,0:T(8,128)}, u32[]{:S(2)}) copy-start(f32[16,80]{1,0:T(8,128)} %param.14) | copy-start | bytes 15364
  3.5 10.4 %collective-permute-start = (bf16[2,80,2,512]{3,2,1,0:T(2,128)(2,1)}, bf16[2,80,2,512]{3,2,1,0:T(2,128)(2,1)S(1)}, u32[]{:S(2)}, u32[]{:S(2)}) collective-permute-start(bf16[2,80,2,512]{3,2,1,0:T(2,128)(2,1)} %get-tuple-element.41), channel_id=1, source_target_pairs={{0,64},{32,96},{64,0},{96,32},{1,65},{33,97},{65,1},{97,33},{2,66}... | collective-permute-start | bytes 983048 | tf_op jit(solution)/shard_map/ppermute | solution.py:277
  3.9 21.7 %collective-permute-start.1 = (f32[3,1,8192]{2,1,0:T(1,128)S(1)}, f32[3,1,8192]{2,1,0:T(1,128)S(1)}, u32[]{:S(2)}, u32[]{:S(2)}) collective-permute-start(f32[3,1,8192]{2,1,0:T(1,128)S(1)} %pad_maximum_fusion.2), channel_id=1, source_target_pairs={{0,64},{32,96},{64,0},{96,32},{1,65},{33,97},{65,1},{97,33},{2,66}... | collective-permute-start | bytes 294920 | tf_op jit(solution)/shard_map/ppermute | solution.py:277
  14.6 23.7 %all-to-all-start = ((bf16[32,2,80,128]{3,2,1,0:T(8,128)(2,1)}), bf16[32,2,80,128]{3,2,1,0:T(8,128)(2,1)}, u32[]{:S(2)}, u32[]{:S(2)}) async-start(bf16[32,2,80,128]{3,2,1,0:T(8,128)(2,1)} %bitcast.10), calls=%async_computation | async-start | bytes 2621440 | tf_op jit(solution)/shard_map/all_to_all | solution.py:259
  25.8 15.3 %copy-start.24 = (bf16[64,64]{1,0:T(8,128)(2,1)S(1)}, bf16[64,64]{1,0:T(8,128)(2,1)}, u32[]{:S(2)}) copy-start(bf16[64,64]{1,0:T(8,128)(2,1)} %param.16) | copy-start | bytes 24580
  25.8 40.7 %collective-permute-start.3 = (bf16[6,80,2,512]{3,2,1,0:T(2,128)(2,1)}, bf16[6,80,2,512]{3,2,1,0:T(2,128)(2,1)S(1)}, u32[]{:S(2)}, u32[]{:S(2)}) collective-permute-start(bf16[6,80,2,512]{3,2,1,0:T(2,128)(2,1)} %get-tuple-element.52), channel_id=1, source_target_pairs={{0,64},{32,96},{64,0},{96,32},{1,65},{33,97},{65,1},{97,33},{2,66}... | collective-permute-start | bytes 2949128 | tf_op jit(solution)/shard_map/ppermute | solution.py:277
  26.4 64.8 %collective-permute-start.4 = (bf16[8,80,2,512]{3,2,1,0:T(2,128)(2,1)}, bf16[8,80,2,512]{3,2,1,0:T(2,128)(2,1)}, u32[]{:S(2)}, u32[]{:S(2)}) collective-permute-start(bf16[8,80,2,512]{3,2,1,0:T(2,128)(2,1)} %get-tuple-element.53), channel_id=1, source_target_pairs={{0,96},{32,64},{64,32},{96,0},{1,97},{33,65},{65,33},{97,1},{2,98}... | collective-permute-start | bytes 3932168 | tf_op jit(solution)/shard_map/ppermute | solution.py:277
  32.2 61.6 %collective-permute-start.2 = (bf16[8,80,2,512]{3,2,1,0:T(2,128)(2,1)}, bf16[8,80,2,512]{3,2,1,0:T(2,128)(2,1)}, u32[]{:S(2)}, u32[]{:S(2)}) collective-permute-start(bf16[8,80,2,512]{3,2,1,0:T(2,128)(2,1)} %get-tuple-element.50), channel_id=1, source_target_pairs={{0,32},{32,0},{64,96},{96,64},{1,33},{33,1},{65,97},{97,65},{2,34}... | collective-permute-start | bytes 3932168 | tf_op jit(solution)/shard_map/ppermute | solution.py:277
  44.0 56.2 %all-to-all-start.1 = ((bf16[32,2,80,128]{3,2,1,0:T(8,128)(2,1)}), bf16[32,2,80,128]{3,2,1,0:T(8,128)(2,1)}, u32[]{:S(2)}, u32[]{:S(2)}) async-start(bf16[32,2,80,128]{3,2,1,0:T(8,128)(2,1)} %bitcast.127), calls=%async_computation.1 | async-start | bytes 2621440 | tf_op jit(solution)/shard_map/all_to_all | solution.py:259
  50.9 15.5 %copy-start.20 = (bf16[2,80,2,512]{3,2,1,0:T(2,128)(2,1)S(1)}, bf16[2,80,2,512]{3,2,1,0:T(2,128)(2,1)}, u32[]{:S(2)}) copy-start(bf16[2,80,2,512]{3,2,1,0:T(2,128)(2,1)} %copy-done.19) | copy-start | bytes 983044
  105.3 17.6 %copy-start.6 = (f32[2,2,80,512]{3,2,1,0:T(8,128)S(1)}, f32[2,2,80,512]{3,2,1,0:T(8,128)}, u32[]{:S(2)}) copy-start(f32[2,2,80,512]{3,2,1,0:T(8,128)} %copy-done.5) | copy-start | bytes 1966084
  105.3 17.6 %copy-start.8 = (f32[2,2,80,512]{3,2,1,0:T(8,128)S(1)}, f32[2,2,80,512]{3,2,1,0:T(8,128)}, u32[]{:S(2)}) copy-start(f32[2,2,80,512]{3,2,1,0:T(8,128)} %copy-done.7) | copy-start | bytes 1966084
  105.4 6.7 %collective-permute-start.5 = (bf16[2,2,80,512]{3,2,1,0:T(8,128)(2,1)S(1)}, bf16[2,2,80,512]{3,2,1,0:T(8,128)(2,1)S(1)}, u32[]{:S(2)}, u32[]{:S(2)}) collective-permute-start(bf16[2,2,80,512]{3,2,1,0:T(8,128)(2,1)S(1)} %get-tuple-element.55), channel_id=1, source_target_pairs={{0,32},{32,0},{64,96},{96,64},{1,33},{33,1},{65,97},{97,65},{2,34}... | collective-permute-start | bytes 983048 | tf_op jit(solution)/shard_map/ppermute | solution.py:277
  112.1 10.7 %collective-permute-start.6 = (bf16[2,2,80,512]{3,2,1,0:T(8,128)(2,1)S(1)}, bf16[2,2,80,512]{3,2,1,0:T(8,128)(2,1)S(1)}, u32[]{:S(2)}, u32[]{:S(2)}) collective-permute-start(bf16[2,2,80,512]{3,2,1,0:T(8,128)(2,1)S(1)} %fusion.18), channel_id=1, source_target_pairs={{0,64},{32,96},{64,0},{96,32},{1,65},{33,97},{65,1},{97,33},{2,66}... | collective-permute-start | bytes 983048 | tf_op jit(solution)/shard_map/ppermute | solution.py:277
  123.3 2.5 %collective-permute-start.7 = (bf16[2,2,80,512]{3,2,1,0:T(8,128)(2,1)S(1)}, bf16[2,2,80,512]{3,2,1,0:T(8,128)(2,1)S(1)}, u32[]{:S(2)}, u32[]{:S(2)}) collective-permute-start(bf16[2,2,80,512]{3,2,1,0:T(8,128)(2,1)S(1)} %multiply_convert_fusion.3.own_ref), channel_id=1, source_target_pairs={{0,32},{32,0},{64,96},{96,64},{1,33},{33,1},{65,97},{97,65},{2,34}... | collective-permute-start | bytes 983048 | tf_op jit(solution)/shard_map/ppermute | solution.py:277
  153.9 14.4 %all-to-all-start.3 = ((bf16[32,2,32,128]{3,2,1,0:T(8,128)(2,1)}), bf16[32,2,32,128]{3,2,1,0:T(8,128)(2,1)S(1)}, u32[]{:S(2)}, u32[]{:S(2)}) async-start(bf16[32,2,32,128]{3,2,1,0:T(8,128)(2,1)} %bitcast.35), calls=%async_computation.3 | async-start | bytes 1048576 | tf_op jit(solution)/shard_map/all_to_all | solution.py:259
  169.1 7.8 %copy-start.10 = (bf16[8,80,2,512]{3,2,1,0:T(2,128)(2,1)S(1)}, bf16[8,80,2,512]{3,2,1,0:T(2,128)(2,1)}, u32[]{:S(2)}) copy-start(bf16[8,80,2,512]{3,2,1,0:T(2,128)(2,1)} %copy-done.9) | copy-start | bytes 3932164
  169.1 26.8 %all-to-all-start.4 = ((bf16[64,2,48,128]{3,2,1,0:T(8,128)(2,1)}), bf16[64,2,48,128]{3,2,1,0:T(8,128)(2,1)S(1)}, u32[]{:S(2)}, u32[]{:S(2)}) async-start(bf16[64,2,48,128]{3,2,1,0:T(8,128)(2,1)} %bitcast.42), calls=%async_computation.4 | async-start | bytes 3145728 | tf_op jit(solution)/shard_map/all_to_all | solution.py:266
  185.6 10.3 %copy-start.18 = (bf16[2,48,512]{2,1,0:T(8,128)(2,1)S(1)}, bf16[2,48,512]{2,1,0:T(8,128)(2,1)}, u32[]{:S(2)}) copy-start(bf16[2,48,512]{2,1,0:T(8,128)(2,1)} %slice.42) | copy-start | bytes 294916
  187.0 15.8 %collective-permute-start.8 = (bf16[8,32,2,512]{3,2,1,0:T(2,128)(2,1)S(1)}, bf16[8,32,2,512]{3,2,1,0:T(2,128)(2,1)S(1)}, u32[]{:S(2)}, u32[]{:S(2)}) collective-permute-start(bf16[8,32,2,512]{3,2,1,0:T(2,128)(2,1)S(1)} %fusion.17.refs_0_), channel_id=1, source_target_pairs={{0,64},{32,96},{64,0},{96,32},{1,65},{33,97},{65,1},{97,33},{2,66}... | collective-permute-start | bytes 1572872 | tf_op jit(solution)/shard_map/ppermute | solution.py:277
  202.8 18.2 %collective-permute-start.10 = (bf16[16,48,2,512]{3,2,1,0:T(2,128)(2,1)S(1)}, bf16[16,48,2,512]{3,2,1,0:T(2,128)(2,1)S(1)}, u32[]{:S(2)}, u32[]{:S(2)}) collective-permute-start(bf16[16,48,2,512]{3,2,1,0:T(2,128)(2,1)S(1)} %fusion.1.refs_3_), channel_id=1, source_target_pairs={{0,32},{32,0},{64,96},{96,64},{1,33},{33,1},{65,97},{97,65},{2,34}... | collective-permute-start | bytes 4718600 | tf_op jit(solution)/shard_map/ppermute | solution.py:277
  215.5 3.8 %collective-permute-start.11 = (bf16[8,32,2,512]{3,2,1,0:T(2,128)(2,1)S(1)}, bf16[8,32,2,512]{3,2,1,0:T(2,128)(2,1)S(1)}, u32[]{:S(2)}, u32[]{:S(2)}) collective-permute-start(bf16[8,32,2,512]{3,2,1,0:T(2,128)(2,1)S(1)} %fusion.17.refs_0_), channel_id=1, source_target_pairs={{0,32},{32,0},{64,96},{96,64},{1,33},{33,1},{65,97},{97,65},{2,34}... | collective-permute-start | bytes 1572872 | tf_op jit(solution)/shard_map/ppermute | solution.py:277
  215.6 5.4 %collective-permute-start.9 = (bf16[8,32,2,512]{3,2,1,0:T(2,128)(2,1)S(1)}, bf16[8,32,2,512]{3,2,1,0:T(2,128)(2,1)S(1)}, u32[]{:S(2)}, u32[]{:S(2)}) collective-permute-start(bf16[8,32,2,512]{3,2,1,0:T(2,128)(2,1)S(1)} %collective-permute-done.8.refs_2_), channel_id=1, source_target_pairs={{0,32},{32,0},{64,96},{96,64},{1,33},{33,1},{65,97},{97,65},{2,34}... | collective-permute-start | bytes 1572872 | tf_op jit(solution)/shard_map/ppermute | solution.py:277
  (20 other events, 39.1 us)

commit v9 on v7

--- a/solution.py
+++ b/solution.py
@@ -10,7 +10,7 @@
 from jax.sharding import PartitionSpec as P
 
 OBS_BLOCK = 1024
-LEVEL_CUT = 48
+LEVEL_CUT = 32
 EARLY_MEMBERS = 2
 
 
@@ -282,10 +282,9 @@
     perturbed = perturbations[0]
 
     early = EARLY_MEMBERS
-    order = ((2, 0, early), (2, early, own), (3, 0, own), (1, 0, own))
-    sent = pick(slot, order, perturbed)
+    sent = pick(slot, ((2, 0, early), (2, early, 2 * early)), perturbed)
     land_mask, tile_id, sent = lax.optimization_barrier((land_mask, tile_id, sent))
-    first = row_major(swap_slot(sent[0], 2))
+    first, second = [row_major(swap_slot(part, 2)) for part in sent]
 
     obs = jnp.stack([obs_cell.astype(jnp.float32), obs_value, obs_weight])
     obs = jnp.stack([obs, swap_slot(obs, 2)])
@@ -300,9 +299,11 @@
         jnp.bfloat16
     )
     along_x = along_x.reshape(own, row_count, levels, tiles, 128).transpose(0, 3, 1, 2, 4)
-    along_x, first, sent = lax.optimization_barrier((along_x, first, sent))
+    along_x, first, later = lax.optimization_barrier((along_x, first, perturbed))
+    order = ((2, 2 * early, own), (3, 0, own), (1, 0, own))
+    sent = pick(slot, order, later)
     rest, mates, near = [
-        row_major(swap_slot(part, k)) for part, (k, _, _) in zip(sent[1:], order[1:])
+        row_major(swap_slot(part, k)) for part, (k, _, _) in zip(sent, order)
     ]
     received = swap_columns(along_x)
     received = received.reshape(-1, levels, 128)
@@ -318,7 +319,7 @@
     pert = [
         lax.dynamic_slice_in_dim(perturbed, slot * own, own, 0),
         near,
-        jnp.concatenate([first, rest]),
+        jnp.concatenate([first, second, rest]),
         mates,
     ]
     pert = [p.transpose(0, 2, 1, 3) for p in pert]
@@ -340,9 +341,11 @@
     back_across = back_across.reshape(tile_shape)
     sea_half = sea.astype(jnp.bfloat16)
     bounds = ((0, LEVEL_CUT), (LEVEL_CUT, levels))
-    gradients = []
+    gradients, far = [], []
     for low, high in bounds:
         returned = swap_columns(back_across[:, :, :, low:high])
+        if gradients:
+            returned, gradients[0] = lax.optimization_barrier((returned, gradients[0]))
         returned = returned.transpose(0, 2, 3, 1, 4).reshape(own, row_count, -1, col_count)
         filtered = weight_mask[:, low:high] * lax.dot_general(
             returned * sea_half[:, low:high],
@@ -352,9 +355,10 @@
         )
         gradient = (mine[:, :, low:high].astype(jnp.float32) + filtered).astype(jnp.bfloat16)
         gradients.append(row_major(gradient.transpose(0, 2, 1, 3)))
+        far.append(row_major(swap_slot(gradients[-1], 2)))
 
     lows = [low for low, _ in bounds]
-    far = [row_major(swap_slot(g, 2)) for g in gradients]
+    gradients[1], far[0] = lax.optimization_barrier((gradients[1], far[0]))
     near = [row_major(swap_slot(g, 1)) for g in gradients]
     result = place(
         slot,

time: 220 us -> 220 us (level)
  starting transfers between devices: 61.8 us -> 51.6 us
  waiting for transfers between devices: 61.9 us -> 69.2 us
  local copies, waits for them, and re-layouts: 26.5 us -> 29.8 us
    ppermute x14 -> x15, starting transfers between devices: 34.3 us -> 23.3 us  [swap_slot(): return lax.ppermute(arr, 'slot', [(i, i ^ k) for i in range(4)])]
    ppermute x14 -> x15, waiting for transfers between devices: 43.7 us -> 53.4 us  [swap_slot(): return lax.ppermute(arr, 'slot', [(i, i ^ k) for i in range(4)])]
    all_to_all x4, waiting for transfers between devices: 18.3 us -> 15.8 us  [swap_columns(): lax.all_to_all(flat, 'horiz', split_axis=0, concat_axis=0, tiled=True)]
    pallas_call x1 -> x2, Pallas kernels: 3.4 us -> 4.98 us  [pick(): pl.pallas_call(functools.partial(pick_kernel, order), in_specs=[pl.BlockS...]
    unnamed x49 -> x55, local copies, waits for them, and re-layouts: 6.35 us -> 7.81 us
    another operation x3 -> x4, local copies, waits for them, and re-layouts: 5.44 us -> 5.39 us  [row_major(): return with_layout_constraint(arr, Layout(tuple(range(arr.ndim))))]
  transfers between devices with their start and end apart: 18 -> 19, of which waited for: 12 -> 12; matrix products, arithmetic and copies ran while one was open for 15% -> 15% of each run, Pallas kernels for 8% -> 9%
where the time goes in v9:
time: 220 us; the launch traced here: 216 us
  waiting for transfers between devices  69.2 us (31%)
  starting transfers between devices  51.6 us (23%)
  local copies, waits for them, and re-layouts  29.8 us (14%)
  Pallas kernels  28.2 us (13%)
  blocking collectives  22.9 us (10%)
  matrix products  8.05 us (4%)
  other arithmetic  5.67 us (3%)
    ppermute x15, waiting for transfers between devices, swap_slot(): return lax.ppermute(arr, 'slot', [(i, i ^ k) for i in range(4)])  53.4 us
    all_to_all x4, starting transfers between devices, swap_columns(): lax.all_to_all(flat, 'horiz', split_axis=0, concat_axis=0, tiled=True)  28.3 us
    ppermute x15, starting transfers between devices, swap_slot(): return lax.ppermute(arr, 'slot', [(i, i ^ k) for i in range(4)])  23.3 us
    all_to_all x1, blocking collectives, swap_columns(): lax.all_to_all(flat, 'horiz', split_axis=0, concat_axis=0, tiled=True)  22.9 us
    all_to_all x4, waiting for transfers between devices, swap_columns(): lax.all_to_all(flat, 'horiz', split_axis=0, concat_axis=0, tiled=True)  15.8 us
    pallas_call x1, Pallas kernels, obs_fields(): pl.pallas_call(obs_kernel, grid=(slots, count // OBS_BLOCK), in_specs=[pa...  14.7 us
    unnamed x55, local copies, waits for them, and re-layouts  7.81 us
    another operation x4, local copies, waits for them, and re-layouts, row_major(): return with_layout_constraint(arr, Layout(tuple(range(arr.ndim))))  5.39 us
  transfers between devices with their start and end apart: 19, of which 12 were waited for; matrix products, arithmetic and copies ran while one was open for 15% of the time, Pallas kernels for 9%

profile of v9, /device:TPU:37, one launch (start us, length us, event | category | flops | bytes accessed | tf_op | source)
XLA Modules:
  0.0 216.2 jit_solution(7817720741058285265)
XLA Ops:
  2.3 2.7 %collective-permute-start.3 = (bf16[2,80,2,512]{3,2,1,0:T(2,128)(2,1)}, bf16[2,80,2,512]{3,2,1,0:T(2,128)(2,1)S(1)}, u32[]{:S(2)}, u32[]{:S(2)}) collective-permute-start(bf16[2,80,2,512]{3,2,1,0:T(2,128)(2,1)} %get-tuple-element.43), channel_id=1, source_target_pairs={{0,64},{32,96},{64,0},{96,32},{1,65},{33,97},{65,1},{97,33},{2,66}... | collective-permute-start | bytes 983048 | tf_op jit(solution)/shard_map/ppermute | solution.py:256
  7.5 2.4 %constant_dynamic-slice_fusion.2 = bf16[8,80,2,512]{3,2,1,0:T(2,128)(2,1)S(1)} fusion(bf16[32,80,2,512]{3,2,1,0:T(2,128)(2,1)} %param.11, s32[]{:T(128)S(6)} %select_n.17), kind=kLoop, calls=%fused_computation.57 | loop fusion | bytes 2621444 | tf_op jit(solution)/shard_map/dynamic_slice | solution.py:296
  13.1 9.2 %all-to-all-start = ((bf16[32,2,80,128]{3,2,1,0:T(8,128)(2,1)}), bf16[32,2,80,128]{3,2,1,0:T(8,128)(2,1)}, u32[]{:S(2)}, u32[]{:S(2)}) async-start(bf16[32,2,80,128]{3,2,1,0:T(8,128)(2,1)} %bitcast.10), calls=%async_computation | async-start | bytes 2621440 | tf_op jit(solution)/shard_map/all_to_all | solution.py:252
  25.2 3.0 %shard_map.111 = (bf16[4,80,2,512]{3,2,1,0:T(2,128)(2,1)}, bf16[8,80,2,512]{3,2,1,0:T(2,128)(2,1)}, bf16[8,80,2,512]{3,2,1,0:T(2,128)(2,1)}) custom-call(s32[1]{0:T(128)} %bitcast.slot_ref, bf16[32,80,2,512]{3,2,1,0:T(2,128)(2,1)} %bitcast.116), custom_call_target="tpu_custom_call" | custom-call | bytes 7864320 | tf_op jit(solution)/shard_map/pallas_call | solution.py:202
  29.6 4.3 %collective-permute-start.5 = (bf16[8,80,2,512]{3,2,1,0:T(2,128)(2,1)}, bf16[8,80,2,512]{3,2,1,0:T(2,128)(2,1)}, u32[]{:S(2)}, u32[]{:S(2)}) collective-permute-start(bf16[8,80,2,512]{3,2,1,0:T(2,128)(2,1)} %get-tuple-element.45), channel_id=1, source_target_pairs={{0,96},{32,64},{64,32},{96,0},{1,97},{33,65},{65,33},{97,1},{2,98}... | collective-permute-start | bytes 3932168 | tf_op jit(solution)/shard_map/ppermute | solution.py:256
  33.9 4.3 %all-to-all-done = bf16[32,2,80,128]{3,2,1,0:T(8,128)(2,1)} async-done(((bf16[32,2,80,128]{3,2,1,0:T(8,128)(2,1)}), bf16[32,2,80,128]{3,2,1,0:T(8,128)(2,1)}, u32[]{:S(2)}, u32[]{:S(2)}) %all-to-all-start) | async-done | bytes 1310752 | tf_op jit(solution)/shard_map/all_to_all | solution.py:252
  38.1 2.8 %copy.78 = bf16[32,2,80,128]{3,1,0,2:T(2,128)(2,1)S(1)} copy(bf16[32,2,80,128]{3,2,1,0:T(8,128)(2,1)} %all-to-all-done) | data formatting | bytes 2621440 | tf_op jit(solution)/shard_map/all_to_all | solution.py:252
  43.8 7.6 %all-to-all-start.1 = ((bf16[32,2,80,128]{3,2,1,0:T(8,128)(2,1)}), bf16[32,2,80,128]{3,2,1,0:T(8,128)(2,1)}, u32[]{:S(2)}, u32[]{:S(2)}) async-start(bf16[32,2,80,128]{3,2,1,0:T(8,128)(2,1)} %bitcast.117), calls=%async_computation.1 | async-start | bytes 2621440 | tf_op jit(solution)/shard_map/all_to_all | solution.py:252
  51.4 14.7 %shard_map.110 = (f32[2,2,80,512]{3,2,1,0:T(8,128)S(1)}, f32[2,2,80,512]{3,2,1,0:T(8,128)S(1)}) custom-call(f32[2,3,1,8192]{3,2,1,0:T(1,128)S(1)} %pad_maximum_fusion.cell_ref.value_ref.weight_ref, f32[2,3,1,8192]{3,2,1,0:T(1,128)S(1)} %pad_maximum_fusion.cell_ref.value_ref.weight_ref, f32[2,3,1,8192]{3,2,1,0:T(1,128)S(1)} %pad_maximum_fusion.cell_ref.value_ref.weight_ref), custom_call_target="tpu_custom_call" | custom-call | flops 21474836480 | bytes 1310720 | tf_op jit(solution)/shard_map/pallas_call | solution.py:77
  67.4 15.7 %collective-permute-done.5 = bf16[8,80,2,512]{3,2,1,0:T(2,128)(2,1)} collective-permute-done((bf16[8,80,2,512]{3,2,1,0:T(2,128)(2,1)}, bf16[8,80,2,512]{3,2,1,0:T(2,128)(2,1)}, u32[]{:S(2)}, u32[]{:S(2)}) %collective-permute-start.5) | collective-permute-done | bytes 1310752 | tf_op jit(solution)/shard_map/ppermute | solution.py:256
  83.2 2.6 %copy.156 = bf16[8,80,2,512]{3,1,2,0:T(8,128)(2,1)} copy(bf16[8,80,2,512]{3,2,1,0:T(2,128)(2,1)} %collective-permute-done.5) | data formatting | bytes 2621440 | tf_op jit(solution)/shard_map/layout_constraint | solution.py:260
  85.8 2.6 %copy.157 = bf16[8,80,2,512]{3,1,2,0:T(8,128)(2,1)} copy(bf16[8,80,2,512]{3,2,1,0:T(2,128)(2,1)} %collective-permute-done.2) | data formatting | bytes 2621440 | tf_op jit(solution)/shard_map/layout_constraint | solution.py:260
  88.5 5.1 %all-to-all-done.1 = bf16[32,2,80,128]{3,2,1,0:T(8,128)(2,1)} async-done(((bf16[32,2,80,128]{3,2,1,0:T(8,128)(2,1)}), bf16[32,2,80,128]{3,2,1,0:T(8,128)(2,1)}, u32[]{:S(2)}, u32[]{:S(2)}) %all-to-all-start.1) | async-done | bytes 1310752 | tf_op jit(solution)/shard_map/all_to_all | solution.py:252
  96.2 2.6 %shard_map.112 = (f32[2,2,80,512]{3,2,1,0:T(8,128)S(1)}, bf16[2,2,80,512]{3,2,1,0:T(8,128)(2,1)S(1)}) custom-call(bf16[8,4,2,80,128]{4,3,2,1,0:T(8,128)(2,1)} %bitcast.17.spread_ref, bf16[8,2,80,512]{3,2,1,0:T(8,128)(2,1)S(1)} %bitcast.108, bf16[8,2,80,512]{3,2,1,0:T(8,128)(2,1)S(1)} %bitcast.112, bf16[8,2,80,512]{3,2,1,0:T(8,128)(2,1)S(1)} %maximum_bitcast_fusion.p2, ...), custom_call_target="tpu_custom_call" | custom-call | flops 5242880 | bytes 6553600 | tf_op jit(solution)/shard_map/pallas_call | solution.py:114
  98.8 4.4 %collective-permute-start.6 = (bf16[2,2,80,512]{3,2,1,0:T(8,128)(2,1)S(1)}, bf16[2,2,80,512]{3,2,1,0:T(8,128)(2,1)S(1)}, u32[]{:S(2)}, u32[]{:S(2)}) collective-permute-start(bf16[2,2,80,512]{3,2,1,0:T(8,128)(2,1)S(1)} %get-tuple-element.47), channel_id=1, source_target_pairs={{0,32},{32,0},{64,96},{96,64},{1,33},{33,1},{65,97},{97,65},{2,34}... | collective-permute-start | bytes 983048 | tf_op jit(solution)/shard_map/ppermute | solution.py:256
  105.9 9.4 %collective-permute-done.7 = bf16[2,2,80,512]{3,2,1,0:T(8,128)(2,1)S(1)} collective-permute-done((bf16[2,2,80,512]{3,2,1,0:T(8,128)(2,1)S(1)}, bf16[2,2,80,512]{3,2,1,0:T(8,128)(2,1)S(1)}, u32[]{:S(2)}, u32[]{:S(2)}) %collective-permute-start.7) | collective-permute-done | bytes 327712 | tf_op jit(solution)/shard_map/ppermute | solution.py:256
  120.6 22.9 %all_to_all.25 = bf16[32,2,80,128]{3,2,1,0:T(8,128)(2,1)S(1)} all-to-all(bf16[32,2,80,128]{3,2,1,0:T(8,128)(2,1)S(1)} %bitcast.114), channel_id=1, replica_groups=mesh['slot'=4,'horiz'=32] {'horiz'}, dimensions={0} | all-to-all | bytes 2621440 | tf_op jit(solution)/shard_map/all_to_all | solution.py:252
  147.4 5.7 %all-to-all-start.4 = ((bf16[32,2,32,128]{3,2,1,0:T(8,128)(2,1)}), bf16[32,2,32,128]{3,2,1,0:T(8,128)(2,1)}, u32[]{:S(2)}, u32[]{:S(2)}) async-start(bf16[32,2,32,128]{3,2,1,0:T(8,128)(2,1)} %bitcast.38), calls=%async_computation.4 | async-start | bytes 1048576 | tf_op jit(solution)/shard_map/all_to_all | solution.py:252
  161.5 5.7 %all-to-all-start.3 = ((bf16[32,2,48,128]{3,2,1,0:T(8,128)(2,1)}), bf16[32,2,48,128]{3,2,1,0:T(8,128)(2,1)}, u32[]{:S(2)}, u32[]{:S(2)}) async-start(bf16[32,2,48,128]{3,2,1,0:T(8,128)(2,1)} %bitcast.124), calls=%async_computation.3 | async-start | bytes 1572864 | tf_op jit(solution)/shard_map/all_to_all | solution.py:252
  172.3 4.4 %all-to-all-done.3 = bf16[32,2,48,128]{3,2,1,0:T(8,128)(2,1)} async-done(((bf16[32,2,48,128]{3,2,1,0:T(8,128)(2,1)}), bf16[32,2,48,128]{3,2,1,0:T(8,128)(2,1)}, u32[]{:S(2)}, u32[]{:S(2)}) %all-to-all-start.3) | async-done | bytes 786464 | tf_op jit(solution)/shard_map/all_to_all | solution.py:252
  180.6 6.0 %collective-permute-done.10.refs_0_ = bf16[8,32,2,512]{3,2,1,0:T(2,128)(2,1)S(1)} collective-permute-done((bf16[8,32,2,512]{3,2,1,0:T(2,128)(2,1)S(1)}, bf16[8,32,2,512]{3,2,1,0:T(2,128)(2,1)S(1)}, u32[]{:S(2)}, u32[]{:S(2)}) %collective-permute-start.10) | collective-permute-done | bytes 524320 | tf_op jit(solution)/shard_map/ppermute | solution.py:256
  186.6 3.2 %collective-permute-start.12 = (bf16[8,48,2,512]{3,2,1,0:T(2,128)(2,1)S(1)}, bf16[8,48,2,512]{3,2,1,0:T(2,128)(2,1)S(1)}, u32[]{:S(2)}, u32[]{:S(2)}) collective-permute-start(bf16[8,48,2,512]{3,2,1,0:T(2,128)(2,1)S(1)} %fusion.10.refs_1_), channel_id=1, source_target_pairs={{0,32},{32,0},{64,96},{96,64},{1,33},{33,1},{65,97},{97,65},{2,34}... | collective-permute-start | bytes 2359304 | tf_op jit(solution)/shard_map/ppermute | solution.py:256
  195.0 15.5 %collective-permute-done.9.refs_2_ = bf16[8,48,2,512]{3,2,1,0:T(2,128)(2,1)S(1)} collective-permute-done((bf16[8,48,2,512]{3,2,1,0:T(2,128)(2,1)S(1)}, bf16[8,48,2,512]{3,2,1,0:T(2,128)(2,1)S(1)}, u32[]{:S(2)}, u32[]{:S(2)}) %collective-permute-start.9) | collective-permute-done | bytes 786464 | tf_op jit(solution)/shard_map/ppermute | solution.py:256
  211.3 2.7 %collective-permute-done.14.refs_1_ = bf16[8,32,2,512]{3,2,1,0:T(2,128)(2,1)S(1)} collective-permute-done((bf16[8,32,2,512]{3,2,1,0:T(2,128)(2,1)S(1)}, bf16[8,32,2,512]{3,2,1,0:T(2,128)(2,1)S(1)}, u32[]{:S(2)}, u32[]{:S(2)}) %collective-permute-start.14) | collective-permute-done | bytes 524320 | tf_op jit(solution)/shard_map/ppermute | solution.py:256
  (126 shorter events, 55.9 us)
Async XLA Ops:
  0.0 10.0 %copy-start = (bf16[512,512]{1,0:T(8,128)(2,1)S(1)}, bf16[512,512]{1,0:T(8,128)(2,1)}, u32[]{:S(2)}) copy-start(bf16[512,512]{1,0:T(8,128)(2,1)} %param.15) | copy-start | bytes 1572868
  2.0 10.4 %collective-permute-start = (bf16[2,80,2,512]{3,2,1,0:T(2,128)(2,1)}, bf16[2,80,2,512]{3,2,1,0:T(2,128)(2,1)S(1)}, u32[]{:S(2)}, u32[]{:S(2)}) collective-permute-start(bf16[2,80,2,512]{3,2,1,0:T(2,128)(2,1)} %get-tuple-element.34), channel_id=1, source_target_pairs={{0,64},{32,96},{64,0},{96,32},{1,65},{33,97},{65,1},{97,33},{2,66}... | collective-permute-start | bytes 983048 | tf_op jit(solution)/shard_map/ppermute | solution.py:256
  2.3 63.9 %collective-permute-start.3 = (bf16[2,80,2,512]{3,2,1,0:T(2,128)(2,1)}, bf16[2,80,2,512]{3,2,1,0:T(2,128)(2,1)S(1)}, u32[]{:S(2)}, u32[]{:S(2)}) collective-permute-start(bf16[2,80,2,512]{3,2,1,0:T(2,128)(2,1)} %get-tuple-element.43), channel_id=1, source_target_pairs={{0,64},{32,96},{64,0},{96,32},{1,65},{33,97},{65,1},{97,33},{2,66}... | collective-permute-start | bytes 983048 | tf_op jit(solution)/shard_map/ppermute | solution.py:256
  5.2 19.9 %collective-permute-start.1 = (f32[3,1,8192]{2,1,0:T(1,128)S(1)}, f32[3,1,8192]{2,1,0:T(1,128)S(1)}, u32[]{:S(2)}, u32[]{:S(2)}) collective-permute-start(f32[3,1,8192]{2,1,0:T(1,128)S(1)} %pad_maximum_fusion.1), channel_id=1, source_target_pairs={{0,64},{32,96},{64,0},{96,32},{1,65},{33,97},{65,1},{97,33},{2,66}... | collective-permute-start | bytes 294920 | tf_op jit(solution)/shard_map/ppermute | solution.py:256
  13.1 25.0 %all-to-all-start = ((bf16[32,2,80,128]{3,2,1,0:T(8,128)(2,1)}), bf16[32,2,80,128]{3,2,1,0:T(8,128)(2,1)}, u32[]{:S(2)}, u32[]{:S(2)}) async-start(bf16[32,2,80,128]{3,2,1,0:T(8,128)(2,1)} %bitcast.10), calls=%async_computation | async-start | bytes 2621440 | tf_op jit(solution)/shard_map/all_to_all | solution.py:252
  28.3 37.9 %collective-permute-start.4 = (bf16[4,80,2,512]{3,2,1,0:T(2,128)(2,1)}, bf16[4,80,2,512]{3,2,1,0:T(2,128)(2,1)S(1)}, u32[]{:S(2)}, u32[]{:S(2)}) collective-permute-start(bf16[4,80,2,512]{3,2,1,0:T(2,128)(2,1)} %get-tuple-element.44), channel_id=1, source_target_pairs={{0,64},{32,96},{64,0},{96,32},{1,65},{33,97},{65,1},{97,33},{2,66}... | collective-permute-start | bytes 1966088 | tf_op jit(solution)/shard_map/ppermute | solution.py:256
  29.6 53.6 %collective-permute-start.5 = (bf16[8,80,2,512]{3,2,1,0:T(2,128)(2,1)}, bf16[8,80,2,512]{3,2,1,0:T(2,128)(2,1)}, u32[]{:S(2)}, u32[]{:S(2)}) collective-permute-start(bf16[8,80,2,512]{3,2,1,0:T(2,128)(2,1)} %get-tuple-element.45), channel_id=1, source_target_pairs={{0,96},{32,64},{64,32},{96,0},{1,97},{33,65},{65,33},{97,1},{2,98}... | collective-permute-start | bytes 3932168 | tf_op jit(solution)/shard_map/ppermute | solution.py:256
  33.9 52.0 %collective-permute-start.2 = (bf16[8,80,2,512]{3,2,1,0:T(2,128)(2,1)}, bf16[8,80,2,512]{3,2,1,0:T(2,128)(2,1)}, u32[]{:S(2)}, u32[]{:S(2)}) collective-permute-start(bf16[8,80,2,512]{3,2,1,0:T(2,128)(2,1)} %get-tuple-element.41), channel_id=1, source_target_pairs={{0,32},{32,0},{64,96},{96,64},{1,33},{33,1},{65,97},{97,65},{2,34}... | collective-permute-start | bytes 3932168 | tf_op jit(solution)/shard_map/ppermute | solution.py:256
  43.8 49.7 %all-to-all-start.1 = ((bf16[32,2,80,128]{3,2,1,0:T(8,128)(2,1)}), bf16[32,2,80,128]{3,2,1,0:T(8,128)(2,1)}, u32[]{:S(2)}, u32[]{:S(2)}) async-start(bf16[32,2,80,128]{3,2,1,0:T(8,128)(2,1)} %bitcast.117), calls=%async_computation.1 | async-start | bytes 2621440 | tf_op jit(solution)/shard_map/all_to_all | solution.py:252
  51.4 14.7 %copy-start.19 = (bf16[2,80,2,512]{3,2,1,0:T(2,128)(2,1)S(1)}, bf16[2,80,2,512]{3,2,1,0:T(2,128)(2,1)}, u32[]{:S(2)}) copy-start(bf16[2,80,2,512]{3,2,1,0:T(2,128)(2,1)} %copy-done.18) | copy-start | bytes 983044
  98.8 16.6 %copy-start.6 = (f32[2,2,80,512]{3,2,1,0:T(8,128)S(1)}, f32[2,2,80,512]{3,2,1,0:T(8,128)}, u32[]{:S(2)}) copy-start(f32[2,2,80,512]{3,2,1,0:T(8,128)} %copy-done.5) | copy-start | bytes 1966084
  98.8 16.6 %copy-start.8 = (f32[2,2,80,512]{3,2,1,0:T(8,128)S(1)}, f32[2,2,80,512]{3,2,1,0:T(8,128)}, u32[]{:S(2)}) copy-start(f32[2,2,80,512]{3,2,1,0:T(8,128)} %copy-done.7) | copy-start | bytes 1966084
  98.8 5.7 %collective-permute-start.6 = (bf16[2,2,80,512]{3,2,1,0:T(8,128)(2,1)S(1)}, bf16[2,2,80,512]{3,2,1,0:T(8,128)(2,1)S(1)}, u32[]{:S(2)}, u32[]{:S(2)}) collective-permute-start(bf16[2,2,80,512]{3,2,1,0:T(8,128)(2,1)S(1)} %get-tuple-element.47), channel_id=1, source_target_pairs={{0,32},{32,0},{64,96},{96,64},{1,33},{33,1},{65,97},{97,65},{2,34}... | collective-permute-start | bytes 983048 | tf_op jit(solution)/shard_map/ppermute | solution.py:256
  104.6 10.7 %collective-permute-start.7 = (bf16[2,2,80,512]{3,2,1,0:T(8,128)(2,1)S(1)}, bf16[2,2,80,512]{3,2,1,0:T(8,128)(2,1)S(1)}, u32[]{:S(2)}, u32[]{:S(2)}) collective-permute-start(bf16[2,2,80,512]{3,2,1,0:T(8,128)(2,1)S(1)} %fusion.17), channel_id=1, source_target_pairs={{0,64},{32,96},{64,0},{96,32},{1,65},{33,97},{65,1},{97,33},{2,66}... | collective-permute-start | bytes 983048 | tf_op jit(solution)/shard_map/ppermute | solution.py:256
  115.8 2.5 %collective-permute-start.8 = (bf16[2,2,80,512]{3,2,1,0:T(8,128)(2,1)S(1)}, bf16[2,2,80,512]{3,2,1,0:T(8,128)(2,1)S(1)}, u32[]{:S(2)}, u32[]{:S(2)}) collective-permute-start(bf16[2,2,80,512]{3,2,1,0:T(8,128)(2,1)S(1)} %multiply_convert_fusion.3.own_ref), channel_id=1, source_target_pairs={{0,32},{32,0},{64,96},{96,64},{1,33},{33,1},{65,97},{97,65},{2,34}... | collective-permute-start | bytes 983048 | tf_op jit(solution)/shard_map/ppermute | solution.py:256
  146.0 7.2 %copy-start.10 = (bf16[8,80,2,512]{3,2,1,0:T(2,128)(2,1)S(1)}, bf16[8,80,2,512]{3,2,1,0:T(2,128)(2,1)}, u32[]{:S(2)}) copy-start(bf16[8,80,2,512]{3,2,1,0:T(2,128)(2,1)} %copy-done.9) | copy-start | bytes 3932164
  147.4 14.1 %all-to-all-start.4 = ((bf16[32,2,32,128]{3,2,1,0:T(8,128)(2,1)}), bf16[32,2,32,128]{3,2,1,0:T(8,128)(2,1)}, u32[]{:S(2)}, u32[]{:S(2)}) async-start(bf16[32,2,32,128]{3,2,1,0:T(8,128)(2,1)} %bitcast.38), calls=%async_computation.4 | async-start | bytes 1048576 | tf_op jit(solution)/shard_map/all_to_all | solution.py:252
  161.5 15.2 %all-to-all-start.3 = ((bf16[32,2,48,128]{3,2,1,0:T(8,128)(2,1)}), bf16[32,2,48,128]{3,2,1,0:T(8,128)(2,1)}, u32[]{:S(2)}, u32[]{:S(2)}) async-start(bf16[32,2,48,128]{3,2,1,0:T(8,128)(2,1)} %bitcast.124), calls=%async_computation.3 | async-start | bytes 1572864 | tf_op jit(solution)/shard_map/all_to_all | solution.py:252
  171.0 15.6 %collective-permute-start.10 = (bf16[8,32,2,512]{3,2,1,0:T(2,128)(2,1)S(1)}, bf16[8,32,2,512]{3,2,1,0:T(2,128)(2,1)S(1)}, u32[]{:S(2)}, u32[]{:S(2)}) collective-permute-start(bf16[8,32,2,512]{3,2,1,0:T(2,128)(2,1)S(1)} %fusion.16.refs_0_), channel_id=1, source_target_pairs={{0,64},{32,96},{64,0},{96,32},{1,65},{33,97},{65,1},{97,33},{2,66}... | collective-permute-start | bytes 1572872 | tf_op jit(solution)/shard_map/ppermute | solution.py:256
  186.6 6.9 %collective-permute-start.12 = (bf16[8,48,2,512]{3,2,1,0:T(2,128)(2,1)S(1)}, bf16[8,48,2,512]{3,2,1,0:T(2,128)(2,1)S(1)}, u32[]{:S(2)}, u32[]{:S(2)}) collective-permute-start(bf16[8,48,2,512]{3,2,1,0:T(2,128)(2,1)S(1)} %fusion.10.refs_1_), channel_id=1, source_target_pairs={{0,32},{32,0},{64,96},{96,64},{1,33},{33,1},{65,97},{97,65},{2,34}... | collective-permute-start | bytes 2359304 | tf_op jit(solution)/shard_map/ppermute | solution.py:256
  189.8 20.7 %collective-permute-start.9 = (bf16[8,48,2,512]{3,2,1,0:T(2,128)(2,1)S(1)}, bf16[8,48,2,512]{3,2,1,0:T(2,128)(2,1)S(1)}, u32[]{:S(2)}, u32[]{:S(2)}) collective-permute-start(bf16[8,48,2,512]{3,2,1,0:T(2,128)(2,1)S(1)} %fusion.10.refs_1_), channel_id=1, source_target_pairs={{0,64},{32,96},{64,0},{96,32},{1,65},{33,97},{65,1},{97,33},{2,66}... | collective-permute-start | bytes 2359304 | tf_op jit(solution)/shard_map/ppermute | solution.py:256
  191.5 1.9 collective-permute-start.11
  210.5 4.7 %collective-permute-start.13 = (bf16[8,48,2,512]{3,2,1,0:T(2,128)(2,1)S(1)}, bf16[8,48,2,512]{3,2,1,0:T(2,128)(2,1)S(1)}, u32[]{:S(2)}, u32[]{:S(2)}) collective-permute-start(bf16[8,48,2,512]{3,2,1,0:T(2,128)(2,1)S(1)} %collective-permute-done.9.refs_2_), channel_id=1, source_target_pairs={{0,32},{32,0},{64,96},{96,64},{1,33},{33,1},{65,97},{97,65},{2,34}... | collective-permute-start | bytes 2359304 | tf_op jit(solution)/shard_map/ppermute | solution.py:256
  211.2 2.7 %collective-permute-start.14 = (bf16[8,32,2,512]{3,2,1,0:T(2,128)(2,1)S(1)}, bf16[8,32,2,512]{3,2,1,0:T(2,128)(2,1)S(1)}, u32[]{:S(2)}, u32[]{:S(2)}) collective-permute-start(bf16[8,32,2,512]{3,2,1,0:T(2,128)(2,1)S(1)} %collective-permute-done.10.refs_0_), channel_id=1, source_target_pairs={{0,32},{32,0},{64,96},{96,64},{1,33},{33,1},{65,97},{97,65},{2,34}... | collective-permute-start | bytes 1572872 | tf_op jit(solution)/shard_map/ppermute | solution.py:256
  (24 other events, 66.2 us)

commit v10 on v9

--- a/solution.py
+++ b/solution.py
@@ -10,7 +10,7 @@
 from jax.sharding import PartitionSpec as P
 
 OBS_BLOCK = 1024
-LEVEL_CUT = 32
+LEVEL_CUT = 48
 EARLY_MEMBERS = 2
 
 
@@ -341,11 +341,9 @@
     back_across = back_across.reshape(tile_shape)
     sea_half = sea.astype(jnp.bfloat16)
     bounds = ((0, LEVEL_CUT), (LEVEL_CUT, levels))
-    gradients, far = [], []
+    gradients = []
     for low, high in bounds:
         returned = swap_columns(back_across[:, :, :, low:high])
-        if gradients:
-            returned, gradients[0] = lax.optimization_barrier((returned, gradients[0]))
         returned = returned.transpose(0, 2, 3, 1, 4).reshape(own, row_count, -1, col_count)
         filtered = weight_mask[:, low:high] * lax.dot_general(
             returned * sea_half[:, low:high],
@@ -355,10 +353,9 @@
         )
         gradient = (mine[:, :, low:high].astype(jnp.float32) + filtered).astype(jnp.bfloat16)
         gradients.append(row_major(gradient.transpose(0, 2, 1, 3)))
-        far.append(row_major(swap_slot(gradients[-1], 2)))
 
     lows = [low for low, _ in bounds]
-    gradients[1], far[0] = lax.optimization_barrier((gradients[1], far[0]))
+    far = [row_major(swap_slot(g, 2)) for g in gradients]
     near = [row_major(swap_slot(g, 1)) for g in gradients]
     result = place(
         slot,

time: 220 us -> 213 us (0.968)
  waiting for transfers between devices: 69.2 us -> 52.7 us
  starting transfers between devices: 51.6 us -> 63 us
  local copies, waits for them, and re-layouts: 29.8 us -> 25.8 us
    ppermute x15, waiting for transfers between devices: 53.4 us -> 35.5 us  [swap_slot(): return lax.ppermute(arr, 'slot', [(i, i ^ k) for i in range(4)])]
    ppermute x15, starting transfers between devices: 23.3 us -> 34 us  [swap_slot(): return lax.ppermute(arr, 'slot', [(i, i ^ k) for i in range(4)])]
    unnamed x55 -> x49, local copies, waits for them, and re-layouts: 7.81 us -> 5.72 us
  transfers between devices with their start and end apart: 19 -> 19, of which waited for: 12 -> 11; matrix products, arithmetic and copies ran while one was open for 15% -> 15% of each run, Pallas kernels for 9% -> 10%
where the time goes in v10:
time: 213 us; the launch traced here: 209 us
  starting transfers between devices  63 us (30%)
  waiting for transfers between devices  52.7 us (25%)
  Pallas kernels  28.2 us (13%)
  local copies, waits for them, and re-layouts  25.8 us (12%)
  blocking collectives  22.9 us (11%)
  matrix products  8.12 us (4%)
  other arithmetic  7.84 us (4%)
    ppermute x15, waiting for transfers between devices, swap_slot(): return lax.ppermute(arr, 'slot', [(i, i ^ k) for i in range(4)])  35.5 us
    ppermute x15, starting transfers between devices, swap_slot(): return lax.ppermute(arr, 'slot', [(i, i ^ k) for i in range(4)])  34 us
    all_to_all x4, starting transfers between devices, swap_columns(): lax.all_to_all(flat, 'horiz', split_axis=0, concat_axis=0, tiled=True)  29 us
    all_to_all x1, blocking collectives, swap_columns(): lax.all_to_all(flat, 'horiz', split_axis=0, concat_axis=0, tiled=True)  22.9 us
    all_to_all x4, waiting for transfers between devices, swap_columns(): lax.all_to_all(flat, 'horiz', split_axis=0, concat_axis=0, tiled=True)  17.2 us
    pallas_call x1, Pallas kernels, obs_fields(): pl.pallas_call(obs_kernel, grid=(slots, count // OBS_BLOCK), in_specs=[pa...  14.7 us
    unnamed x49, local copies, waits for them, and re-layouts  5.72 us
    another operation x4, local copies, waits for them, and re-layouts, row_major(): return with_layout_constraint(arr, Layout(tuple(range(arr.ndim))))  5.39 us
  transfers between devices with their start and end apart: 19, of which 11 were waited for; matrix products, arithmetic and copies ran while one was open for 15% of the time, Pallas kernels for 10%

profile of v10, /device:TPU:37, one launch (start us, length us, event | category | flops | bytes accessed | tf_op | source)
XLA Modules:
  0.0 209.3 jit_solution(5212299089422388921)
XLA Ops:
  2.3 2.7 %collective-permute-start.3 = (bf16[2,80,2,512]{3,2,1,0:T(2,128)(2,1)}, bf16[2,80,2,512]{3,2,1,0:T(2,128)(2,1)S(1)}, u32[]{:S(2)}, u32[]{:S(2)}) collective-permute-start(bf16[2,80,2,512]{3,2,1,0:T(2,128)(2,1)} %get-tuple-element.39), channel_id=1, source_target_pairs={{0,64},{32,96},{64,0},{96,32},{1,65},{33,97},{65,1},{97,33},{2,66}... | collective-permute-start | bytes 983048 | tf_op jit(solution)/shard_map/ppermute | solution.py:256
  13.1 9.2 %all-to-all-start = ((bf16[32,2,80,128]{3,2,1,0:T(8,128)(2,1)}), bf16[32,2,80,128]{3,2,1,0:T(8,128)(2,1)}, u32[]{:S(2)}, u32[]{:S(2)}) async-start(bf16[32,2,80,128]{3,2,1,0:T(8,128)(2,1)} %bitcast.10), calls=%async_computation | async-start | bytes 2621440 | tf_op jit(solution)/shard_map/all_to_all | solution.py:252
  25.2 3.0 %shard_map.111 = (bf16[4,80,2,512]{3,2,1,0:T(2,128)(2,1)}, bf16[8,80,2,512]{3,2,1,0:T(2,128)(2,1)}, bf16[8,80,2,512]{3,2,1,0:T(2,128)(2,1)}) custom-call(s32[1]{0:T(128)} %bitcast.slot_ref, bf16[32,80,2,512]{3,2,1,0:T(2,128)(2,1)} %bitcast.114), custom_call_target="tpu_custom_call" | custom-call | bytes 7864320 | tf_op jit(solution)/shard_map/pallas_call | solution.py:202
  29.6 4.2 %collective-permute-start.5 = (bf16[8,80,2,512]{3,2,1,0:T(2,128)(2,1)}, bf16[8,80,2,512]{3,2,1,0:T(2,128)(2,1)}, u32[]{:S(2)}, u32[]{:S(2)}) collective-permute-start(bf16[8,80,2,512]{3,2,1,0:T(2,128)(2,1)} %get-tuple-element.41), channel_id=1, source_target_pairs={{0,96},{32,64},{64,32},{96,0},{1,97},{33,65},{65,33},{97,1},{2,98}... | collective-permute-start | bytes 3932168 | tf_op jit(solution)/shard_map/ppermute | solution.py:256
  33.8 4.3 %all-to-all-done = bf16[32,2,80,128]{3,2,1,0:T(8,128)(2,1)} async-done(((bf16[32,2,80,128]{3,2,1,0:T(8,128)(2,1)}), bf16[32,2,80,128]{3,2,1,0:T(8,128)(2,1)}, u32[]{:S(2)}, u32[]{:S(2)}) %all-to-all-start) | async-done | bytes 1310752 | tf_op jit(solution)/shard_map/all_to_all | solution.py:252
  38.1 2.8 %copy.78 = bf16[32,2,80,128]{3,1,0,2:T(2,128)(2,1)S(1)} copy(bf16[32,2,80,128]{3,2,1,0:T(8,128)(2,1)} %all-to-all-done) | data formatting | bytes 2621440 | tf_op jit(solution)/shard_map/all_to_all | solution.py:252
  43.8 7.6 %all-to-all-start.1 = ((bf16[32,2,80,128]{3,2,1,0:T(8,128)(2,1)}), bf16[32,2,80,128]{3,2,1,0:T(8,128)(2,1)}, u32[]{:S(2)}, u32[]{:S(2)}) async-start(bf16[32,2,80,128]{3,2,1,0:T(8,128)(2,1)} %bitcast.115), calls=%async_computation.1 | async-start | bytes 2621440 | tf_op jit(solution)/shard_map/all_to_all | solution.py:252
  51.4 14.7 %shard_map.110 = (f32[2,2,80,512]{3,2,1,0:T(8,128)S(1)}, f32[2,2,80,512]{3,2,1,0:T(8,128)S(1)}) custom-call(f32[2,3,1,8192]{3,2,1,0:T(1,128)S(1)} %pad_maximum_fusion.cell_ref.value_ref.weight_ref, f32[2,3,1,8192]{3,2,1,0:T(1,128)S(1)} %pad_maximum_fusion.cell_ref.value_ref.weight_ref, f32[2,3,1,8192]{3,2,1,0:T(1,128)S(1)} %pad_maximum_fusion.cell_ref.value_ref.weight_ref), custom_call_target="tpu_custom_call" | custom-call | flops 21474836480 | bytes 1310720 | tf_op jit(solution)/shard_map/pallas_call | solution.py:77
  67.4 15.7 %collective-permute-done.5 = bf16[8,80,2,512]{3,2,1,0:T(2,128)(2,1)} collective-permute-done((bf16[8,80,2,512]{3,2,1,0:T(2,128)(2,1)}, bf16[8,80,2,512]{3,2,1,0:T(2,128)(2,1)}, u32[]{:S(2)}, u32[]{:S(2)}) %collective-permute-start.5) | collective-permute-done | bytes 1310752 | tf_op jit(solution)/shard_map/ppermute | solution.py:256
  83.2 2.6 %copy.156 = bf16[8,80,2,512]{3,1,2,0:T(8,128)(2,1)} copy(bf16[8,80,2,512]{3,2,1,0:T(2,128)(2,1)} %collective-permute-done.5) | data formatting | bytes 2621440 | tf_op jit(solution)/shard_map/layout_constraint | solution.py:260
  85.8 2.6 %copy.157 = bf16[8,80,2,512]{3,1,2,0:T(8,128)(2,1)} copy(bf16[8,80,2,512]{3,2,1,0:T(2,128)(2,1)} %collective-permute-done.2) | data formatting | bytes 2621440 | tf_op jit(solution)/shard_map/layout_constraint | solution.py:260
  88.4 5.1 %all-to-all-done.1 = bf16[32,2,80,128]{3,2,1,0:T(8,128)(2,1)} async-done(((bf16[32,2,80,128]{3,2,1,0:T(8,128)(2,1)}), bf16[32,2,80,128]{3,2,1,0:T(8,128)(2,1)}, u32[]{:S(2)}, u32[]{:S(2)}) %all-to-all-start.1) | async-done | bytes 1310752 | tf_op jit(solution)/shard_map/all_to_all | solution.py:252
  98.8 4.4 %collective-permute-start.6 = (bf16[2,2,80,512]{3,2,1,0:T(8,128)(2,1)S(1)}, bf16[2,2,80,512]{3,2,1,0:T(8,128)(2,1)S(1)}, u32[]{:S(2)}, u32[]{:S(2)}) collective-permute-start(bf16[2,2,80,512]{3,2,1,0:T(8,128)(2,1)S(1)} %get-tuple-element.43), channel_id=1, source_target_pairs={{0,32},{32,0},{64,96},{96,64},{1,33},{33,1},{65,97},{97,65},{2,34}... | collective-permute-start | bytes 983048 | tf_op jit(solution)/shard_map/ppermute | solution.py:256
  105.9 9.3 %collective-permute-done.7 = bf16[2,2,80,512]{3,2,1,0:T(8,128)(2,1)S(1)} collective-permute-done((bf16[2,2,80,512]{3,2,1,0:T(8,128)(2,1)S(1)}, bf16[2,2,80,512]{3,2,1,0:T(8,128)(2,1)S(1)}, u32[]{:S(2)}, u32[]{:S(2)}) %collective-permute-start.7) | collective-permute-done | bytes 327712 | tf_op jit(solution)/shard_map/ppermute | solution.py:256
  120.6 22.9 %all_to_all.25 = bf16[32,2,80,128]{3,2,1,0:T(8,128)(2,1)S(1)} all-to-all(bf16[32,2,80,128]{3,2,1,0:T(8,128)(2,1)S(1)} %bitcast.112), channel_id=1, replica_groups=mesh['slot'=4,'horiz'=32] {'horiz'}, dimensions={0} | all-to-all | bytes 2621440 | tf_op jit(solution)/shard_map/all_to_all | solution.py:252
  146.9 5.9 %all-to-all-start.4 = ((bf16[32,2,48,128]{3,2,1,0:T(8,128)(2,1)}), bf16[32,2,48,128]{3,2,1,0:T(8,128)(2,1)}, u32[]{:S(2)}, u32[]{:S(2)}) async-start(bf16[32,2,48,128]{3,2,1,0:T(8,128)(2,1)} %bitcast.122), calls=%async_computation.4 | async-start | bytes 1572864 | tf_op jit(solution)/shard_map/all_to_all | solution.py:252
  158.4 4.9 %all-to-all-done.4 = bf16[32,2,48,128]{3,2,1,0:T(8,128)(2,1)} async-done(((bf16[32,2,48,128]{3,2,1,0:T(8,128)(2,1)}), bf16[32,2,48,128]{3,2,1,0:T(8,128)(2,1)}, u32[]{:S(2)}, u32[]{:S(2)}) %all-to-all-start.4) | async-done | bytes 786464 | tf_op jit(solution)/shard_map/all_to_all | solution.py:252
  163.3 6.3 %all-to-all-start.3 = ((bf16[32,2,32,128]{3,2,1,0:T(8,128)(2,1)}), bf16[32,2,32,128]{3,2,1,0:T(8,128)(2,1)}, u32[]{:S(2)}, u32[]{:S(2)}) async-start(bf16[32,2,32,128]{3,2,1,0:T(8,128)(2,1)} %bitcast.35), calls=%async_computation.3 | async-start | bytes 1048576 | tf_op jit(solution)/shard_map/all_to_all | solution.py:252
  174.9 3.0 %all-to-all-done.3 = bf16[32,2,32,128]{3,2,1,0:T(8,128)(2,1)} async-done(((bf16[32,2,32,128]{3,2,1,0:T(8,128)(2,1)}), bf16[32,2,32,128]{3,2,1,0:T(8,128)(2,1)}, u32[]{:S(2)}, u32[]{:S(2)}) %all-to-all-start.3) | async-done | bytes 524320 | tf_op jit(solution)/shard_map/all_to_all | solution.py:252
  179.4 4.4 %collective-permute-start.10 = (bf16[8,48,2,512]{3,2,1,0:T(2,128)(2,1)S(1)}, bf16[8,48,2,512]{3,2,1,0:T(2,128)(2,1)S(1)}, u32[]{:S(2)}, u32[]{:S(2)}) collective-permute-start(bf16[8,48,2,512]{3,2,1,0:T(2,128)(2,1)S(1)} %fusion.10.refs_0_), channel_id=1, source_target_pairs={{0,32},{32,0},{64,96},{96,64},{1,33},{33,1},{65,97},{97,65},{2,34}... | collective-permute-start | bytes 2359304 | tf_op jit(solution)/shard_map/ppermute | solution.py:256
  186.9 5.0 %collective-permute-done.13.refs_0_ = bf16[8,48,2,512]{3,2,1,0:T(2,128)(2,1)S(1)} collective-permute-done((bf16[8,48,2,512]{3,2,1,0:T(2,128)(2,1)S(1)}, bf16[8,48,2,512]{3,2,1,0:T(2,128)(2,1)S(1)}, u32[]{:S(2)}, u32[]{:S(2)}) %collective-permute-start.13) | collective-permute-done | bytes 786464 | tf_op jit(solution)/shard_map/ppermute | solution.py:256
  191.9 7.0 %collective-permute-start.14 = (bf16[8,48,2,512]{3,2,1,0:T(2,128)(2,1)S(1)}, bf16[8,48,2,512]{3,2,1,0:T(2,128)(2,1)S(1)}, u32[]{:S(2)}, u32[]{:S(2)}) collective-permute-start(bf16[8,48,2,512]{3,2,1,0:T(2,128)(2,1)S(1)} %collective-permute-done.13.refs_0_), channel_id=1, source_target_pairs={{0,32},{32,0},{64,96},{96,64},{1,33},{33,1},{65,97},{97,65},{2,34}... | collective-permute-start | bytes 2359304 | tf_op jit(solution)/shard_map/ppermute | solution.py:256
  200.4 2.7 %collective-permute-done.9.refs_2_ = bf16[8,32,2,512]{3,2,1,0:T(2,128)(2,1)S(1)} collective-permute-done((bf16[8,32,2,512]{3,2,1,0:T(2,128)(2,1)S(1)}, bf16[8,32,2,512]{3,2,1,0:T(2,128)(2,1)S(1)}, u32[]{:S(2)}, u32[]{:S(2)}) %collective-permute-start.9) | collective-permute-done | bytes 524320 | tf_op jit(solution)/shard_map/ppermute | solution.py:256
  203.1 3.7 %collective-permute-start.12 = (bf16[8,32,2,512]{3,2,1,0:T(2,128)(2,1)S(1)}, bf16[8,32,2,512]{3,2,1,0:T(2,128)(2,1)S(1)}, u32[]{:S(2)}, u32[]{:S(2)}) collective-permute-start(bf16[8,32,2,512]{3,2,1,0:T(2,128)(2,1)S(1)} %collective-permute-done.9.refs_2_), channel_id=1, source_target_pairs={{0,32},{32,0},{64,96},{96,64},{1,33},{33,1},{65,97},{97,65},{2,34}... | collective-permute-start | bytes 1572872 | tf_op jit(solution)/shard_map/ppermute | solution.py:256
  (120 shorter events, 54.5 us)
Async XLA Ops:
  0.0 10.0 %copy-start = (bf16[512,512]{1,0:T(8,128)(2,1)S(1)}, bf16[512,512]{1,0:T(8,128)(2,1)}, u32[]{:S(2)}) copy-start(bf16[512,512]{1,0:T(8,128)(2,1)} %param.15) | copy-start | bytes 1572868
  2.0 10.4 %collective-permute-start = (bf16[2,80,2,512]{3,2,1,0:T(2,128)(2,1)}, bf16[2,80,2,512]{3,2,1,0:T(2,128)(2,1)S(1)}, u32[]{:S(2)}, u32[]{:S(2)}) collective-permute-start(bf16[2,80,2,512]{3,2,1,0:T(2,128)(2,1)} %get-tuple-element.30), channel_id=1, source_target_pairs={{0,64},{32,96},{64,0},{96,32},{1,65},{33,97},{65,1},{97,33},{2,66}... | collective-permute-start | bytes 983048 | tf_op jit(solution)/shard_map/ppermute | solution.py:256
  2.3 63.9 %collective-permute-start.3 = (bf16[2,80,2,512]{3,2,1,0:T(2,128)(2,1)}, bf16[2,80,2,512]{3,2,1,0:T(2,128)(2,1)S(1)}, u32[]{:S(2)}, u32[]{:S(2)}) collective-permute-start(bf16[2,80,2,512]{3,2,1,0:T(2,128)(2,1)} %get-tuple-element.39), channel_id=1, source_target_pairs={{0,64},{32,96},{64,0},{96,32},{1,65},{33,97},{65,1},{97,33},{2,66}... | collective-permute-start | bytes 983048 | tf_op jit(solution)/shard_map/ppermute | solution.py:256
  5.2 19.9 %collective-permute-start.1 = (f32[3,1,8192]{2,1,0:T(1,128)S(1)}, f32[3,1,8192]{2,1,0:T(1,128)S(1)}, u32[]{:S(2)}, u32[]{:S(2)}) collective-permute-start(f32[3,1,8192]{2,1,0:T(1,128)S(1)} %pad_maximum_fusion.1), channel_id=1, source_target_pairs={{0,64},{32,96},{64,0},{96,32},{1,65},{33,97},{65,1},{97,33},{2,66}... | collective-permute-start | bytes 294920 | tf_op jit(solution)/shard_map/ppermute | solution.py:256
  13.1 25.0 %all-to-all-start = ((bf16[32,2,80,128]{3,2,1,0:T(8,128)(2,1)}), bf16[32,2,80,128]{3,2,1,0:T(8,128)(2,1)}, u32[]{:S(2)}, u32[]{:S(2)}) async-start(bf16[32,2,80,128]{3,2,1,0:T(8,128)(2,1)} %bitcast.10), calls=%async_computation | async-start | bytes 2621440 | tf_op jit(solution)/shard_map/all_to_all | solution.py:252
  28.3 37.9 %collective-permute-start.4 = (bf16[4,80,2,512]{3,2,1,0:T(2,128)(2,1)}, bf16[4,80,2,512]{3,2,1,0:T(2,128)(2,1)S(1)}, u32[]{:S(2)}, u32[]{:S(2)}) collective-permute-start(bf16[4,80,2,512]{3,2,1,0:T(2,128)(2,1)} %get-tuple-element.40), channel_id=1, source_target_pairs={{0,64},{32,96},{64,0},{96,32},{1,65},{33,97},{65,1},{97,33},{2,66}... | collective-permute-start | bytes 1966088 | tf_op jit(solution)/shard_map/ppermute | solution.py:256
  29.6 53.6 %collective-permute-start.5 = (bf16[8,80,2,512]{3,2,1,0:T(2,128)(2,1)}, bf16[8,80,2,512]{3,2,1,0:T(2,128)(2,1)}, u32[]{:S(2)}, u32[]{:S(2)}) collective-permute-start(bf16[8,80,2,512]{3,2,1,0:T(2,128)(2,1)} %get-tuple-element.41), channel_id=1, source_target_pairs={{0,96},{32,64},{64,32},{96,0},{1,97},{33,65},{65,33},{97,1},{2,98}... | collective-permute-start | bytes 3932168 | tf_op jit(solution)/shard_map/ppermute | solution.py:256
  33.8 52.0 %collective-permute-start.2 = (bf16[8,80,2,512]{3,2,1,0:T(2,128)(2,1)}, bf16[8,80,2,512]{3,2,1,0:T(2,128)(2,1)}, u32[]{:S(2)}, u32[]{:S(2)}) collective-permute-start(bf16[8,80,2,512]{3,2,1,0:T(2,128)(2,1)} %get-tuple-element.37), channel_id=1, source_target_pairs={{0,32},{32,0},{64,96},{96,64},{1,33},{33,1},{65,97},{97,65},{2,34}... | collective-permute-start | bytes 3932168 | tf_op jit(solution)/shard_map/ppermute | solution.py:256
  43.8 49.7 %all-to-all-start.1 = ((bf16[32,2,80,128]{3,2,1,0:T(8,128)(2,1)}), bf16[32,2,80,128]{3,2,1,0:T(8,128)(2,1)}, u32[]{:S(2)}, u32[]{:S(2)}) async-start(bf16[32,2,80,128]{3,2,1,0:T(8,128)(2,1)} %bitcast.115), calls=%async_computation.1 | async-start | bytes 2621440 | tf_op jit(solution)/shard_map/all_to_all | solution.py:252
  51.4 14.7 %copy-start.17 = (bf16[2,80,2,512]{3,2,1,0:T(2,128)(2,1)S(1)}, bf16[2,80,2,512]{3,2,1,0:T(2,128)(2,1)}, u32[]{:S(2)}) copy-start(bf16[2,80,2,512]{3,2,1,0:T(2,128)(2,1)} %copy-done.16) | copy-start | bytes 983044
  98.7 16.6 %copy-start.6 = (f32[2,2,80,512]{3,2,1,0:T(8,128)S(1)}, f32[2,2,80,512]{3,2,1,0:T(8,128)}, u32[]{:S(2)}) copy-start(f32[2,2,80,512]{3,2,1,0:T(8,128)} %copy-done.5) | copy-start | bytes 1966084
  98.7 16.6 %copy-start.8 = (f32[2,2,80,512]{3,2,1,0:T(8,128)S(1)}, f32[2,2,80,512]{3,2,1,0:T(8,128)}, u32[]{:S(2)}) copy-start(f32[2,2,80,512]{3,2,1,0:T(8,128)} %copy-done.7) | copy-start | bytes 1966084
  98.8 5.7 %collective-permute-start.6 = (bf16[2,2,80,512]{3,2,1,0:T(8,128)(2,1)S(1)}, bf16[2,2,80,512]{3,2,1,0:T(8,128)(2,1)S(1)}, u32[]{:S(2)}, u32[]{:S(2)}) collective-permute-start(bf16[2,2,80,512]{3,2,1,0:T(8,128)(2,1)S(1)} %get-tuple-element.43), channel_id=1, source_target_pairs={{0,32},{32,0},{64,96},{96,64},{1,33},{33,1},{65,97},{97,65},{2,34}... | collective-permute-start | bytes 983048 | tf_op jit(solution)/shard_map/ppermute | solution.py:256
  104.5 10.7 %collective-permute-start.7 = (bf16[2,2,80,512]{3,2,1,0:T(8,128)(2,1)S(1)}, bf16[2,2,80,512]{3,2,1,0:T(8,128)(2,1)S(1)}, u32[]{:S(2)}, u32[]{:S(2)}) collective-permute-start(bf16[2,2,80,512]{3,2,1,0:T(8,128)(2,1)S(1)} %fusion.17), channel_id=1, source_target_pairs={{0,64},{32,96},{64,0},{96,32},{1,65},{33,97},{65,1},{97,33},{2,66}... | collective-permute-start | bytes 983048 | tf_op jit(solution)/shard_map/ppermute | solution.py:256
  115.7 2.5 %collective-permute-start.8 = (bf16[2,2,80,512]{3,2,1,0:T(8,128)(2,1)S(1)}, bf16[2,2,80,512]{3,2,1,0:T(8,128)(2,1)S(1)}, u32[]{:S(2)}, u32[]{:S(2)}) collective-permute-start(bf16[2,2,80,512]{3,2,1,0:T(8,128)(2,1)S(1)} %multiply_convert_fusion.3.own_ref), channel_id=1, source_target_pairs={{0,32},{32,0},{64,96},{96,64},{1,33},{33,1},{65,97},{97,65},{2,34}... | collective-permute-start | bytes 983048 | tf_op jit(solution)/shard_map/ppermute | solution.py:256
  146.9 16.4 %all-to-all-start.4 = ((bf16[32,2,48,128]{3,2,1,0:T(8,128)(2,1)}), bf16[32,2,48,128]{3,2,1,0:T(8,128)(2,1)}, u32[]{:S(2)}, u32[]{:S(2)}) async-start(bf16[32,2,48,128]{3,2,1,0:T(8,128)(2,1)} %bitcast.122), calls=%async_computation.4 | async-start | bytes 1572864 | tf_op jit(solution)/shard_map/all_to_all | solution.py:252
  163.3 14.6 %all-to-all-start.3 = ((bf16[32,2,32,128]{3,2,1,0:T(8,128)(2,1)}), bf16[32,2,32,128]{3,2,1,0:T(8,128)(2,1)}, u32[]{:S(2)}, u32[]{:S(2)}) async-start(bf16[32,2,32,128]{3,2,1,0:T(8,128)(2,1)} %bitcast.35), calls=%async_computation.3 | async-start | bytes 1048576 | tf_op jit(solution)/shard_map/all_to_all | solution.py:252
  173.6 10.2 %copy-start.12 = (f32[8,2,32,512]{3,2,1,0:T(8,128)S(1)}, f32[8,2,32,512]{3,2,1,0:T(8,128)}, u32[]{:S(2)}) copy-start(f32[8,2,32,512]{3,2,1,0:T(8,128)} %slice_convert_fusion.1) | copy-start | bytes 3145732
  173.6 18.3 %collective-permute-start.13 = (bf16[8,48,2,512]{3,2,1,0:T(2,128)(2,1)S(1)}, bf16[8,48,2,512]{3,2,1,0:T(2,128)(2,1)S(1)}, u32[]{:S(2)}, u32[]{:S(2)}) collective-permute-start(bf16[8,48,2,512]{3,2,1,0:T(2,128)(2,1)S(1)} %fusion.10.refs_0_), channel_id=1, source_target_pairs={{0,64},{32,96},{64,0},{96,32},{1,65},{33,97},{65,1},{97,33},{2,66}... | collective-permute-start | bytes 2359304 | tf_op jit(solution)/shard_map/ppermute | solution.py:256
  179.4 19.5 %collective-permute-start.10 = (bf16[8,48,2,512]{3,2,1,0:T(2,128)(2,1)S(1)}, bf16[8,48,2,512]{3,2,1,0:T(2,128)(2,1)S(1)}, u32[]{:S(2)}, u32[]{:S(2)}) collective-permute-start(bf16[8,48,2,512]{3,2,1,0:T(2,128)(2,1)S(1)} %fusion.10.refs_0_), channel_id=1, source_target_pairs={{0,32},{32,0},{64,96},{96,64},{1,33},{33,1},{65,97},{97,65},{2,34}... | collective-permute-start | bytes 2359304 | tf_op jit(solution)/shard_map/ppermute | solution.py:256
  185.2 13.7 %collective-permute-start.11 = (bf16[8,32,2,512]{3,2,1,0:T(2,128)(2,1)S(1)}, bf16[8,32,2,512]{3,2,1,0:T(2,128)(2,1)S(1)}, u32[]{:S(2)}, u32[]{:S(2)}) collective-permute-start(bf16[8,32,2,512]{3,2,1,0:T(2,128)(2,1)S(1)} %fusion.16.refs_1_), channel_id=1, source_target_pairs={{0,32},{32,0},{64,96},{96,64},{1,33},{33,1},{65,97},{97,65},{2,34}... | collective-permute-start | bytes 1572872 | tf_op jit(solution)/shard_map/ppermute | solution.py:256
  185.3 17.9 %collective-permute-start.9 = (bf16[8,32,2,512]{3,2,1,0:T(2,128)(2,1)S(1)}, bf16[8,32,2,512]{3,2,1,0:T(2,128)(2,1)S(1)}, u32[]{:S(2)}, u32[]{:S(2)}) collective-permute-start(bf16[8,32,2,512]{3,2,1,0:T(2,128)(2,1)S(1)} %fusion.16.refs_1_), channel_id=1, source_target_pairs={{0,64},{32,96},{64,0},{96,32},{1,65},{33,97},{65,1},{97,33},{2,66}... | collective-permute-start | bytes 1572872 | tf_op jit(solution)/shard_map/ppermute | solution.py:256
  191.9 14.9 %collective-permute-start.14 = (bf16[8,48,2,512]{3,2,1,0:T(2,128)(2,1)S(1)}, bf16[8,48,2,512]{3,2,1,0:T(2,128)(2,1)S(1)}, u32[]{:S(2)}, u32[]{:S(2)}) collective-permute-start(bf16[8,48,2,512]{3,2,1,0:T(2,128)(2,1)S(1)} %collective-permute-done.13.refs_0_), channel_id=1, source_target_pairs={{0,32},{32,0},{64,96},{96,64},{1,33},{33,1},{65,97},{97,65},{2,34}... | collective-permute-start | bytes 2359304 | tf_op jit(solution)/shard_map/ppermute | solution.py:256
  203.1 5.2 %collective-permute-start.12 = (bf16[8,32,2,512]{3,2,1,0:T(2,128)(2,1)S(1)}, bf16[8,32,2,512]{3,2,1,0:T(2,128)(2,1)S(1)}, u32[]{:S(2)}, u32[]{:S(2)}) collective-permute-start(bf16[8,32,2,512]{3,2,1,0:T(2,128)(2,1)S(1)} %collective-permute-done.9.refs_2_), channel_id=1, source_target_pairs={{0,32},{32,0},{64,96},{96,64},{1,33},{33,1},{65,97},{97,65},{2,34}... | collective-permute-start | bytes 1572872 | tf_op jit(solution)/shard_map/ppermute | solution.py:256
  (21 other events, 59.4 us)

commit v11 on v8

--- a/solution.py
+++ b/solution.py
@@ -10,7 +10,7 @@
 from jax.sharding import PartitionSpec as P
 
 OBS_BLOCK = 1024
-LEVEL_CUT = 32
+LEVEL_CUT = 48
 EARLY_MEMBERS = 2
 
 
@@ -303,10 +303,9 @@
     perturbed = perturbations[0]
 
     early = EARLY_MEMBERS
-    order = ((2, 0, early), (2, early, own), (3, 0, own), (1, 0, own))
-    sent = pick(slot, order, perturbed)
+    sent = pick(slot, ((2, 0, early), (2, early, 2 * early)), perturbed)
     land_mask, tile_id, sent = lax.optimization_barrier((land_mask, tile_id, sent))
-    first = row_major(swap_slot(sent[0], 2))
+    first, second = [row_major(swap_slot(part, 2)) for part in sent]
 
     obs = jnp.stack([obs_cell.astype(jnp.float32), obs_value, obs_weight])
     obs = jnp.stack([obs, swap_slot(obs, 2)])
@@ -321,9 +320,11 @@
         jnp.bfloat16
     )
     along_x = along_x.reshape(own, row_count, levels, tiles, 128).transpose(0, 3, 1, 2, 4)
-    along_x, first, sent = lax.optimization_barrier((along_x, first, sent))
+    along_x, first, later = lax.optimization_barrier((along_x, first, perturbed))
+    order = ((2, 2 * early, own), (3, 0, own), (1, 0, own))
+    sent = pick(slot, order, later)
     rest, mates, near = [
-        row_major(swap_slot(part, k)) for part, (k, _, _) in zip(sent[1:], order[1:])
+        row_major(swap_slot(part, k)) for part, (k, _, _) in zip(sent, order)
     ]
     received = swap_columns(along_x)
     received = received.reshape(-1, levels, 128)
@@ -339,7 +340,7 @@
     pert = [
         lax.dynamic_slice_in_dim(perturbed, slot * own, own, 0),
         near,
-        jnp.concatenate([first, rest]),
+        jnp.concatenate([first, second, rest]),
         mates,
     ]
     pert = [p.transpose(0, 2, 1, 3) for p in pert]
@@ -351,7 +352,13 @@
     adjoint = ((weight_sum * increment - value_sum) * norm_scale).astype(jnp.bfloat16)
     back_first = slot_sums(sea, adjoint, swap_slot(adjoint, 1), pert)
 
-    received = swap_columns(back_first).reshape(-1, levels, 128)
+    cut = LEVEL_CUT
+    core = slot & 1
+    both_start = jnp.concatenate(
+        [lax.dynamic_slice_in_dim(control, (2 * i + core) * own, own, 0)[:, cut:] for i in range(2)]
+    ).transpose(0, 2, 1, 3)
+    received, both_start = lax.optimization_barrier((swap_columns(back_first), both_start))
+    received = received.reshape(-1, levels, 128)
     back_deep = jnp.einsum(
         "kwx,zw->kzx", received, inverse_z, preferred_element_type=jnp.float32
     ).astype(jnp.bfloat16)
@@ -371,17 +378,12 @@
         )
         return row_major((start.astype(jnp.float32) + filtered).astype(jnp.bfloat16).transpose(0, 2, 1, 3))
 
-    cut = LEVEL_CUT
     twice = jnp.stack([back_across[:, :, :, cut:]] * 2)
     blocks, twice = lax.optimization_barrier((swap_columns(back_across[:, :, :, :cut]), twice))
     own_part = finish(blocks, mine[:, :, :cut], 0, cut)
-    core = slot & 1
-    both_start = jnp.concatenate(
-        [lax.dynamic_slice_in_dim(control, (2 * i + core) * own, own, 0)[:, cut:] for i in range(2)]
-    ).transpose(0, 2, 1, 3)
     far = row_major(swap_slot(own_part, 2))
     near = row_major(swap_slot(own_part, 1))
-    blocks, own_part = lax.optimization_barrier((swap_to_both(twice), own_part))
+    blocks, own_part, near = lax.optimization_barrier((swap_to_both(twice), own_part, near))
     both_part = finish(blocks.reshape(2 * own, *blocks.shape[2:]), both_start, cut, levels)
 
     far, both_part = lax.optimization_barrier((far, both_part))

time: 224 us -> 219 us (0.978)
  blocking collectives: 22.9 us -> 0 us
  waiting for transfers between devices: 65.6 us -> 74.4 us
  starting transfers between devices: 59.4 us -> 67.6 us
  local copies, waits for them, and re-layouts: 32.5 us -> 29.2 us
  matrix products: 6.24 us -> 8.55 us
    all_to_all x1 -> x0, blocking collectives: 22.9 us -> none  [swap_columns(): lax.all_to_all(flat, 'horiz', split_axis=0, concat_axis=0, tiled=True)]
    all_to_all x3 -> x4, waiting for transfers between devices: 15.6 us -> 28.6 us  [swap_columns(): lax.all_to_all(flat, 'horiz', split_axis=0, concat_axis=0, tiled=True)]
    all_to_all x3 -> x4, starting transfers between devices: 21 us -> 29.5 us  [swap_columns(): lax.all_to_all(flat, 'horiz', split_axis=0, concat_axis=0, tiled=True)]
    convert_element_type x1 -> x0, other arithmetic: 3.38 us -> none  [finish(): (start.astype(jnp.float32) + filtered).astype(jnp.bfloat16)]
    transpose x1 -> x2, other arithmetic: 1.39 us -> 4.31 us  [finish(): (start.astype(jnp.float32) + filtered).astype(jnp.bfloat16)]
    all_to_all x1, waiting for transfers between devices: 8.47 us -> 5.7 us  [swap_to_both(): lax.all_to_all(flat, ('slot', 'horiz'), split_axis=0, concat_axis=0, axis...]
    transpose x0 -> x1, other arithmetic: none -> 2.33 us  [per_device(): both_start = jnp.concatenate([lax.dynamic_slice_in_dim(control, (2 * i +...]
    dot_general x2, matrix products: 1.49 us -> 3.79 us  [finish(): lax.dot_general(rows * sea_half[:, low:high], inverse_x, (((3,), (1,)), (...]
  transfers between devices with their start and end apart: 16 -> 18, of which waited for: 11 -> 13; matrix products, arithmetic and copies ran while one was open for 17% -> 17% of each run, Pallas kernels for 7% -> 9%
where the time goes in v11:
time: 219 us; the launch traced here: 218 us
  waiting for transfers between devices  74.4 us (34%)
  starting transfers between devices  67.6 us (31%)
  local copies, waits for them, and re-layouts  29.2 us (13%)
  Pallas kernels  27.6 us (13%)
  other arithmetic  9.77 us (4%)
  matrix products  8.55 us (4%)
    ppermute x13, waiting for transfers between devices, swap_slot(): return lax.ppermute(arr, 'slot', [(i, i ^ k) for i in range(4)])  40.1 us
    all_to_all x4, starting transfers between devices, swap_columns(): lax.all_to_all(flat, 'horiz', split_axis=0, concat_axis=0, tiled=True)  29.5 us
    ppermute x13, starting transfers between devices, swap_slot(): return lax.ppermute(arr, 'slot', [(i, i ^ k) for i in range(4)])  29.2 us
    all_to_all x4, waiting for transfers between devices, swap_columns(): lax.all_to_all(flat, 'horiz', split_axis=0, concat_axis=0, tiled=True)  28.6 us
    pallas_call x1, Pallas kernels, obs_fields(): pl.pallas_call(obs_kernel, grid=(slots, count // OBS_BLOCK), in_specs=[pa...  14.7 us
    all_to_all x1, starting transfers between devices, swap_to_both(): lax.all_to_all(flat, ('slot', 'horiz'), split_axis=0, concat_axis=0, axis...  8.92 us
    unnamed x52, local copies, waits for them, and re-layouts  7.36 us
    all_to_all x1, waiting for transfers between devices, swap_to_both(): lax.all_to_all(flat, ('slot', 'horiz'), split_axis=0, concat_axis=0, axis...  5.7 us
  transfers between devices with their start and end apart: 18, of which 13 were waited for; matrix products, arithmetic and copies ran while one was open for 17% of the time, Pallas kernels for 9%

profile of v11, /device:TPU:37, one launch (start us, length us, event | category | flops | bytes accessed | tf_op | source)
XLA Modules:
  0.0 217.8 jit_solution(8344419293355675310)
XLA Ops:
  2.3 2.7 %collective-permute-start.3 = (bf16[2,80,2,512]{3,2,1,0:T(2,128)(2,1)}, bf16[2,80,2,512]{3,2,1,0:T(2,128)(2,1)S(1)}, u32[]{:S(2)}, u32[]{:S(2)}) collective-permute-start(bf16[2,80,2,512]{3,2,1,0:T(2,128)(2,1)} %get-tuple-element.48), channel_id=1, source_target_pairs={{0,64},{32,96},{64,0},{96,32},{1,65},{33,97},{65,1},{97,33},{2,66}... | collective-permute-start | bytes 983048 | tf_op jit(solution)/shard_map/ppermute | solution.py:277
  7.5 2.4 %constant_dynamic-slice_fusion.4 = bf16[8,80,2,512]{3,2,1,0:T(2,128)(2,1)S(1)} fusion(bf16[32,80,2,512]{3,2,1,0:T(2,128)(2,1)} %param.11, s32[]{:T(128)S(6)} %select_n.23), kind=kLoop, calls=%fused_computation.61 | loop fusion | bytes 2621444 | tf_op jit(solution)/shard_map/dynamic_slice | solution.py:317
  13.1 9.2 %all-to-all-start = ((bf16[32,2,80,128]{3,2,1,0:T(8,128)(2,1)}), bf16[32,2,80,128]{3,2,1,0:T(8,128)(2,1)}, u32[]{:S(2)}, u32[]{:S(2)}) async-start(bf16[32,2,80,128]{3,2,1,0:T(8,128)(2,1)} %bitcast.10), calls=%async_computation | async-start | bytes 2621440 | tf_op jit(solution)/shard_map/all_to_all | solution.py:259
  25.2 3.0 %shard_map.111 = (bf16[4,80,2,512]{3,2,1,0:T(2,128)(2,1)}, bf16[8,80,2,512]{3,2,1,0:T(2,128)(2,1)}, bf16[8,80,2,512]{3,2,1,0:T(2,128)(2,1)}) custom-call(s32[1]{0:T(128)} %bitcast.slot_ref, bf16[32,80,2,512]{3,2,1,0:T(2,128)(2,1)} %bitcast.123), custom_call_target="tpu_custom_call" | custom-call | bytes 7864320 | tf_op jit(solution)/shard_map/pallas_call | solution.py:202
  29.6 4.3 %collective-permute-start.5 = (bf16[8,80,2,512]{3,2,1,0:T(2,128)(2,1)}, bf16[8,80,2,512]{3,2,1,0:T(2,128)(2,1)}, u32[]{:S(2)}, u32[]{:S(2)}) collective-permute-start(bf16[8,80,2,512]{3,2,1,0:T(2,128)(2,1)} %get-tuple-element.50), channel_id=1, source_target_pairs={{0,96},{32,64},{64,32},{96,0},{1,97},{33,65},{65,33},{97,1},{2,98}... | collective-permute-start | bytes 3932168 | tf_op jit(solution)/shard_map/ppermute | solution.py:277
  33.9 4.3 %all-to-all-done = bf16[32,2,80,128]{3,2,1,0:T(8,128)(2,1)} async-done(((bf16[32,2,80,128]{3,2,1,0:T(8,128)(2,1)}), bf16[32,2,80,128]{3,2,1,0:T(8,128)(2,1)}, u32[]{:S(2)}, u32[]{:S(2)}) %all-to-all-start) | async-done | bytes 1310752 | tf_op jit(solution)/shard_map/all_to_all | solution.py:259
  38.1 2.8 %copy.78 = bf16[32,2,80,128]{3,1,0,2:T(2,128)(2,1)S(1)} copy(bf16[32,2,80,128]{3,2,1,0:T(8,128)(2,1)} %all-to-all-done) | data formatting | bytes 2621440 | tf_op jit(solution)/shard_map/all_to_all | solution.py:259
  43.8 7.6 %all-to-all-start.1 = ((bf16[32,2,80,128]{3,2,1,0:T(8,128)(2,1)}), bf16[32,2,80,128]{3,2,1,0:T(8,128)(2,1)}, u32[]{:S(2)}, u32[]{:S(2)}) async-start(bf16[32,2,80,128]{3,2,1,0:T(8,128)(2,1)} %bitcast.125), calls=%async_computation.1 | async-start | bytes 2621440 | tf_op jit(solution)/shard_map/all_to_all | solution.py:259
  51.4 14.7 %shard_map.110 = (f32[2,2,80,512]{3,2,1,0:T(8,128)S(1)}, f32[2,2,80,512]{3,2,1,0:T(8,128)S(1)}) custom-call(f32[2,3,1,8192]{3,2,1,0:T(1,128)S(1)} %pad_maximum_fusion.1.cell_ref.value_ref.weight_ref, f32[2,3,1,8192]{3,2,1,0:T(1,128)S(1)} %pad_maximum_fusion.1.cell_ref.value_ref.weight_ref, f32[2,3,1,8192]{3,2,1,0:T(1,128)S(1)} %pad_maximum_fusion.1.cell_ref.value_ref.weight_ref), custom_call_target="tpu_custom_call" | custom-call | flops 21474836480 | bytes 1310720 | tf_op jit(solution)/shard_map/pallas_call | solution.py:77
  67.4 15.8 %collective-permute-done.5 = bf16[8,80,2,512]{3,2,1,0:T(2,128)(2,1)} collective-permute-done((bf16[8,80,2,512]{3,2,1,0:T(2,128)(2,1)}, bf16[8,80,2,512]{3,2,1,0:T(2,128)(2,1)}, u32[]{:S(2)}, u32[]{:S(2)}) %collective-permute-start.5) | collective-permute-done | bytes 1310752 | tf_op jit(solution)/shard_map/ppermute | solution.py:277
  83.2 2.6 %copy.154 = bf16[8,80,2,512]{3,1,2,0:T(8,128)(2,1)} copy(bf16[8,80,2,512]{3,2,1,0:T(2,128)(2,1)} %collective-permute-done.5) | data formatting | bytes 2621440 | tf_op jit(solution)/shard_map/layout_constraint | solution.py:281
  85.8 2.6 %copy.155 = bf16[8,80,2,512]{3,1,2,0:T(8,128)(2,1)} copy(bf16[8,80,2,512]{3,2,1,0:T(2,128)(2,1)} %collective-permute-done.2) | data formatting | bytes 2621440 | tf_op jit(solution)/shard_map/layout_constraint | solution.py:281
  88.5 5.1 %all-to-all-done.1 = bf16[32,2,80,128]{3,2,1,0:T(8,128)(2,1)} async-done(((bf16[32,2,80,128]{3,2,1,0:T(8,128)(2,1)}), bf16[32,2,80,128]{3,2,1,0:T(8,128)(2,1)}, u32[]{:S(2)}, u32[]{:S(2)}) %all-to-all-start.1) | async-done | bytes 1310752 | tf_op jit(solution)/shard_map/all_to_all | solution.py:259
  96.2 2.6 %shard_map.112 = (f32[2,2,80,512]{3,2,1,0:T(8,128)S(1)}, bf16[2,2,80,512]{3,2,1,0:T(8,128)(2,1)S(1)}) custom-call(bf16[8,4,2,80,128]{4,3,2,1,0:T(8,128)(2,1)} %bitcast.17.spread_ref, bf16[8,2,80,512]{3,2,1,0:T(8,128)(2,1)S(1)} %bitcast.115, bf16[8,2,80,512]{3,2,1,0:T(8,128)(2,1)S(1)} %bitcast.119, bf16[8,2,80,512]{3,2,1,0:T(8,128)(2,1)S(1)} %maximum_bitcast_fusion.p2, ...), custom_call_target="tpu_custom_call" | custom-call | flops 5242880 | bytes 6553600 | tf_op jit(solution)/shard_map/pallas_call | solution.py:114
  98.8 4.4 %collective-permute-start.6 = (bf16[2,2,80,512]{3,2,1,0:T(8,128)(2,1)S(1)}, bf16[2,2,80,512]{3,2,1,0:T(8,128)(2,1)S(1)}, u32[]{:S(2)}, u32[]{:S(2)}) collective-permute-start(bf16[2,2,80,512]{3,2,1,0:T(8,128)(2,1)S(1)} %get-tuple-element.52), channel_id=1, source_target_pairs={{0,32},{32,0},{64,96},{96,64},{1,33},{33,1},{65,97},{97,65},{2,34}... | collective-permute-start | bytes 983048 | tf_op jit(solution)/shard_map/ppermute | solution.py:277
  105.9 9.4 %collective-permute-done.7 = bf16[2,2,80,512]{3,2,1,0:T(8,128)(2,1)S(1)} collective-permute-done((bf16[2,2,80,512]{3,2,1,0:T(8,128)(2,1)S(1)}, bf16[2,2,80,512]{3,2,1,0:T(8,128)(2,1)S(1)}, u32[]{:S(2)}, u32[]{:S(2)}) %collective-permute-start.7) | collective-permute-done | bytes 327712 | tf_op jit(solution)/shard_map/ppermute | solution.py:277
  121.7 4.9 %all-to-all-start.2 = ((bf16[32,2,80,128]{3,2,1,0:T(8,128)(2,1)}), bf16[32,2,80,128]{3,2,1,0:T(8,128)(2,1)S(1)}, u32[]{:S(2)}, u32[]{:S(2)}) async-start(bf16[32,2,80,128]{3,2,1,0:T(8,128)(2,1)} %bitcast.121), calls=%async_computation.2 | async-start | bytes 2621440 | tf_op jit(solution)/shard_map/all_to_all | solution.py:259
  130.9 12.3 %all-to-all-done.2 = bf16[32,2,80,128]{3,2,1,0:T(8,128)(2,1)S(1)} async-done(((bf16[32,2,80,128]{3,2,1,0:T(8,128)(2,1)}), bf16[32,2,80,128]{3,2,1,0:T(8,128)(2,1)S(1)}, u32[]{:S(2)}, u32[]{:S(2)}) %all-to-all-start.2) | async-done | bytes 1310752 | tf_op jit(solution)/shard_map/all_to_all | solution.py:259
  146.8 7.8 %all-to-all-start.3 = ((bf16[32,2,48,128]{3,2,1,0:T(8,128)(2,1)}), bf16[32,2,48,128]{3,2,1,0:T(8,128)(2,1)}, u32[]{:S(2)}, u32[]{:S(2)}) async-start(bf16[32,2,48,128]{3,2,1,0:T(8,128)(2,1)} %bitcast.37), calls=%async_computation.3 | async-start | bytes 1572864 | tf_op jit(solution)/shard_map/all_to_all | solution.py:259
  159.1 6.9 %all-to-all-done.3 = bf16[32,2,48,128]{3,2,1,0:T(8,128)(2,1)} async-done(((bf16[32,2,48,128]{3,2,1,0:T(8,128)(2,1)}), bf16[32,2,48,128]{3,2,1,0:T(8,128)(2,1)}, u32[]{:S(2)}, u32[]{:S(2)}) %all-to-all-start.3) | async-done | bytes 786464 | tf_op jit(solution)/shard_map/all_to_all | solution.py:259
  166.0 8.9 %all-to-all-start.4 = ((bf16[64,2,32,128]{3,2,1,0:T(8,128)(2,1)}), bf16[64,2,32,128]{3,2,1,0:T(8,128)(2,1)}, u32[]{:S(2)}, u32[]{:S(2)}) async-start(bf16[64,2,32,128]{3,2,1,0:T(8,128)(2,1)} %bitcast.129), calls=%async_computation.4 | async-start | bytes 2097152 | tf_op jit(solution)/shard_map/all_to_all | solution.py:266
  183.1 5.7 %all-to-all-done.4 = bf16[64,2,32,128]{3,2,1,0:T(8,128)(2,1)} async-done(((bf16[64,2,32,128]{3,2,1,0:T(8,128)(2,1)}), bf16[64,2,32,128]{3,2,1,0:T(8,128)(2,1)}, u32[]{:S(2)}, u32[]{:S(2)}) %all-to-all-start.4) | async-done | bytes 1048608 | tf_op jit(solution)/shard_map/all_to_all | solution.py:266
  193.1 9.3 %collective-permute-done.9.refs_2_ = bf16[8,48,2,512]{3,2,1,0:T(2,128)(2,1)S(1)} collective-permute-done((bf16[8,48,2,512]{3,2,1,0:T(2,128)(2,1)S(1)}, bf16[8,48,2,512]{3,2,1,0:T(2,128)(2,1)S(1)}, u32[]{:S(2)}, u32[]{:S(2)}) %collective-permute-start.9) | collective-permute-done | bytes 786464 | tf_op jit(solution)/shard_map/ppermute | solution.py:277
  202.4 10.6 %collective-permute-start.12 = (bf16[16,32,2,512]{3,2,1,0:T(2,128)(2,1)S(1)}, bf16[16,32,2,512]{3,2,1,0:T(2,128)(2,1)S(1)}, u32[]{:S(2)}, u32[]{:S(2)}) collective-permute-start(bf16[16,32,2,512]{3,2,1,0:T(2,128)(2,1)S(1)} %fusion.11.refs_3_), channel_id=1, source_target_pairs={{0,32},{32,0},{64,96},{96,64},{1,33},{33,1},{65,97},{97,65},{2,34}... | collective-permute-start | bytes 3145736 | tf_op jit(solution)/shard_map/ppermute | solution.py:277
  (120 shorter events, 57.1 us)
Async XLA Ops:
  0.0 10.0 %copy-start = (bf16[512,512]{1,0:T(8,128)(2,1)S(1)}, bf16[512,512]{1,0:T(8,128)(2,1)}, u32[]{:S(2)}) copy-start(bf16[512,512]{1,0:T(8,128)(2,1)} %param.15) | copy-start | bytes 1572868
  2.0 10.4 %collective-permute-start = (bf16[2,80,2,512]{3,2,1,0:T(2,128)(2,1)}, bf16[2,80,2,512]{3,2,1,0:T(2,128)(2,1)S(1)}, u32[]{:S(2)}, u32[]{:S(2)}) collective-permute-start(bf16[2,80,2,512]{3,2,1,0:T(2,128)(2,1)} %get-tuple-element.39), channel_id=1, source_target_pairs={{0,64},{32,96},{64,0},{96,32},{1,65},{33,97},{65,1},{97,33},{2,66}... | collective-permute-start | bytes 983048 | tf_op jit(solution)/shard_map/ppermute | solution.py:277
  2.3 63.9 %collective-permute-start.3 = (bf16[2,80,2,512]{3,2,1,0:T(2,128)(2,1)}, bf16[2,80,2,512]{3,2,1,0:T(2,128)(2,1)S(1)}, u32[]{:S(2)}, u32[]{:S(2)}) collective-permute-start(bf16[2,80,2,512]{3,2,1,0:T(2,128)(2,1)} %get-tuple-element.48), channel_id=1, source_target_pairs={{0,64},{32,96},{64,0},{96,32},{1,65},{33,97},{65,1},{97,33},{2,66}... | collective-permute-start | bytes 983048 | tf_op jit(solution)/shard_map/ppermute | solution.py:277
  5.2 19.9 %collective-permute-start.1 = (f32[3,1,8192]{2,1,0:T(1,128)S(1)}, f32[3,1,8192]{2,1,0:T(1,128)S(1)}, u32[]{:S(2)}, u32[]{:S(2)}) collective-permute-start(f32[3,1,8192]{2,1,0:T(1,128)S(1)} %pad_maximum_fusion.2), channel_id=1, source_target_pairs={{0,64},{32,96},{64,0},{96,32},{1,65},{33,97},{65,1},{97,33},{2,66}... | collective-permute-start | bytes 294920 | tf_op jit(solution)/shard_map/ppermute | solution.py:277
  13.1 25.0 %all-to-all-start = ((bf16[32,2,80,128]{3,2,1,0:T(8,128)(2,1)}), bf16[32,2,80,128]{3,2,1,0:T(8,128)(2,1)}, u32[]{:S(2)}, u32[]{:S(2)}) async-start(bf16[32,2,80,128]{3,2,1,0:T(8,128)(2,1)} %bitcast.10), calls=%async_computation | async-start | bytes 2621440 | tf_op jit(solution)/shard_map/all_to_all | solution.py:259
  28.3 37.9 %collective-permute-start.4 = (bf16[4,80,2,512]{3,2,1,0:T(2,128)(2,1)}, bf16[4,80,2,512]{3,2,1,0:T(2,128)(2,1)S(1)}, u32[]{:S(2)}, u32[]{:S(2)}) collective-permute-start(bf16[4,80,2,512]{3,2,1,0:T(2,128)(2,1)} %get-tuple-element.49), channel_id=1, source_target_pairs={{0,64},{32,96},{64,0},{96,32},{1,65},{33,97},{65,1},{97,33},{2,66}... | collective-permute-start | bytes 1966088 | tf_op jit(solution)/shard_map/ppermute | solution.py:277
  29.6 53.6 %collective-permute-start.5 = (bf16[8,80,2,512]{3,2,1,0:T(2,128)(2,1)}, bf16[8,80,2,512]{3,2,1,0:T(2,128)(2,1)}, u32[]{:S(2)}, u32[]{:S(2)}) collective-permute-start(bf16[8,80,2,512]{3,2,1,0:T(2,128)(2,1)} %get-tuple-element.50), channel_id=1, source_target_pairs={{0,96},{32,64},{64,32},{96,0},{1,97},{33,65},{65,33},{97,1},{2,98}... | collective-permute-start | bytes 3932168 | tf_op jit(solution)/shard_map/ppermute | solution.py:277
  33.9 7.1 %copy-start.22 = (bf16[64,64]{1,0:T(8,128)(2,1)S(1)}, bf16[64,64]{1,0:T(8,128)(2,1)}, u32[]{:S(2)}) copy-start(bf16[64,64]{1,0:T(8,128)(2,1)} %param.16) | copy-start | bytes 24580
  33.9 52.0 %collective-permute-start.2 = (bf16[8,80,2,512]{3,2,1,0:T(2,128)(2,1)}, bf16[8,80,2,512]{3,2,1,0:T(2,128)(2,1)}, u32[]{:S(2)}, u32[]{:S(2)}) collective-permute-start(bf16[8,80,2,512]{3,2,1,0:T(2,128)(2,1)} %get-tuple-element.46), channel_id=1, source_target_pairs={{0,32},{32,0},{64,96},{96,64},{1,33},{33,1},{65,97},{97,65},{2,34}... | collective-permute-start | bytes 3932168 | tf_op jit(solution)/shard_map/ppermute | solution.py:277
  43.8 49.7 %all-to-all-start.1 = ((bf16[32,2,80,128]{3,2,1,0:T(8,128)(2,1)}), bf16[32,2,80,128]{3,2,1,0:T(8,128)(2,1)}, u32[]{:S(2)}, u32[]{:S(2)}) async-start(bf16[32,2,80,128]{3,2,1,0:T(8,128)(2,1)} %bitcast.125), calls=%async_computation.1 | async-start | bytes 2621440 | tf_op jit(solution)/shard_map/all_to_all | solution.py:259
  51.4 14.7 %copy-start.18 = (bf16[2,80,2,512]{3,2,1,0:T(2,128)(2,1)S(1)}, bf16[2,80,2,512]{3,2,1,0:T(2,128)(2,1)}, u32[]{:S(2)}) copy-start(bf16[2,80,2,512]{3,2,1,0:T(2,128)(2,1)} %copy-done.17) | copy-start | bytes 983044
  98.8 16.6 %copy-start.7 = (f32[2,2,80,512]{3,2,1,0:T(8,128)S(1)}, f32[2,2,80,512]{3,2,1,0:T(8,128)}, u32[]{:S(2)}) copy-start(f32[2,2,80,512]{3,2,1,0:T(8,128)} %copy-done.6) | copy-start | bytes 1966084
  98.8 16.6 %copy-start.9 = (f32[2,2,80,512]{3,2,1,0:T(8,128)S(1)}, f32[2,2,80,512]{3,2,1,0:T(8,128)}, u32[]{:S(2)}) copy-start(f32[2,2,80,512]{3,2,1,0:T(8,128)} %copy-done.8) | copy-start | bytes 1966084
  98.8 5.7 %collective-permute-start.6 = (bf16[2,2,80,512]{3,2,1,0:T(8,128)(2,1)S(1)}, bf16[2,2,80,512]{3,2,1,0:T(8,128)(2,1)S(1)}, u32[]{:S(2)}, u32[]{:S(2)}) collective-permute-start(bf16[2,2,80,512]{3,2,1,0:T(8,128)(2,1)S(1)} %get-tuple-element.52), channel_id=1, source_target_pairs={{0,32},{32,0},{64,96},{96,64},{1,33},{33,1},{65,97},{97,65},{2,34}... | collective-permute-start | bytes 983048 | tf_op jit(solution)/shard_map/ppermute | solution.py:277
  104.5 10.7 %collective-permute-start.7 = (bf16[2,2,80,512]{3,2,1,0:T(8,128)(2,1)S(1)}, bf16[2,2,80,512]{3,2,1,0:T(8,128)(2,1)S(1)}, u32[]{:S(2)}, u32[]{:S(2)}) collective-permute-start(bf16[2,2,80,512]{3,2,1,0:T(8,128)(2,1)S(1)} %fusion.19), channel_id=1, source_target_pairs={{0,64},{32,96},{64,0},{96,32},{1,65},{33,97},{65,1},{97,33},{2,66}... | collective-permute-start | bytes 983048 | tf_op jit(solution)/shard_map/ppermute | solution.py:277
  115.7 2.5 %collective-permute-start.8 = (bf16[2,2,80,512]{3,2,1,0:T(8,128)(2,1)S(1)}, bf16[2,2,80,512]{3,2,1,0:T(8,128)(2,1)S(1)}, u32[]{:S(2)}, u32[]{:S(2)}) collective-permute-start(bf16[2,2,80,512]{3,2,1,0:T(8,128)(2,1)S(1)} %multiply_convert_fusion.3.own_ref), channel_id=1, source_target_pairs={{0,32},{32,0},{64,96},{96,64},{1,33},{33,1},{65,97},{97,65},{2,34}... | collective-permute-start | bytes 983048 | tf_op jit(solution)/shard_map/ppermute | solution.py:277
  121.7 21.5 %all-to-all-start.2 = ((bf16[32,2,80,128]{3,2,1,0:T(8,128)(2,1)}), bf16[32,2,80,128]{3,2,1,0:T(8,128)(2,1)S(1)}, u32[]{:S(2)}, u32[]{:S(2)}) async-start(bf16[32,2,80,128]{3,2,1,0:T(8,128)(2,1)} %bitcast.121), calls=%async_computation.2 | async-start | bytes 2621440 | tf_op jit(solution)/shard_map/all_to_all | solution.py:259
  146.8 7.8 %copy-start.11 = (bf16[8,80,2,512]{3,2,1,0:T(2,128)(2,1)S(1)}, bf16[8,80,2,512]{3,2,1,0:T(2,128)(2,1)}, u32[]{:S(2)}) copy-start(bf16[8,80,2,512]{3,2,1,0:T(2,128)(2,1)} %copy-done.10) | copy-start | bytes 3932164
  146.8 19.3 %all-to-all-start.3 = ((bf16[32,2,48,128]{3,2,1,0:T(8,128)(2,1)}), bf16[32,2,48,128]{3,2,1,0:T(8,128)(2,1)}, u32[]{:S(2)}, u32[]{:S(2)}) async-start(bf16[32,2,48,128]{3,2,1,0:T(8,128)(2,1)} %bitcast.37), calls=%async_computation.3 | async-start | bytes 1572864 | tf_op jit(solution)/shard_map/all_to_all | solution.py:259
  166.0 22.7 %all-to-all-start.4 = ((bf16[64,2,32,128]{3,2,1,0:T(8,128)(2,1)}), bf16[64,2,32,128]{3,2,1,0:T(8,128)(2,1)}, u32[]{:S(2)}, u32[]{:S(2)}) async-start(bf16[64,2,32,128]{3,2,1,0:T(8,128)(2,1)} %bitcast.129), calls=%async_computation.4 | async-start | bytes 2097152 | tf_op jit(solution)/shard_map/all_to_all | solution.py:266
  178.8 4.3 %collective-permute-start.10 = (bf16[8,48,2,512]{3,2,1,0:T(2,128)(2,1)S(1)}, bf16[8,48,2,512]{3,2,1,0:T(2,128)(2,1)S(1)}, u32[]{:S(2)}, u32[]{:S(2)}) collective-permute-start(bf16[8,48,2,512]{3,2,1,0:T(2,128)(2,1)S(1)} %fusion.14.refs_0_), channel_id=1, source_target_pairs={{0,32},{32,0},{64,96},{96,64},{1,33},{33,1},{65,97},{97,65},{2,34}... | collective-permute-start | bytes 2359304 | tf_op jit(solution)/shard_map/ppermute | solution.py:277
  181.1 21.2 %collective-permute-start.9 = (bf16[8,48,2,512]{3,2,1,0:T(2,128)(2,1)S(1)}, bf16[8,48,2,512]{3,2,1,0:T(2,128)(2,1)S(1)}, u32[]{:S(2)}, u32[]{:S(2)}) collective-permute-start(bf16[8,48,2,512]{3,2,1,0:T(2,128)(2,1)S(1)} %fusion.14.refs_0_), channel_id=1, source_target_pairs={{0,64},{32,96},{64,0},{96,32},{1,65},{33,97},{65,1},{97,33},{2,66}... | collective-permute-start | bytes 2359304 | tf_op jit(solution)/shard_map/ppermute | solution.py:277
  202.4 12.9 %collective-permute-start.12 = (bf16[16,32,2,512]{3,2,1,0:T(2,128)(2,1)S(1)}, bf16[16,32,2,512]{3,2,1,0:T(2,128)(2,1)S(1)}, u32[]{:S(2)}, u32[]{:S(2)}) collective-permute-start(bf16[16,32,2,512]{3,2,1,0:T(2,128)(2,1)S(1)} %fusion.11.refs_3_), channel_id=1, source_target_pairs={{0,32},{32,0},{64,96},{96,64},{1,33},{33,1},{65,97},{97,65},{2,34}... | collective-permute-start | bytes 3145736 | tf_op jit(solution)/shard_map/ppermute | solution.py:277
  213.0 3.4 %collective-permute-start.11 = (bf16[8,48,2,512]{3,2,1,0:T(2,128)(2,1)S(1)}, bf16[8,48,2,512]{3,2,1,0:T(2,128)(2,1)S(1)}, u32[]{:S(2)}, u32[]{:S(2)}) collective-permute-start(bf16[8,48,2,512]{3,2,1,0:T(2,128)(2,1)S(1)} %collective-permute-done.9.refs_2_), channel_id=1, source_target_pairs={{0,32},{32,0},{64,96},{96,64},{1,33},{33,1},{65,97},{97,65},{2,34}... | collective-permute-start | bytes 2359304 | tf_op jit(solution)/shard_map/ppermute | solution.py:277
  (21 other events, 53.8 us)

commit v12 on v10

--- a/solution.py
+++ b/solution.py
@@ -10,7 +10,7 @@
 from jax.sharding import PartitionSpec as P
 
 OBS_BLOCK = 1024
-LEVEL_CUT = 48
+LEVEL_CUT = 40
 EARLY_MEMBERS = 2
 
 
@@ -356,6 +356,7 @@
 
     lows = [low for low, _ in bounds]
     far = [row_major(swap_slot(g, 2)) for g in gradients]
+    gradients = list(lax.optimization_barrier(tuple(gradients)))
     near = [row_major(swap_slot(g, 1)) for g in gradients]
     result = place(
         slot,

time: 213 us -> 214 us (level)
  waiting for transfers between devices: 52.7 us -> 55.7 us
    ppermute x15, waiting for transfers between devices: 35.5 us -> 37.9 us  [swap_slot(): return lax.ppermute(arr, 'slot', [(i, i ^ k) for i in range(4)])]
    ppermute x15, starting transfers between devices: 34 us -> 31.8 us  [swap_slot(): return lax.ppermute(arr, 'slot', [(i, i ^ k) for i in range(4)])]
    slice x4 -> x3, local copies, waits for them, and re-layouts: 4.29 us -> 5.14 us  [per_device(): returned = swap_columns(back_across[:, :, :, low:high])]
    unnamed x49 -> x51, local copies, waits for them, and re-layouts: 5.72 us -> 5.8 us
where the time goes in v12:
time: 214 us; the launch traced here: 210 us
  starting transfers between devices  60.9 us (28%)
  waiting for transfers between devices  55.7 us (26%)
  Pallas kernels  28.2 us (13%)
  local copies, waits for them, and re-layouts  26.7 us (12%)
  blocking collectives  22.9 us (11%)
  matrix products  8.13 us (4%)
  other arithmetic  6.77 us (3%)
    ppermute x15, waiting for transfers between devices, swap_slot(): return lax.ppermute(arr, 'slot', [(i, i ^ k) for i in range(4)])  37.9 us
    ppermute x15, starting transfers between devices, swap_slot(): return lax.ppermute(arr, 'slot', [(i, i ^ k) for i in range(4)])  31.8 us
    all_to_all x4, starting transfers between devices, swap_columns(): lax.all_to_all(flat, 'horiz', split_axis=0, concat_axis=0, tiled=True)  29.1 us
    all_to_all x1, blocking collectives, swap_columns(): lax.all_to_all(flat, 'horiz', split_axis=0, concat_axis=0, tiled=True)  22.9 us
    all_to_all x4, waiting for transfers between devices, swap_columns(): lax.all_to_all(flat, 'horiz', split_axis=0, concat_axis=0, tiled=True)  17.8 us
    pallas_call x1, Pallas kernels, obs_fields(): pl.pallas_call(obs_kernel, grid=(slots, count // OBS_BLOCK), in_specs=[pa...  14.7 us
    unnamed x51, local copies, waits for them, and re-layouts  5.8 us
    another operation x4, local copies, waits for them, and re-layouts, row_major(): return with_layout_constraint(arr, Layout(tuple(range(arr.ndim))))  5.4 us
  transfers between devices with their start and end apart: 19, of which 11 were waited for; matrix products, arithmetic and copies ran while one was open for 15% of the time, Pallas kernels for 10%

profile of v12, /device:TPU:37, one launch (start us, length us, event | category | flops | bytes accessed | tf_op | source)
XLA Modules:
  0.0 210.0 jit_solution(8202431391455465052)
XLA Ops:
  2.3 2.7 %collective-permute-start.3 = (bf16[2,80,2,512]{3,2,1,0:T(2,128)(2,1)}, bf16[2,80,2,512]{3,2,1,0:T(2,128)(2,1)S(1)}, u32[]{:S(2)}, u32[]{:S(2)}) collective-permute-start(bf16[2,80,2,512]{3,2,1,0:T(2,128)(2,1)} %get-tuple-element.41), channel_id=1, source_target_pairs={{0,64},{32,96},{64,0},{96,32},{1,65},{33,97},{65,1},{97,33},{2,66}... | collective-permute-start | bytes 983048 | tf_op jit(solution)/shard_map/ppermute | solution.py:256
  13.1 9.2 %all-to-all-start = ((bf16[32,2,80,128]{3,2,1,0:T(8,128)(2,1)}), bf16[32,2,80,128]{3,2,1,0:T(8,128)(2,1)}, u32[]{:S(2)}, u32[]{:S(2)}) async-start(bf16[32,2,80,128]{3,2,1,0:T(8,128)(2,1)} %bitcast.10), calls=%async_computation | async-start | bytes 2621440 | tf_op jit(solution)/shard_map/all_to_all | solution.py:252
  25.2 3.1 %shard_map.111 = (bf16[4,80,2,512]{3,2,1,0:T(2,128)(2,1)}, bf16[8,80,2,512]{3,2,1,0:T(2,128)(2,1)}, bf16[8,80,2,512]{3,2,1,0:T(2,128)(2,1)}) custom-call(s32[1]{0:T(128)} %bitcast.slot_ref, bf16[32,80,2,512]{3,2,1,0:T(2,128)(2,1)} %bitcast.114), custom_call_target="tpu_custom_call" | custom-call | bytes 7864320 | tf_op jit(solution)/shard_map/pallas_call | solution.py:202
  29.6 4.2 %collective-permute-start.5 = (bf16[8,80,2,512]{3,2,1,0:T(2,128)(2,1)}, bf16[8,80,2,512]{3,2,1,0:T(2,128)(2,1)}, u32[]{:S(2)}, u32[]{:S(2)}) collective-permute-start(bf16[8,80,2,512]{3,2,1,0:T(2,128)(2,1)} %get-tuple-element.43), channel_id=1, source_target_pairs={{0,96},{32,64},{64,32},{96,0},{1,97},{33,65},{65,33},{97,1},{2,98}... | collective-permute-start | bytes 3932168 | tf_op jit(solution)/shard_map/ppermute | solution.py:256
  33.9 4.2 %all-to-all-done = bf16[32,2,80,128]{3,2,1,0:T(8,128)(2,1)} async-done(((bf16[32,2,80,128]{3,2,1,0:T(8,128)(2,1)}), bf16[32,2,80,128]{3,2,1,0:T(8,128)(2,1)}, u32[]{:S(2)}, u32[]{:S(2)}) %all-to-all-start) | async-done | bytes 1310752 | tf_op jit(solution)/shard_map/all_to_all | solution.py:252
  38.1 2.8 %copy.78 = bf16[32,2,80,128]{3,1,0,2:T(2,128)(2,1)S(1)} copy(bf16[32,2,80,128]{3,2,1,0:T(8,128)(2,1)} %all-to-all-done) | data formatting | bytes 2621440 | tf_op jit(solution)/shard_map/all_to_all | solution.py:252
  43.8 7.6 %all-to-all-start.1 = ((bf16[32,2,80,128]{3,2,1,0:T(8,128)(2,1)}), bf16[32,2,80,128]{3,2,1,0:T(8,128)(2,1)}, u32[]{:S(2)}, u32[]{:S(2)}) async-start(bf16[32,2,80,128]{3,2,1,0:T(8,128)(2,1)} %bitcast.115), calls=%async_computation.1 | async-start | bytes 2621440 | tf_op jit(solution)/shard_map/all_to_all | solution.py:252
  51.4 14.7 %shard_map.110 = (f32[2,2,80,512]{3,2,1,0:T(8,128)S(1)}, f32[2,2,80,512]{3,2,1,0:T(8,128)S(1)}) custom-call(f32[2,3,1,8192]{3,2,1,0:T(1,128)S(1)} %pad_maximum_fusion.cell_ref.value_ref.weight_ref, f32[2,3,1,8192]{3,2,1,0:T(1,128)S(1)} %pad_maximum_fusion.cell_ref.value_ref.weight_ref, f32[2,3,1,8192]{3,2,1,0:T(1,128)S(1)} %pad_maximum_fusion.cell_ref.value_ref.weight_ref), custom_call_target="tpu_custom_call" | custom-call | flops 21474836480 | bytes 1310720 | tf_op jit(solution)/shard_map/pallas_call | solution.py:77
  67.5 15.7 %collective-permute-done.5 = bf16[8,80,2,512]{3,2,1,0:T(2,128)(2,1)} collective-permute-done((bf16[8,80,2,512]{3,2,1,0:T(2,128)(2,1)}, bf16[8,80,2,512]{3,2,1,0:T(2,128)(2,1)}, u32[]{:S(2)}, u32[]{:S(2)}) %collective-permute-start.5) | collective-permute-done | bytes 1310752 | tf_op jit(solution)/shard_map/ppermute | solution.py:256
  83.2 2.6 %copy.156 = bf16[8,80,2,512]{3,1,2,0:T(8,128)(2,1)} copy(bf16[8,80,2,512]{3,2,1,0:T(2,128)(2,1)} %collective-permute-done.5) | data formatting | bytes 2621440 | tf_op jit(solution)/shard_map/layout_constraint | solution.py:260
  85.8 2.6 %copy.157 = bf16[8,80,2,512]{3,1,2,0:T(8,128)(2,1)} copy(bf16[8,80,2,512]{3,2,1,0:T(2,128)(2,1)} %collective-permute-done.2) | data formatting | bytes 2621440 | tf_op jit(solution)/shard_map/layout_constraint | solution.py:260
  88.5 5.0 %all-to-all-done.1 = bf16[32,2,80,128]{3,2,1,0:T(8,128)(2,1)} async-done(((bf16[32,2,80,128]{3,2,1,0:T(8,128)(2,1)}), bf16[32,2,80,128]{3,2,1,0:T(8,128)(2,1)}, u32[]{:S(2)}, u32[]{:S(2)}) %all-to-all-start.1) | async-done | bytes 1310752 | tf_op jit(solution)/shard_map/all_to_all | solution.py:252
  98.7 4.4 %collective-permute-start.6 = (bf16[2,2,80,512]{3,2,1,0:T(8,128)(2,1)S(1)}, bf16[2,2,80,512]{3,2,1,0:T(8,128)(2,1)S(1)}, u32[]{:S(2)}, u32[]{:S(2)}) collective-permute-start(bf16[2,2,80,512]{3,2,1,0:T(8,128)(2,1)S(1)} %get-tuple-element.45), channel_id=1, source_target_pairs={{0,32},{32,0},{64,96},{96,64},{1,33},{33,1},{65,97},{97,65},{2,34}... | collective-permute-start | bytes 983048 | tf_op jit(solution)/shard_map/ppermute | solution.py:256
  105.9 9.3 %collective-permute-done.7 = bf16[2,2,80,512]{3,2,1,0:T(8,128)(2,1)S(1)} collective-permute-done((bf16[2,2,80,512]{3,2,1,0:T(8,128)(2,1)S(1)}, bf16[2,2,80,512]{3,2,1,0:T(8,128)(2,1)S(1)}, u32[]{:S(2)}, u32[]{:S(2)}) %collective-permute-start.7) | collective-permute-done | bytes 327712 | tf_op jit(solution)/shard_map/ppermute | solution.py:256
  120.6 22.9 %all_to_all.25 = bf16[32,2,80,128]{3,2,1,0:T(8,128)(2,1)S(1)} all-to-all(bf16[32,2,80,128]{3,2,1,0:T(8,128)(2,1)S(1)} %bitcast.112), channel_id=1, replica_groups=mesh['slot'=4,'horiz'=32] {'horiz'}, dimensions={0} | all-to-all | bytes 2621440 | tf_op jit(solution)/shard_map/all_to_all | solution.py:252
  148.0 5.7 %all-to-all-start.4 = ((bf16[32,2,40,128]{3,2,1,0:T(8,128)(2,1)}), bf16[32,2,40,128]{3,2,1,0:T(8,128)(2,1)}, u32[]{:S(2)}, u32[]{:S(2)}) async-start(bf16[32,2,40,128]{3,2,1,0:T(8,128)(2,1)} %bitcast.40), calls=%async_computation.4 | async-start | bytes 1310720 | tf_op jit(solution)/shard_map/all_to_all | solution.py:252
  157.8 4.9 %all-to-all-done.4 = bf16[32,2,40,128]{3,2,1,0:T(8,128)(2,1)} async-done(((bf16[32,2,40,128]{3,2,1,0:T(8,128)(2,1)}), bf16[32,2,40,128]{3,2,1,0:T(8,128)(2,1)}, u32[]{:S(2)}, u32[]{:S(2)}) %all-to-all-start.4) | async-done | bytes 655392 | tf_op jit(solution)/shard_map/all_to_all | solution.py:252
  162.7 6.5 %all-to-all-start.3 = ((bf16[32,2,40,128]{3,2,1,0:T(8,128)(2,1)}), bf16[32,2,40,128]{3,2,1,0:T(8,128)(2,1)}, u32[]{:S(2)}, u32[]{:S(2)}) async-start(bf16[32,2,40,128]{3,2,1,0:T(8,128)(2,1)} %bitcast.35), calls=%async_computation.3 | async-start | bytes 1310720 | tf_op jit(solution)/shard_map/all_to_all | solution.py:252
  174.6 3.6 %all-to-all-done.3 = bf16[32,2,40,128]{3,2,1,0:T(8,128)(2,1)} async-done(((bf16[32,2,40,128]{3,2,1,0:T(8,128)(2,1)}), bf16[32,2,40,128]{3,2,1,0:T(8,128)(2,1)}, u32[]{:S(2)}, u32[]{:S(2)}) %all-to-all-start.3) | async-done | bytes 655392 | tf_op jit(solution)/shard_map/all_to_all | solution.py:252
  181.6 4.2 %collective-permute-start.10 = (bf16[8,40,2,512]{3,2,1,0:T(2,128)(2,1)S(1)}, bf16[8,40,2,512]{3,2,1,0:T(2,128)(2,1)S(1)}, u32[]{:S(2)}, u32[]{:S(2)}) collective-permute-start(bf16[8,40,2,512]{3,2,1,0:T(2,128)(2,1)S(1)} %fusion.13.refs_0_), channel_id=1, source_target_pairs={{0,32},{32,0},{64,96},{96,64},{1,33},{33,1},{65,97},{97,65},{2,34}... | collective-permute-start | bytes 1966088 | tf_op jit(solution)/shard_map/ppermute | solution.py:256
  187.8 2.7 %collective-permute-done.13.refs_0_ = bf16[8,40,2,512]{3,2,1,0:T(2,128)(2,1)S(1)} collective-permute-done((bf16[8,40,2,512]{3,2,1,0:T(2,128)(2,1)S(1)}, bf16[8,40,2,512]{3,2,1,0:T(2,128)(2,1)S(1)}, u32[]{:S(2)}, u32[]{:S(2)}) %collective-permute-start.13) | collective-permute-done | bytes 655392 | tf_op jit(solution)/shard_map/ppermute | solution.py:256
  190.4 5.2 %collective-permute-start.14 = (bf16[8,40,2,512]{3,2,1,0:T(2,128)(2,1)S(1)}, bf16[8,40,2,512]{3,2,1,0:T(2,128)(2,1)S(1)}, u32[]{:S(2)}, u32[]{:S(2)}) collective-permute-start(bf16[8,40,2,512]{3,2,1,0:T(2,128)(2,1)S(1)} %collective-permute-done.13.refs_0_), channel_id=1, source_target_pairs={{0,32},{32,0},{64,96},{96,64},{1,33},{33,1},{65,97},{97,65},{2,34}... | collective-permute-start | bytes 1966088 | tf_op jit(solution)/shard_map/ppermute | solution.py:256
  197.2 7.3 %collective-permute-done.9.refs_2_ = bf16[8,40,2,512]{3,2,1,0:T(2,128)(2,1)S(1)} collective-permute-done((bf16[8,40,2,512]{3,2,1,0:T(2,128)(2,1)S(1)}, bf16[8,40,2,512]{3,2,1,0:T(2,128)(2,1)S(1)}, u32[]{:S(2)}, u32[]{:S(2)}) %collective-permute-start.9) | collective-permute-done | bytes 655392 | tf_op jit(solution)/shard_map/ppermute | solution.py:256
  204.5 2.8 %collective-permute-start.12 = (bf16[8,40,2,512]{3,2,1,0:T(2,128)(2,1)S(1)}, bf16[8,40,2,512]{3,2,1,0:T(2,128)(2,1)S(1)}, u32[]{:S(2)}, u32[]{:S(2)}) collective-permute-start(bf16[8,40,2,512]{3,2,1,0:T(2,128)(2,1)S(1)} %collective-permute-done.9.refs_2_), channel_id=1, source_target_pairs={{0,32},{32,0},{64,96},{96,64},{1,33},{33,1},{65,97},{97,65},{2,34}... | collective-permute-start | bytes 1966088 | tf_op jit(solution)/shard_map/ppermute | solution.py:256
  (116 shorter events, 55.1 us)
Async XLA Ops:
  0.0 10.0 %copy-start = (bf16[512,512]{1,0:T(8,128)(2,1)S(1)}, bf16[512,512]{1,0:T(8,128)(2,1)}, u32[]{:S(2)}) copy-start(bf16[512,512]{1,0:T(8,128)(2,1)} %param.15) | copy-start | bytes 1572868
  2.0 10.4 %collective-permute-start = (bf16[2,80,2,512]{3,2,1,0:T(2,128)(2,1)}, bf16[2,80,2,512]{3,2,1,0:T(2,128)(2,1)S(1)}, u32[]{:S(2)}, u32[]{:S(2)}) collective-permute-start(bf16[2,80,2,512]{3,2,1,0:T(2,128)(2,1)} %get-tuple-element.32), channel_id=1, source_target_pairs={{0,64},{32,96},{64,0},{96,32},{1,65},{33,97},{65,1},{97,33},{2,66}... | collective-permute-start | bytes 983048 | tf_op jit(solution)/shard_map/ppermute | solution.py:256
  2.3 63.9 %collective-permute-start.3 = (bf16[2,80,2,512]{3,2,1,0:T(2,128)(2,1)}, bf16[2,80,2,512]{3,2,1,0:T(2,128)(2,1)S(1)}, u32[]{:S(2)}, u32[]{:S(2)}) collective-permute-start(bf16[2,80,2,512]{3,2,1,0:T(2,128)(2,1)} %get-tuple-element.41), channel_id=1, source_target_pairs={{0,64},{32,96},{64,0},{96,32},{1,65},{33,97},{65,1},{97,33},{2,66}... | collective-permute-start | bytes 983048 | tf_op jit(solution)/shard_map/ppermute | solution.py:256
  5.2 19.9 %collective-permute-start.1 = (f32[3,1,8192]{2,1,0:T(1,128)S(1)}, f32[3,1,8192]{2,1,0:T(1,128)S(1)}, u32[]{:S(2)}, u32[]{:S(2)}) collective-permute-start(f32[3,1,8192]{2,1,0:T(1,128)S(1)} %pad_maximum_fusion.1), channel_id=1, source_target_pairs={{0,64},{32,96},{64,0},{96,32},{1,65},{33,97},{65,1},{97,33},{2,66}... | collective-permute-start | bytes 294920 | tf_op jit(solution)/shard_map/ppermute | solution.py:256
  13.1 25.0 %all-to-all-start = ((bf16[32,2,80,128]{3,2,1,0:T(8,128)(2,1)}), bf16[32,2,80,128]{3,2,1,0:T(8,128)(2,1)}, u32[]{:S(2)}, u32[]{:S(2)}) async-start(bf16[32,2,80,128]{3,2,1,0:T(8,128)(2,1)} %bitcast.10), calls=%async_computation | async-start | bytes 2621440 | tf_op jit(solution)/shard_map/all_to_all | solution.py:252
  28.3 37.9 %collective-permute-start.4 = (bf16[4,80,2,512]{3,2,1,0:T(2,128)(2,1)}, bf16[4,80,2,512]{3,2,1,0:T(2,128)(2,1)S(1)}, u32[]{:S(2)}, u32[]{:S(2)}) collective-permute-start(bf16[4,80,2,512]{3,2,1,0:T(2,128)(2,1)} %get-tuple-element.42), channel_id=1, source_target_pairs={{0,64},{32,96},{64,0},{96,32},{1,65},{33,97},{65,1},{97,33},{2,66}... | collective-permute-start | bytes 1966088 | tf_op jit(solution)/shard_map/ppermute | solution.py:256
  29.6 53.6 %collective-permute-start.5 = (bf16[8,80,2,512]{3,2,1,0:T(2,128)(2,1)}, bf16[8,80,2,512]{3,2,1,0:T(2,128)(2,1)}, u32[]{:S(2)}, u32[]{:S(2)}) collective-permute-start(bf16[8,80,2,512]{3,2,1,0:T(2,128)(2,1)} %get-tuple-element.43), channel_id=1, source_target_pairs={{0,96},{32,64},{64,32},{96,0},{1,97},{33,65},{65,33},{97,1},{2,98}... | collective-permute-start | bytes 3932168 | tf_op jit(solution)/shard_map/ppermute | solution.py:256
  33.9 52.0 %collective-permute-start.2 = (bf16[8,80,2,512]{3,2,1,0:T(2,128)(2,1)}, bf16[8,80,2,512]{3,2,1,0:T(2,128)(2,1)}, u32[]{:S(2)}, u32[]{:S(2)}) collective-permute-start(bf16[8,80,2,512]{3,2,1,0:T(2,128)(2,1)} %get-tuple-element.39), channel_id=1, source_target_pairs={{0,32},{32,0},{64,96},{96,64},{1,33},{33,1},{65,97},{97,65},{2,34}... | collective-permute-start | bytes 3932168 | tf_op jit(solution)/shard_map/ppermute | solution.py:256
  43.8 49.7 %all-to-all-start.1 = ((bf16[32,2,80,128]{3,2,1,0:T(8,128)(2,1)}), bf16[32,2,80,128]{3,2,1,0:T(8,128)(2,1)}, u32[]{:S(2)}, u32[]{:S(2)}) async-start(bf16[32,2,80,128]{3,2,1,0:T(8,128)(2,1)} %bitcast.115), calls=%async_computation.1 | async-start | bytes 2621440 | tf_op jit(solution)/shard_map/all_to_all | solution.py:252
  51.4 14.7 %copy-start.18 = (bf16[2,80,2,512]{3,2,1,0:T(2,128)(2,1)S(1)}, bf16[2,80,2,512]{3,2,1,0:T(2,128)(2,1)}, u32[]{:S(2)}) copy-start(bf16[2,80,2,512]{3,2,1,0:T(2,128)(2,1)} %copy-done.17) | copy-start | bytes 983044
  98.7 16.6 %copy-start.6 = (f32[2,2,80,512]{3,2,1,0:T(8,128)S(1)}, f32[2,2,80,512]{3,2,1,0:T(8,128)}, u32[]{:S(2)}) copy-start(f32[2,2,80,512]{3,2,1,0:T(8,128)} %copy-done.5) | copy-start | bytes 1966084
  98.7 16.6 %copy-start.8 = (f32[2,2,80,512]{3,2,1,0:T(8,128)S(1)}, f32[2,2,80,512]{3,2,1,0:T(8,128)}, u32[]{:S(2)}) copy-start(f32[2,2,80,512]{3,2,1,0:T(8,128)} %copy-done.7) | copy-start | bytes 1966084
  98.7 5.7 %collective-permute-start.6 = (bf16[2,2,80,512]{3,2,1,0:T(8,128)(2,1)S(1)}, bf16[2,2,80,512]{3,2,1,0:T(8,128)(2,1)S(1)}, u32[]{:S(2)}, u32[]{:S(2)}) collective-permute-start(bf16[2,2,80,512]{3,2,1,0:T(8,128)(2,1)S(1)} %get-tuple-element.45), channel_id=1, source_target_pairs={{0,32},{32,0},{64,96},{96,64},{1,33},{33,1},{65,97},{97,65},{2,34}... | collective-permute-start | bytes 983048 | tf_op jit(solution)/shard_map/ppermute | solution.py:256
  104.5 10.7 %collective-permute-start.7 = (bf16[2,2,80,512]{3,2,1,0:T(8,128)(2,1)S(1)}, bf16[2,2,80,512]{3,2,1,0:T(8,128)(2,1)S(1)}, u32[]{:S(2)}, u32[]{:S(2)}) collective-permute-start(bf16[2,2,80,512]{3,2,1,0:T(8,128)(2,1)S(1)} %fusion.17), channel_id=1, source_target_pairs={{0,64},{32,96},{64,0},{96,32},{1,65},{33,97},{65,1},{97,33},{2,66}... | collective-permute-start | bytes 983048 | tf_op jit(solution)/shard_map/ppermute | solution.py:256
  115.7 2.5 %collective-permute-start.8 = (bf16[2,2,80,512]{3,2,1,0:T(8,128)(2,1)S(1)}, bf16[2,2,80,512]{3,2,1,0:T(8,128)(2,1)S(1)}, u32[]{:S(2)}, u32[]{:S(2)}) collective-permute-start(bf16[2,2,80,512]{3,2,1,0:T(8,128)(2,1)S(1)} %multiply_convert_fusion.3.own_ref), channel_id=1, source_target_pairs={{0,32},{32,0},{64,96},{96,64},{1,33},{33,1},{65,97},{97,65},{2,34}... | collective-permute-start | bytes 983048 | tf_op jit(solution)/shard_map/ppermute | solution.py:256
  148.0 14.7 %all-to-all-start.4 = ((bf16[32,2,40,128]{3,2,1,0:T(8,128)(2,1)}), bf16[32,2,40,128]{3,2,1,0:T(8,128)(2,1)}, u32[]{:S(2)}, u32[]{:S(2)}) async-start(bf16[32,2,40,128]{3,2,1,0:T(8,128)(2,1)} %bitcast.40), calls=%async_computation.4 | async-start | bytes 1310720 | tf_op jit(solution)/shard_map/all_to_all | solution.py:252
  156.2 13.1 %copy-start.16 = (bf16[2,80,512]{2,1,0:T(8,128)(2,1)S(1)}, bf16[2,80,512]{2,1,0:T(8,128)(2,1)}, u32[]{:S(2)}) copy-start(bf16[2,80,512]{2,1,0:T(8,128)(2,1)} %get-tuple-element.57) | copy-start | bytes 491524
  162.7 15.4 %all-to-all-start.3 = ((bf16[32,2,40,128]{3,2,1,0:T(8,128)(2,1)}), bf16[32,2,40,128]{3,2,1,0:T(8,128)(2,1)}, u32[]{:S(2)}, u32[]{:S(2)}) async-start(bf16[32,2,40,128]{3,2,1,0:T(8,128)(2,1)} %bitcast.35), calls=%async_computation.3 | async-start | bytes 1310720 | tf_op jit(solution)/shard_map/all_to_all | solution.py:252
  173.1 17.4 %collective-permute-start.13 = (bf16[8,40,2,512]{3,2,1,0:T(2,128)(2,1)S(1)}, bf16[8,40,2,512]{3,2,1,0:T(2,128)(2,1)S(1)}, u32[]{:S(2)}, u32[]{:S(2)}) collective-permute-start(bf16[8,40,2,512]{3,2,1,0:T(2,128)(2,1)S(1)} %fusion.13.refs_0_), channel_id=1, source_target_pairs={{0,64},{32,96},{64,0},{96,32},{1,65},{33,97},{65,1},{97,33},{2,66}... | collective-permute-start | bytes 1966088 | tf_op jit(solution)/shard_map/ppermute | solution.py:256
  181.6 14.1 %collective-permute-start.10 = (bf16[8,40,2,512]{3,2,1,0:T(2,128)(2,1)S(1)}, bf16[8,40,2,512]{3,2,1,0:T(2,128)(2,1)S(1)}, u32[]{:S(2)}, u32[]{:S(2)}) collective-permute-start(bf16[8,40,2,512]{3,2,1,0:T(2,128)(2,1)S(1)} %fusion.13.refs_0_), channel_id=1, source_target_pairs={{0,32},{32,0},{64,96},{96,64},{1,33},{33,1},{65,97},{97,65},{2,34}... | collective-permute-start | bytes 1966088 | tf_op jit(solution)/shard_map/ppermute | solution.py:256
  185.7 9.9 %collective-permute-start.11 = (bf16[8,40,2,512]{3,2,1,0:T(2,128)(2,1)S(1)}, bf16[8,40,2,512]{3,2,1,0:T(2,128)(2,1)S(1)}, u32[]{:S(2)}, u32[]{:S(2)}) collective-permute-start(bf16[8,40,2,512]{3,2,1,0:T(2,128)(2,1)S(1)} %fusion.12.refs_1_), channel_id=1, source_target_pairs={{0,32},{32,0},{64,96},{96,64},{1,33},{33,1},{65,97},{97,65},{2,34}... | collective-permute-start | bytes 1966088 | tf_op jit(solution)/shard_map/ppermute | solution.py:256
  185.8 18.6 %collective-permute-start.9 = (bf16[8,40,2,512]{3,2,1,0:T(2,128)(2,1)S(1)}, bf16[8,40,2,512]{3,2,1,0:T(2,128)(2,1)S(1)}, u32[]{:S(2)}, u32[]{:S(2)}) collective-permute-start(bf16[8,40,2,512]{3,2,1,0:T(2,128)(2,1)S(1)} %fusion.12.refs_1_), channel_id=1, source_target_pairs={{0,64},{32,96},{64,0},{96,32},{1,65},{33,97},{65,1},{97,33},{2,66}... | collective-permute-start | bytes 1966088 | tf_op jit(solution)/shard_map/ppermute | solution.py:256
  190.4 16.9 %collective-permute-start.14 = (bf16[8,40,2,512]{3,2,1,0:T(2,128)(2,1)S(1)}, bf16[8,40,2,512]{3,2,1,0:T(2,128)(2,1)S(1)}, u32[]{:S(2)}, u32[]{:S(2)}) collective-permute-start(bf16[8,40,2,512]{3,2,1,0:T(2,128)(2,1)S(1)} %collective-permute-done.13.refs_0_), channel_id=1, source_target_pairs={{0,32},{32,0},{64,96},{96,64},{1,33},{33,1},{65,97},{97,65},{2,34}... | collective-permute-start | bytes 1966088 | tf_op jit(solution)/shard_map/ppermute | solution.py:256
  204.5 4.5 %collective-permute-start.12 = (bf16[8,40,2,512]{3,2,1,0:T(2,128)(2,1)S(1)}, bf16[8,40,2,512]{3,2,1,0:T(2,128)(2,1)S(1)}, u32[]{:S(2)}, u32[]{:S(2)}) collective-permute-start(bf16[8,40,2,512]{3,2,1,0:T(2,128)(2,1)S(1)} %collective-permute-done.9.refs_2_), channel_id=1, source_target_pairs={{0,32},{32,0},{64,96},{96,64},{1,33},{33,1},{65,97},{97,65},{2,34}... | collective-permute-start | bytes 1966088 | tf_op jit(solution)/shard_map/ppermute | solution.py:256
  (20 other events, 60.1 us)

commit v13 on v10

--- a/solution.py
+++ b/solution.py
@@ -126,7 +126,7 @@
             jax.ShapeDtypeStruct(shape, jnp.float32),
             jax.ShapeDtypeStruct(shape, jnp.bfloat16),
         ],
-        compiler_params=pltpu.CompilerParams(vmem_limit_bytes=12 << 20),
+        compiler_params=pltpu.CompilerParams(vmem_limit_bytes=56 << 20),
         cost_estimate=pl.CostEstimate(
             flops=8 * spread.size, bytes_accessed=10 * spread.size, transcendentals=0
         ),

time: 213 us -> 213 us (level)
  local copies, waits for them, and re-layouts: 25.8 us -> 22.2 us
  other arithmetic: 7.84 us -> 10.1 us
    unnamed x49 -> x37, local copies, waits for them, and re-layouts: 5.72 us -> 1.35 us
  transfers between devices with their start and end apart: 19 -> 19, of which waited for: 11 -> 12; matrix products, arithmetic and copies ran while one was open for 15% -> 16% of each run, Pallas kernels for 10% -> 10%
where the time goes in v13:
time: 213 us; the launch traced here: 209 us
  starting transfers between devices  62.7 us (29%)
  waiting for transfers between devices  52.2 us (25%)
  Pallas kernels  30.2 us (14%)
  blocking collectives  22.8 us (11%)
  local copies, waits for them, and re-layouts  22.2 us (10%)
  other arithmetic  10.1 us (5%)
  matrix products  8.1 us (4%)
    ppermute x15, waiting for transfers between devices, swap_slot(): return lax.ppermute(arr, 'slot', [(i, i ^ k) for i in range(4)])  36.5 us
    ppermute x15, starting transfers between devices, swap_slot(): return lax.ppermute(arr, 'slot', [(i, i ^ k) for i in range(4)])  34.1 us
    all_to_all x4, starting transfers between devices, swap_columns(): lax.all_to_all(flat, 'horiz', split_axis=0, concat_axis=0, tiled=True)  28.6 us
    all_to_all x1, blocking collectives, swap_columns(): lax.all_to_all(flat, 'horiz', split_axis=0, concat_axis=0, tiled=True)  22.8 us
    all_to_all x4, waiting for transfers between devices, swap_columns(): lax.all_to_all(flat, 'horiz', split_axis=0, concat_axis=0, tiled=True)  15.7 us
    pallas_call x1, Pallas kernels, obs_fields(): pl.pallas_call(obs_kernel, grid=(slots, count // OBS_BLOCK), in_specs=[pa...  14.7 us
    another operation x4, local copies, waits for them, and re-layouts, row_major(): return with_layout_constraint(arr, Layout(tuple(range(arr.ndim))))  6.59 us
    pallas_call x2, Pallas kernels, pick(): pl.pallas_call(functools.partial(pick_kernel, order), in_specs=[pl.BlockS...  5.07 us
  transfers between devices with their start and end apart: 19, of which 12 were waited for; matrix products, arithmetic and copies ran while one was open for 16% of the time, Pallas kernels for 10%

profile of v13, /device:TPU:37, one launch (start us, length us, event | category | flops | bytes accessed | tf_op | source)
XLA Modules:
  0.0 209.2 jit_solution(13979052404148856427)
XLA Ops:
  2.3 2.7 %collective-permute-start.3 = (bf16[2,80,2,512]{3,2,1,0:T(2,128)(2,1)}, bf16[2,80,2,512]{3,2,1,0:T(2,128)(2,1)S(1)}, u32[]{:S(2)}, u32[]{:S(2)}) collective-permute-start(bf16[2,80,2,512]{3,2,1,0:T(2,128)(2,1)} %get-tuple-element.39), channel_id=1, source_target_pairs={{0,64},{32,96},{64,0},{96,32},{1,65},{33,97},{65,1},{97,33},{2,66}... | collective-permute-start | bytes 983048 | tf_op jit(solution)/shard_map/ppermute | solution.py:256
  12.4 9.0 %all-to-all-start = ((bf16[32,2,80,128]{3,2,1,0:T(8,128)(2,1)}), bf16[32,2,80,128]{3,2,1,0:T(8,128)(2,1)S(1)}, u32[]{:S(2)}, u32[]{:S(2)}) async-start(bf16[32,2,80,128]{3,2,1,0:T(8,128)(2,1)} %bitcast.10), calls=%async_computation | async-start | bytes 2621440 | tf_op jit(solution)/shard_map/all_to_all | solution.py:252
  25.4 3.1 %shard_map.111 = (bf16[4,80,2,512]{3,2,1,0:T(2,128)(2,1)}, bf16[8,80,2,512]{3,2,1,0:T(2,128)(2,1)}, bf16[8,80,2,512]{3,2,1,0:T(2,128)(2,1)}) custom-call(s32[1]{0:T(128)} %bitcast.slot_ref, bf16[32,80,2,512]{3,2,1,0:T(2,128)(2,1)} %bitcast.114), custom_call_target="tpu_custom_call" | custom-call | bytes 7864320 | tf_op jit(solution)/shard_map/pallas_call | solution.py:202
  29.8 4.4 %collective-permute-start.5 = (bf16[8,80,2,512]{3,2,1,0:T(2,128)(2,1)}, bf16[8,80,2,512]{3,2,1,0:T(2,128)(2,1)}, u32[]{:S(2)}, u32[]{:S(2)}) collective-permute-start(bf16[8,80,2,512]{3,2,1,0:T(2,128)(2,1)} %get-tuple-element.41), channel_id=1, source_target_pairs={{0,96},{32,64},{64,32},{96,0},{1,97},{33,65},{65,33},{97,1},{2,98}... | collective-permute-start | bytes 3932168 | tf_op jit(solution)/shard_map/ppermute | solution.py:256
  34.2 2.9 %all-to-all-done = bf16[32,2,80,128]{3,2,1,0:T(8,128)(2,1)S(1)} async-done(((bf16[32,2,80,128]{3,2,1,0:T(8,128)(2,1)}), bf16[32,2,80,128]{3,2,1,0:T(8,128)(2,1)S(1)}, u32[]{:S(2)}, u32[]{:S(2)}) %all-to-all-start) | async-done | bytes 1310752 | tf_op jit(solution)/shard_map/all_to_all | solution.py:252
  41.5 7.4 %all-to-all-start.1 = ((bf16[32,2,80,128]{3,2,1,0:T(8,128)(2,1)}), bf16[32,2,80,128]{3,2,1,0:T(8,128)(2,1)}, u32[]{:S(2)}, u32[]{:S(2)}) async-start(bf16[32,2,80,128]{3,2,1,0:T(8,128)(2,1)} %bitcast.115), calls=%async_computation.1 | async-start | bytes 2621440 | tf_op jit(solution)/shard_map/all_to_all | solution.py:252
  48.9 14.7 %shard_map.110 = (f32[2,2,80,512]{3,2,1,0:T(8,128)S(1)}, f32[2,2,80,512]{3,2,1,0:T(8,128)S(1)}) custom-call(f32[2,3,1,8192]{3,2,1,0:T(1,128)S(1)} %pad_maximum_fusion.cell_ref.value_ref.weight_ref, f32[2,3,1,8192]{3,2,1,0:T(1,128)S(1)} %pad_maximum_fusion.cell_ref.value_ref.weight_ref, f32[2,3,1,8192]{3,2,1,0:T(1,128)S(1)} %pad_maximum_fusion.cell_ref.value_ref.weight_ref), custom_call_target="tpu_custom_call" | custom-call | flops 21474836480 | bytes 1310720 | tf_op jit(solution)/shard_map/pallas_call | solution.py:77
  66.0 16.3 %collective-permute-done.5 = bf16[8,80,2,512]{3,2,1,0:T(2,128)(2,1)} collective-permute-done((bf16[8,80,2,512]{3,2,1,0:T(2,128)(2,1)}, bf16[8,80,2,512]{3,2,1,0:T(2,128)(2,1)}, u32[]{:S(2)}, u32[]{:S(2)}) %collective-permute-start.5) | collective-permute-done | bytes 1310752 | tf_op jit(solution)/shard_map/ppermute | solution.py:256
  82.3 2.7 %copy.156 = bf16[8,80,2,512]{3,1,2,0:T(8,128)(2,1)} copy(bf16[8,80,2,512]{3,2,1,0:T(2,128)(2,1)} %collective-permute-done.5) | data formatting | bytes 2621440 | tf_op jit(solution)/shard_map/layout_constraint | solution.py:260
  85.0 2.7 %copy.157 = bf16[8,80,2,512]{3,1,2,0:T(8,128)(2,1)} copy(bf16[8,80,2,512]{3,2,1,0:T(2,128)(2,1)} %collective-permute-done.2) | data formatting | bytes 2621440 | tf_op jit(solution)/shard_map/layout_constraint | solution.py:260
  87.7 5.0 %all-to-all-done.1 = bf16[32,2,80,128]{3,2,1,0:T(8,128)(2,1)} async-done(((bf16[32,2,80,128]{3,2,1,0:T(8,128)(2,1)}), bf16[32,2,80,128]{3,2,1,0:T(8,128)(2,1)}, u32[]{:S(2)}, u32[]{:S(2)}) %all-to-all-start.1) | async-done | bytes 1310752 | tf_op jit(solution)/shard_map/all_to_all | solution.py:252
  92.8 4.5 %shard_map.112 = (f32[2,2,80,512]{3,2,1,0:T(8,128)}, bf16[2,2,80,512]{3,2,1,0:T(8,128)(2,1)}) custom-call(bf16[8,4,2,80,128]{4,3,2,1,0:T(8,128)(2,1)} %bitcast.17.spread_ref, bf16[8,2,80,512]{3,2,1,0:T(8,128)(2,1)} %bitcast.106, bf16[8,2,80,512]{3,2,1,0:T(8,128)(2,1)} %bitcast.110, bf16[8,2,80,512]{3,2,1,0:T(8,128)(2,1)} %maximum_bitcast_fusion.p2, ...), custom_call_target="tpu_custom_call" | custom-call | flops 5242880 | bytes 6553600 | tf_op jit(solution)/shard_map/pallas_call | solution.py:114
  97.3 4.3 %collective-permute-start.6 = (bf16[2,2,80,512]{3,2,1,0:T(8,128)(2,1)}, bf16[2,2,80,512]{3,2,1,0:T(8,128)(2,1)S(1)}, u32[]{:S(2)}, u32[]{:S(2)}) collective-permute-start(bf16[2,2,80,512]{3,2,1,0:T(8,128)(2,1)} %get-tuple-element.43), channel_id=1, source_target_pairs={{0,32},{32,0},{64,96},{96,64},{1,33},{33,1},{65,97},{97,65},{2,34}... | collective-permute-start | bytes 983048 | tf_op jit(solution)/shard_map/ppermute | solution.py:256
  105.7 9.4 %collective-permute-done.7 = bf16[2,2,80,512]{3,2,1,0:T(8,128)(2,1)S(1)} collective-permute-done((bf16[2,2,80,512]{3,2,1,0:T(8,128)(2,1)S(1)}, bf16[2,2,80,512]{3,2,1,0:T(8,128)(2,1)S(1)}, u32[]{:S(2)}, u32[]{:S(2)}) %collective-permute-start.7) | collective-permute-done | bytes 327712 | tf_op jit(solution)/shard_map/ppermute | solution.py:256
  120.5 22.8 %all_to_all.25 = bf16[32,2,80,128]{3,2,1,0:T(8,128)(2,1)S(1)} all-to-all(bf16[32,2,80,128]{3,2,1,0:T(8,128)(2,1)S(1)} %bitcast.112), channel_id=1, replica_groups=mesh['slot'=4,'horiz'=32] {'horiz'}, dimensions={0} | all-to-all | bytes 2621440 | tf_op jit(solution)/shard_map/all_to_all | solution.py:252
  146.7 5.9 %all-to-all-start.4 = ((bf16[32,2,48,128]{3,2,1,0:T(8,128)(2,1)}), bf16[32,2,48,128]{3,2,1,0:T(8,128)(2,1)}, u32[]{:S(2)}, u32[]{:S(2)}) async-start(bf16[32,2,48,128]{3,2,1,0:T(8,128)(2,1)} %bitcast.122), calls=%async_computation.4 | async-start | bytes 1572864 | tf_op jit(solution)/shard_map/all_to_all | solution.py:252
  158.2 4.8 %all-to-all-done.4 = bf16[32,2,48,128]{3,2,1,0:T(8,128)(2,1)} async-done(((bf16[32,2,48,128]{3,2,1,0:T(8,128)(2,1)}), bf16[32,2,48,128]{3,2,1,0:T(8,128)(2,1)}, u32[]{:S(2)}, u32[]{:S(2)}) %all-to-all-start.4) | async-done | bytes 786464 | tf_op jit(solution)/shard_map/all_to_all | solution.py:252
  163.0 6.4 %all-to-all-start.3 = ((bf16[32,2,32,128]{3,2,1,0:T(8,128)(2,1)}), bf16[32,2,32,128]{3,2,1,0:T(8,128)(2,1)}, u32[]{:S(2)}, u32[]{:S(2)}) async-start(bf16[32,2,32,128]{3,2,1,0:T(8,128)(2,1)} %bitcast.35), calls=%async_computation.3 | async-start | bytes 1048576 | tf_op jit(solution)/shard_map/all_to_all | solution.py:252
  174.7 3.0 %all-to-all-done.3 = bf16[32,2,32,128]{3,2,1,0:T(8,128)(2,1)} async-done(((bf16[32,2,32,128]{3,2,1,0:T(8,128)(2,1)}), bf16[32,2,32,128]{3,2,1,0:T(8,128)(2,1)}, u32[]{:S(2)}, u32[]{:S(2)}) %all-to-all-start.3) | async-done | bytes 524320 | tf_op jit(solution)/shard_map/all_to_all | solution.py:252
  179.2 4.4 %collective-permute-start.10 = (bf16[8,48,2,512]{3,2,1,0:T(2,128)(2,1)S(1)}, bf16[8,48,2,512]{3,2,1,0:T(2,128)(2,1)S(1)}, u32[]{:S(2)}, u32[]{:S(2)}) collective-permute-start(bf16[8,48,2,512]{3,2,1,0:T(2,128)(2,1)S(1)} %fusion.10.refs_0_), channel_id=1, source_target_pairs={{0,32},{32,0},{64,96},{96,64},{1,33},{33,1},{65,97},{97,65},{2,34}... | collective-permute-start | bytes 2359304 | tf_op jit(solution)/shard_map/ppermute | solution.py:256
  186.7 5.0 %collective-permute-done.13.refs_0_ = bf16[8,48,2,512]{3,2,1,0:T(2,128)(2,1)S(1)} collective-permute-done((bf16[8,48,2,512]{3,2,1,0:T(2,128)(2,1)S(1)}, bf16[8,48,2,512]{3,2,1,0:T(2,128)(2,1)S(1)}, u32[]{:S(2)}, u32[]{:S(2)}) %collective-permute-start.13) | collective-permute-done | bytes 786464 | tf_op jit(solution)/shard_map/ppermute | solution.py:256
  191.7 7.0 %collective-permute-start.14 = (bf16[8,48,2,512]{3,2,1,0:T(2,128)(2,1)S(1)}, bf16[8,48,2,512]{3,2,1,0:T(2,128)(2,1)S(1)}, u32[]{:S(2)}, u32[]{:S(2)}) collective-permute-start(bf16[8,48,2,512]{3,2,1,0:T(2,128)(2,1)S(1)} %collective-permute-done.13.refs_0_), channel_id=1, source_target_pairs={{0,32},{32,0},{64,96},{96,64},{1,33},{33,1},{65,97},{97,65},{2,34}... | collective-permute-start | bytes 2359304 | tf_op jit(solution)/shard_map/ppermute | solution.py:256
  200.2 2.7 %collective-permute-done.9.refs_2_ = bf16[8,32,2,512]{3,2,1,0:T(2,128)(2,1)S(1)} collective-permute-done((bf16[8,32,2,512]{3,2,1,0:T(2,128)(2,1)S(1)}, bf16[8,32,2,512]{3,2,1,0:T(2,128)(2,1)S(1)}, u32[]{:S(2)}, u32[]{:S(2)}) %collective-permute-start.9) | collective-permute-done | bytes 524320 | tf_op jit(solution)/shard_map/ppermute | solution.py:256
  203.0 3.7 %collective-permute-start.12 = (bf16[8,32,2,512]{3,2,1,0:T(2,128)(2,1)S(1)}, bf16[8,32,2,512]{3,2,1,0:T(2,128)(2,1)S(1)}, u32[]{:S(2)}, u32[]{:S(2)}) collective-permute-start(bf16[8,32,2,512]{3,2,1,0:T(2,128)(2,1)S(1)} %collective-permute-done.9.refs_2_), channel_id=1, source_target_pairs={{0,32},{32,0},{64,96},{96,64},{1,33},{33,1},{65,97},{97,65},{2,34}... | collective-permute-start | bytes 1572872 | tf_op jit(solution)/shard_map/ppermute | solution.py:256
  (106 shorter events, 53.7 us)
Async XLA Ops:
  0.0 9.9 %copy-start = (bf16[512,512]{1,0:T(8,128)(2,1)S(1)}, bf16[512,512]{1,0:T(8,128)(2,1)}, u32[]{:S(2)}) copy-start(bf16[512,512]{1,0:T(8,128)(2,1)} %param.15) | copy-start | bytes 1572868
  0.0 6.2 %copy-start.17 = (f32[16,80]{1,0:T(8,128)S(1)}, f32[16,80]{1,0:T(8,128)}, u32[]{:S(2)}) copy-start(f32[16,80]{1,0:T(8,128)} %param.14) | copy-start | bytes 15364
  2.0 10.4 %collective-permute-start = (bf16[2,80,2,512]{3,2,1,0:T(2,128)(2,1)}, bf16[2,80,2,512]{3,2,1,0:T(2,128)(2,1)S(1)}, u32[]{:S(2)}, u32[]{:S(2)}) collective-permute-start(bf16[2,80,2,512]{3,2,1,0:T(2,128)(2,1)} %get-tuple-element.30), channel_id=1, source_target_pairs={{0,64},{32,96},{64,0},{96,32},{1,65},{33,97},{65,1},{97,33},{2,66}... | collective-permute-start | bytes 983048 | tf_op jit(solution)/shard_map/ppermute | solution.py:256
  2.3 61.3 %collective-permute-start.3 = (bf16[2,80,2,512]{3,2,1,0:T(2,128)(2,1)}, bf16[2,80,2,512]{3,2,1,0:T(2,128)(2,1)S(1)}, u32[]{:S(2)}, u32[]{:S(2)}) collective-permute-start(bf16[2,80,2,512]{3,2,1,0:T(2,128)(2,1)} %get-tuple-element.39), channel_id=1, source_target_pairs={{0,64},{32,96},{64,0},{96,32},{1,65},{33,97},{65,1},{97,33},{2,66}... | collective-permute-start | bytes 983048 | tf_op jit(solution)/shard_map/ppermute | solution.py:256
  5.2 20.0 %collective-permute-start.1 = (f32[3,1,8192]{2,1,0:T(1,128)S(1)}, f32[3,1,8192]{2,1,0:T(1,128)S(1)}, u32[]{:S(2)}, u32[]{:S(2)}) collective-permute-start(f32[3,1,8192]{2,1,0:T(1,128)S(1)} %pad_maximum_fusion.1), channel_id=1, source_target_pairs={{0,64},{32,96},{64,0},{96,32},{1,65},{33,97},{65,1},{97,33},{2,66}... | collective-permute-start | bytes 294920 | tf_op jit(solution)/shard_map/ppermute | solution.py:256
  12.4 24.8 %all-to-all-start = ((bf16[32,2,80,128]{3,2,1,0:T(8,128)(2,1)}), bf16[32,2,80,128]{3,2,1,0:T(8,128)(2,1)S(1)}, u32[]{:S(2)}, u32[]{:S(2)}) async-start(bf16[32,2,80,128]{3,2,1,0:T(8,128)(2,1)} %bitcast.10), calls=%async_computation | async-start | bytes 2621440 | tf_op jit(solution)/shard_map/all_to_all | solution.py:252
  28.5 35.1 %collective-permute-start.4 = (bf16[4,80,2,512]{3,2,1,0:T(2,128)(2,1)}, bf16[4,80,2,512]{3,2,1,0:T(2,128)(2,1)}, u32[]{:S(2)}, u32[]{:S(2)}) collective-permute-start(bf16[4,80,2,512]{3,2,1,0:T(2,128)(2,1)} %get-tuple-element.40), channel_id=1, source_target_pairs={{0,64},{32,96},{64,0},{96,32},{1,65},{33,97},{65,1},{97,33},{2,66}... | collective-permute-start | bytes 1966088 | tf_op jit(solution)/shard_map/ppermute | solution.py:256
  29.8 52.5 %collective-permute-start.5 = (bf16[8,80,2,512]{3,2,1,0:T(2,128)(2,1)}, bf16[8,80,2,512]{3,2,1,0:T(2,128)(2,1)}, u32[]{:S(2)}, u32[]{:S(2)}) collective-permute-start(bf16[8,80,2,512]{3,2,1,0:T(2,128)(2,1)} %get-tuple-element.41), channel_id=1, source_target_pairs={{0,96},{32,64},{64,32},{96,0},{1,97},{33,65},{65,33},{97,1},{2,98}... | collective-permute-start | bytes 3932168 | tf_op jit(solution)/shard_map/ppermute | solution.py:256
  34.2 50.8 %collective-permute-start.2 = (bf16[8,80,2,512]{3,2,1,0:T(2,128)(2,1)}, bf16[8,80,2,512]{3,2,1,0:T(2,128)(2,1)}, u32[]{:S(2)}, u32[]{:S(2)}) collective-permute-start(bf16[8,80,2,512]{3,2,1,0:T(2,128)(2,1)} %get-tuple-element.37), channel_id=1, source_target_pairs={{0,32},{32,0},{64,96},{96,64},{1,33},{33,1},{65,97},{97,65},{2,34}... | collective-permute-start | bytes 3932168 | tf_op jit(solution)/shard_map/ppermute | solution.py:256
  41.5 51.2 %all-to-all-start.1 = ((bf16[32,2,80,128]{3,2,1,0:T(8,128)(2,1)}), bf16[32,2,80,128]{3,2,1,0:T(8,128)(2,1)}, u32[]{:S(2)}, u32[]{:S(2)}) async-start(bf16[32,2,80,128]{3,2,1,0:T(8,128)(2,1)} %bitcast.115), calls=%async_computation.1 | async-start | bytes 2621440 | tf_op jit(solution)/shard_map/all_to_all | solution.py:252
  97.3 17.9 %copy-start.9 = (f32[2,2,80,512]{3,2,1,0:T(8,128)S(1)}, f32[2,2,80,512]{3,2,1,0:T(8,128)}, u32[]{:S(2)}) copy-start(f32[2,2,80,512]{3,2,1,0:T(8,128)} %get-tuple-element.42) | copy-start | bytes 1966084
  97.3 5.8 %collective-permute-start.6 = (bf16[2,2,80,512]{3,2,1,0:T(8,128)(2,1)}, bf16[2,2,80,512]{3,2,1,0:T(8,128)(2,1)S(1)}, u32[]{:S(2)}, u32[]{:S(2)}) collective-permute-start(bf16[2,2,80,512]{3,2,1,0:T(8,128)(2,1)} %get-tuple-element.43), channel_id=1, source_target_pairs={{0,32},{32,0},{64,96},{96,64},{1,33},{33,1},{65,97},{97,65},{2,34}... | collective-permute-start | bytes 983048 | tf_op jit(solution)/shard_map/ppermute | solution.py:256
  103.1 15.0 %copy-start.4 = (bf16[8,80,2,512]{3,1,2,0:T(8,128)(2,1)S(1)}, bf16[8,80,2,512]{3,1,2,0:T(8,128)(2,1)}, u32[]{:S(2)}) copy-start(bf16[8,80,2,512]{3,1,2,0:T(8,128)(2,1)} %copy.157) | copy-start | bytes 3932164
  104.3 10.7 %collective-permute-start.7 = (bf16[2,2,80,512]{3,2,1,0:T(8,128)(2,1)S(1)}, bf16[2,2,80,512]{3,2,1,0:T(8,128)(2,1)S(1)}, u32[]{:S(2)}, u32[]{:S(2)}) collective-permute-start(bf16[2,2,80,512]{3,2,1,0:T(8,128)(2,1)S(1)} %fusion.17), channel_id=1, source_target_pairs={{0,64},{32,96},{64,0},{96,32},{1,65},{33,97},{65,1},{97,33},{2,66}... | collective-permute-start | bytes 983048 | tf_op jit(solution)/shard_map/ppermute | solution.py:256
  115.6 2.5 %collective-permute-start.8 = (bf16[2,2,80,512]{3,2,1,0:T(8,128)(2,1)S(1)}, bf16[2,2,80,512]{3,2,1,0:T(8,128)(2,1)S(1)}, u32[]{:S(2)}, u32[]{:S(2)}) collective-permute-start(bf16[2,2,80,512]{3,2,1,0:T(8,128)(2,1)S(1)} %multiply_convert_fusion.3.own_ref), channel_id=1, source_target_pairs={{0,32},{32,0},{64,96},{96,64},{1,33},{33,1},{65,97},{97,65},{2,34}... | collective-permute-start | bytes 983048 | tf_op jit(solution)/shard_map/ppermute | solution.py:256
  146.7 16.3 %all-to-all-start.4 = ((bf16[32,2,48,128]{3,2,1,0:T(8,128)(2,1)}), bf16[32,2,48,128]{3,2,1,0:T(8,128)(2,1)}, u32[]{:S(2)}, u32[]{:S(2)}) async-start(bf16[32,2,48,128]{3,2,1,0:T(8,128)(2,1)} %bitcast.122), calls=%async_computation.4 | async-start | bytes 1572864 | tf_op jit(solution)/shard_map/all_to_all | solution.py:252
  163.0 14.6 %all-to-all-start.3 = ((bf16[32,2,32,128]{3,2,1,0:T(8,128)(2,1)}), bf16[32,2,32,128]{3,2,1,0:T(8,128)(2,1)}, u32[]{:S(2)}, u32[]{:S(2)}) async-start(bf16[32,2,32,128]{3,2,1,0:T(8,128)(2,1)} %bitcast.35), calls=%async_computation.3 | async-start | bytes 1048576 | tf_op jit(solution)/shard_map/all_to_all | solution.py:252
  173.4 10.2 %copy-start.8 = (f32[8,2,32,512]{3,2,1,0:T(8,128)S(1)}, f32[8,2,32,512]{3,2,1,0:T(8,128)}, u32[]{:S(2)}) copy-start(f32[8,2,32,512]{3,2,1,0:T(8,128)} %slice_convert_fusion.1) | copy-start | bytes 3145732
  173.4 18.3 %collective-permute-start.13 = (bf16[8,48,2,512]{3,2,1,0:T(2,128)(2,1)S(1)}, bf16[8,48,2,512]{3,2,1,0:T(2,128)(2,1)S(1)}, u32[]{:S(2)}, u32[]{:S(2)}) collective-permute-start(bf16[8,48,2,512]{3,2,1,0:T(2,128)(2,1)S(1)} %fusion.10.refs_0_), channel_id=1, source_target_pairs={{0,64},{32,96},{64,0},{96,32},{1,65},{33,97},{65,1},{97,33},{2,66}... | collective-permute-start | bytes 2359304 | tf_op jit(solution)/shard_map/ppermute | solution.py:256
  179.2 19.5 %collective-permute-start.10 = (bf16[8,48,2,512]{3,2,1,0:T(2,128)(2,1)S(1)}, bf16[8,48,2,512]{3,2,1,0:T(2,128)(2,1)S(1)}, u32[]{:S(2)}, u32[]{:S(2)}) collective-permute-start(bf16[8,48,2,512]{3,2,1,0:T(2,128)(2,1)S(1)} %fusion.10.refs_0_), channel_id=1, source_target_pairs={{0,32},{32,0},{64,96},{96,64},{1,33},{33,1},{65,97},{97,65},{2,34}... | collective-permute-start | bytes 2359304 | tf_op jit(solution)/shard_map/ppermute | solution.py:256
  185.0 13.7 %collective-permute-start.11 = (bf16[8,32,2,512]{3,2,1,0:T(2,128)(2,1)S(1)}, bf16[8,32,2,512]{3,2,1,0:T(2,128)(2,1)S(1)}, u32[]{:S(2)}, u32[]{:S(2)}) collective-permute-start(bf16[8,32,2,512]{3,2,1,0:T(2,128)(2,1)S(1)} %fusion.16.refs_1_), channel_id=1, source_target_pairs={{0,32},{32,0},{64,96},{96,64},{1,33},{33,1},{65,97},{97,65},{2,34}... | collective-permute-start | bytes 1572872 | tf_op jit(solution)/shard_map/ppermute | solution.py:256
  185.1 17.9 %collective-permute-start.9 = (bf16[8,32,2,512]{3,2,1,0:T(2,128)(2,1)S(1)}, bf16[8,32,2,512]{3,2,1,0:T(2,128)(2,1)S(1)}, u32[]{:S(2)}, u32[]{:S(2)}) collective-permute-start(bf16[8,32,2,512]{3,2,1,0:T(2,128)(2,1)S(1)} %fusion.16.refs_1_), channel_id=1, source_target_pairs={{0,64},{32,96},{64,0},{96,32},{1,65},{33,97},{65,1},{97,33},{2,66}... | collective-permute-start | bytes 1572872 | tf_op jit(solution)/shard_map/ppermute | solution.py:256
  191.7 14.9 %collective-permute-start.14 = (bf16[8,48,2,512]{3,2,1,0:T(2,128)(2,1)S(1)}, bf16[8,48,2,512]{3,2,1,0:T(2,128)(2,1)S(1)}, u32[]{:S(2)}, u32[]{:S(2)}) collective-permute-start(bf16[8,48,2,512]{3,2,1,0:T(2,128)(2,1)S(1)} %collective-permute-done.13.refs_0_), channel_id=1, source_target_pairs={{0,32},{32,0},{64,96},{96,64},{1,33},{33,1},{65,97},{97,65},{2,34}... | collective-permute-start | bytes 2359304 | tf_op jit(solution)/shard_map/ppermute | solution.py:256
  203.0 5.2 %collective-permute-start.12 = (bf16[8,32,2,512]{3,2,1,0:T(2,128)(2,1)S(1)}, bf16[8,32,2,512]{3,2,1,0:T(2,128)(2,1)S(1)}, u32[]{:S(2)}, u32[]{:S(2)}) collective-permute-start(bf16[8,32,2,512]{3,2,1,0:T(2,128)(2,1)S(1)} %collective-permute-done.9.refs_2_), channel_id=1, source_target_pairs={{0,32},{32,0},{64,96},{96,64},{1,33},{33,1},{65,97},{97,65},{2,34}... | collective-permute-start | bytes 1572872 | tf_op jit(solution)/shard_map/ppermute | solution.py:256
  (13 other events, 43.9 us)

commit v14 on v13

--- a/solution.py
+++ b/solution.py
@@ -356,6 +356,7 @@
 
     lows = [low for low, _ in bounds]
     far = [row_major(swap_slot(g, 2)) for g in gradients]
+    gradients = list(lax.optimization_barrier(tuple(gradients)))
     near = [row_major(swap_slot(g, 1)) for g in gradients]
     result = place(
         slot,

time: 213 us -> 220 us (1.033)
  starting transfers between devices: 62.7 us -> 67 us
  local copies, waits for them, and re-layouts: 22.2 us -> 25.9 us
    ppermute x15, starting transfers between devices: 34.1 us -> 39.2 us  [swap_slot(): return lax.ppermute(arr, 'slot', [(i, i ^ k) for i in range(4)])]
  transfers between devices with their start and end apart: 19 -> 19, of which waited for: 12 -> 11; matrix products, arithmetic and copies ran while one was open for 16% -> 15% of each run, Pallas kernels for 10% -> 10%
where the time goes in v14:
time: 220 us; the launch traced here: 216 us
  starting transfers between devices  67 us (30%)
  waiting for transfers between devices  51.3 us (23%)
  Pallas kernels  30.2 us (14%)
  local copies, waits for them, and re-layouts  25.9 us (12%)
  blocking collectives  22.9 us (10%)
  other arithmetic  9.83 us (4%)
  matrix products  8.04 us (4%)
    ppermute x15, starting transfers between devices, swap_slot(): return lax.ppermute(arr, 'slot', [(i, i ^ k) for i in range(4)])  39.2 us
    ppermute x15, waiting for transfers between devices, swap_slot(): return lax.ppermute(arr, 'slot', [(i, i ^ k) for i in range(4)])  35.2 us
    all_to_all x4, starting transfers between devices, swap_columns(): lax.all_to_all(flat, 'horiz', split_axis=0, concat_axis=0, tiled=True)  27.8 us
    all_to_all x1, blocking collectives, swap_columns(): lax.all_to_all(flat, 'horiz', split_axis=0, concat_axis=0, tiled=True)  22.9 us
    all_to_all x4, waiting for transfers between devices, swap_columns(): lax.all_to_all(flat, 'horiz', split_axis=0, concat_axis=0, tiled=True)  16.1 us
    pallas_call x1, Pallas kernels, obs_fields(): pl.pallas_call(obs_kernel, grid=(slots, count // OBS_BLOCK), in_specs=[pa...  14.7 us
    another operation x4, local copies, waits for them, and re-layouts, row_major(): return with_layout_constraint(arr, Layout(tuple(range(arr.ndim))))  6.58 us
    pallas_call x2, Pallas kernels, pick(): pl.pallas_call(functools.partial(pick_kernel, order), in_specs=[pl.BlockS...  5.04 us
  transfers between devices with their start and end apart: 19, of which 11 were waited for; matrix products, arithmetic and copies ran while one was open for 15% of the time, Pallas kernels for 10%

profile of v14, /device:TPU:37, one launch (start us, length us, event | category | flops | bytes accessed | tf_op | source)
XLA Modules:
  0.0 215.9 jit_solution(3040723314522588362)
XLA Ops:
  2.3 2.7 %collective-permute-start.3 = (bf16[2,80,2,512]{3,2,1,0:T(2,128)(2,1)}, bf16[2,80,2,512]{3,2,1,0:T(2,128)(2,1)S(1)}, u32[]{:S(2)}, u32[]{:S(2)}) collective-permute-start(bf16[2,80,2,512]{3,2,1,0:T(2,128)(2,1)} %get-tuple-element.41), channel_id=1, source_target_pairs={{0,64},{32,96},{64,0},{96,32},{1,65},{33,97},{65,1},{97,33},{2,66}... | collective-permute-start | bytes 983048 | tf_op jit(solution)/shard_map/ppermute | solution.py:256
  12.4 9.1 %all-to-all-start = ((bf16[32,2,80,128]{3,2,1,0:T(8,128)(2,1)}), bf16[32,2,80,128]{3,2,1,0:T(8,128)(2,1)S(1)}, u32[]{:S(2)}, u32[]{:S(2)}) async-start(bf16[32,2,80,128]{3,2,1,0:T(8,128)(2,1)} %bitcast.10), calls=%async_computation | async-start | bytes 2621440 | tf_op jit(solution)/shard_map/all_to_all | solution.py:252
  21.5 2.3 %constant_dynamic-slice_fusion = bf16[1,8,80,2,512]{4,3,2,1,0:T(2,128)(2,1)S(1)} fusion(bf16[1,32,80,2,512]{4,3,2,1,0:T(2,128)(2,1)} %param.18, s32[]{:T(128)S(6)} %select_n.17), kind=kLoop, calls=%fused_computation.55 | loop fusion | bytes 2621444 | tf_op jit(solution)/shard_map/dynamic_slice | solution.py:320
  26.3 3.1 %shard_map.111 = (bf16[4,80,2,512]{3,2,1,0:T(2,128)(2,1)}, bf16[8,80,2,512]{3,2,1,0:T(2,128)(2,1)}, bf16[8,80,2,512]{3,2,1,0:T(2,128)(2,1)}) custom-call(s32[1]{0:T(128)} %bitcast.slot_ref, bf16[32,80,2,512]{3,2,1,0:T(2,128)(2,1)} %bitcast.114), custom_call_target="tpu_custom_call" | custom-call | bytes 7864320 | tf_op jit(solution)/shard_map/pallas_call | solution.py:202
  30.7 4.4 %collective-permute-start.5 = (bf16[8,80,2,512]{3,2,1,0:T(2,128)(2,1)}, bf16[8,80,2,512]{3,2,1,0:T(2,128)(2,1)}, u32[]{:S(2)}, u32[]{:S(2)}) collective-permute-start(bf16[8,80,2,512]{3,2,1,0:T(2,128)(2,1)} %get-tuple-element.43), channel_id=1, source_target_pairs={{0,96},{32,64},{64,32},{96,0},{1,97},{33,65},{65,33},{97,1},{2,98}... | collective-permute-start | bytes 3932168 | tf_op jit(solution)/shard_map/ppermute | solution.py:256
  41.6 7.4 %all-to-all-start.1 = ((bf16[32,2,80,128]{3,2,1,0:T(8,128)(2,1)}), bf16[32,2,80,128]{3,2,1,0:T(8,128)(2,1)}, u32[]{:S(2)}, u32[]{:S(2)}) async-start(bf16[32,2,80,128]{3,2,1,0:T(8,128)(2,1)} %bitcast.115), calls=%async_computation.1 | async-start | bytes 2621440 | tf_op jit(solution)/shard_map/all_to_all | solution.py:252
  48.9 14.7 %shard_map.110 = (f32[2,2,80,512]{3,2,1,0:T(8,128)S(1)}, f32[2,2,80,512]{3,2,1,0:T(8,128)S(1)}) custom-call(f32[2,3,1,8192]{3,2,1,0:T(1,128)S(1)} %pad_maximum_fusion.cell_ref.value_ref.weight_ref, f32[2,3,1,8192]{3,2,1,0:T(1,128)S(1)} %pad_maximum_fusion.cell_ref.value_ref.weight_ref, f32[2,3,1,8192]{3,2,1,0:T(1,128)S(1)} %pad_maximum_fusion.cell_ref.value_ref.weight_ref), custom_call_target="tpu_custom_call" | custom-call | flops 21474836480 | bytes 1310720 | tf_op jit(solution)/shard_map/pallas_call | solution.py:77
  66.1 16.3 %collective-permute-done.5 = bf16[8,80,2,512]{3,2,1,0:T(2,128)(2,1)} collective-permute-done((bf16[8,80,2,512]{3,2,1,0:T(2,128)(2,1)}, bf16[8,80,2,512]{3,2,1,0:T(2,128)(2,1)}, u32[]{:S(2)}, u32[]{:S(2)}) %collective-permute-start.5) | collective-permute-done | bytes 1310752 | tf_op jit(solution)/shard_map/ppermute | solution.py:256
  82.3 2.7 %copy.156 = bf16[8,80,2,512]{3,1,2,0:T(8,128)(2,1)} copy(bf16[8,80,2,512]{3,2,1,0:T(2,128)(2,1)} %collective-permute-done.5) | data formatting | bytes 2621440 | tf_op jit(solution)/shard_map/layout_constraint | solution.py:260
  85.0 2.7 %copy.157 = bf16[8,80,2,512]{3,1,2,0:T(8,128)(2,1)} copy(bf16[8,80,2,512]{3,2,1,0:T(2,128)(2,1)} %collective-permute-done.2) | data formatting | bytes 2621440 | tf_op jit(solution)/shard_map/layout_constraint | solution.py:260
  87.7 5.0 %all-to-all-done.1 = bf16[32,2,80,128]{3,2,1,0:T(8,128)(2,1)} async-done(((bf16[32,2,80,128]{3,2,1,0:T(8,128)(2,1)}), bf16[32,2,80,128]{3,2,1,0:T(8,128)(2,1)}, u32[]{:S(2)}, u32[]{:S(2)}) %all-to-all-start.1) | async-done | bytes 1310752 | tf_op jit(solution)/shard_map/all_to_all | solution.py:252
  92.8 4.5 %shard_map.112 = (f32[2,2,80,512]{3,2,1,0:T(8,128)}, bf16[2,2,80,512]{3,2,1,0:T(8,128)(2,1)}) custom-call(bf16[8,4,2,80,128]{4,3,2,1,0:T(8,128)(2,1)} %bitcast.17.spread_ref, bf16[8,2,80,512]{3,2,1,0:T(8,128)(2,1)} %bitcast.106, bf16[8,2,80,512]{3,2,1,0:T(8,128)(2,1)} %bitcast.110, bf16[8,2,80,512]{3,2,1,0:T(8,128)(2,1)} %maximum_bitcast_fusion.p2, ...), custom_call_target="tpu_custom_call" | custom-call | flops 5242880 | bytes 6553600 | tf_op jit(solution)/shard_map/pallas_call | solution.py:114
  97.3 4.3 %collective-permute-start.6 = (bf16[2,2,80,512]{3,2,1,0:T(8,128)(2,1)}, bf16[2,2,80,512]{3,2,1,0:T(8,128)(2,1)S(1)}, u32[]{:S(2)}, u32[]{:S(2)}) collective-permute-start(bf16[2,2,80,512]{3,2,1,0:T(8,128)(2,1)} %get-tuple-element.45), channel_id=1, source_target_pairs={{0,32},{32,0},{64,96},{96,64},{1,33},{33,1},{65,97},{97,65},{2,34}... | collective-permute-start | bytes 983048 | tf_op jit(solution)/shard_map/ppermute | solution.py:256
  105.7 9.4 %collective-permute-done.7 = bf16[2,2,80,512]{3,2,1,0:T(8,128)(2,1)S(1)} collective-permute-done((bf16[2,2,80,512]{3,2,1,0:T(8,128)(2,1)S(1)}, bf16[2,2,80,512]{3,2,1,0:T(8,128)(2,1)S(1)}, u32[]{:S(2)}, u32[]{:S(2)}) %collective-permute-start.7) | collective-permute-done | bytes 327712 | tf_op jit(solution)/shard_map/ppermute | solution.py:256
  118.1 2.3 %shard_map.113 = bf16[8,4,2,80,128]{4,3,2,1,0:T(8,128)(2,1)S(1)} custom-call(f32[2,80,512]{2,1,0:T(8,128)S(1)} %get-tuple-element.52.sea_ref, bf16[2,2,80,512]{3,2,1,0:T(8,128)(2,1)S(1)} %multiply_convert_fusion.3.own_ref, bf16[2,2,80,512]{3,2,1,0:T(8,128)(2,1)S(1)} %collective-permute-done.8.other_ref, bf16[8,2,80,512]{3,2,1,0:T(8,128)(2,1)S(1)} %bitcast.107, ...), custom_call_target="tpu_custom_call" | custom-call | flops 5242880 | bytes 6553600 | tf_op jit(solution)/shard_map/pallas_call | solution.py:158
  120.5 22.9 %all_to_all.25 = bf16[32,2,80,128]{3,2,1,0:T(8,128)(2,1)S(1)} all-to-all(bf16[32,2,80,128]{3,2,1,0:T(8,128)(2,1)S(1)} %bitcast.112), channel_id=1, replica_groups=mesh['slot'=4,'horiz'=32] {'horiz'}, dimensions={0} | all-to-all | bytes 2621440 | tf_op jit(solution)/shard_map/all_to_all | solution.py:252
  147.2 5.7 %all-to-all-start.3 = ((bf16[32,2,32,128]{3,2,1,0:T(8,128)(2,1)}), bf16[32,2,32,128]{3,2,1,0:T(8,128)(2,1)}, u32[]{:S(2)}, u32[]{:S(2)}) async-start(bf16[32,2,32,128]{3,2,1,0:T(8,128)(2,1)} %bitcast.35), calls=%async_computation.3 | async-start | bytes 1048576 | tf_op jit(solution)/shard_map/all_to_all | solution.py:252
  158.7 2.6 %all-to-all-done.3 = bf16[32,2,32,128]{3,2,1,0:T(8,128)(2,1)} async-done(((bf16[32,2,32,128]{3,2,1,0:T(8,128)(2,1)}), bf16[32,2,32,128]{3,2,1,0:T(8,128)(2,1)}, u32[]{:S(2)}, u32[]{:S(2)}) %all-to-all-start.3) | async-done | bytes 524320 | tf_op jit(solution)/shard_map/all_to_all | solution.py:252
  161.3 5.6 %all-to-all-start.4 = ((bf16[32,2,48,128]{3,2,1,0:T(8,128)(2,1)}), bf16[32,2,48,128]{3,2,1,0:T(8,128)(2,1)}, u32[]{:S(2)}, u32[]{:S(2)}) async-start(bf16[32,2,48,128]{3,2,1,0:T(8,128)(2,1)} %bitcast.40), calls=%async_computation.4 | async-start | bytes 1572864 | tf_op jit(solution)/shard_map/all_to_all | solution.py:252
  170.4 6.3 %all-to-all-done.4 = bf16[32,2,48,128]{3,2,1,0:T(8,128)(2,1)} async-done(((bf16[32,2,48,128]{3,2,1,0:T(8,128)(2,1)}), bf16[32,2,48,128]{3,2,1,0:T(8,128)(2,1)}, u32[]{:S(2)}, u32[]{:S(2)}) %all-to-all-start.4) | async-done | bytes 786464 | tf_op jit(solution)/shard_map/all_to_all | solution.py:252
  183.3 4.9 %collective-permute-start.10 = (bf16[8,48,2,512]{3,2,1,0:T(2,128)(2,1)S(1)}, bf16[8,48,2,512]{3,2,1,0:T(2,128)(2,1)S(1)}, u32[]{:S(2)}, u32[]{:S(2)}) collective-permute-start(bf16[8,48,2,512]{3,2,1,0:T(2,128)(2,1)S(1)} %fusion.10.refs_0_), channel_id=1, source_target_pairs={{0,32},{32,0},{64,96},{96,64},{1,33},{33,1},{65,97},{97,65},{2,34}... | collective-permute-start | bytes 2359304 | tf_op jit(solution)/shard_map/ppermute | solution.py:256
  190.1 6.6 %collective-permute-done.13.refs_0_ = bf16[8,48,2,512]{3,2,1,0:T(2,128)(2,1)S(1)} collective-permute-done((bf16[8,48,2,512]{3,2,1,0:T(2,128)(2,1)S(1)}, bf16[8,48,2,512]{3,2,1,0:T(2,128)(2,1)S(1)}, u32[]{:S(2)}, u32[]{:S(2)}) %collective-permute-start.13) | collective-permute-done | bytes 786464 | tf_op jit(solution)/shard_map/ppermute | solution.py:256
  196.6 10.6 %collective-permute-start.14 = (bf16[8,48,2,512]{3,2,1,0:T(2,128)(2,1)S(1)}, bf16[8,48,2,512]{3,2,1,0:T(2,128)(2,1)S(1)}, u32[]{:S(2)}, u32[]{:S(2)}) collective-permute-start(bf16[8,48,2,512]{3,2,1,0:T(2,128)(2,1)S(1)} %collective-permute-done.13.refs_0_), channel_id=1, source_target_pairs={{0,32},{32,0},{64,96},{96,64},{1,33},{33,1},{65,97},{97,65},{2,34}... | collective-permute-start | bytes 2359304 | tf_op jit(solution)/shard_map/ppermute | solution.py:256
  208.8 4.6 %collective-permute-start.12 = (bf16[8,32,2,512]{3,2,1,0:T(2,128)(2,1)S(1)}, bf16[8,32,2,512]{3,2,1,0:T(2,128)(2,1)S(1)}, u32[]{:S(2)}, u32[]{:S(2)}) collective-permute-start(bf16[8,32,2,512]{3,2,1,0:T(2,128)(2,1)S(1)} %collective-permute-done.9.refs_2_), channel_id=1, source_target_pairs={{0,32},{32,0},{64,96},{96,64},{1,33},{33,1},{65,97},{97,65},{2,34}... | collective-permute-start | bytes 1572872 | tf_op jit(solution)/shard_map/ppermute | solution.py:256
  (112 shorter events, 54.6 us)
Async XLA Ops:
  0.0 9.9 %copy-start = (bf16[512,512]{1,0:T(8,128)(2,1)S(1)}, bf16[512,512]{1,0:T(8,128)(2,1)}, u32[]{:S(2)}) copy-start(bf16[512,512]{1,0:T(8,128)(2,1)} %param.15) | copy-start | bytes 1572868
  0.0 6.2 %copy-start.20 = (f32[16,80]{1,0:T(8,128)S(1)}, f32[16,80]{1,0:T(8,128)}, u32[]{:S(2)}) copy-start(f32[16,80]{1,0:T(8,128)} %param.14) | copy-start | bytes 15364
  2.0 10.4 %collective-permute-start = (bf16[2,80,2,512]{3,2,1,0:T(2,128)(2,1)}, bf16[2,80,2,512]{3,2,1,0:T(2,128)(2,1)S(1)}, u32[]{:S(2)}, u32[]{:S(2)}) collective-permute-start(bf16[2,80,2,512]{3,2,1,0:T(2,128)(2,1)} %get-tuple-element.32), channel_id=1, source_target_pairs={{0,64},{32,96},{64,0},{96,32},{1,65},{33,97},{65,1},{97,33},{2,66}... | collective-permute-start | bytes 983048 | tf_op jit(solution)/shard_map/ppermute | solution.py:256
  2.3 61.3 %collective-permute-start.3 = (bf16[2,80,2,512]{3,2,1,0:T(2,128)(2,1)}, bf16[2,80,2,512]{3,2,1,0:T(2,128)(2,1)S(1)}, u32[]{:S(2)}, u32[]{:S(2)}) collective-permute-start(bf16[2,80,2,512]{3,2,1,0:T(2,128)(2,1)} %get-tuple-element.41), channel_id=1, source_target_pairs={{0,64},{32,96},{64,0},{96,32},{1,65},{33,97},{65,1},{97,33},{2,66}... | collective-permute-start | bytes 983048 | tf_op jit(solution)/shard_map/ppermute | solution.py:256
  5.2 20.0 %collective-permute-start.1 = (f32[3,1,8192]{2,1,0:T(1,128)S(1)}, f32[3,1,8192]{2,1,0:T(1,128)}, u32[]{:S(2)}, u32[]{:S(2)}) collective-permute-start(f32[3,1,8192]{2,1,0:T(1,128)S(1)} %pad_maximum_fusion.1), channel_id=1, source_target_pairs={{0,64},{32,96},{64,0},{96,32},{1,65},{33,97},{65,1},{97,33},{2,66}... | collective-permute-start | bytes 294920 | tf_op jit(solution)/shard_map/ppermute | solution.py:256
  12.4 24.8 %all-to-all-start = ((bf16[32,2,80,128]{3,2,1,0:T(8,128)(2,1)}), bf16[32,2,80,128]{3,2,1,0:T(8,128)(2,1)S(1)}, u32[]{:S(2)}, u32[]{:S(2)}) async-start(bf16[32,2,80,128]{3,2,1,0:T(8,128)(2,1)} %bitcast.10), calls=%async_computation | async-start | bytes 2621440 | tf_op jit(solution)/shard_map/all_to_all | solution.py:252
  29.4 34.3 %collective-permute-start.4 = (bf16[4,80,2,512]{3,2,1,0:T(2,128)(2,1)}, bf16[4,80,2,512]{3,2,1,0:T(2,128)(2,1)}, u32[]{:S(2)}, u32[]{:S(2)}) collective-permute-start(bf16[4,80,2,512]{3,2,1,0:T(2,128)(2,1)} %get-tuple-element.42), channel_id=1, source_target_pairs={{0,64},{32,96},{64,0},{96,32},{1,65},{33,97},{65,1},{97,33},{2,66}... | collective-permute-start | bytes 1966088 | tf_op jit(solution)/shard_map/ppermute | solution.py:256
  30.7 51.6 %collective-permute-start.5 = (bf16[8,80,2,512]{3,2,1,0:T(2,128)(2,1)}, bf16[8,80,2,512]{3,2,1,0:T(2,128)(2,1)}, u32[]{:S(2)}, u32[]{:S(2)}) collective-permute-start(bf16[8,80,2,512]{3,2,1,0:T(2,128)(2,1)} %get-tuple-element.43), channel_id=1, source_target_pairs={{0,96},{32,64},{64,32},{96,0},{1,97},{33,65},{65,33},{97,1},{2,98}... | collective-permute-start | bytes 3932168 | tf_op jit(solution)/shard_map/ppermute | solution.py:256
  35.1 50.0 %collective-permute-start.2 = (bf16[8,80,2,512]{3,2,1,0:T(2,128)(2,1)}, bf16[8,80,2,512]{3,2,1,0:T(2,128)(2,1)}, u32[]{:S(2)}, u32[]{:S(2)}) collective-permute-start(bf16[8,80,2,512]{3,2,1,0:T(2,128)(2,1)} %get-tuple-element.39), channel_id=1, source_target_pairs={{0,32},{32,0},{64,96},{96,64},{1,33},{33,1},{65,97},{97,65},{2,34}... | collective-permute-start | bytes 3932168 | tf_op jit(solution)/shard_map/ppermute | solution.py:256
  41.6 51.2 %all-to-all-start.1 = ((bf16[32,2,80,128]{3,2,1,0:T(8,128)(2,1)}), bf16[32,2,80,128]{3,2,1,0:T(8,128)(2,1)}, u32[]{:S(2)}, u32[]{:S(2)}) async-start(bf16[32,2,80,128]{3,2,1,0:T(8,128)(2,1)} %bitcast.115), calls=%async_computation.1 | async-start | bytes 2621440 | tf_op jit(solution)/shard_map/all_to_all | solution.py:252
  97.3 17.8 %copy-start.10 = (f32[2,2,80,512]{3,2,1,0:T(8,128)S(1)}, f32[2,2,80,512]{3,2,1,0:T(8,128)}, u32[]{:S(2)}) copy-start(f32[2,2,80,512]{3,2,1,0:T(8,128)} %get-tuple-element.44) | copy-start | bytes 1966084
  97.3 5.8 %collective-permute-start.6 = (bf16[2,2,80,512]{3,2,1,0:T(8,128)(2,1)}, bf16[2,2,80,512]{3,2,1,0:T(8,128)(2,1)S(1)}, u32[]{:S(2)}, u32[]{:S(2)}) collective-permute-start(bf16[2,2,80,512]{3,2,1,0:T(8,128)(2,1)} %get-tuple-element.45), channel_id=1, source_target_pairs={{0,32},{32,0},{64,96},{96,64},{1,33},{33,1},{65,97},{97,65},{2,34}... | collective-permute-start | bytes 983048 | tf_op jit(solution)/shard_map/ppermute | solution.py:256
  103.0 15.0 %copy-start.4 = (bf16[8,80,2,512]{3,1,2,0:T(8,128)(2,1)S(1)}, bf16[8,80,2,512]{3,1,2,0:T(8,128)(2,1)}, u32[]{:S(2)}) copy-start(bf16[8,80,2,512]{3,1,2,0:T(8,128)(2,1)} %copy.157) | copy-start | bytes 3932164
  104.3 10.7 %collective-permute-start.7 = (bf16[2,2,80,512]{3,2,1,0:T(8,128)(2,1)S(1)}, bf16[2,2,80,512]{3,2,1,0:T(8,128)(2,1)S(1)}, u32[]{:S(2)}, u32[]{:S(2)}) collective-permute-start(bf16[2,2,80,512]{3,2,1,0:T(8,128)(2,1)S(1)} %fusion.17), channel_id=1, source_target_pairs={{0,64},{32,96},{64,0},{96,32},{1,65},{33,97},{65,1},{97,33},{2,66}... | collective-permute-start | bytes 983048 | tf_op jit(solution)/shard_map/ppermute | solution.py:256
  115.6 2.5 %collective-permute-start.8 = (bf16[2,2,80,512]{3,2,1,0:T(8,128)(2,1)S(1)}, bf16[2,2,80,512]{3,2,1,0:T(8,128)(2,1)S(1)}, u32[]{:S(2)}, u32[]{:S(2)}) collective-permute-start(bf16[2,2,80,512]{3,2,1,0:T(8,128)(2,1)S(1)} %multiply_convert_fusion.3.own_ref), channel_id=1, source_target_pairs={{0,32},{32,0},{64,96},{96,64},{1,33},{33,1},{65,97},{97,65},{2,34}... | collective-permute-start | bytes 983048 | tf_op jit(solution)/shard_map/ppermute | solution.py:256
  145.8 7.2 %copy-start.6 = (bf16[8,80,2,512]{3,2,1,0:T(2,128)(2,1)S(1)}, bf16[8,80,2,512]{3,2,1,0:T(2,128)(2,1)}, u32[]{:S(2)}) copy-start(bf16[8,80,2,512]{3,2,1,0:T(2,128)(2,1)} %copy-done.5) | copy-start | bytes 3932164
  147.2 14.1 %all-to-all-start.3 = ((bf16[32,2,32,128]{3,2,1,0:T(8,128)(2,1)}), bf16[32,2,32,128]{3,2,1,0:T(8,128)(2,1)}, u32[]{:S(2)}, u32[]{:S(2)}) async-start(bf16[32,2,32,128]{3,2,1,0:T(8,128)(2,1)} %bitcast.35), calls=%async_computation.3 | async-start | bytes 1048576 | tf_op jit(solution)/shard_map/all_to_all | solution.py:252
  161.3 15.4 %all-to-all-start.4 = ((bf16[32,2,48,128]{3,2,1,0:T(8,128)(2,1)}), bf16[32,2,48,128]{3,2,1,0:T(8,128)(2,1)}, u32[]{:S(2)}, u32[]{:S(2)}) async-start(bf16[32,2,48,128]{3,2,1,0:T(8,128)(2,1)} %bitcast.40), calls=%async_computation.4 | async-start | bytes 1572864 | tf_op jit(solution)/shard_map/all_to_all | solution.py:252
  180.6 16.0 %collective-permute-start.13 = (bf16[8,48,2,512]{3,2,1,0:T(2,128)(2,1)S(1)}, bf16[8,48,2,512]{3,2,1,0:T(2,128)(2,1)S(1)}, u32[]{:S(2)}, u32[]{:S(2)}) collective-permute-start(bf16[8,48,2,512]{3,2,1,0:T(2,128)(2,1)S(1)} %fusion.10.refs_0_), channel_id=1, source_target_pairs={{0,64},{32,96},{64,0},{96,32},{1,65},{33,97},{65,1},{97,33},{2,66}... | collective-permute-start | bytes 2359304 | tf_op jit(solution)/shard_map/ppermute | solution.py:256
  183.3 23.9 %collective-permute-start.10 = (bf16[8,48,2,512]{3,2,1,0:T(2,128)(2,1)S(1)}, bf16[8,48,2,512]{3,2,1,0:T(2,128)(2,1)S(1)}, u32[]{:S(2)}, u32[]{:S(2)}) collective-permute-start(bf16[8,48,2,512]{3,2,1,0:T(2,128)(2,1)S(1)} %fusion.10.refs_0_), channel_id=1, source_target_pairs={{0,32},{32,0},{64,96},{96,64},{1,33},{33,1},{65,97},{97,65},{2,34}... | collective-permute-start | bytes 2359304 | tf_op jit(solution)/shard_map/ppermute | solution.py:256
  188.3 19.0 %collective-permute-start.11 = (bf16[8,32,2,512]{3,2,1,0:T(2,128)(2,1)S(1)}, bf16[8,32,2,512]{3,2,1,0:T(2,128)(2,1)S(1)}, u32[]{:S(2)}, u32[]{:S(2)}) collective-permute-start(bf16[8,32,2,512]{3,2,1,0:T(2,128)(2,1)S(1)} %fusion.16.refs_1_), channel_id=1, source_target_pairs={{0,32},{32,0},{64,96},{96,64},{1,33},{33,1},{65,97},{97,65},{2,34}... | collective-permute-start | bytes 1572872 | tf_op jit(solution)/shard_map/ppermute | solution.py:256
  188.4 20.4 %collective-permute-start.9 = (bf16[8,32,2,512]{3,2,1,0:T(2,128)(2,1)S(1)}, bf16[8,32,2,512]{3,2,1,0:T(2,128)(2,1)S(1)}, u32[]{:S(2)}, u32[]{:S(2)}) collective-permute-start(bf16[8,32,2,512]{3,2,1,0:T(2,128)(2,1)S(1)} %fusion.16.refs_1_), channel_id=1, source_target_pairs={{0,64},{32,96},{64,0},{96,32},{1,65},{33,97},{65,1},{97,33},{2,66}... | collective-permute-start | bytes 1572872 | tf_op jit(solution)/shard_map/ppermute | solution.py:256
  196.6 16.7 %collective-permute-start.14 = (bf16[8,48,2,512]{3,2,1,0:T(2,128)(2,1)S(1)}, bf16[8,48,2,512]{3,2,1,0:T(2,128)(2,1)S(1)}, u32[]{:S(2)}, u32[]{:S(2)}) collective-permute-start(bf16[8,48,2,512]{3,2,1,0:T(2,128)(2,1)S(1)} %collective-permute-done.13.refs_0_), channel_id=1, source_target_pairs={{0,32},{32,0},{64,96},{96,64},{1,33},{33,1},{65,97},{97,65},{2,34}... | collective-permute-start | bytes 2359304 | tf_op jit(solution)/shard_map/ppermute | solution.py:256
  208.8 6.1 %collective-permute-start.12 = (bf16[8,32,2,512]{3,2,1,0:T(2,128)(2,1)S(1)}, bf16[8,32,2,512]{3,2,1,0:T(2,128)(2,1)S(1)}, u32[]{:S(2)}, u32[]{:S(2)}) collective-permute-start(bf16[8,32,2,512]{3,2,1,0:T(2,128)(2,1)S(1)} %collective-permute-done.9.refs_2_), channel_id=1, source_target_pairs={{0,32},{32,0},{64,96},{96,64},{1,33},{33,1},{65,97},{97,65},{2,34}... | collective-permute-start | bytes 1572872 | tf_op jit(solution)/shard_map/ppermute | solution.py:256
  (16 other events, 45.5 us)
